TPU v7x, 32 devices: a whole 2x2x4 slice. The times are simulated.
32 devices in a mesh: groups: 2 (over x), dp: 16 (over z, y, core).
Axes of the slice: x: 2, y: 2, z: 4, core: 2. Of those that a mesh axis runs over, the one named last changes fastest.
Arguments:
- embeddings: float32 [24576, 512], P(('groups', 'dp')), parts along dimension 0, as said below
- owner_index: int32 [24576], P(('groups', 'dp')), parts along dimension 0, may hold values from 0 to 15, as said below
- sub_label: int32 [24576], P(('groups', 'dp')), parts along dimension 0, may hold values from 0 to 2, as said below
- run_start: int32 [32], P('groups'), parts along dimension 0, may hold values from 0 to 15, as said below
Outputs:
- nearest: float32 [24576], P(('groups', 'dp')), parts along dimension 0
There are 2 independent parts, one for each index of `groups`. A program takes and returns all parts, laid end to end along the dimension named above; each array names one. Nothing has to cross between parts.
Inputs may be any that keep to these rules, and one draw needn't show every extreme that they name: `owner_index`: from the rows of one device at most 96 go to one owner; in every draw one owner receives exactly 96 rows from every device. From the rows of one device at most 48 with sub_label 0 go to one owner; in every draw one owner receives exactly 48 such rows from every device. Of the embeddings of one owner at most one has sub_label 3 - 1. Owners form groups of 1 to 3 consecutive indices covering all owners in order, with a group of 3 in every draw; run_start gives each owner the first index of its group. `embeddings`: finite real values.
All inputs are finite; a program needn't handle non-finite values.
Results may differ from a plain program's by a relative error of at most 0.00032.
Values may be sent and summed in bfloat16 or wider, within the bound.
No kernel may reach another device: no remote copies, remote signals or barrier semaphores. Data moves between devices by JAX's collectives and lax.ppermute only.
A program may use at most 64 MiB of HBM per device.

v0:
```python
import jax
import jax.numpy as jnp
from jax import lax
from jax.sharding import PartitionSpec as P

LABELS = 3


def passed_along(value, axis, steps):
    count = lax.axis_size(axis)
    leading, last = (max(0, -steps), min(count, count - steps))
    return lax.ppermute(value, axis, [(source, source + steps) for source in range(leading, last)])


def row_best(queries, query_tags, candidates, cand_tags, exclude_self):
    scores = lax.dot_general(
        queries, candidates, (((1,), (1,)), ((), ())), preferred_element_type=jnp.float32
    )
    matches = (query_tags[:, None] == cand_tags[None, :]) & (query_tags[:, None] > 0)
    if exclude_self:
        count = queries.shape[0]
        matches = matches & (jnp.arange(count)[:, None] != jnp.arange(count)[None, :])
    masked = jnp.where(matches, scores, jnp.float32(-1.0))
    return (jnp.max(masked, axis=1), jnp.max(masked, axis=0))


def local(embeddings, owner_index, sub_label, run_start):
    row_count = embeddings.shape[0]
    width = embeddings.shape[1]
    peer_count = lax.axis_size("dp")
    per_peer = 2 * row_count // peer_count
    capacity = peer_count * per_peer
    owners = jnp.arange(peer_count, dtype=jnp.int32)
    group_first = jnp.sum(
        jnp.where(owner_index[:, None] == owners[None, :], run_start[None, :], 0), axis=1
    )
    labels = jnp.where(sub_label == 0, group_first * LABELS, owner_index * LABELS + sub_label)
    squares = jnp.sum(embeddings * embeddings, axis=1, keepdims=True)
    unit_rows = (embeddings * lax.rsqrt(squares + 1e-06)).astype(jnp.bfloat16)
    shared = sub_label == 0
    same_owner = owner_index[:, None] == owner_index[None, :]
    same_kind = shared[:, None] == shared[None, :]
    earlier = jnp.arange(row_count)[:, None] > jnp.arange(row_count)[None, :]
    rank_kind = jnp.sum((same_owner & same_kind & earlier).astype(jnp.int32), axis=1)
    slot_index = jnp.where(shared, rank_kind, per_peer - 1 - rank_kind)
    position = owner_index * per_peer + slot_index
    outgoing = (
        jnp.zeros((capacity, width), jnp.bfloat16)
        .at[position]
        .set(unit_rows)
        .reshape(peer_count, per_peer, width)
    )
    out_tags = (
        jnp.zeros((capacity,), jnp.int32).at[position].set(labels + 1).reshape(peer_count, per_peer)
    )
    arrived, arrived_tags = (
        lax.all_to_all(outgoing, "dp", split_axis=0, concat_axis=0, tiled=True),
        lax.all_to_all(out_tags, "dp", split_axis=0, concat_axis=0, tiled=True),
    )
    mine = arrived.reshape(capacity, width)
    mine_tags = arrived_tags.reshape(capacity)
    result, unused = row_best(mine, mine_tags, mine, mine_tags, True)
    for distance in (1, 2, -1, -2):
        neighbour, neighbour_tags = passed_along((mine, mine_tags), "dp", distance)
        found, unused = row_best(mine, mine_tags, neighbour, neighbour_tags, False)
        result = jnp.maximum(result, found)
    answers = lax.all_to_all(
        result.reshape(peer_count, per_peer), "dp", split_axis=0, concat_axis=0, tiled=True
    )
    return answers.reshape(capacity)[position]


def solution(mesh):
    in_specs = (P(("groups", "dp"), None), P(("groups", "dp")), P(("groups", "dp")), P("groups"))
    out_specs = P(("groups", "dp"))
    return jax.shard_map(local, mesh=mesh, in_specs=in_specs, out_specs=out_specs, check_vma=False)
```

profile of v0, /device:TPU:0, one launch (start us, length us, event | category | flops | bytes accessed | tf_op | source)
XLA Modules:
  0.0 220.5 jit_solution(14917387983191870511)
XLA Ops:
  0.0 0.9 select_reduce_fusion.5
  1.6 1.2 convert_reduce_fusion
  3.6 1.6 multiply_reduce_fusion
  5.2 6.8 %scatter_custom_fusion.1 = bf16[1536,512]{1,0:T(8,128)(2,1)S(1)} fusion(s32[768]{0:T(1024)S(1)} %compare_select_fusion, f32[768,512]{1,0:T(8,128)S(1)} %copy-done, f32[768]{0:T(1024)S(1)} %add_rsqrt_fusion, bf16[]{:T(256)} %constant.3.clone.1), kind=kCustom, calls=%fused_computation.15 | custom fusion | flops 786432 | bytes 3149826 | tf_op jit(solution)/shard_map/scatter | solution.py:50
  12.0 43.3 %all_to_all.20 = bf16[16,96,512]{2,1,0:T(8,128)(2,1)S(1)} all-to-all(bf16[16,96,512]{2,1,0:T(8,128)(2,1)S(1)} %bitcast.12), channel_id=1, replica_groups=mesh['groups'=2,'dp'=16] {'dp'}, dimensions={0} | all-to-all | bytes 3145728 | tf_op jit(solution)/shard_map/all_to_all | solution.py:57
  55.2 1.3 collective-permute-start.7
  56.5 3.4 %scatter_custom_fusion = s32[1536]{0:T(1024)S(1)} fusion(s32[768]{0:T(1024)S(1)} %compare_select_fusion, s32[768]{0:T(1024)S(1)} %get-tuple-element.9, s32[]{:T(128)} %constant.11.clone.1), kind=kCustom, calls=%fused_computation.28 | custom fusion | bytes 6148 | tf_op jit(solution)/shard_map/scatter | solution.py:54
  60.0 35.9 %all_to_all.21 = s32[16,1,96]{2,1,0:T(1,128)S(1)} all-to-all(s32[16,1,96]{2,1,0:T(1,128)S(1)} %all_to_all.13), channel_id=1, replica_groups=mesh['groups'=2,'dp'=16] {'dp'}, dimensions={0} | all-to-all | bytes 12288 | tf_op jit(solution)/shard_map/all_to_all | solution.py:58
  97.2 1.7 collective-permute-start
  98.9 3.5 %collective-permute-start.2 = (s32[1536]{0:T(1024)S(1)}, s32[1536]{0:T(1024)S(1)}, u32[]{:S(2)}, u32[]{:S(2)}) collective-permute-start(s32[1536]{0:T(1024)S(1)} %eq.54), channel_id=1, source_target_pairs={{0,2},{1,3},{2,4},{3,5},{4,6},{5,7},{6,8},{7,9},{8,10},{9,11},{10,... | collective-permute-start | bytes 18440 | tf_op jit(solution)/shard_map/ppermute | solution.py:12
  102.5 1.3 collective-permute-start.5
  103.8 4.6 %collective-permute-start.3 = (bf16[1536,512]{1,0:T(8,128)(2,1)S(1)}, bf16[1536,512]{1,0:T(8,128)(2,1)S(1)}, u32[]{:S(2)}, u32[]{:S(2)}) collective-permute-start(bf16[1536,512]{1,0:T(8,128)(2,1)S(1)} %bitcast.15), channel_id=1, source_target_pairs={{0,2},{1,3},{2,4},{3,5},{4,6},{5,7},{6,8},{7,9},{8,10},{9,11},{10,... | collective-permute-start | bytes 4718600 | tf_op jit(solution)/shard_map/ppermute | solution.py:12
  108.5 4.4 %select_reduce_fusion.4 = f32[1536]{0:T(1024)S(1)} fusion(bf16[1536,512]{1,0:T(8,128)(2,1)S(1)} %bitcast.16, s32[1536]{0:T(1024)S(1)} %eq.54, pred[1536]{0:T(1024)(128)(4,1)S(1)} %broadcast_compare_fusion), kind=kOutput, calls=%fused_computation.7 | convolution fusion | flops 2430073344 | bytes 1586688 | tf_op jit(solution)/shard_map/dot_general | solution.py:16
  112.9 1.7 collective-permute-start.1
  114.6 4.1 %fusion.10 = f32[1536,1536]{0,1:T(8,128)S(1)} fusion(bf16[1536,512]{1,0:T(8,128)(2,1)S(1)} %bitcast.18, bf16[1536,512]{1,0:T(8,128)(2,1)} %collective-permute-done.7), kind=kOutput, calls=%fused_computation.33 | convolution fusion | flops 2415919104 | bytes 12582912 | tf_op jit(solution)/shard_map/dot_general | solution.py:16
  118.7 1.5 collective-permute-start.4
  120.2 5.1 %fusion.9 = f32[1536,1536]{0,1:T(8,128)} fusion(bf16[1536,512]{1,0:T(8,128)(2,1)S(1)} %bitcast.19, bf16[1536,512]{1,0:T(8,128)(2,1)S(1)} %collective-permute-done.5), kind=kOutput, calls=%fused_computation.32 | convolution fusion | flops 2415919104 | bytes 12582912 | tf_op jit(solution)/shard_map/dot_general | solution.py:16
  125.3 33.4 %collective-permute-done.3 = bf16[1536,512]{1,0:T(8,128)(2,1)S(1)} collective-permute-done((bf16[1536,512]{1,0:T(8,128)(2,1)S(1)}, bf16[1536,512]{1,0:T(8,128)(2,1)S(1)}, u32[]{:S(2)}, u32[]{:S(2)}) %collective-permute-start.3) | collective-permute-done | bytes 1572896 | tf_op jit(solution)/shard_map/ppermute | solution.py:12
  158.7 1.3 collective-permute-start.6
  160.0 5.1 %fusion.8 = f32[1536,1536]{0,1:T(8,128)} fusion(bf16[1536,512]{1,0:T(8,128)(2,1)S(1)} %bitcast.20, bf16[1536,512]{1,0:T(8,128)(2,1)S(1)} %collective-permute-done.3), kind=kOutput, calls=%fused_computation.31 | convolution fusion | flops 2415919104 | bytes 12582912 | tf_op jit(solution)/shard_map/dot_general | solution.py:16
  165.1 12.2 %select_reduce_fusion.3 = (f32[1536]{0:T(1024)S(1)}, f32[1536]{0:T(1024)S(1)}, f32[1536]{0:T(1024)S(1)}, f32[1536]{0:T(1024)S(1)}) fusion(s32[1536]{0:T(1024)S(1)} %eq.54, s32[1536]{0:T(1024)S(1)} %collective-permute-done, pred[1536]{0:T(1024)(128)(4,1)S(1)} %broadcast_compare_fusion, f32[1536,1536]{0,1:T(8,128)} %fusion.8, ...), kind=kOutput, calls=%fused_computation.6 | convolution fusion | flops 2453661696 | bytes 31514112 | tf_op jit(solution)/shard_map/dot_general | solution.py:16
  178.0 28.7 %all-to-all-start.2 = ((f32[16,1,96]{2,1,0:T(1,128)}), f32[16,1,96]{2,1,0:T(1,128)S(1)}, u32[]{:S(2)}, u32[]{:S(2)}) async-start(f32[16,1,96]{2,1,0:T(1,128)} %max.54), calls=%async_computation.2 | async-start | bytes 16384 | tf_op jit(solution)/shard_map/all_to_all | solution.py:67
  206.7 6.4 %all-to-all-done.2 = f32[16,1,96]{2,1,0:T(1,128)S(1)} async-done(((f32[16,1,96]{2,1,0:T(1,128)}), f32[16,1,96]{2,1,0:T(1,128)S(1)}, u32[]{:S(2)}, u32[]{:S(2)}) %all-to-all-start.2) | async-done | bytes 6176 | tf_op jit(solution)/shard_map/all_to_all | solution.py:67
  214.3 6.1 %gather_fusion = f32[768]{0:T(1024)} fusion(f32[1536]{0:T(1024)S(1)} %reshape.104, s32[1024]{0:T(1024)S(1)} %pad_clamp_fusion), kind=kCustom, calls=%fused_computation | custom fusion | bytes 9216 | tf_op jit(solution)/shard_map/gather | solution.py:70
  (23 shorter events, 4.7 us)
Async XLA Ops:
  0.0 5.2 %copy-start = (f32[768,512]{1,0:T(8,128)S(1)}, f32[768,512]{1,0:T(8,128)}, u32[]{:S(2)}) copy-start(f32[768,512]{1,0:T(8,128)} %param.4) | copy-start | bytes 4718596
  55.2 57.7 %collective-permute-start.7 = (bf16[1536,512]{1,0:T(8,128)(2,1)S(1)}, bf16[1536,512]{1,0:T(8,128)(2,1)}, u32[]{:S(2)}, u32[]{:S(2)}) collective-permute-start(bf16[1536,512]{1,0:T(8,128)(2,1)S(1)} %bitcast.13), channel_id=1, source_target_pairs={{2,0},{3,1},{4,2},{5,3},{6,4},{7,5},{8,6},{9,7},{10,8},{11,9},{12,... | collective-permute-start | bytes 4718600 | tf_op jit(solution)/shard_map/ppermute | solution.py:12
  97.2 67.8 %collective-permute-start = (s32[1536]{0:T(1024)S(1)}, s32[1536]{0:T(1024)S(1)}, u32[]{:S(2)}, u32[]{:S(2)}) collective-permute-start(s32[1536]{0:T(1024)S(1)} %eq.54), channel_id=1, source_target_pairs={{0,1},{1,2},{2,3},{3,4},{4,5},{5,6},{6,7},{7,8},{8,9},{9,10},{10,1... | collective-permute-start | bytes 18440 | tf_op jit(solution)/shard_map/ppermute | solution.py:12
  98.9 66.1 %collective-permute-start.2 = (s32[1536]{0:T(1024)S(1)}, s32[1536]{0:T(1024)S(1)}, u32[]{:S(2)}, u32[]{:S(2)}) collective-permute-start(s32[1536]{0:T(1024)S(1)} %eq.54), channel_id=1, source_target_pairs={{0,2},{1,3},{2,4},{3,5},{4,6},{5,7},{6,8},{7,9},{8,10},{9,11},{10,... | collective-permute-start | bytes 18440 | tf_op jit(solution)/shard_map/ppermute | solution.py:12
  102.5 16.2 %collective-permute-start.5 = (bf16[1536,512]{1,0:T(8,128)(2,1)S(1)}, bf16[1536,512]{1,0:T(8,128)(2,1)S(1)}, u32[]{:S(2)}, u32[]{:S(2)}) collective-permute-start(bf16[1536,512]{1,0:T(8,128)(2,1)S(1)} %bitcast.14), channel_id=1, source_target_pairs={{1,0},{2,1},{3,2},{4,3},{5,4},{6,5},{7,6},{8,7},{9,8},{10,9},{11,1... | collective-permute-start | bytes 4718600 | tf_op jit(solution)/shard_map/ppermute | solution.py:12
  103.8 54.9 %collective-permute-start.3 = (bf16[1536,512]{1,0:T(8,128)(2,1)S(1)}, bf16[1536,512]{1,0:T(8,128)(2,1)S(1)}, u32[]{:S(2)}, u32[]{:S(2)}) collective-permute-start(bf16[1536,512]{1,0:T(8,128)(2,1)S(1)} %bitcast.15), channel_id=1, source_target_pairs={{0,2},{1,3},{2,4},{3,5},{4,6},{5,7},{6,8},{7,9},{8,10},{9,11},{10,... | collective-permute-start | bytes 4718600 | tf_op jit(solution)/shard_map/ppermute | solution.py:12
  112.9 52.2 %collective-permute-start.1 = (bf16[1536,512]{1,0:T(8,128)(2,1)S(1)}, bf16[1536,512]{1,0:T(8,128)(2,1)S(1)}, u32[]{:S(2)}, u32[]{:S(2)}) collective-permute-start(bf16[1536,512]{1,0:T(8,128)(2,1)S(1)} %bitcast.17), channel_id=1, source_target_pairs={{0,1},{1,2},{2,3},{3,4},{4,5},{5,6},{6,7},{7,8},{8,9},{9,10},{10,1... | collective-permute-start | bytes 4718600 | tf_op jit(solution)/shard_map/ppermute | solution.py:12
  118.7 46.3 %collective-permute-start.4 = (s32[1536]{0:T(1024)S(1)}, s32[1536]{0:T(1024)S(1)}, u32[]{:S(2)}, u32[]{:S(2)}) collective-permute-start(s32[1536]{0:T(1024)S(1)} %eq.54), channel_id=1, source_target_pairs={{1,0},{2,1},{3,2},{4,3},{5,4},{6,5},{7,6},{8,7},{9,8},{10,9},{11,1... | collective-permute-start | bytes 18440 | tf_op jit(solution)/shard_map/ppermute | solution.py:12
  158.7 6.4 %collective-permute-start.6 = (s32[1536]{0:T(1024)S(1)}, s32[1536]{0:T(1024)S(1)}, u32[]{:S(2)}, u32[]{:S(2)}) collective-permute-start(s32[1536]{0:T(1024)S(1)} %eq.54), channel_id=1, source_target_pairs={{2,0},{3,1},{4,2},{5,3},{6,4},{7,5},{8,6},{9,7},{10,8},{11,9},{12,... | collective-permute-start | bytes 18440 | tf_op jit(solution)/shard_map/ppermute | solution.py:12
  178.0 35.1 %all-to-all-start.2 = ((f32[16,1,96]{2,1,0:T(1,128)}), f32[16,1,96]{2,1,0:T(1,128)S(1)}, u32[]{:S(2)}, u32[]{:S(2)}) async-start(f32[16,1,96]{2,1,0:T(1,128)} %max.54), calls=%async_computation.2 | async-start | bytes 16384 | tf_op jit(solution)/shard_map/all_to_all | solution.py:67
where the time goes:
time: 221 us; the launch traced here: 220 us
  blocking collectives  79.2 us (36%)
  starting transfers between devices  45.6 us (21%)
  waiting for transfers between devices  39.8 us (18%)
  matrix products  30.9 us (14%)
  other arithmetic  13.3 us (6%)
  local copies, waits for them, and re-layouts  11.5 us (5%)
    all_to_all x1, blocking collectives, local(): lax.all_to_all(outgoing, 'dp', split_axis=0, concat_axis=0, tiled=True)  43.3 us
    all_to_all x1, blocking collectives, local(): lax.all_to_all(out_tags, 'dp', split_axis=0, concat_axis=0, tiled=True)  35.9 us
    ppermute x8, waiting for transfers between devices, passed_along(): lax.ppermute(value, axis, [(source, source + steps) for source in range(l...  33.4 us
    dot_general x5, matrix products, row_best(): lax.dot_general(queries, candidates, (((1,), (1,)), ((), ())), preferred_...  30.9 us
    all_to_all x1, starting transfers between devices, local(): lax.all_to_all(result.reshape(peer_count, per_peer), 'dp', split_axis=0,...  28.7 us
    ppermute x8, starting transfers between devices, passed_along(): lax.ppermute(value, axis, [(source, source + steps) for source in range(l...  16.9 us
    scatter x1, other arithmetic, local(): outgoing = jnp.zeros((capacity, width), jnp.bfloat16).at[position].set(un...  6.79 us
    all_to_all x1, waiting for transfers between devices, local(): lax.all_to_all(result.reshape(peer_count, per_peer), 'dp', split_axis=0,...  6.39 us
  transfers between devices with their start and end apart: 9, of which 2 were waited for; matrix products, arithmetic and copies ran while one was open for 11% of the time, Pallas kernels for 0%

commit v1 on v0

v1 whole, which is shorter than its diff:
```python
import jax
import jax.numpy as jnp
from jax import lax
from jax.sharding import PartitionSpec as P

LABELS = 3
CHUNK_BYTES = 7 * 2**20


def chunk_count(rows, width, peers):
    count = 1
    while rows % (2 * count) == 0 and (rows // count) * width * 2 * peers > CHUNK_BYTES:
        count *= 2
    return count


def best_in_chunk(queries, query_tags, query_ids, candidates, cand_tags, cand_ids):
    scores = lax.dot_general(
        queries, candidates, (((1,), (1,)), ((), ())), preferred_element_type=jnp.float32
    )
    matches = (query_tags[:, None] == cand_tags[None, :]) & (
        query_ids[:, None] != cand_ids[None, :]
    )
    return jnp.max(jnp.where(matches, scores, jnp.float32(-1.0)), axis=1)


def local(embeddings, owner_index, sub_label, run_start):
    rows, width = embeddings.shape
    peers = lax.axis_size("dp")
    me = lax.axis_index("dp")
    owners = jnp.arange(peers, dtype=jnp.int32)
    group_first = jnp.sum(
        jnp.where(owner_index[:, None] == owners[None, :], run_start[None, :], 0), axis=1
    )
    tags = jnp.where(sub_label == 0, group_first * LABELS, owner_index * LABELS + sub_label)
    all_tags = lax.all_gather(tags, "dp", axis=0)
    squares = jnp.sum(embeddings * embeddings, axis=1, keepdims=True)
    unit_rows = (embeddings * lax.rsqrt(squares + 1e-06)).astype(jnp.bfloat16)
    all_ids = jnp.arange(peers * rows, dtype=jnp.int32).reshape(peers, rows)
    my_ids = me * rows + jnp.arange(rows, dtype=jnp.int32)
    chunks = chunk_count(rows, width, peers)
    size = rows // chunks

    def step(k, best):
        part = lax.dynamic_slice_in_dim(unit_rows, k * size, size, 0)
        gathered = lax.all_gather(part, "dp", axis=0, tiled=True)
        part_tags = lax.dynamic_slice_in_dim(all_tags, k * size, size, 1).reshape(-1)
        part_ids = lax.dynamic_slice_in_dim(all_ids, k * size, size, 1).reshape(-1)
        found = best_in_chunk(unit_rows, tags, my_ids, gathered, part_tags, part_ids)
        return jnp.maximum(best, found)

    best = jnp.full((rows,), -1.0, jnp.float32)
    if chunks <= 4:
        for k in range(chunks):
            best = step(k, best)
        return best
    return lax.fori_loop(0, chunks, step, best)


def solution(mesh):
    in_specs = (P(("groups", "dp"), None), P(("groups", "dp")), P(("groups", "dp")), P("groups"))
    out_specs = P(("groups", "dp"))
    return jax.shard_map(local, mesh=mesh, in_specs=in_specs, out_specs=out_specs, check_vma=False)
```

time: 221 us -> 155 us (0.70)
  blocking collectives: 79.2 us -> 23.4 us
  waiting for transfers between devices: 39.8 us -> 94.8 us
  starting transfers between devices: 45.6 us -> 0.04 us
  between operations: 0.2 us -> 13.5 us
  matrix products: 30.9 us -> 18.2 us
  local copies, waits for them, and re-layouts: 11.5 us -> 1.03 us
  other arithmetic: 13.3 us -> 3.91 us
    all_gather x0 -> x2, waiting for transfers between devices: none -> 94.1 us  [step(): gathered = lax.all_gather(part, 'dp', axis=0, tiled=True)]
    all_to_all x2 -> x0, blocking collectives: 79.2 us -> none  [the longest x1 43.3 us: local(): lax.all_to_all(outgoing, 'dp', split_axis=0, concat_axis=0, tiled=True)]
    ppermute x8 -> x0, waiting for transfers between devices: 33.4 us -> none  [passed_along(): lax.ppermute(value, axis, [(source, source + steps) for source in range(l...]
    all_to_all x1 -> x0, starting transfers between devices: 28.7 us -> none  [local(): lax.all_to_all(result.reshape(peer_count, per_peer), 'dp', split_axis=0,...]
    all_gather x0 -> x1, blocking collectives: none -> 23.4 us  [local(): all_tags = lax.all_gather(tags, 'dp', axis=0)]
    ppermute x8 -> x0, starting transfers between devices: 16.9 us -> none  [passed_along(): lax.ppermute(value, axis, [(source, source + steps) for source in range(l...]
    dot_general x5 -> x2, matrix products: 30.9 us -> 18.2 us  [best_in_chunk(): lax.dot_general(queries, candidates, (((1,), (1,)), ((), ())), preferred_...]
    scatter x1 -> x0, other arithmetic: 6.79 us -> none  [local(): outgoing = jnp.zeros((capacity, width), jnp.bfloat16).at[position].set(un...]
  transfers between devices with their start and end apart: 9 -> 2, of which waited for: 2 -> 2; matrix products, arithmetic and copies ran while one was open for 11% -> 6% of each run, Pallas kernels for 0% -> 0%
where the time goes in v1:
time: 155 us
  waiting for transfers between devices  94.8 us (61%)
  blocking collectives  23.4 us (15%)
  matrix products  18.2 us (12%)
  between operations  13.5 us (9%)
  other arithmetic  3.91 us (3%)
    all_gather x2, waiting for transfers between devices, step(): gathered = lax.all_gather(part, 'dp', axis=0, tiled=True)  94.1 us
    all_gather x1, blocking collectives, local(): all_tags = lax.all_gather(tags, 'dp', axis=0)  23.4 us
    dot_general x2, matrix products, best_in_chunk(): lax.dot_general(queries, candidates, (((1,), (1,)), ((), ())), preferred_...  18.2 us
  transfers between devices with their start and end apart: 2, of which 2 were waited for; matrix products, arithmetic and copies ran while one was open for 6% of the time, Pallas kernels for 0%

profile of v1, /device:TPU:0, one launch (start us, length us, event | category | flops | bytes accessed | tf_op | source)
XLA Modules:
  0.0 154.9 jit_solution(1708932462842006077)
XLA Ops:
  6.5 0.0 copy-start
  6.5 0.0 copy-start.2
  6.5 0.0 copy-start.1
  6.5 0.0 all-gather.5.cloned.1.call-start
  6.5 1.6 %multiply_reduce_fusion = f32[768]{0:T(1024)S(1)} fusion(f32[768,512]{1,0:T(8,128)} %param.4), kind=kLoop, calls=%fused_computation.3 | loop fusion | flops 785664 | bytes 1575936 | tf_op jit(solution)/shard_map/reduce_sum | solution.py:37
  8.2 1.6 %multiply_convert_fusion = bf16[768,512]{1,0:T(8,128)(2,1)S(1)} fusion(f32[768,512]{1,0:T(8,128)} %param.4, f32[768]{0:T(1024)S(1)} %add_rsqrt_fusion), kind=kLoop, calls=%fused_computation.2 | loop fusion | flops 786432 | bytes 2362368 | tf_op jit(solution)/shard_map/convert_element_type | solution.py:38
  9.8 1.0 fusion
  10.8 0.0 all-gather.5.cloned.1.call-update
  10.8 0.0 all-gather.7.cloned.1.call-start
  10.8 0.7 all-gather.7.cloned.1.call-update
  11.5 0.0 copy-done
  11.5 0.0 copy-done.2
  11.6 0.1 select_reduce_fusion.2
  11.6 0.0 copy-done.1
  11.7 23.4 %all-gather.1 = s32[16,1,768]{2,1,0:T(1,128)S(1)} all-gather(s32[1,1,768]{2,1,0:T(1,128)S(1)} %reshape.32), channel_id=2, replica_groups=mesh['groups'=2,'dp'=16] {'dp'}, dimensions={0}, use_global_device_ids=true | all-gather | bytes 52224 | tf_op jit(solution)/shard_map/all_gather | solution.py:36
  35.1 40.4 %all-gather.5.cloned.1.call-done = bf16[6144,512]{1,0:T(8,128)(2,1)} async-done(((bf16[384,512]{1,0:T(8,128)(2,1)}), bf16[6144,512]{1,0:T(8,128)(2,1)}) %all-gather.5.cloned.1.call-update) | async-done | bytes 6291472 | tf_op jit(solution)/shard_map/all_gather | solution.py:46
  75.6 9.1 %select_reduce_fusion.1 = f32[768]{0:T(1024)S(1)} fusion(s32[6144]{0:T(1024)S(1)} %ne.29, s32[6144]{0:T(1024)S(1)} %eq.53, s32[768]{0:T(1024)S(1)} %get-tuple-element.11, s32[768]{0:T(1024)S(1)} %get-tuple-element.12, bf16[768,512]{1,0:T(8,128)(2,1)S(1)} %multiply_convert_fusion, bf16[6144,512]{1,0:T(8,128)(2,1)} %all-gather.5.cloned.1.call-done), kind=kOutput, calls=%fused_computation.1 | convolution fusion | flops 4855430144 | bytes 7136256 | tf_op jit(solution)/shard_map/dot_general | solution.py:18
  84.7 53.7 %all-gather.7.cloned.1.call-done = bf16[6144,512]{1,0:T(8,128)(2,1)} async-done(((bf16[384,512]{1,0:T(8,128)(2,1)}), bf16[6144,512]{1,0:T(8,128)(2,1)}) %all-gather.7.cloned.1.call-update) | async-done | bytes 6291472 | tf_op jit(solution)/shard_map/all_gather | solution.py:46
  138.3 9.1 %select_reduce_fusion = f32[768]{0:T(1024)S(1)} fusion(s32[6144]{0:T(1024)S(1)} %ne.32, s32[6144]{0:T(1024)S(1)} %eq.56, s32[768]{0:T(1024)S(1)} %get-tuple-element.11, s32[768]{0:T(1024)S(1)} %get-tuple-element.12, bf16[768,512]{1,0:T(8,128)(2,1)S(1)} %multiply_convert_fusion, bf16[6144,512]{1,0:T(8,128)(2,1)} %all-gather.7.cloned.1.call-done), kind=kOutput, calls=%fused_computation | convolution fusion | flops 4855430144 | bytes 7136256 | tf_op jit(solution)/shard_map/dot_general | solution.py:18
  147.4 0.6 maximum_maximum_fusion
  (11 shorter events, 0.1 us)
Async XLA Ops:
  6.5 5.0 %copy-start = (s32[768]{0:T(1024)S(1)}, s32[768]{0:T(1024)}, u32[]{:S(2)}) copy-start(s32[768]{0:T(1024)} %param.5) | copy-start | bytes 9220
  6.5 5.0 %copy-start.2 = (s32[16]{0:T(128)S(1)}, s32[16]{0:T(128)}, u32[]{:S(2)}) copy-start(s32[16]{0:T(128)} %param.7) | copy-start | bytes 196
  6.5 5.1 %copy-start.1 = (s32[768]{0:T(1024)S(1)}, s32[768]{0:T(1024)}, u32[]{:S(2)}) copy-start(s32[768]{0:T(1024)} %param.6) | copy-start | bytes 9220
  6.5 69.0 %all-gather.5.cloned.1.call-start = ((), (), s32[]{:S(2)}) async-start(), calls=%async_computation | async-start | bytes 6684672 | tf_op jit(solution)/shard_map/all_gather | solution.py:46
  10.8 127.6 %all-gather.7.cloned.1.call-start = ((), (), s32[]{:S(2)}) async-start(), calls=%async_computation.1 | async-start | bytes 6684672 | tf_op jit(solution)/shard_map/all_gather | solution.py:46
Sparse Core Ops, SparseCore 0:
  10.9 64.6 all-gather.4
  77.9 60.4 all-gather.6

commit v2 on v1

v2 whole, which is shorter than its diff:
```python
import functools

import jax
import jax.numpy as jnp
from jax import lax
from jax.experimental import pallas as pl
from jax.experimental.pallas import tpu as pltpu
from jax.sharding import PartitionSpec as P

LABELS = 3
PLANE = 4
PAD = 16
BASE = 64.0
TILE = 256
VMEM_LIMIT = 24 * 2**20


def whole(count):
    return [pl.BlockSpec(memory_space=pltpu.VMEM)] * count


def params():
    return pltpu.CompilerParams(vmem_limit_bytes=VMEM_LIMIT)


def pack_kernel(rows, embeddings_ref, tags_ref, block_ref):
    values = embeddings_ref[...]
    squares = jnp.sum(values * values, axis=1, keepdims=True)
    block_ref[0:rows, :] = (values * lax.rsqrt(squares + 1e-06)).astype(jnp.bfloat16)
    block_ref[rows : rows + PAD, :] = tags_ref[...].astype(jnp.bfloat16)


def tag_lanes(block_ref, rows):
    width = block_ref.shape[1]
    count = -(-rows // width)
    tail = block_ref[rows : rows + PAD, :].astype(jnp.float32)
    parts = [tail[2 * n : 2 * n + 1] * BASE + tail[2 * n + 1 : 2 * n + 2] for n in range(count)]
    return jnp.concatenate(parts, axis=1)[:, :rows]


def tag_columns(block_ref, rows):
    return jnp.transpose(jnp.broadcast_to(tag_lanes(block_ref, rows), (128, rows)))


def scores(rows_ref, lanes_ref, rows, first):
    return lax.dot_general(
        rows_ref[0:rows, :],
        lanes_ref[first : first + TILE, :],
        (((1,), (1,)), ((), ())),
        preferred_element_type=jnp.float32,
    )


def fold_sublanes(values):
    rows, lanes = values.shape
    return jnp.max(values.reshape(rows // 8, 8, lanes), axis=0)


def fold_lanes(values):
    return jnp.max(jnp.transpose(values), axis=0, keepdims=True)


def plane_kernel(rows, own_ref, *refs):
    others, best_ref = refs[:-1], refs[-1]
    own_tags = tag_lanes(own_ref, rows)
    for first in range(0, rows, TILE):
        lane_tags = own_tags[:, first : first + TILE]
        best = jnp.full((8, TILE), -1.0, jnp.float32)
        for which, block_ref in enumerate((own_ref,) + others):
            found = scores(block_ref, own_ref, rows, first)
            columns = tag_columns(block_ref, rows)
            match = jnp.concatenate([columns] * (TILE // 128), axis=1) == lane_tags
            if which == 0:
                row_id = lax.broadcasted_iota(jnp.int32, (rows, TILE), 0)
                lane_id = lax.broadcasted_iota(jnp.int32, (rows, TILE), 1) + first
                match = match & (row_id != lane_id)
            best = jnp.maximum(best, fold_sublanes(jnp.where(match, found, -1.0)))
        best_ref[:, first : first + TILE] = jnp.max(best, axis=0, keepdims=True)


def cross_kernel(rows, count, away_ref, *refs):
    blocks = refs[:count]
    away_best_ref, plane_best_ref = refs[count:]
    away_tags = tag_lanes(away_ref, rows)
    best = [jnp.full((8, TILE), -1.0, jnp.float32) for _ in range(0, rows, TILE)]
    for which, block_ref in enumerate(blocks):
        columns = tag_columns(block_ref, rows)
        wide = jnp.concatenate([columns] * (TILE // 128), axis=1)
        row_best = jnp.full((rows, 128), -1.0, jnp.float32)
        for n, first in enumerate(range(0, rows, TILE)):
            found = scores(block_ref, away_ref, rows, first)
            masked = jnp.where(wide == away_tags[:, first : first + TILE], found, -1.0)
            best[n] = jnp.maximum(best[n], fold_sublanes(masked))
            for lane in range(0, TILE, 128):
                row_best = jnp.maximum(row_best, masked[:, lane : lane + 128])
        plane_best_ref[which : which + 1, :] = fold_lanes(row_best)
    for n, first in enumerate(range(0, rows, TILE)):
        away_best_ref[:, first : first + TILE] = jnp.max(best[n], axis=0, keepdims=True)


def cost(pairs, rows, width):
    return pl.CostEstimate(
        flops=2 * pairs * rows * rows * width,
        bytes_accessed=5 * rows * width * 2,
        transcendentals=0,
    )


def plane_steps(planes):
    steps = []
    for distance in range(1, planes // 2 + 1):
        if 2 * distance < planes:
            steps.append([(z, (z + distance) % planes) for z in range(planes)])
        else:
            steps.append(
                [(z, z + distance) if z % 2 == 0 else (z + distance, z) for z in range(distance)]
            )
    return steps


def local(embeddings, owner_index, sub_label, run_start):
    rows, width = embeddings.shape
    peers = lax.axis_size("dp")
    planes = peers // PLANE
    me = lax.axis_index("dp")
    owners = jnp.arange(peers, dtype=jnp.int32)
    group_first = jnp.sum(
        jnp.where(owner_index[:, None] == owners[None, :], run_start[None, :], 0), axis=1
    )
    tags = 1 + jnp.where(sub_label == 0, group_first * LABELS, owner_index * LABELS + sub_label)
    base = int(BASE)
    padded = jnp.pad(tags, (0, -rows % width)).reshape(-1, width)
    digits = jnp.stack([padded // base, padded % base], axis=1).reshape(-1, width)
    digits = jnp.pad(digits, ((0, PAD - digits.shape[0]), (0, 0))).astype(jnp.float32)
    block = pl.pallas_call(
        functools.partial(pack_kernel, rows),
        out_shape=jax.ShapeDtypeStruct((rows + PAD, width), jnp.bfloat16),
        in_specs=whole(2),
        out_specs=pl.BlockSpec(memory_space=pltpu.VMEM),
        compiler_params=params(),
        name="pack",
    )(embeddings, digits)

    away = []
    for step in plane_steps(planes):
        pairs = [(s * PLANE + j, t * PLANE + j) for s, t in step for j in range(PLANE)]
        away.append((pairs, lax.ppermute(block, "dp", pairs)))
    mates = [
        lax.ppermute(block, "dp", [(i, i ^ m) for i in range(peers)]) for m in (2, 3, 1)
    ]
    best = pl.pallas_call(
        functools.partial(plane_kernel, rows),
        out_shape=jax.ShapeDtypeStruct((1, rows), jnp.float32),
        in_specs=whole(PLANE),
        out_specs=pl.BlockSpec(memory_space=pltpu.VMEM),
        compiler_params=params(),
        cost_estimate=cost(PLANE, rows, width),
        name="plane",
    )(block, *mates)
    plane_best = None
    for pairs, received in away:
        away_best, found = pl.pallas_call(
            functools.partial(cross_kernel, rows, PLANE),
            out_shape=(
                jax.ShapeDtypeStruct((1, rows), jnp.float32),
                jax.ShapeDtypeStruct((PLANE, rows), jnp.float32),
            ),
            in_specs=whole(1 + PLANE),
            out_specs=tuple(whole(2)),
            compiler_params=params(),
            cost_estimate=cost(PLANE, rows, width),
            name="cross",
        )(received, block, *mates)
        back = lax.ppermute(away_best, "dp", [(t, s) for s, t in pairs])
        if len(pairs) < peers:
            half = planes // 2
            z = me // PLANE
            sent = ((z % half) % 2 == 0) == (z < half)
            back = jnp.where(sent, back, -1.0)
        best = jnp.maximum(best, back)
        plane_best = found if plane_best is None else jnp.maximum(plane_best, found)
    best = jnp.maximum(best, plane_best[0:1])
    for n, m in enumerate((2, 3, 1)):
        back = lax.ppermute(plane_best[n + 1 : n + 2], "dp", [(i, i ^ m) for i in range(peers)])
        best = jnp.maximum(best, back)
    return best.reshape(rows)


def solution(mesh):
    in_specs = (P(("groups", "dp"), None), P(("groups", "dp")), P(("groups", "dp")), P("groups"))
    out_specs = P(("groups", "dp"))
    return jax.shard_map(local, mesh=mesh, in_specs=in_specs, out_specs=out_specs, check_vma=False)
```

time: 155 us -> 59.7 us (0.39)
  waiting for transfers between devices: 94.8 us -> 28.1 us
  blocking collectives: 23.4 us -> 0 us
  matrix products: 18.2 us -> 0 us
  starting transfers between devices: 0.04 us -> 16.9 us
  between operations: 13.5 us -> 0.12 us
  Pallas kernels: 0 us -> 10.6 us
  other arithmetic: 3.91 us -> 2.17 us
    all_gather x2 -> x0, waiting for transfers between devices: 94.1 us -> none  [step(): gathered = lax.all_gather(part, 'dp', axis=0, tiled=True)]
    ppermute x0 -> x10, waiting for transfers between devices: none -> 28.1 us  [the longest x3 14.7 us: local(): lax.ppermute(block, 'dp', [(i, i ^ m) for i in range(peers)])]
    all_gather x1 -> x0, blocking collectives: 23.4 us -> none  [local(): all_tags = lax.all_gather(tags, 'dp', axis=0)]
    dot_general x2 -> x0, matrix products: 18.2 us -> none  [best_in_chunk(): lax.dot_general(queries, candidates, (((1,), (1,)), ((), ())), preferred_...]
    ppermute x0 -> x10, starting transfers between devices: none -> 16.9 us  [the longest x2 8.49 us: local(): away.append((pairs, lax.ppermute(block, 'dp', pairs)))]
    pallas_call x0 -> x4, Pallas kernels: none -> 10.6 us  [the longest x2 7.79 us: local(): pl.pallas_call(functools.partial(cross_kernel, rows, PLANE), out_shape=(j...]
    reduce_sum x1 -> x0, other arithmetic: 1.63 us -> none  [local(): squares = jnp.sum(embeddings * embeddings, axis=1, keepdims=True)]
    convert_element_type x1, other arithmetic: 1.58 us -> 0.01 us  [local(): jnp.pad(digits, ((0, PAD - digits.shape[0]), (0, 0))).astype(jnp.float32)]
  transfers between devices with their start and end apart: 2 -> 10, of which waited for: 2 -> 3; matrix products, arithmetic and copies ran while one was open for 6% -> 0% of each run, Pallas kernels for 0% -> 11%
where the time goes in v2:
time: 59.7 us; the launch traced here: 59.4 us
  waiting for transfers between devices  28.1 us (47%)
  starting transfers between devices  16.9 us (28%)
  Pallas kernels  10.6 us (18%)
  other arithmetic  2.17 us (4%)
  local copies, waits for them, and re-layouts  1.43 us (2%)
    ppermute x3, waiting for transfers between devices, local(): lax.ppermute(block, 'dp', [(i, i ^ m) for i in range(peers)])  14.7 us
    ppermute x2, waiting for transfers between devices, local(): away.append((pairs, lax.ppermute(block, 'dp', pairs)))  13.3 us
    ppermute x2, starting transfers between devices, local(): away.append((pairs, lax.ppermute(block, 'dp', pairs)))  8.49 us
    pallas_call x2, Pallas kernels, local(): pl.pallas_call(functools.partial(cross_kernel, rows, PLANE), out_shape=(j...  7.79 us
    ppermute x2, starting transfers between devices, local(): back = lax.ppermute(away_best, 'dp', [(t, s) for s, t in pairs])  3.72 us
    pallas_call x1, Pallas kernels, local(): pl.pallas_call(functools.partial(plane_kernel, rows), out_shape=jax.Shape...  2.64 us
    ppermute x3, starting transfers between devices, local(): lax.ppermute(plane_best[n + 1:n + 2], 'dp', [(i, i ^ m) for i in range(pe...  2.55 us
    ppermute x3, starting transfers between devices, local(): lax.ppermute(block, 'dp', [(i, i ^ m) for i in range(peers)])  2.14 us
  transfers between devices with their start and end apart: 10, of which 3 were waited for; matrix products, arithmetic and copies ran while one was open for 0% of the time, Pallas kernels for 11%

profile of v2, /device:TPU:0, one launch (start us, length us, event | category | flops | bytes accessed | tf_op | source)
XLA Modules:
  0.0 59.4 jit_solution(15132400675970404495)
XLA Ops:
  0.0 0.8 %select_reduce_fusion = s32[768]{0:T(1024)S(1)} fusion(s32[16]{0:T(128)} %param.7, s32[768]{0:T(1024)} %param.5), kind=kLoop, calls=%fused_computation | loop fusion | flops 36096 | bytes 6208 | tf_op jit(solution)/shard_map/reduce_sum | solution.py:127
  0.8 0.7 %select_add_fusion = s32[768]{0:T(1024)S(1)} fusion(s32[768]{0:T(1024)} %param.6, s32[768]{0:T(1024)} %param.5, s32[768]{0:T(1024)S(1)} %select_reduce_fusion), kind=kLoop, calls=%fused_computation.10 | loop fusion | flops 4608 | bytes 12288 | tf_op jit(solution)/shard_map/add | solution.py:130
  1.6 0.0 copy-start
  1.6 1.4 %copy-done = f32[768,512]{1,0:T(8,128)S(1)} copy-done((f32[768,512]{1,0:T(8,128)S(1)}, f32[768,512]{1,0:T(8,128)}, u32[]{:S(2)}) %copy-start) | copy-done | bytes 1572888
  3.0 0.2 pack.1.own_ref.refs_0_
  3.2 3.1 %collective-permute-start.3 = (bf16[784,512]{1,0:T(8,128)(2,1)S(1)}, bf16[784,512]{1,0:T(8,128)(2,1)}, u32[]{:S(2)}, u32[]{:S(2)}) collective-permute-start(bf16[784,512]{1,0:T(8,128)(2,1)S(1)} %pack.1.own_ref.refs_0_), channel_id=1, source_target_pairs={{0,4},{1,5},{2,6},{3,7},{4,8},{5,9},{6,10},{7,11},{8,12},{9,13},{1... | collective-permute-start | bytes 2408456 | tf_op jit(solution)/shard_map/ppermute | solution.py:147
  6.3 1.5 %collective-permute-start = (bf16[784,512]{1,0:T(8,128)(2,1)S(1)}, bf16[784,512]{1,0:T(8,128)(2,1)S(1)}, u32[]{:S(2)}, u32[]{:S(2)}) collective-permute-start(bf16[784,512]{1,0:T(8,128)(2,1)S(1)} %pack.1.own_ref.refs_0_), channel_id=1, source_target_pairs={{0,2},{1,3},{2,0},{3,1},{4,6},{5,7},{6,4},{7,5},{8,10},{9,11},{10,... | collective-permute-start | bytes 2408456 | tf_op jit(solution)/shard_map/ppermute | solution.py:149
  7.8 0.0 collective-permute-start.1
  7.8 0.6 %collective-permute-start.2 = (bf16[784,512]{1,0:T(8,128)(2,1)S(1)}, bf16[784,512]{1,0:T(8,128)(2,1)S(1)}, u32[]{:S(2)}, u32[]{:S(2)}) collective-permute-start(bf16[784,512]{1,0:T(8,128)(2,1)S(1)} %pack.1.own_ref.refs_0_), channel_id=1, source_target_pairs={{0,1},{1,0},{2,3},{3,2},{4,5},{5,4},{6,7},{7,6},{8,9},{9,8},{10,11... | collective-permute-start | bytes 2408456 | tf_op jit(solution)/shard_map/ppermute | solution.py:149
  8.4 5.4 %collective-permute-start.5 = (bf16[784,512]{1,0:T(8,128)(2,1)S(1)}, bf16[784,512]{1,0:T(8,128)(2,1)}, u32[]{:S(2)}, u32[]{:S(2)}) collective-permute-start(bf16[784,512]{1,0:T(8,128)(2,1)S(1)} %pack.1.own_ref.refs_0_), channel_id=1, source_target_pairs={{0,8},{1,9},{2,10},{3,11},{12,4},{13,5},{14,6},{15,7},{16,24},{17,... | collective-permute-start | bytes 2408456 | tf_op jit(solution)/shard_map/ppermute | solution.py:147
  13.8 13.3 %collective-permute-done.3.away_ref = bf16[784,512]{1,0:T(8,128)(2,1)} collective-permute-done((bf16[784,512]{1,0:T(8,128)(2,1)S(1)}, bf16[784,512]{1,0:T(8,128)(2,1)}, u32[]{:S(2)}, u32[]{:S(2)}) %collective-permute-start.3) | collective-permute-done | bytes 802848 | tf_op jit(solution)/shard_map/ppermute | solution.py:147
  27.1 0.0 collective-permute-done.refs_0_.refs_1_
  27.1 14.7 %collective-permute-done.1.refs_1_.refs_2_ = bf16[784,512]{1,0:T(8,128)(2,1)S(1)} collective-permute-done((bf16[784,512]{1,0:T(8,128)(2,1)S(1)}, bf16[784,512]{1,0:T(8,128)(2,1)S(1)}, u32[]{:S(2)}, u32[]{:S(2)}) %collective-permute-start.1) | collective-permute-done | bytes 802848 | tf_op jit(solution)/shard_map/ppermute | solution.py:149
  41.9 0.0 collective-permute-done.2.refs_2_.refs_3_
  41.9 3.9 %cross.2 = (f32[1,768]{1,0:T(1,128)S(1)}, f32[4,768]{1,0:T(4,128)S(1)}) custom-call(bf16[784,512]{1,0:T(8,128)(2,1)} %collective-permute-done.3.away_ref, bf16[784,512]{1,0:T(8,128)(2,1)S(1)} %pack.1.own_ref.refs_0_, bf16[784,512]{1,0:T(8,128)(2,1)S(1)} %collective-permute-done.refs_0_.refs_1_, bf16[784,512]{1,0:T(8,128)(2,1)S(1)} %collective-permute-done.1.refs_1_.refs_2_, ...), custom_call_target="tpu_custom_call" | custom-call | flops 2415919104 | bytes 3932160 | tf_op jit(solution)/shard_map/cross/pallas_call | solution.py:162
  45.8 3.9 %cross.3 = (f32[1,768]{1,0:T(1,128)S(1)}, f32[4,768]{1,0:T(4,128)S(1)}) custom-call(bf16[784,512]{1,0:T(8,128)(2,1)} %collective-permute-done.5.away_ref, bf16[784,512]{1,0:T(8,128)(2,1)S(1)} %pack.1.own_ref.refs_0_, bf16[784,512]{1,0:T(8,128)(2,1)S(1)} %collective-permute-done.refs_0_.refs_1_, bf16[784,512]{1,0:T(8,128)(2,1)S(1)} %collective-permute-done.1.refs_1_.refs_2_, ...), custom_call_target="tpu_custom_call" | custom-call | flops 2415919104 | bytes 3932160 | tf_op jit(solution)/shard_map/cross/pallas_call | solution.py:162
  49.7 0.8 %collective-permute-start.9 = (f32[1,768]{1,0:T(1,128)S(1)}, f32[1,768]{1,0:T(1,128)S(1)}, u32[]{:S(2)}, u32[]{:S(2)}) collective-permute-start(f32[1,768]{1,0:T(1,128)S(1)} %get-tuple-element.16), channel_id=1, source_target_pairs={{0,1},{1,0},{2,3},{3,2},{4,5},{5,4},{6,7},{7,6},{8,9},{9,8},{10,11... | collective-permute-start | bytes 9224 | tf_op jit(solution)/shard_map/ppermute | solution.py:184
  50.6 1.2 %collective-permute-start.8 = (f32[1,768]{1,0:T(1,128)S(1)}, f32[1,768]{1,0:T(1,128)S(1)}, u32[]{:S(2)}, u32[]{:S(2)}) collective-permute-start(f32[1,768]{1,0:T(1,128)S(1)} %get-tuple-element.17), channel_id=1, source_target_pairs={{0,3},{1,2},{2,1},{3,0},{4,7},{5,6},{6,5},{7,4},{8,11},{9,10},{10,... | collective-permute-start | bytes 9224 | tf_op jit(solution)/shard_map/ppermute | solution.py:184
  51.8 0.5 collective-permute-start.7
  52.3 1.3 %collective-permute-start.6 = (f32[1,768]{1,0:T(1,128)S(1)}, f32[1,768]{1,0:T(1,128)S(1)}, u32[]{:S(2)}, u32[]{:S(2)}) collective-permute-start(f32[1,768]{1,0:T(1,128)S(1)} %get-tuple-element.10), channel_id=1, source_target_pairs={{8,0},{9,1},{10,2},{11,3},{4,12},{5,13},{6,14},{7,15},{24,16},{25,... | collective-permute-start | bytes 9224 | tf_op jit(solution)/shard_map/ppermute | solution.py:174
  53.6 2.4 %collective-permute-start.4 = (f32[1,768]{1,0:T(1,128)S(1)}, f32[1,768]{1,0:T(1,128)S(1)}, u32[]{:S(2)}, u32[]{:S(2)}) collective-permute-start(f32[1,768]{1,0:T(1,128)S(1)} %get-tuple-element.9), channel_id=1, source_target_pairs={{4,0},{5,1},{6,2},{7,3},{8,4},{9,5},{10,6},{11,7},{12,8},{13,9},{1... | collective-permute-start | bytes 9224 | tf_op jit(solution)/shard_map/ppermute | solution.py:174
  56.0 2.6 %plane.1 = f32[1,768]{1,0:T(1,128)S(1)} custom-call(bf16[784,512]{1,0:T(8,128)(2,1)S(1)} %pack.1.own_ref.refs_0_, bf16[784,512]{1,0:T(8,128)(2,1)S(1)} %collective-permute-done.refs_0_.refs_1_, bf16[784,512]{1,0:T(8,128)(2,1)S(1)} %collective-permute-done.1.refs_1_.refs_2_, bf16[784,512]{1,0:T(8,128)(2,1)S(1)} %collective-permute-done.2.refs_2_.refs_3_), custom_call_target="tpu_custom_call" | custom-call | flops 2415919104 | bytes 3932160 | tf_op jit(solution)/shard_map/plane/pallas_call | solution.py:151
  58.7 0.1 collective-permute-done.4
  58.8 0.6 %maximum_reduce_fusion = f32[768]{0:T(1024)} fusion(f32[1,768]{1,0:T(1,128)S(1)} %collective-permute-done.9, f32[1,768]{1,0:T(1,128)S(1)} %collective-permute-done.8, f32[1,768]{1,0:T(1,128)S(1)} %collective-permute-done.7, f32[4,768]{1,0:T(4,128)S(1)} %max.23, f32[1,768]{1,0:T(1,128)S(1)} %collective-permute-done.6, pred[]{:T(512)S(6)} %eq.36, ...), kind=kLoop, calls=%fused_computation.14 | loop fusion | flops 5376 | bytes 24577 | tf_op jit(solution)/shard_map/max | solution.py:185
  (13 shorter events, 0.1 us)
Async XLA Ops:
  1.6 1.4 %copy-start = (f32[768,512]{1,0:T(8,128)S(1)}, f32[768,512]{1,0:T(8,128)}, u32[]{:S(2)}) copy-start(f32[768,512]{1,0:T(8,128)} %embeddings_ref.1) | copy-start | bytes 4718596
  3.2 23.9 %collective-permute-start.3 = (bf16[784,512]{1,0:T(8,128)(2,1)S(1)}, bf16[784,512]{1,0:T(8,128)(2,1)}, u32[]{:S(2)}, u32[]{:S(2)}) collective-permute-start(bf16[784,512]{1,0:T(8,128)(2,1)S(1)} %pack.1.own_ref.refs_0_), channel_id=1, source_target_pairs={{0,4},{1,5},{2,6},{3,7},{4,8},{5,9},{6,10},{7,11},{8,12},{9,13},{1... | collective-permute-start | bytes 2408456 | tf_op jit(solution)/shard_map/ppermute | solution.py:147
  6.3 20.9 %collective-permute-start = (bf16[784,512]{1,0:T(8,128)(2,1)S(1)}, bf16[784,512]{1,0:T(8,128)(2,1)S(1)}, u32[]{:S(2)}, u32[]{:S(2)}) collective-permute-start(bf16[784,512]{1,0:T(8,128)(2,1)S(1)} %pack.1.own_ref.refs_0_), channel_id=1, source_target_pairs={{0,2},{1,3},{2,0},{3,1},{4,6},{5,7},{6,4},{7,5},{8,10},{9,11},{10,... | collective-permute-start | bytes 2408456 | tf_op jit(solution)/shard_map/ppermute | solution.py:149
  7.8 34.1 %collective-permute-start.1 = (bf16[784,512]{1,0:T(8,128)(2,1)S(1)}, bf16[784,512]{1,0:T(8,128)(2,1)S(1)}, u32[]{:S(2)}, u32[]{:S(2)}) collective-permute-start(bf16[784,512]{1,0:T(8,128)(2,1)S(1)} %pack.1.own_ref.refs_0_), channel_id=1, source_target_pairs={{0,3},{1,2},{2,1},{3,0},{4,7},{5,6},{6,5},{7,4},{8,11},{9,10},{10,... | collective-permute-start | bytes 2408456 | tf_op jit(solution)/shard_map/ppermute | solution.py:149
  7.8 34.1 %collective-permute-start.2 = (bf16[784,512]{1,0:T(8,128)(2,1)S(1)}, bf16[784,512]{1,0:T(8,128)(2,1)S(1)}, u32[]{:S(2)}, u32[]{:S(2)}) collective-permute-start(bf16[784,512]{1,0:T(8,128)(2,1)S(1)} %pack.1.own_ref.refs_0_), channel_id=1, source_target_pairs={{0,1},{1,0},{2,3},{3,2},{4,5},{5,4},{6,7},{7,6},{8,9},{9,8},{10,11... | collective-permute-start | bytes 2408456 | tf_op jit(solution)/shard_map/ppermute | solution.py:149
  8.4 37.4 %collective-permute-start.5 = (bf16[784,512]{1,0:T(8,128)(2,1)S(1)}, bf16[784,512]{1,0:T(8,128)(2,1)}, u32[]{:S(2)}, u32[]{:S(2)}) collective-permute-start(bf16[784,512]{1,0:T(8,128)(2,1)S(1)} %pack.1.own_ref.refs_0_), channel_id=1, source_target_pairs={{0,8},{1,9},{2,10},{3,11},{12,4},{13,5},{14,6},{15,7},{16,24},{17,... | collective-permute-start | bytes 2408456 | tf_op jit(solution)/shard_map/ppermute | solution.py:147
  49.7 8.9 %collective-permute-start.9 = (f32[1,768]{1,0:T(1,128)S(1)}, f32[1,768]{1,0:T(1,128)S(1)}, u32[]{:S(2)}, u32[]{:S(2)}) collective-permute-start(f32[1,768]{1,0:T(1,128)S(1)} %get-tuple-element.16), channel_id=1, source_target_pairs={{0,1},{1,0},{2,3},{3,2},{4,5},{5,4},{6,7},{7,6},{8,9},{9,8},{10,11... | collective-permute-start | bytes 9224 | tf_op jit(solution)/shard_map/ppermute | solution.py:184
  50.6 8.1 %collective-permute-start.8 = (f32[1,768]{1,0:T(1,128)S(1)}, f32[1,768]{1,0:T(1,128)S(1)}, u32[]{:S(2)}, u32[]{:S(2)}) collective-permute-start(f32[1,768]{1,0:T(1,128)S(1)} %get-tuple-element.17), channel_id=1, source_target_pairs={{0,3},{1,2},{2,1},{3,0},{4,7},{5,6},{6,5},{7,4},{8,11},{9,10},{10,... | collective-permute-start | bytes 9224 | tf_op jit(solution)/shard_map/ppermute | solution.py:184
  51.8 6.9 %collective-permute-start.7 = (f32[1,768]{1,0:T(1,128)S(1)}, f32[1,768]{1,0:T(1,128)S(1)}, u32[]{:S(2)}, u32[]{:S(2)}) collective-permute-start(f32[1,768]{1,0:T(1,128)S(1)} %get-tuple-element.15), channel_id=1, source_target_pairs={{0,2},{1,3},{2,0},{3,1},{4,6},{5,7},{6,4},{7,5},{8,10},{9,11},{10,... | collective-permute-start | bytes 9224 | tf_op jit(solution)/shard_map/ppermute | solution.py:184
  52.3 6.4 %collective-permute-start.6 = (f32[1,768]{1,0:T(1,128)S(1)}, f32[1,768]{1,0:T(1,128)S(1)}, u32[]{:S(2)}, u32[]{:S(2)}) collective-permute-start(f32[1,768]{1,0:T(1,128)S(1)} %get-tuple-element.10), channel_id=1, source_target_pairs={{8,0},{9,1},{10,2},{11,3},{4,12},{5,13},{6,14},{7,15},{24,16},{25,... | collective-permute-start | bytes 9224 | tf_op jit(solution)/shard_map/ppermute | solution.py:174
  53.6 5.2 %collective-permute-start.4 = (f32[1,768]{1,0:T(1,128)S(1)}, f32[1,768]{1,0:T(1,128)S(1)}, u32[]{:S(2)}, u32[]{:S(2)}) collective-permute-start(f32[1,768]{1,0:T(1,128)S(1)} %get-tuple-element.9), channel_id=1, source_target_pairs={{4,0},{5,1},{6,2},{7,3},{8,4},{9,5},{10,6},{11,7},{12,8},{13,9},{1... | collective-permute-start | bytes 9224 | tf_op jit(solution)/shard_map/ppermute | solution.py:174

commit v3 on v1

v3 whole, which is shorter than its diff:
```python
import functools

import jax
import jax.numpy as jnp
import numpy as np
from jax import lax
from jax.experimental import pallas as pl
from jax.experimental.pallas import tpu as pltpu
from jax.sharding import PartitionSpec as P

LABELS = 3
PLANE = 4
PAD = 16
BASE = 64.0
TILE = 256
HEAD = 256
VMEM_LIMIT = 24 * 2**20


def whole(count):
    return [pl.BlockSpec(memory_space=pltpu.VMEM)] * count


def params():
    return pltpu.CompilerParams(vmem_limit_bytes=VMEM_LIMIT)


def lanes_shape(rows):
    return jax.ShapeDtypeStruct((-(-rows // 1024) * 8, 128), jnp.float32)


def pack_kernel(
    rows, peers, embeddings, owner_ref, label_ref, run_ref, head_ref, tail_ref, held, sems
):
    copies = []
    for n, first in enumerate(range(0, rows, TILE)):
        part = pl.ds(first, TILE)
        copies.append(pltpu.make_async_copy(embeddings.at[part], held.at[part], sems.at[n]))
        copies[-1].start()
    owner = owner_ref[...]
    first_owner = jnp.zeros_like(owner)
    for n in range(peers):
        first_owner = jnp.where(owner == n, run_ref[n], first_owner)
    label = label_ref[...]
    tags = 1 + jnp.where(label == 0, first_owner * LABELS, owner * LABELS + label)
    tags = tags.astype(jnp.float32)
    high = jnp.floor(tags * (1.0 / BASE))
    digits = jnp.concatenate([high, tags - high * BASE], axis=0).astype(jnp.bfloat16)
    width = head_ref.shape[1]
    head_ref[0:PAD, :] = jnp.concatenate(
        [digits, jnp.zeros((PAD, width - 128), jnp.bfloat16)], axis=1
    )
    for n, first in enumerate(range(0, rows, TILE)):
        copies[n].wait()
        values = held[first : first + TILE, :]
        squares = jnp.sum(values * values, axis=1, keepdims=True)
        unit = (values * lax.rsqrt(squares + 1e-06)).astype(jnp.bfloat16)
        if first < HEAD:
            head_ref[PAD + first : PAD + first + TILE, :] = unit
        else:
            tail_ref[first - HEAD : first - HEAD + TILE, :] = unit


def tag_rows(block_ref):
    digits = block_ref[0:PAD, 0:128].astype(jnp.float32)
    return digits[0:8] * BASE + digits[8:16]


def tag_columns(block_ref, rows):
    tags = tag_rows(block_ref)
    return jnp.concatenate(
        [jnp.transpose(jnp.broadcast_to(tags[n : n + 1], (128, 128))) for n in range(rows // 128)],
        axis=0,
    )


def dot_rows(values, lanes):
    return lax.dot_general(
        values, lanes, (((1,), (1,)), ((), ())), preferred_element_type=jnp.float32
    )


def unit_rows(part_ref, has_tags):
    return part_ref.at[PAD:] if has_tags else part_ref


def unit_parts(refs):
    head, tail = unit_rows(refs[0], True), refs[1]
    return ((0, head), (head.shape[0], tail))


def fold_sublanes(values):
    rows, lanes = values.shape
    return jnp.max(values.reshape(rows // 8, 8, lanes), axis=0)


def fold_lanes(values):
    return jnp.concatenate(
        [
            jnp.max(jnp.transpose(values[first : first + 128]), axis=0, keepdims=True)
            for first in range(0, values.shape[0], 128)
        ],
        axis=0,
    )


def plane_kernel(rows, count, with_self, *refs):
    own, refs = refs[:2], refs[2:]
    blocks, refs = [refs[2 * n : 2 * n + 2] for n in range(count)], refs[2 * count :]
    before_ref, refs = (None, refs) if with_self else (refs[0], refs[1:])
    best_ref, column_refs = refs[0], refs[1:]
    own_tags = tag_rows(own[0])
    for block, column_ref in zip(blocks, column_refs):
        column_ref[...] = tag_columns(block[0], rows)
    if with_self:
        best_ref[...] = jnp.full(best_ref.shape, -1.0, jnp.float32)
    else:
        best_ref[...] = before_ref[...]
    for own_first, own_part in unit_parts(own):
        for tile in range(0, own_part.shape[0], TILE):
            lanes = own_part[tile : tile + TILE, :]
            for which, (block, column_ref) in enumerate(zip(blocks, column_refs)):
                for first, part in unit_parts(block):
                    count = part.shape[0]
                    found = dot_rows(part[...], lanes)
                    for lane in range(0, TILE, 128):
                        lane_row = own_first + tile + lane
                        row = lane_row // 128
                        match = column_ref[first : first + count, :] == own_tags[row : row + 1]
                        if with_self and which == 0 and first < lane_row + 128 <= first + count:
                            row_id = lax.broadcasted_iota(jnp.int32, (count, 128), 0) + first
                            lane_id = lax.broadcasted_iota(jnp.int32, (count, 128), 1) + lane_row
                            match = match & (row_id != lane_id)
                        masked = jnp.where(match, found[:, lane : lane + 128], -1.0)
                        folded = jnp.max(fold_sublanes(masked), axis=0, keepdims=True)
                        place = pl.ds(row, 1)
                        best_ref[place, :] = jnp.maximum(best_ref[place, :], folded)


def cross_kernel(rows, first, has_tags, tags_ref, part_ref, *refs):
    blocks, refs = [refs[2 * n : 2 * n + 2] for n in range(PLANE)], refs[2 * PLANE :]
    columns, refs = refs[:PLANE], refs[PLANE:]
    away_before, plane_before, away_best, plane_best = refs
    away_tags = tag_rows(tags_ref)
    away = unit_rows(part_ref, has_tags)
    away_best[...] = away_before[...]
    for which in range(PLANE):
        for start, part in unit_parts(blocks[which]):
            count = part.shape[0]
            row_best = jnp.full((count, 128), -1.0, jnp.float32)
            column = columns[which][start : start + count, :]
            for tile in range(0, away.shape[0], TILE):
                found = dot_rows(part[...], away[tile : tile + TILE, :])
                for lane in range(0, TILE, 128):
                    row = (first + tile + lane) // 128
                    match = column == away_tags[row : row + 1]
                    masked = jnp.where(match, found[:, lane : lane + 128], -1.0)
                    row_best = jnp.maximum(row_best, masked)
                    folded = jnp.max(fold_sublanes(masked), axis=0, keepdims=True)
                    place = pl.ds(row, 1)
                    away_best[place, :] = jnp.maximum(away_best[place, :], folded)
            place = pl.ds(start // 128, count // 128)
            folded = fold_lanes(row_best)
            plane_best[which, place, :] = jnp.maximum(folded, plane_before[which, place, :])


def cost(pairs, rows, width):
    return pl.CostEstimate(
        flops=int(2 * pairs * rows * rows * width),
        bytes_accessed=5 * rows * width * 2,
        transcendentals=0,
    )


def plane_steps(planes):
    steps = []
    for distance in range(1, planes // 2 + 1):
        if 2 * distance < planes:
            steps.append([(z, (z + distance) % planes) for z in range(planes)])
        else:
            steps.append(
                [(z, z + distance) if z % 2 == 0 else (z + distance, z) for z in range(distance)]
            )
    return steps


def after(value, *others):
    return lax.optimization_barrier((value,) + others)[0]


def local(embeddings, owner_index, sub_label, run_start):
    rows, width = embeddings.shape
    peers = lax.axis_size("dp")
    planes = peers // PLANE
    me = lax.axis_index("dp")
    lanes = lanes_shape(rows)

    def in_lanes(values):
        return jnp.pad(values, (0, lanes.shape[0] * 128 - rows)).reshape(lanes.shape)

    own = pl.pallas_call(
        functools.partial(pack_kernel, rows, peers),
        out_shape=(
            jax.ShapeDtypeStruct((PAD + HEAD, width), jnp.bfloat16),
            jax.ShapeDtypeStruct((rows - HEAD, width), jnp.bfloat16),
        ),
        in_specs=[pl.BlockSpec(memory_space=pltpu.HBM)]
        + whole(2)
        + [pl.BlockSpec(memory_space=pltpu.SMEM)],
        out_specs=tuple(whole(2)),
        scratch_shapes=[
            pltpu.VMEM((rows, width), jnp.float32),
            pltpu.SemaphoreType.DMA((rows // TILE,)),
        ],
        compiler_params=params(),
        name="pack",
    )(embeddings, in_lanes(owner_index), in_lanes(sub_label), run_start)

    def mate(value, distance):
        return lax.ppermute(value, "dp", [(i, i ^ distance) for i in range(peers)])

    away = []
    beside = tuple(mate(part, 2) for part in own)
    near = tuple(mate(part, 1) for part in own)
    across = ()
    for step in plane_steps(planes):
        pairs = [(s * PLANE + j, t * PLANE + j) for s, t in step for j in range(PLANE)]
        received = []
        for n, part in enumerate(own):
            if len(away) == 1:
                waited = (away[0][1][n], beside[n]) + across
                across += (mate(after(beside[n], *waited), 1),)
                part = after(part, *waited) if n else part
            elif away:
                part = after(part, away[-1][1][n])
            received.append(lax.ppermute(part, "dp", pairs))
        away.append((pairs, received))

    columns = jax.ShapeDtypeStruct((rows, 128), jnp.float32)
    best, own_columns, near_columns = pl.pallas_call(
        functools.partial(plane_kernel, rows, 2, True),
        out_shape=(lanes, columns, columns),
        in_specs=whole(6),
        out_specs=tuple(whole(3)),
        compiler_params=params(),
        cost_estimate=cost(2, rows, width),
        name="plane_near",
    )(*own, *own, *near)
    best, beside_columns, across_columns = pl.pallas_call(
        functools.partial(plane_kernel, rows, 2, False),
        out_shape=(lanes, columns, columns),
        in_specs=whole(7),
        out_specs=tuple(whole(3)),
        compiler_params=params(),
        cost_estimate=cost(2, rows, width),
        name="plane_far",
    )(*own, *beside, *across, best)

    plane = (*own, *near, *beside, *across)
    plane_columns = (own_columns, near_columns, beside_columns, across_columns)
    plane_best = jnp.full((PLANE,) + lanes.shape, -1.0, jnp.float32)
    for pairs, received in away:
        away_best = jnp.full(lanes.shape, -1.0, jnp.float32)
        first = 0
        for n, part in enumerate(received):
            part_rows = part.shape[0] - (PAD if n == 0 else 0)
            away_best, plane_best = pl.pallas_call(
                functools.partial(cross_kernel, rows, first, n == 0),
                out_shape=(lanes, jax.ShapeDtypeStruct(plane_best.shape, jnp.float32)),
                in_specs=whole(4 + 3 * PLANE),
                out_specs=tuple(whole(2)),
                compiler_params=params(),
                cost_estimate=cost(PLANE * part_rows / rows, rows, width),
                name="cross",
            )(received[0], part, *plane, *plane_columns, away_best, plane_best)
            first += part_rows
        back = lax.ppermute(away_best, "dp", [(t, s) for s, t in pairs])
        if len(pairs) < peers:
            sent = np.zeros((peers,), np.bool_)
            sent[[s for s, _ in pairs]] = True
            back = jnp.where(jnp.asarray(sent)[me], back, -1.0)
        best = jnp.maximum(best, back)
    best = jnp.maximum(best, plane_best[0])
    for n, distance in ((3, 3), (2, 2), (1, 1)):
        best = jnp.maximum(best, mate(plane_best[n], distance))
    return best.reshape(-1)[:rows]


def solution(mesh):
    in_specs = (P(("groups", "dp"), None), P(("groups", "dp")), P(("groups", "dp")), P("groups"))
    out_specs = P(("groups", "dp"))
    return jax.shard_map(local, mesh=mesh, in_specs=in_specs, out_specs=out_specs, check_vma=False)
```

time: 155 us -> 60.4 us (0.39)
  waiting for transfers between devices: 94.8 us -> 28.8 us
  blocking collectives: 23.4 us -> 0 us
  matrix products: 18.2 us -> 0 us
  starting transfers between devices: 0.04 us -> 16.3 us
  between operations: 13.5 us -> 0.12 us
  Pallas kernels: 0 us -> 10.3 us
  other arithmetic: 3.91 us -> 0.65 us
  local copies, waits for them, and re-layouts: 1.03 us -> 3.96 us
    all_gather x2 -> x0, waiting for transfers between devices: 94.1 us -> none  [step(): gathered = lax.all_gather(part, 'dp', axis=0, tiled=True)]
    ppermute x0 -> x15, waiting for transfers between devices: none -> 28.8 us  [the longest x4 15.8 us: local(): received.append(lax.ppermute(part, 'dp', pairs))]
    all_gather x1 -> x0, blocking collectives: 23.4 us -> none  [local(): all_tags = lax.all_gather(tags, 'dp', axis=0)]
    dot_general x2 -> x0, matrix products: 18.2 us -> none  [best_in_chunk(): lax.dot_general(queries, candidates, (((1,), (1,)), ((), ())), preferred_...]
    ppermute x0 -> x15, starting transfers between devices: none -> 16.3 us  [the longest x4 7.11 us: local(): received.append(lax.ppermute(part, 'dp', pairs))]
    pallas_call x0 -> x7, Pallas kernels: none -> 10.3 us  [the longest x4 6.25 us: local(): pl.pallas_call(functools.partial(cross_kernel, rows, first, n == 0), out_...]
    unnamed x8 -> x6, local copies, waits for them, and re-layouts: 0.02 us -> 2.07 us
    reduce_sum x2 -> x0, other arithmetic: 1.71 us -> none  [the longest x1 1.63 us: local(): squares = jnp.sum(embeddings * embeddings, axis=1, keepdims=True)]
  transfers between devices with their start and end apart: 2 -> 15, of which waited for: 2 -> 6; matrix products, arithmetic and copies ran while one was open for 6% -> 1% of each run, Pallas kernels for 0% -> 12%
where the time goes in v3:
time: 60.4 us; the launch traced here: 60.1 us
  waiting for transfers between devices  28.8 us (48%)
  starting transfers between devices  16.3 us (27%)
  Pallas kernels  10.3 us (17%)
  local copies, waits for them, and re-layouts  3.96 us (7%)
  other arithmetic  0.65 us (1%)
    ppermute x4, waiting for transfers between devices, local(): received.append(lax.ppermute(part, 'dp', pairs))  15.8 us
    ppermute x9, waiting for transfers between devices, mate(): return lax.ppermute(value, 'dp', [(i, i ^ distance) for i in range(peers)])  9.85 us
    ppermute x4, starting transfers between devices, local(): received.append(lax.ppermute(part, 'dp', pairs))  7.11 us
    ppermute x9, starting transfers between devices, mate(): return lax.ppermute(value, 'dp', [(i, i ^ distance) for i in range(peers)])  6.48 us
    pallas_call x4, Pallas kernels, local(): pl.pallas_call(functools.partial(cross_kernel, rows, first, n == 0), out_...  6.25 us
    ppermute x2, waiting for transfers between devices, local(): back = lax.ppermute(away_best, 'dp', [(t, s) for s, t in pairs])  3.1 us
    ppermute x2, starting transfers between devices, local(): back = lax.ppermute(away_best, 'dp', [(t, s) for s, t in pairs])  2.68 us
    unnamed x6, local copies, waits for them, and re-layouts  2.07 us
  transfers between devices with their start and end apart: 15, of which 6 were waited for; matrix products, arithmetic and copies ran while one was open for 1% of the time, Pallas kernels for 12%

profile of v3, /device:TPU:0, one launch (start us, length us, event | category | flops | bytes accessed | tf_op | source)
XLA Modules:
  0.0 60.1 jit_solution(15698252754973924756)
XLA Ops:
  0.0 0.7 %pad_bitcast_fusion = (s32[8,128]{1,0:T(8,128)S(1)}, s32[8,128]{1,0:T(8,128)S(1)}) fusion(s32[768]{0:T(1024)} %param.7, s32[768]{0:T(1024)} %param.6), kind=kLoop, calls=%fused_computation.8 | loop fusion | bytes 14336 | tf_op jit(solution)/shard_map/reshape | solution.py:199
  0.7 1.4 %copy-done = f32[768,512]{1,0:T(8,128)S(1)} copy-done((f32[768,512]{1,0:T(8,128)S(1)}, f32[768,512]{1,0:T(8,128)}, u32[]{:S(2)}) %copy-start) | copy-done | bytes 1572888
  2.8 1.1 %pack.1 = (bf16[272,512]{1,0:T(8,128)(2,1)S(1)}, bf16[512,512]{1,0:T(8,128)(2,1)S(1)}) custom-call(f32[768,512]{1,0:T(8,128)S(1)} %copy-done, s32[8,128]{1,0:T(8,128)S(1)} %get-tuple-element.47.owner_ref, s32[8,128]{1,0:T(8,128)S(1)} %get-tuple-element.46.label_ref, s32[16]{0:T(128)S(1)} %copy-done.1), custom_call_target="tpu_custom_call" | custom-call | tf_op jit(solution)/shard_map/pack/pallas_call | solution.py:201
  3.9 3.0 %collective-permute-start = (bf16[272,512]{1,0:T(8,128)(2,1)S(1)}, bf16[272,512]{1,0:T(8,128)(2,1)S(1)}, u32[]{:S(2)}, u32[]{:S(2)}) collective-permute-start(bf16[272,512]{1,0:T(8,128)(2,1)S(1)} %get-tuple-element.24.refs_0_.refs_2_), channel_id=1, source_target_pairs={{0,2},{1,3},{2,0},{3,1},{4,6},{5,7},{6,4},{7,5},{8,10},{9,11},{10,... | collective-permute-start | bytes 835592 | tf_op jit(solution)/shard_map/ppermute | solution.py:220
  6.9 1.6 %collective-permute-start.2 = (bf16[272,512]{1,0:T(8,128)(2,1)S(1)}, bf16[272,512]{1,0:T(8,128)(2,1)S(1)}, u32[]{:S(2)}, u32[]{:S(2)}) collective-permute-start(bf16[272,512]{1,0:T(8,128)(2,1)S(1)} %get-tuple-element.24.refs_0_.refs_2_), channel_id=1, source_target_pairs={{0,4},{1,5},{2,6},{3,7},{4,8},{5,9},{6,10},{7,11},{8,12},{9,13},{1... | collective-permute-start | bytes 835592 | tf_op jit(solution)/shard_map/ppermute | solution.py:236
  9.0 1.6 %collective-permute-start.4 = (bf16[512,512]{1,0:T(8,128)(2,1)S(1)}, bf16[512,512]{1,0:T(8,128)(2,1)S(1)}, u32[]{:S(2)}, u32[]{:S(2)}) collective-permute-start(bf16[512,512]{1,0:T(8,128)(2,1)S(1)} %get-tuple-element.37.refs_1_.refs_3_), channel_id=1, source_target_pairs={{0,4},{1,5},{2,6},{3,7},{4,8},{5,9},{6,10},{7,11},{8,12},{9,13},{1... | collective-permute-start | bytes 1572872 | tf_op jit(solution)/shard_map/ppermute | solution.py:236
  10.6 3.8 %collective-permute-done.refs_2_.refs_4_ = bf16[272,512]{1,0:T(8,128)(2,1)S(1)} collective-permute-done((bf16[272,512]{1,0:T(8,128)(2,1)S(1)}, bf16[272,512]{1,0:T(8,128)(2,1)S(1)}, u32[]{:S(2)}, u32[]{:S(2)}) %collective-permute-start) | collective-permute-done | bytes 278560 | tf_op jit(solution)/shard_map/ppermute | solution.py:220
  14.4 3.9 %collective-permute-done.2.tags_ref.part_ref = bf16[272,512]{1,0:T(8,128)(2,1)S(1)} collective-permute-done((bf16[272,512]{1,0:T(8,128)(2,1)S(1)}, bf16[272,512]{1,0:T(8,128)(2,1)S(1)}, u32[]{:S(2)}, u32[]{:S(2)}) %collective-permute-start.2) | collective-permute-done | bytes 278560 | tf_op jit(solution)/shard_map/ppermute | solution.py:236
  18.8 6.0 %collective-permute-done.1.refs_3_.refs_5_ = bf16[512,512]{1,0:T(8,128)(2,1)S(1)} collective-permute-done((bf16[512,512]{1,0:T(8,128)(2,1)S(1)}, bf16[512,512]{1,0:T(8,128)(2,1)S(1)}, u32[]{:S(2)}, u32[]{:S(2)}) %collective-permute-start.1) | collective-permute-done | bytes 524320 | tf_op jit(solution)/shard_map/ppermute | solution.py:220
  24.8 3.3 %collective-permute-done.4.part_ref = bf16[512,512]{1,0:T(8,128)(2,1)S(1)} collective-permute-done((bf16[512,512]{1,0:T(8,128)(2,1)S(1)}, bf16[512,512]{1,0:T(8,128)(2,1)S(1)}, u32[]{:S(2)}, u32[]{:S(2)}) %collective-permute-start.4) | collective-permute-done | bytes 524320 | tf_op jit(solution)/shard_map/ppermute | solution.py:236
  28.6 2.6 %collective-permute-start.9 = (bf16[272,512]{1,0:T(8,128)(2,1)S(1)}, bf16[272,512]{1,0:T(8,128)(2,1)S(1)}, u32[]{:S(2)}, u32[]{:S(2)}) collective-permute-start(bf16[272,512]{1,0:T(8,128)(2,1)S(1)} %get-tuple-element.24.refs_0_.refs_2_), channel_id=1, source_target_pairs={{0,8},{1,9},{2,10},{3,11},{12,4},{13,5},{14,6},{15,7},{16,24},{17,... | collective-permute-start | bytes 835592 | tf_op jit(solution)/shard_map/ppermute | solution.py:236
  31.3 1.3 %collective-permute-start.10 = (bf16[512,512]{1,0:T(8,128)(2,1)S(1)}, bf16[512,512]{1,0:T(8,128)(2,1)S(1)}, u32[]{:S(2)}, u32[]{:S(2)}) collective-permute-start(bf16[512,512]{1,0:T(8,128)(2,1)S(1)} %get-tuple-element.37.refs_1_.refs_3_), channel_id=1, source_target_pairs={{0,8},{1,9},{2,10},{3,11},{12,4},{13,5},{14,6},{15,7},{16,24},{17,... | collective-permute-start | bytes 1572872 | tf_op jit(solution)/shard_map/ppermute | solution.py:236
  32.6 1.5 %plane_near.1 = (f32[8,128]{1,0:T(8,128)S(1)}, f32[768,128]{1,0:T(8,128)S(1)}, f32[768,128]{1,0:T(8,128)S(1)}) custom-call(bf16[272,512]{1,0:T(8,128)(2,1)S(1)} %get-tuple-element.24.refs_0_.refs_2_, bf16[512,512]{1,0:T(8,128)(2,1)S(1)} %get-tuple-element.37.refs_1_.refs_3_, bf16[272,512]{1,0:T(8,128)(2,1)S(1)} %get-tuple-element.24.refs_0_.refs_2_, ...), custom_call_target="tpu_custom_call" | custom-call | flops 1207959552 | bytes 3932160 | tf_op jit(solution)/shard_map/plane_near/pallas_call | solution.py:240
  34.1 1.5 %plane_far.1 = (f32[8,128]{1,0:T(8,128)S(1)}, f32[768,128]{1,0:T(8,128)S(1)}, f32[768,128]{1,0:T(8,128)S(1)}) custom-call(bf16[272,512]{1,0:T(8,128)(2,1)S(1)} %get-tuple-element.24.refs_0_.refs_2_, bf16[512,512]{1,0:T(8,128)(2,1)S(1)} %get-tuple-element.37.refs_1_.refs_3_, bf16[272,512]{1,0:T(8,128)(2,1)S(1)} %collective-permute-done.refs_2_.refs_4_, ...), custom_call_target="tpu_custom_call" | custom-call | flops 1207959552 | bytes 3932160 | tf_op jit(solution)/shard_map/plane_far/pallas_call | solution.py:249
  35.6 1.2 %cross.4 = (f32[8,128]{1,0:T(8,128)S(1)}, f32[4,8,128]{2,1,0:T(8,128)S(1)}) custom-call(bf16[272,512]{1,0:T(8,128)(2,1)S(1)} %collective-permute-done.2.tags_ref.part_ref, bf16[272,512]{1,0:T(8,128)(2,1)S(1)} %collective-permute-done.2.tags_ref.part_ref, bf16[272,512]{1,0:T(8,128)(2,1)S(1)} %get-tuple-element.24.refs_0_.refs_2_, ...), custom_call_target="tpu_custom_call" | custom-call | flops 805306368 | bytes 3932160 | tf_op jit(solution)/shard_map/cross/pallas_call | solution.py:267
  36.8 2.0 %cross.5 = (f32[8,128]{1,0:T(8,128)S(1)}, f32[4,8,128]{2,1,0:T(8,128)S(1)}) custom-call(bf16[272,512]{1,0:T(8,128)(2,1)S(1)} %collective-permute-done.2.tags_ref.part_ref, bf16[512,512]{1,0:T(8,128)(2,1)S(1)} %collective-permute-done.4.part_ref, bf16[272,512]{1,0:T(8,128)(2,1)S(1)} %get-tuple-element.24.refs_0_.refs_2_, ...), custom_call_target="tpu_custom_call" | custom-call | flops 1610612736 | bytes 3932160 | tf_op jit(solution)/shard_map/cross/pallas_call | solution.py:267
  38.8 1.2 %cross.6 = (f32[8,128]{1,0:T(8,128)S(1)}, f32[4,8,128]{2,1,0:T(8,128)S(1)}) custom-call(bf16[272,512]{1,0:T(8,128)(2,1)S(1)} %collective-permute-done.9.tags_ref.part_ref, bf16[272,512]{1,0:T(8,128)(2,1)S(1)} %collective-permute-done.9.tags_ref.part_ref, bf16[272,512]{1,0:T(8,128)(2,1)S(1)} %get-tuple-element.24.refs_0_.refs_2_, ...), custom_call_target="tpu_custom_call" | custom-call | flops 805306368 | bytes 3932160 | tf_op jit(solution)/shard_map/cross/pallas_call | solution.py:267
  39.9 8.6 %collective-permute-done.10.part_ref = bf16[512,512]{1,0:T(8,128)(2,1)S(1)} collective-permute-done((bf16[512,512]{1,0:T(8,128)(2,1)S(1)}, bf16[512,512]{1,0:T(8,128)(2,1)S(1)}, u32[]{:S(2)}, u32[]{:S(2)}) %collective-permute-start.10) | collective-permute-done | bytes 524320 | tf_op jit(solution)/shard_map/ppermute | solution.py:236
  48.6 1.9 %cross.7 = (f32[8,128]{1,0:T(8,128)S(1)}, f32[4,8,128]{2,1,0:T(8,128)S(1)}) custom-call(bf16[272,512]{1,0:T(8,128)(2,1)S(1)} %collective-permute-done.9.tags_ref.part_ref, bf16[512,512]{1,0:T(8,128)(2,1)S(1)} %collective-permute-done.10.part_ref, bf16[272,512]{1,0:T(8,128)(2,1)S(1)} %get-tuple-element.24.refs_0_.refs_2_, ...), custom_call_target="tpu_custom_call" | custom-call | flops 1610612736 | bytes 3932160 | tf_op jit(solution)/shard_map/cross/pallas_call | solution.py:267
  50.6 0.8 %collective-permute-start.13 = (f32[8,128]{1,0:T(8,128)S(1)}, f32[8,128]{1,0:T(8,128)S(1)}, u32[]{:S(2)}, u32[]{:S(2)}) collective-permute-start(f32[8,128]{1,0:T(8,128)S(1)} %get-tuple-element.45), channel_id=1, source_target_pairs={{0,2},{1,3},{2,0},{3,1},{4,6},{5,7},{6,4},{7,5},{8,10},{9,11},{10,... | collective-permute-start | bytes 12296 | tf_op jit(solution)/shard_map/ppermute | solution.py:220
  51.4 1.1 %collective-permute-start.14 = (f32[8,128]{1,0:T(8,128)S(1)}, f32[8,128]{1,0:T(8,128)S(1)}, u32[]{:S(2)}, u32[]{:S(2)}) collective-permute-start(f32[8,128]{1,0:T(8,128)S(1)} %get-tuple-element.44), channel_id=1, source_target_pairs={{0,1},{1,0},{2,3},{3,2},{4,5},{5,4},{6,7},{7,6},{8,9},{9,8},{10,11... | collective-permute-start | bytes 12296 | tf_op jit(solution)/shard_map/ppermute | solution.py:220
  52.4 1.3 %collective-permute-start.11 = (f32[8,128]{1,0:T(8,128)S(1)}, f32[8,128]{1,0:T(8,128)S(1)}, u32[]{:S(2)}, u32[]{:S(2)}) collective-permute-start(f32[8,128]{1,0:T(8,128)S(1)} %get-tuple-element.41), channel_id=1, source_target_pairs={{8,0},{9,1},{10,2},{11,3},{4,12},{5,13},{6,14},{7,15},{24,16},{25,... | collective-permute-start | bytes 12296 | tf_op jit(solution)/shard_map/ppermute | solution.py:277
  53.7 1.4 %collective-permute-start.8 = (f32[8,128]{1,0:T(8,128)S(1)}, f32[8,128]{1,0:T(8,128)S(1)}, u32[]{:S(2)}, u32[]{:S(2)}) collective-permute-start(f32[8,128]{1,0:T(8,128)S(1)} %get-tuple-element.36), channel_id=1, source_target_pairs={{4,0},{5,1},{6,2},{7,3},{8,4},{9,5},{10,6},{11,7},{12,8},{13,9},{1... | collective-permute-start | bytes 12296 | tf_op jit(solution)/shard_map/ppermute | solution.py:277
  55.7 3.1 %collective-permute-done.11 = f32[8,128]{1,0:T(8,128)S(1)} collective-permute-done((f32[8,128]{1,0:T(8,128)S(1)}, f32[8,128]{1,0:T(8,128)S(1)}, u32[]{:S(2)}, u32[]{:S(2)}) %collective-permute-start.11) | collective-permute-done | bytes 4128 | tf_op jit(solution)/shard_map/ppermute | solution.py:277
  (26 shorter events, 4.1 us)
Async XLA Ops:
  0.7 1.4 %copy-start = (f32[768,512]{1,0:T(8,128)S(1)}, f32[768,512]{1,0:T(8,128)}, u32[]{:S(2)}) copy-start(f32[768,512]{1,0:T(8,128)} %embeddings.1) | copy-start | bytes 4718596
  2.1 0.7 %copy-start.1 = (s32[16]{0:T(128)S(1)}, s32[16]{0:T(128)}, u32[]{:S(2)}) copy-start(s32[16]{0:T(128)} %run_ref.1) | copy-start | bytes 196
  3.9 10.5 %collective-permute-start = (bf16[272,512]{1,0:T(8,128)(2,1)S(1)}, bf16[272,512]{1,0:T(8,128)(2,1)S(1)}, u32[]{:S(2)}, u32[]{:S(2)}) collective-permute-start(bf16[272,512]{1,0:T(8,128)(2,1)S(1)} %get-tuple-element.24.refs_0_.refs_2_), channel_id=1, source_target_pairs={{0,2},{1,3},{2,0},{3,1},{4,6},{5,7},{6,4},{7,5},{8,10},{9,11},{10,... | collective-permute-start | bytes 835592 | tf_op jit(solution)/shard_map/ppermute | solution.py:220
  6.9 11.4 %collective-permute-start.2 = (bf16[272,512]{1,0:T(8,128)(2,1)S(1)}, bf16[272,512]{1,0:T(8,128)(2,1)S(1)}, u32[]{:S(2)}, u32[]{:S(2)}) collective-permute-start(bf16[272,512]{1,0:T(8,128)(2,1)S(1)} %get-tuple-element.24.refs_0_.refs_2_), channel_id=1, source_target_pairs={{0,4},{1,5},{2,6},{3,7},{4,8},{5,9},{6,10},{7,11},{8,12},{9,13},{1... | collective-permute-start | bytes 835592 | tf_op jit(solution)/shard_map/ppermute | solution.py:236
  8.5 16.3 %collective-permute-start.1 = (bf16[512,512]{1,0:T(8,128)(2,1)S(1)}, bf16[512,512]{1,0:T(8,128)(2,1)S(1)}, u32[]{:S(2)}, u32[]{:S(2)}) collective-permute-start(bf16[512,512]{1,0:T(8,128)(2,1)S(1)} %get-tuple-element.37.refs_1_.refs_3_), channel_id=1, source_target_pairs={{0,2},{1,3},{2,0},{3,1},{4,6},{5,7},{6,4},{7,5},{8,10},{9,11},{10,... | collective-permute-start | bytes 1572872 | tf_op jit(solution)/shard_map/ppermute | solution.py:220
  9.0 19.1 %collective-permute-start.4 = (bf16[512,512]{1,0:T(8,128)(2,1)S(1)}, bf16[512,512]{1,0:T(8,128)(2,1)S(1)}, u32[]{:S(2)}, u32[]{:S(2)}) collective-permute-start(bf16[512,512]{1,0:T(8,128)(2,1)S(1)} %get-tuple-element.37.refs_1_.refs_3_), channel_id=1, source_target_pairs={{0,4},{1,5},{2,6},{3,7},{4,8},{5,9},{6,10},{7,11},{8,12},{9,13},{1... | collective-permute-start | bytes 1572872 | tf_op jit(solution)/shard_map/ppermute | solution.py:236
  18.3 9.8 %collective-permute-start.3 = (bf16[272,512]{1,0:T(8,128)(2,1)S(1)}, bf16[272,512]{1,0:T(8,128)(2,1)S(1)}, u32[]{:S(2)}, u32[]{:S(2)}) collective-permute-start(bf16[272,512]{1,0:T(8,128)(2,1)S(1)} %collective-permute-done.refs_2_.refs_4_), channel_id=1, source_target_pairs={{0,1},{1,0},{2,3},{3,2},{4,5},{5,4},{6,7},{7,6},{8,9},{9,8},{10,11... | collective-permute-start | bytes 835592 | tf_op jit(solution)/shard_map/ppermute | solution.py:220
  18.3 14.3 %collective-permute-start.7 = (bf16[512,512]{1,0:T(8,128)(2,1)S(1)}, bf16[512,512]{1,0:T(8,128)(2,1)S(1)}, u32[]{:S(2)}, u32[]{:S(2)}) collective-permute-start(bf16[512,512]{1,0:T(8,128)(2,1)S(1)} %get-tuple-element.37.refs_1_.refs_3_), channel_id=1, source_target_pairs={{0,1},{1,0},{2,3},{3,2},{4,5},{5,4},{6,7},{7,6},{8,9},{9,8},{10,11... | collective-permute-start | bytes 1572872 | tf_op jit(solution)/shard_map/ppermute | solution.py:220
  28.1 6.0 %collective-permute-start.5 = (bf16[512,512]{1,0:T(8,128)(2,1)S(1)}, bf16[512,512]{1,0:T(8,128)(2,1)S(1)}, u32[]{:S(2)}, u32[]{:S(2)}) collective-permute-start(bf16[512,512]{1,0:T(8,128)(2,1)S(1)} %collective-permute-done.1.refs_3_.refs_5_), channel_id=1, source_target_pairs={{0,1},{1,0},{2,3},{3,2},{4,5},{5,4},{6,7},{7,6},{8,9},{9,8},{10,11... | collective-permute-start | bytes 1572872 | tf_op jit(solution)/shard_map/ppermute | solution.py:220
  28.1 4.5 %collective-permute-start.6 = (bf16[272,512]{1,0:T(8,128)(2,1)S(1)}, bf16[272,512]{1,0:T(8,128)(2,1)S(1)}, u32[]{:S(2)}, u32[]{:S(2)}) collective-permute-start(bf16[272,512]{1,0:T(8,128)(2,1)S(1)} %get-tuple-element.24.refs_0_.refs_2_), channel_id=1, source_target_pairs={{0,1},{1,0},{2,3},{3,2},{4,5},{5,4},{6,7},{7,6},{8,9},{9,8},{10,11... | collective-permute-start | bytes 835592 | tf_op jit(solution)/shard_map/ppermute | solution.py:220
  28.6 10.1 %collective-permute-start.9 = (bf16[272,512]{1,0:T(8,128)(2,1)S(1)}, bf16[272,512]{1,0:T(8,128)(2,1)S(1)}, u32[]{:S(2)}, u32[]{:S(2)}) collective-permute-start(bf16[272,512]{1,0:T(8,128)(2,1)S(1)} %get-tuple-element.24.refs_0_.refs_2_), channel_id=1, source_target_pairs={{0,8},{1,9},{2,10},{3,11},{12,4},{13,5},{14,6},{15,7},{16,24},{17,... | collective-permute-start | bytes 835592 | tf_op jit(solution)/shard_map/ppermute | solution.py:236
  31.3 17.3 %collective-permute-start.10 = (bf16[512,512]{1,0:T(8,128)(2,1)S(1)}, bf16[512,512]{1,0:T(8,128)(2,1)S(1)}, u32[]{:S(2)}, u32[]{:S(2)}) collective-permute-start(bf16[512,512]{1,0:T(8,128)(2,1)S(1)} %get-tuple-element.37.refs_1_.refs_3_), channel_id=1, source_target_pairs={{0,8},{1,9},{2,10},{3,11},{12,4},{13,5},{14,6},{15,7},{16,24},{17,... | collective-permute-start | bytes 1572872 | tf_op jit(solution)/shard_map/ppermute | solution.py:236
  48.6 6.6 %copy-start.2 = (pred[16]{0:T(512)(128)(4,1)S(1)}, pred[16]{0:T(512)(128)(4,1)}, u32[]{:S(2)}) copy-start(pred[16]{0:T(512)(128)(4,1)} %constant.3.clone) | copy-start | bytes 52
  50.5 5.2 %collective-permute-start.12 = (f32[8,128]{1,0:T(8,128)S(1)}, f32[8,128]{1,0:T(8,128)S(1)}, u32[]{:S(2)}, u32[]{:S(2)}) collective-permute-start(f32[8,128]{1,0:T(8,128)S(1)} %get-tuple-element.43), channel_id=1, source_target_pairs={{0,3},{1,2},{2,1},{3,0},{4,7},{5,6},{6,5},{7,4},{8,11},{9,10},{10,... | collective-permute-start | bytes 12296 | tf_op jit(solution)/shard_map/ppermute | solution.py:220
  50.6 5.1 %collective-permute-start.13 = (f32[8,128]{1,0:T(8,128)S(1)}, f32[8,128]{1,0:T(8,128)S(1)}, u32[]{:S(2)}, u32[]{:S(2)}) collective-permute-start(f32[8,128]{1,0:T(8,128)S(1)} %get-tuple-element.45), channel_id=1, source_target_pairs={{0,2},{1,3},{2,0},{3,1},{4,6},{5,7},{6,4},{7,5},{8,10},{9,11},{10,... | collective-permute-start | bytes 12296 | tf_op jit(solution)/shard_map/ppermute | solution.py:220
  51.4 4.4 %collective-permute-start.14 = (f32[8,128]{1,0:T(8,128)S(1)}, f32[8,128]{1,0:T(8,128)S(1)}, u32[]{:S(2)}, u32[]{:S(2)}) collective-permute-start(f32[8,128]{1,0:T(8,128)S(1)} %get-tuple-element.44), channel_id=1, source_target_pairs={{0,1},{1,0},{2,3},{3,2},{4,5},{5,4},{6,7},{7,6},{8,9},{9,8},{10,11... | collective-permute-start | bytes 12296 | tf_op jit(solution)/shard_map/ppermute | solution.py:220
  52.4 6.4 %collective-permute-start.11 = (f32[8,128]{1,0:T(8,128)S(1)}, f32[8,128]{1,0:T(8,128)S(1)}, u32[]{:S(2)}, u32[]{:S(2)}) collective-permute-start(f32[8,128]{1,0:T(8,128)S(1)} %get-tuple-element.41), channel_id=1, source_target_pairs={{8,0},{9,1},{10,2},{11,3},{4,12},{5,13},{6,14},{7,15},{24,16},{25,... | collective-permute-start | bytes 12296 | tf_op jit(solution)/shard_map/ppermute | solution.py:277
  53.7 5.1 %collective-permute-start.8 = (f32[8,128]{1,0:T(8,128)S(1)}, f32[8,128]{1,0:T(8,128)S(1)}, u32[]{:S(2)}, u32[]{:S(2)}) collective-permute-start(f32[8,128]{1,0:T(8,128)S(1)} %get-tuple-element.36), channel_id=1, source_target_pairs={{4,0},{5,1},{6,2},{7,3},{8,4},{9,5},{10,6},{11,7},{12,8},{13,9},{1... | collective-permute-start | bytes 12296 | tf_op jit(solution)/shard_map/ppermute | solution.py:277

commit v4 on v3

v4 whole, which is shorter than its diff:
```python
import functools

import jax
import jax.numpy as jnp
from jax import lax
from jax.experimental import pallas as pl
from jax.experimental.pallas import tpu as pltpu
from jax.sharding import PartitionSpec as P

LABELS = 3
PLANE = 4
PAD = 16
BASE = 64.0
TILE = 256
AWAY_CUT = (3,)
MATE_CUT = (1, 1)
NEAR_CUT = (3,)
VMEM_LIMIT = 24 * 2**20


def whole(count):
    return [pl.BlockSpec(memory_space=pltpu.VMEM)] * count


def params():
    return pltpu.CompilerParams(vmem_limit_bytes=VMEM_LIMIT)


def cuts(rows, cut):
    return [rows * share // sum(cut) + (PAD if n == 0 else 0) for n, share in enumerate(cut)]


def lanes_shape(rows):
    return jax.ShapeDtypeStruct((-(-rows // 1024) * 8, 128), jnp.float32)


def pack_kernel(rows, embeddings_ref, owner_ref, label_ref, run_ref, *part_refs):
    owner = owner_ref[...]
    runs = jnp.broadcast_to(run_ref[0:1, :], owner.shape)
    first_owner = jnp.take_along_axis(runs, owner, axis=1)
    label = label_ref[...]
    tags = 1 + jnp.where(label == 0, first_owner * LABELS, owner * LABELS + label)
    tags = tags.astype(jnp.float32)
    high = jnp.floor(tags * (1.0 / BASE))
    digits = jnp.concatenate([high, tags - high * BASE], axis=0).astype(jnp.bfloat16)
    width = embeddings_ref.shape[1]
    digits = jnp.concatenate([digits, jnp.zeros((PAD, width - 128), jnp.bfloat16)], axis=1)
    values = embeddings_ref[...]
    squares = jnp.sum(values * values, axis=1, keepdims=True)
    unit = (values * lax.rsqrt(squares + 1e-06)).astype(jnp.bfloat16)
    first = 0
    for part_ref in part_refs:
        if first == 0:
            part_ref[0:PAD, :] = digits
            count = part_ref.shape[0] - PAD
            part_ref[PAD:, :] = unit[0:count]
        else:
            count = part_ref.shape[0]
            part_ref[...] = unit[first : first + count]
        first = (first + count) % rows


def tag_rows(block_ref):
    digits = block_ref[0:PAD, 0:128].astype(jnp.float32)
    return digits[0:8] * BASE + digits[8:16]


def tag_columns(block_ref, rows):
    tags = tag_rows(block_ref)
    return jnp.concatenate(
        [jnp.transpose(jnp.broadcast_to(tags[n : n + 1], (128, 128))) for n in range(rows // 128)],
        axis=0,
    )


def dot_rows(values, lanes):
    return lax.dot_general(
        values, lanes, (((1,), (1,)), ((), ())), preferred_element_type=jnp.float32
    )


def unit_parts(refs):
    parts, first = [], 0
    for n, ref in enumerate(refs):
        part = ref if n else ref.at[PAD:]
        parts.append((first, part))
        first += part.shape[0]
    return parts


def take(refs, counts):
    groups = []
    for count in counts:
        groups.append(refs[:count])
        refs = refs[count:]
    return groups, refs


def fold_sublanes(values):
    rows, lanes = values.shape
    return jnp.max(values.reshape(rows // 8, 8, lanes), axis=0)


def fold_lanes(values):
    return jnp.concatenate(
        [
            jnp.max(jnp.transpose(values[first : first + 128]), axis=0, keepdims=True)
            for first in range(0, values.shape[0], 128)
        ],
        axis=0,
    )


def plane_kernel(rows, counts, with_self, own_ref, *refs):
    blocks, refs = take(refs, counts)
    best_ref, column_refs = refs[-1 - len(counts)], refs[-len(counts) :]
    if with_self:
        best_ref[...] = refs[0][...]
    else:
        best_ref[...] = jnp.full(best_ref.shape, -1.0, jnp.float32)
    own_tags = tag_rows(own_ref)
    for block, column_ref in zip(blocks, column_refs):
        column_ref[...] = tag_columns(block[0], rows)
    for tile in range(0, rows, TILE):
        lanes = own_ref[PAD + tile : PAD + tile + TILE, :]
        for which, (block, column_ref) in enumerate(zip(blocks, column_refs)):
            for first, part in unit_parts(block):
                count = part.shape[0]
                found = dot_rows(part[...], lanes)
                for lane in range(0, TILE, 128):
                    row = (tile + lane) // 128
                    match = column_ref[first : first + count, :] == own_tags[row : row + 1]
                    if with_self and which == 0:
                        row_id = lax.broadcasted_iota(jnp.int32, (count, 128), 0) + first
                        lane_id = lax.broadcasted_iota(jnp.int32, (count, 128), 1) + tile + lane
                        match = match & (row_id != lane_id)
                    masked = jnp.where(match, found[:, lane : lane + 128], -1.0)
                    folded = jnp.max(fold_sublanes(masked), axis=0, keepdims=True)
                    place = pl.ds(row, 1)
                    best_ref[place, :] = jnp.maximum(best_ref[place, :], folded)


def cross_kernel(rows, index, counts, tags_ref, away_ref, *refs):
    blocks, refs = take(refs, counts)
    columns, refs = refs[:PLANE], refs[PLANE:]
    away_before, plane_before, away_best, plane_best = refs
    away_tags = tag_rows(tags_ref)
    away = away_ref if index else away_ref.at[PAD:]
    away_rows = away.shape[0]
    away_best[...] = away_before[...]
    for which in range(PLANE):
        for start, part in unit_parts(blocks[which]):
            count = part.shape[0]
            row_best = jnp.full((count, 128), -1.0, jnp.float32)
            column = columns[which][start : start + count, :]
            for tile in range(0, away_rows, TILE):
                lanes = min(TILE, away_rows - tile)
                found = dot_rows(part[...], away[tile : tile + lanes, :])
                for lane in range(0, lanes, 128):
                    row = (index * away_rows + tile + lane) // 128
                    match = column == away_tags[row : row + 1]
                    masked = jnp.where(match, found[:, lane : lane + 128], -1.0)
                    row_best = jnp.maximum(row_best, masked)
                    folded = jnp.max(fold_sublanes(masked), axis=0, keepdims=True)
                    place = pl.ds(row, 1)
                    away_best[place, :] = jnp.maximum(away_best[place, :], folded)
            place = pl.ds(start // 128, count // 128)
            folded = fold_lanes(row_best)
            plane_best[which, place, :] = jnp.maximum(folded, plane_before[which, place, :])


def small_cost():
    return pl.CostEstimate(flops=1, bytes_accessed=1, transcendentals=0)


def plane_steps(planes):
    steps = []
    for distance in range(1, planes // 2 + 1):
        if 2 * distance < planes:
            steps.append([(z, (z + distance) % planes) for z in range(planes)])
        else:
            steps.append(
                [(z, z + distance) if z % 2 == 0 else (z + distance, z) for z in range(distance)]
            )
    return steps


def after(value, *others):
    return lax.optimization_barrier((value,) + others)[0]


def local(embeddings, owner_index, sub_label, run_start):
    rows, width = embeddings.shape
    peers = lax.axis_size("dp")
    planes = peers // PLANE
    me = lax.axis_index("dp")
    lanes = lanes_shape(rows)

    def in_lanes(values):
        space = lanes.shape[0] * 128 - values.shape[0]
        return jnp.pad(values, (0, space)).reshape(lanes.shape)

    ways = ((1,), AWAY_CUT, MATE_CUT, NEAR_CUT)
    sizes = sum((cuts(rows, way) for way in ways), [])
    packed = pl.pallas_call(
        functools.partial(pack_kernel, rows),
        out_shape=tuple(jax.ShapeDtypeStruct((size, width), jnp.bfloat16) for size in sizes),
        in_specs=whole(4),
        out_specs=tuple(whole(len(sizes))),
        compiler_params=params(),
        cost_estimate=small_cost(),
        name="pack",
    )(embeddings, in_lanes(owner_index), in_lanes(sub_label), in_lanes(run_start))
    own, to_away, to_mate, to_near = take(packed, [len(way) for way in ways])[0]

    def mate(value, distance):
        return lax.ppermute(value, "dp", [(i, i ^ distance) for i in range(peers)])

    away = []
    for n, step in enumerate(plane_steps(planes)):
        pairs = [(s * PLANE + j, t * PLANE + j) for s, t in step for j in range(PLANE)]
        parts = to_away if n else own
        if n > 1:
            parts = [after(part, away[-1][1][-1]) for part in parts]
        away.append((pairs, [lax.ppermute(part, "dp", pairs) for part in parts]))
    beside = [mate(part, 2) for part in to_mate]
    near = [mate(part, 1) for part in to_near]
    across = [mate(part, 1) for part in beside]

    columns = jax.ShapeDtypeStruct((rows, 128), jnp.float32)
    best, beside_columns, across_columns = pl.pallas_call(
        functools.partial(plane_kernel, rows, (len(beside), len(across)), False),
        out_shape=(lanes, columns, columns),
        in_specs=whole(1 + len(beside) + len(across)),
        out_specs=tuple(whole(3)),
        compiler_params=params(),
        cost_estimate=small_cost(),
        name="plane_far",
    )(own[0], *beside, *across)
    best, own_columns, near_columns = pl.pallas_call(
        functools.partial(plane_kernel, rows, (1, len(near)), True),
        out_shape=(lanes, columns, columns),
        in_specs=whole(3 + len(near)),
        out_specs=tuple(whole(3)),
        compiler_params=params(),
        cost_estimate=small_cost(),
        name="plane_near",
    )(own[0], own[0], *near, best)

    plane = (own[0], *near, *beside, *across)
    plane_columns = (own_columns, near_columns, beside_columns, across_columns)
    plane_best = jnp.full((PLANE,) + lanes.shape, -1.0, jnp.float32)
    counts = (1, len(near), len(beside), len(across))
    for pairs, received in away:
        away_best = jnp.full(lanes.shape, -1.0, jnp.float32)
        for n, part in enumerate(received):
            away_best, plane_best = pl.pallas_call(
                functools.partial(cross_kernel, rows, n, counts),
                out_shape=(lanes, jax.ShapeDtypeStruct(plane_best.shape, jnp.float32)),
                in_specs=whole(len(plane) + PLANE + 4),
                out_specs=tuple(whole(2)),
                compiler_params=params(),
                cost_estimate=small_cost(),
                name="cross",
            )(received[0], part, *plane, *plane_columns, away_best, plane_best)
        back = lax.ppermute(away_best, "dp", [(t, s) for s, t in pairs])
        if len(pairs) < peers:
            z = me // PLANE
            half = planes // 2
            back = jnp.where((z % 2 == 0) == (z < half), back, -1.0)
        best = jnp.maximum(best, back)
    best = best.reshape(-1)[:rows]
    best = jnp.maximum(best, plane_best[0].reshape(-1)[:rows])
    for n, distance in ((3, 3), (2, 2), (1, 1)):
        back = mate(plane_best[n], distance)
        best = jnp.maximum(best, back.reshape(-1)[:rows])
    return best


def solution(mesh):
    in_specs = (P(("groups", "dp"), None), P(("groups", "dp")), P(("groups", "dp")), P("groups"))
    out_specs = P(("groups", "dp"))
    return jax.shard_map(local, mesh=mesh, in_specs=in_specs, out_specs=out_specs, check_vma=False)
```

time: 60.4 us -> 59.6 us (0.987)
  Pallas kernels: 10.3 us -> 12.8 us
  waiting for transfers between devices: 28.8 us -> 27.1 us
  local copies, waits for them, and re-layouts: 3.96 us -> 2.81 us
    ppermute x4 -> x2, waiting for transfers between devices: 15.8 us -> 9.91 us  [local(): away.append((pairs, [lax.ppermute(part, 'dp', pairs) for part in parts]))]
    pallas_call x7 -> x5, Pallas kernels: 10.3 us -> 12.8 us  [the longest x2 8.34 us: local(): pl.pallas_call(functools.partial(cross_kernel, rows, n, counts), out_shap...]
    ppermute x9 -> x8, waiting for transfers between devices: 9.85 us -> 12.2 us  [mate(): return lax.ppermute(value, 'dp', [(i, i ^ distance) for i in range(peers)])]
    ppermute x2, waiting for transfers between devices: 3.1 us -> 5.03 us  [local(): back = lax.ppermute(away_best, 'dp', [(t, s) for s, t in pairs])]
    ppermute x9 -> x8, starting transfers between devices: 6.48 us -> 5.34 us  [mate(): return lax.ppermute(value, 'dp', [(i, i ^ distance) for i in range(peers)])]
    ppermute x2, starting transfers between devices: 2.68 us -> 3.61 us  [local(): back = lax.ppermute(away_best, 'dp', [(t, s) for s, t in pairs])]
    reshape x1 -> x2, local copies, waits for them, and re-layouts: 0.71 us -> 1.39 us  [in_lanes(): return jnp.pad(values, (0, space)).reshape(lanes.shape)]
    unnamed x6 -> x2, local copies, waits for them, and re-layouts: 2.07 us -> 1.41 us
  transfers between devices with their start and end apart: 15 -> 12, of which waited for: 6 -> 5; matrix products, arithmetic and copies ran while one was open for 1% -> 0% of each run, Pallas kernels for 12% -> 12%
where the time goes in v4:
time: 59.6 us; the launch traced here: 59.3 us
  waiting for transfers between devices  27.1 us (45%)
  starting transfers between devices  15.9 us (27%)
  Pallas kernels  12.8 us (21%)
  local copies, waits for them, and re-layouts  2.81 us (5%)
  other arithmetic  0.6 us (1%)
    ppermute x8, waiting for transfers between devices, mate(): return lax.ppermute(value, 'dp', [(i, i ^ distance) for i in range(peers)])  12.2 us
    ppermute x2, waiting for transfers between devices, local(): away.append((pairs, [lax.ppermute(part, 'dp', pairs) for part in parts]))  9.91 us
    pallas_call x2, Pallas kernels, local(): pl.pallas_call(functools.partial(cross_kernel, rows, n, counts), out_shap...  8.34 us
    ppermute x2, starting transfers between devices, local(): away.append((pairs, [lax.ppermute(part, 'dp', pairs) for part in parts]))  6.96 us
    ppermute x8, starting transfers between devices, mate(): return lax.ppermute(value, 'dp', [(i, i ^ distance) for i in range(peers)])  5.34 us
    ppermute x2, waiting for transfers between devices, local(): back = lax.ppermute(away_best, 'dp', [(t, s) for s, t in pairs])  5.03 us
    ppermute x2, starting transfers between devices, local(): back = lax.ppermute(away_best, 'dp', [(t, s) for s, t in pairs])  3.61 us
    pallas_call x1, Pallas kernels, local(): pl.pallas_call(functools.partial(plane_kernel, rows, (len(beside), len(ac...  1.48 us
  transfers between devices with their start and end apart: 12, of which 5 were waited for; matrix products, arithmetic and copies ran while one was open for 0% of the time, Pallas kernels for 12%

profile of v4, /device:TPU:0, one launch (start us, length us, event | category | flops | bytes accessed | tf_op | source)
XLA Modules:
  0.0 59.3 jit_solution(12218326373312182636)
XLA Ops:
  0.0 0.7 %pad_bitcast_fusion.2.owner_ref = s32[8,128]{1,0:T(8,128)S(1)} fusion(s32[768]{0:T(1024)} %param.5), kind=kLoop, calls=%fused_computation.10 | loop fusion | bytes 7168 | tf_op jit(solution)/shard_map/reshape | solution.py:201
  0.7 0.7 %pad_bitcast_fusion = (s32[8,128]{1,0:T(8,128)S(1)}, s32[8,128]{1,0:T(8,128)S(1)}) fusion(s32[16]{0:T(128)} %param.7, s32[768]{0:T(1024)} %param.6), kind=kLoop, calls=%fused_computation.8 | loop fusion | bytes 11328 | tf_op jit(solution)/shard_map/reshape | solution.py:201
  1.4 1.4 %copy-done = f32[768,512]{1,0:T(8,128)S(1)} copy-done((f32[768,512]{1,0:T(8,128)S(1)}, f32[768,512]{1,0:T(8,128)}, u32[]{:S(2)}) %copy-start) | copy-done | bytes 1572888
  2.8 1.5 %pack.1 = (bf16[784,512]{1,0:T(8,128)(2,1)S(1)}, bf16[784,512]{1,0:T(8,128)(2,1)}, bf16[400,512]{1,0:T(8,128)(2,1)S(1)}, bf16[384,512]{1,0:T(8,128)(2,1)S(1)}, bf16[784,512]{1,0:T(8,128)(2,1)}) custom-call(f32[768,512]{1,0:T(8,128)S(1)} %copy-done, s32[8,128]{1,0:T(8,128)S(1)} %pad_bitcast_fusion.2.owner_ref, s32[8,128]{1,0:T(8,128)S(1)} %get-tuple-element.39.label_ref, ...), custom_call_target="tpu_custom_call" | custom-call | flops 1 | bytes 1 | tf_op jit(solution)/shard_map/pack/pallas_call | solution.py:205
  4.3 3.0 %collective-permute-start.1 = (bf16[400,512]{1,0:T(8,128)(2,1)S(1)}, bf16[400,512]{1,0:T(8,128)(2,1)S(1)}, u32[]{:S(2)}, u32[]{:S(2)}) collective-permute-start(bf16[400,512]{1,0:T(8,128)(2,1)S(1)} %get-tuple-element.22), channel_id=1, source_target_pairs={{0,2},{1,3},{2,0},{3,1},{4,6},{5,7},{6,4},{7,5},{8,10},{9,11},{10,... | collective-permute-start | bytes 1228808 | tf_op jit(solution)/shard_map/ppermute | solution.py:217
  7.2 0.0 collective-permute-start
  7.2 1.6 %collective-permute-start.5 = (bf16[784,512]{1,0:T(8,128)(2,1)S(1)}, bf16[784,512]{1,0:T(8,128)(2,1)}, u32[]{:S(2)}, u32[]{:S(2)}) collective-permute-start(bf16[784,512]{1,0:T(8,128)(2,1)S(1)} %get-tuple-element.20.own_ref.refs_0_), channel_id=1, source_target_pairs={{0,4},{1,5},{2,6},{3,7},{4,8},{5,9},{6,10},{7,11},{8,12},{9,13},{1... | collective-permute-start | bytes 2408456 | tf_op jit(solution)/shard_map/ppermute | solution.py:225
  8.8 5.4 %collective-permute-start.7 = (bf16[784,512]{1,0:T(8,128)(2,1)}, bf16[784,512]{1,0:T(8,128)(2,1)}, u32[]{:S(2)}, u32[]{:S(2)}) collective-permute-start(bf16[784,512]{1,0:T(8,128)(2,1)} %get-tuple-element.31), channel_id=1, source_target_pairs={{0,8},{1,9},{2,10},{3,11},{12,4},{13,5},{14,6},{15,7},{16,24},{17,... | collective-permute-start | bytes 2408456 | tf_op jit(solution)/shard_map/ppermute | solution.py:225
  14.2 0.5 collective-permute-start.2
  14.7 2.4 %collective-permute-done.1.refs_0_.refs_2_ = bf16[400,512]{1,0:T(8,128)(2,1)S(1)} collective-permute-done((bf16[400,512]{1,0:T(8,128)(2,1)S(1)}, bf16[400,512]{1,0:T(8,128)(2,1)S(1)}, u32[]{:S(2)}, u32[]{:S(2)}) %collective-permute-start.1) | collective-permute-done | bytes 409632 | tf_op jit(solution)/shard_map/ppermute | solution.py:217
  17.1 0.0 collective-permute-start.3
  17.1 8.1 %collective-permute-done.2.refs_1_.refs_3_ = bf16[384,512]{1,0:T(8,128)(2,1)S(1)} collective-permute-done((bf16[384,512]{1,0:T(8,128)(2,1)S(1)}, bf16[384,512]{1,0:T(8,128)(2,1)S(1)}, u32[]{:S(2)}, u32[]{:S(2)}) %collective-permute-start.2) | collective-permute-done | bytes 393248 | tf_op jit(solution)/shard_map/ppermute | solution.py:217
  25.2 1.7 %collective-permute-done.4.refs_3_.refs_5_ = bf16[384,512]{1,0:T(8,128)(2,1)S(1)} collective-permute-done((bf16[384,512]{1,0:T(8,128)(2,1)S(1)}, bf16[384,512]{1,0:T(8,128)(2,1)S(1)}, u32[]{:S(2)}, u32[]{:S(2)}) %collective-permute-start.4) | collective-permute-done | bytes 393248 | tf_op jit(solution)/shard_map/ppermute | solution.py:217
  26.9 1.5 %plane_far.1 = (f32[8,128]{1,0:T(8,128)S(1)}, f32[768,128]{1,0:T(8,128)S(1)}, f32[768,128]{1,0:T(8,128)S(1)}) custom-call(bf16[784,512]{1,0:T(8,128)(2,1)S(1)} %get-tuple-element.20.own_ref.refs_0_, bf16[400,512]{1,0:T(8,128)(2,1)S(1)} %collective-permute-done.1.refs_0_.refs_2_, bf16[384,512]{1,0:T(8,128)(2,1)S(1)} %collective-permute-done.2.refs_1_.refs_3_, ...), custom_call_target="tpu_custom_call" | custom-call | flops 1 | bytes 1 | tf_op jit(solution)/shard_map/plane_far/pallas_call | solution.py:231
  28.4 1.5 %plane_near.1 = (f32[8,128]{1,0:T(8,128)S(1)}, f32[768,128]{1,0:T(8,128)S(1)}, f32[768,128]{1,0:T(8,128)S(1)}) custom-call(bf16[784,512]{1,0:T(8,128)(2,1)S(1)} %get-tuple-element.20.own_ref.refs_0_, bf16[784,512]{1,0:T(8,128)(2,1)S(1)} %get-tuple-element.20.own_ref.refs_0_, bf16[784,512]{1,0:T(8,128)(2,1)S(1)} %collective-permute-done.refs_1_, ...), custom_call_target="tpu_custom_call" | custom-call | flops 1 | bytes 1 | tf_op jit(solution)/shard_map/plane_near/pallas_call | solution.py:240
  29.9 4.2 %cross.2 = (f32[8,128]{1,0:T(8,128)S(1)}, f32[4,8,128]{2,1,0:T(8,128)S(1)}) custom-call(bf16[784,512]{1,0:T(8,128)(2,1)} %collective-permute-done.5.tags_ref.away_ref, bf16[784,512]{1,0:T(8,128)(2,1)} %collective-permute-done.5.tags_ref.away_ref, bf16[784,512]{1,0:T(8,128)(2,1)S(1)} %get-tuple-element.20.own_ref.refs_0_, ...), custom_call_target="tpu_custom_call" | custom-call | flops 1 | bytes 1 | tf_op jit(solution)/shard_map/cross/pallas_call | solution.py:257
  34.1 9.9 %collective-permute-done.7.tags_ref.away_ref = bf16[784,512]{1,0:T(8,128)(2,1)} collective-permute-done((bf16[784,512]{1,0:T(8,128)(2,1)}, bf16[784,512]{1,0:T(8,128)(2,1)}, u32[]{:S(2)}, u32[]{:S(2)}) %collective-permute-start.7) | collective-permute-done | bytes 802848 | tf_op jit(solution)/shard_map/ppermute | solution.py:225
  44.0 4.2 %cross.3 = (f32[8,128]{1,0:T(8,128)S(1)}, f32[4,8,128]{2,1,0:T(8,128)S(1)}) custom-call(bf16[784,512]{1,0:T(8,128)(2,1)} %collective-permute-done.7.tags_ref.away_ref, bf16[784,512]{1,0:T(8,128)(2,1)} %collective-permute-done.7.tags_ref.away_ref, bf16[784,512]{1,0:T(8,128)(2,1)S(1)} %get-tuple-element.20.own_ref.refs_0_, ...), custom_call_target="tpu_custom_call" | custom-call | flops 1 | bytes 1 | tf_op jit(solution)/shard_map/cross/pallas_call | solution.py:257
  48.2 1.3 %collective-permute-start.8 = (f32[8,128]{1,0:T(8,128)S(1)}, f32[8,128]{1,0:T(8,128)S(1)}, u32[]{:S(2)}, u32[]{:S(2)}) collective-permute-start(f32[8,128]{1,0:T(8,128)S(1)} %get-tuple-element.33), channel_id=1, source_target_pairs={{8,0},{9,1},{10,2},{11,3},{4,12},{5,13},{6,14},{7,15},{24,16},{25,... | collective-permute-start | bytes 12296 | tf_op jit(solution)/shard_map/ppermute | solution.py:266
  49.5 2.3 %collective-permute-start.6 = (f32[8,128]{1,0:T(8,128)S(1)}, f32[8,128]{1,0:T(8,128)S(1)}, u32[]{:S(2)}, u32[]{:S(2)}) collective-permute-start(f32[8,128]{1,0:T(8,128)S(1)} %get-tuple-element.30), channel_id=1, source_target_pairs={{4,0},{5,1},{6,2},{7,3},{8,4},{9,5},{10,6},{11,7},{12,8},{13,9},{1... | collective-permute-start | bytes 12296 | tf_op jit(solution)/shard_map/ppermute | solution.py:266
  51.8 0.5 collective-permute-start.10
  52.3 1.4 %collective-permute-start.9 = (f32[8,128]{1,0:T(8,128)S(1)}, f32[8,128]{1,0:T(8,128)S(1)}, u32[]{:S(2)}, u32[]{:S(2)}) collective-permute-start(f32[8,128]{1,0:T(8,128)S(1)} %get-tuple-element.35), channel_id=1, source_target_pairs={{0,3},{1,2},{2,1},{3,0},{4,7},{5,6},{6,5},{7,4},{8,11},{9,10},{10,... | collective-permute-start | bytes 12296 | tf_op jit(solution)/shard_map/ppermute | solution.py:217
  53.7 5.0 %collective-permute-done.8 = f32[8,128]{1,0:T(8,128)S(1)} collective-permute-done((f32[8,128]{1,0:T(8,128)S(1)}, f32[8,128]{1,0:T(8,128)S(1)}, u32[]{:S(2)}, u32[]{:S(2)}) %collective-permute-start.8) | collective-permute-done | bytes 4128 | tf_op jit(solution)/shard_map/ppermute | solution.py:266
  58.7 0.6 %bitcast_maximum_fusion = f32[768]{0:T(1024)} fusion(f32[8,128]{1,0:T(8,128)S(1)} %collective-permute-done.11, f32[8,128]{1,0:T(8,128)S(1)} %collective-permute-done.10, f32[8,128]{1,0:T(8,128)S(1)} %collective-permute-done.9, f32[4,8,128]{2,1,0:T(8,128)S(1)} %get-tuple-element.34, f32[8,128]{1,0:T(8,128)S(1)} %select_maximum_fusion), kind=kLoop, calls=%fused_computation | loop fusion | flops 3072 | bytes 18432 | tf_op jit(solution)/shard_map/max | solution.py:276
  (14 shorter events, 0.0 us)
Async XLA Ops:
  1.4 1.4 %copy-start = (f32[768,512]{1,0:T(8,128)S(1)}, f32[768,512]{1,0:T(8,128)}, u32[]{:S(2)}) copy-start(f32[768,512]{1,0:T(8,128)} %embeddings_ref.1) | copy-start | bytes 4718596
  4.3 12.8 %collective-permute-start.1 = (bf16[400,512]{1,0:T(8,128)(2,1)S(1)}, bf16[400,512]{1,0:T(8,128)(2,1)S(1)}, u32[]{:S(2)}, u32[]{:S(2)}) collective-permute-start(bf16[400,512]{1,0:T(8,128)(2,1)S(1)} %get-tuple-element.22), channel_id=1, source_target_pairs={{0,2},{1,3},{2,0},{3,1},{4,6},{5,7},{6,4},{7,5},{8,10},{9,11},{10,... | collective-permute-start | bytes 1228808 | tf_op jit(solution)/shard_map/ppermute | solution.py:217
  7.2 21.1 %collective-permute-start = (bf16[784,512]{1,0:T(8,128)(2,1)}, bf16[784,512]{1,0:T(8,128)(2,1)S(1)}, u32[]{:S(2)}, u32[]{:S(2)}) collective-permute-start(bf16[784,512]{1,0:T(8,128)(2,1)} %get-tuple-element.21), channel_id=1, source_target_pairs={{0,1},{1,0},{2,3},{3,2},{4,5},{5,4},{6,7},{7,6},{8,9},{9,8},{10,11... | collective-permute-start | bytes 2408456 | tf_op jit(solution)/shard_map/ppermute | solution.py:217
  7.2 22.6 %collective-permute-start.5 = (bf16[784,512]{1,0:T(8,128)(2,1)S(1)}, bf16[784,512]{1,0:T(8,128)(2,1)}, u32[]{:S(2)}, u32[]{:S(2)}) collective-permute-start(bf16[784,512]{1,0:T(8,128)(2,1)S(1)} %get-tuple-element.20.own_ref.refs_0_), channel_id=1, source_target_pairs={{0,4},{1,5},{2,6},{3,7},{4,8},{5,9},{6,10},{7,11},{8,12},{9,13},{1... | collective-permute-start | bytes 2408456 | tf_op jit(solution)/shard_map/ppermute | solution.py:225
  8.8 35.2 %collective-permute-start.7 = (bf16[784,512]{1,0:T(8,128)(2,1)}, bf16[784,512]{1,0:T(8,128)(2,1)}, u32[]{:S(2)}, u32[]{:S(2)}) collective-permute-start(bf16[784,512]{1,0:T(8,128)(2,1)} %get-tuple-element.31), channel_id=1, source_target_pairs={{0,8},{1,9},{2,10},{3,11},{12,4},{13,5},{14,6},{15,7},{16,24},{17,... | collective-permute-start | bytes 2408456 | tf_op jit(solution)/shard_map/ppermute | solution.py:225
  14.2 11.0 %collective-permute-start.2 = (bf16[384,512]{1,0:T(8,128)(2,1)S(1)}, bf16[384,512]{1,0:T(8,128)(2,1)S(1)}, u32[]{:S(2)}, u32[]{:S(2)}) collective-permute-start(bf16[384,512]{1,0:T(8,128)(2,1)S(1)} %get-tuple-element.23), channel_id=1, source_target_pairs={{0,2},{1,3},{2,0},{3,1},{4,6},{5,7},{6,4},{7,5},{8,10},{9,11},{10,... | collective-permute-start | bytes 1179656 | tf_op jit(solution)/shard_map/ppermute | solution.py:217
  17.1 9.8 %collective-permute-start.3 = (bf16[400,512]{1,0:T(8,128)(2,1)S(1)}, bf16[400,512]{1,0:T(8,128)(2,1)S(1)}, u32[]{:S(2)}, u32[]{:S(2)}) collective-permute-start(bf16[400,512]{1,0:T(8,128)(2,1)S(1)} %collective-permute-done.1.refs_0_.refs_2_), channel_id=1, source_target_pairs={{0,1},{1,0},{2,3},{3,2},{4,5},{5,4},{6,7},{7,6},{8,9},{9,8},{10,11... | collective-permute-start | bytes 1228808 | tf_op jit(solution)/shard_map/ppermute | solution.py:217
  25.2 1.7 %collective-permute-start.4 = (bf16[384,512]{1,0:T(8,128)(2,1)S(1)}, bf16[384,512]{1,0:T(8,128)(2,1)S(1)}, u32[]{:S(2)}, u32[]{:S(2)}) collective-permute-start(bf16[384,512]{1,0:T(8,128)(2,1)S(1)} %collective-permute-done.2.refs_1_.refs_3_), channel_id=1, source_target_pairs={{0,1},{1,0},{2,3},{3,2},{4,5},{5,4},{6,7},{7,6},{8,9},{9,8},{10,11... | collective-permute-start | bytes 1179656 | tf_op jit(solution)/shard_map/ppermute | solution.py:217
  48.2 10.5 %collective-permute-start.8 = (f32[8,128]{1,0:T(8,128)S(1)}, f32[8,128]{1,0:T(8,128)S(1)}, u32[]{:S(2)}, u32[]{:S(2)}) collective-permute-start(f32[8,128]{1,0:T(8,128)S(1)} %get-tuple-element.33), channel_id=1, source_target_pairs={{8,0},{9,1},{10,2},{11,3},{4,12},{5,13},{6,14},{7,15},{24,16},{25,... | collective-permute-start | bytes 12296 | tf_op jit(solution)/shard_map/ppermute | solution.py:266
  49.5 9.2 %collective-permute-start.6 = (f32[8,128]{1,0:T(8,128)S(1)}, f32[8,128]{1,0:T(8,128)S(1)}, u32[]{:S(2)}, u32[]{:S(2)}) collective-permute-start(f32[8,128]{1,0:T(8,128)S(1)} %get-tuple-element.30), channel_id=1, source_target_pairs={{4,0},{5,1},{6,2},{7,3},{8,4},{9,5},{10,6},{11,7},{12,8},{13,9},{1... | collective-permute-start | bytes 12296 | tf_op jit(solution)/shard_map/ppermute | solution.py:266
  51.8 6.9 %collective-permute-start.11 = (f32[8,128]{1,0:T(8,128)S(1)}, f32[8,128]{1,0:T(8,128)S(1)}, u32[]{:S(2)}, u32[]{:S(2)}) collective-permute-start(f32[8,128]{1,0:T(8,128)S(1)} %get-tuple-element.36), channel_id=1, source_target_pairs={{0,1},{1,0},{2,3},{3,2},{4,5},{5,4},{6,7},{7,6},{8,9},{9,8},{10,11... | collective-permute-start | bytes 12296 | tf_op jit(solution)/shard_map/ppermute | solution.py:217
  51.8 6.9 %collective-permute-start.10 = (f32[8,128]{1,0:T(8,128)S(1)}, f32[8,128]{1,0:T(8,128)S(1)}, u32[]{:S(2)}, u32[]{:S(2)}) collective-permute-start(f32[8,128]{1,0:T(8,128)S(1)} %get-tuple-element.37), channel_id=1, source_target_pairs={{0,2},{1,3},{2,0},{3,1},{4,6},{5,7},{6,4},{7,5},{8,10},{9,11},{10,... | collective-permute-start | bytes 12296 | tf_op jit(solution)/shard_map/ppermute | solution.py:217
  52.3 6.4 %collective-permute-start.9 = (f32[8,128]{1,0:T(8,128)S(1)}, f32[8,128]{1,0:T(8,128)S(1)}, u32[]{:S(2)}, u32[]{:S(2)}) collective-permute-start(f32[8,128]{1,0:T(8,128)S(1)} %get-tuple-element.35), channel_id=1, source_target_pairs={{0,3},{1,2},{2,1},{3,0},{4,7},{5,6},{6,5},{7,4},{8,11},{9,10},{10,... | collective-permute-start | bytes 12296 | tf_op jit(solution)/shard_map/ppermute | solution.py:217

commit v5 on v4

--- a/solution.py
+++ b/solution.py
@@ -13,8 +13,8 @@
 BASE = 64.0
 TILE = 256
 AWAY_CUT = (3,)
-MATE_CUT = (1, 1)
-NEAR_CUT = (3,)
+MATE_CUT = (2, 1)
+NEAR_CUT = (2, 1)
 VMEM_LIMIT = 24 * 2**20
 
 
@@ -34,30 +34,32 @@
     return jax.ShapeDtypeStruct((-(-rows // 1024) * 8, 128), jnp.float32)
 
 
-def pack_kernel(rows, embeddings_ref, owner_ref, label_ref, run_ref, *part_refs):
-    owner = owner_ref[...]
-    runs = jnp.broadcast_to(run_ref[0:1, :], owner.shape)
-    first_owner = jnp.take_along_axis(runs, owner, axis=1)
-    label = label_ref[...]
+def pack_kernel(rows, embeddings_ref, ints_ref, *part_refs):
+    label_row = rows // 128
+    owner, label = ints_ref[0:8, :], ints_ref[label_row : label_row + 8, :]
+    runs = ints_ref[2 * label_row : 2 * label_row + 1, :]
+    first_owner = jnp.take_along_axis(jnp.broadcast_to(runs, owner.shape), owner, axis=1)
     tags = 1 + jnp.where(label == 0, first_owner * LABELS, owner * LABELS + label)
     tags = tags.astype(jnp.float32)
     high = jnp.floor(tags * (1.0 / BASE))
     digits = jnp.concatenate([high, tags - high * BASE], axis=0).astype(jnp.bfloat16)
     width = embeddings_ref.shape[1]
     digits = jnp.concatenate([digits, jnp.zeros((PAD, width - 128), jnp.bfloat16)], axis=1)
-    values = embeddings_ref[...]
-    squares = jnp.sum(values * values, axis=1, keepdims=True)
-    unit = (values * lax.rsqrt(squares + 1e-06)).astype(jnp.bfloat16)
-    first = 0
+    places, first = [], 0
     for part_ref in part_refs:
-        if first == 0:
+        base = PAD if first == 0 else 0
+        if base:
             part_ref[0:PAD, :] = digits
-            count = part_ref.shape[0] - PAD
-            part_ref[PAD:, :] = unit[0:count]
-        else:
-            count = part_ref.shape[0]
-            part_ref[...] = unit[first : first + count]
+        count = part_ref.shape[0] - base
+        places.append((part_ref, base - first, first, first + count))
         first = (first + count) % rows
+    for row in range(0, rows, 128):
+        values = embeddings_ref[row : row + 128, :]
+        squares = jnp.sum(values * values, axis=1, keepdims=True)
+        unit = (values * lax.rsqrt(squares + 1e-06)).astype(jnp.bfloat16)
+        for part_ref, shift, start, stop in places:
+            if start <= row < stop:
+                part_ref[row + shift : row + shift + 128, :] = unit
 
 
 def tag_rows(block_ref):
@@ -111,33 +113,45 @@
     )
 
 
+def row_slices(block):
+    slices = []
+    for first, part in unit_parts(block):
+        count = part.shape[0]
+        for row in range(0, count, TILE):
+            size = min(TILE, count - row)
+            slices.append((first + row, part.at[row : row + size]))
+    return slices
+
+
 def plane_kernel(rows, counts, with_self, own_ref, *refs):
     blocks, refs = take(refs, counts)
     best_ref, column_refs = refs[-1 - len(counts)], refs[-len(counts) :]
-    if with_self:
-        best_ref[...] = refs[0][...]
-    else:
-        best_ref[...] = jnp.full(best_ref.shape, -1.0, jnp.float32)
     own_tags = tag_rows(own_ref)
     for block, column_ref in zip(blocks, column_refs):
         column_ref[...] = tag_columns(block[0], rows)
     for tile in range(0, rows, TILE):
         lanes = own_ref[PAD + tile : PAD + tile + TILE, :]
+        best = [jnp.full((8, 128), -1.0, jnp.float32) for _ in range(0, TILE, 128)]
         for which, (block, column_ref) in enumerate(zip(blocks, column_refs)):
-            for first, part in unit_parts(block):
+            for first, part in row_slices(block):
                 count = part.shape[0]
                 found = dot_rows(part[...], lanes)
-                for lane in range(0, TILE, 128):
-                    row = (tile + lane) // 128
-                    match = column_ref[first : first + count, :] == own_tags[row : row + 1]
-                    if with_self and which == 0:
+                column = column_ref[first : first + count, :]
+                for n in range(TILE // 128):
+                    lane = tile + n * 128
+                    match = column == own_tags[lane // 128 : lane // 128 + 1]
+                    if with_self and which == 0 and first < lane + 128 and lane < first + count:
                         row_id = lax.broadcasted_iota(jnp.int32, (count, 128), 0) + first
-                        lane_id = lax.broadcasted_iota(jnp.int32, (count, 128), 1) + tile + lane
+                        lane_id = lax.broadcasted_iota(jnp.int32, (count, 128), 1) + lane
                         match = match & (row_id != lane_id)
-                    masked = jnp.where(match, found[:, lane : lane + 128], -1.0)
-                    folded = jnp.max(fold_sublanes(masked), axis=0, keepdims=True)
-                    place = pl.ds(row, 1)
-                    best_ref[place, :] = jnp.maximum(best_ref[place, :], folded)
+                    masked = jnp.where(match, found[:, n * 128 : n * 128 + 128], -1.0)
+                    best[n] = jnp.maximum(best[n], fold_sublanes(masked))
+        for n in range(TILE // 128):
+            place = pl.ds((tile + n * 128) // 128, 1)
+            folded = jnp.max(best[n], axis=0, keepdims=True)
+            if with_self:
+                folded = jnp.maximum(folded, refs[0][place, :])
+            best_ref[place, :] = folded
 
 
 def cross_kernel(rows, index, counts, tags_ref, away_ref, *refs):
@@ -147,26 +161,28 @@
     away_tags = tag_rows(tags_ref)
     away = away_ref if index else away_ref.at[PAD:]
     away_rows = away.shape[0]
-    away_best[...] = away_before[...]
+    best = [jnp.full((8, 128), -1.0, jnp.float32) for _ in range(0, away_rows, 128)]
     for which in range(PLANE):
-        for start, part in unit_parts(blocks[which]):
+        for first, part in row_slices(blocks[which]):
             count = part.shape[0]
             row_best = jnp.full((count, 128), -1.0, jnp.float32)
-            column = columns[which][start : start + count, :]
             for tile in range(0, away_rows, TILE):
                 lanes = min(TILE, away_rows - tile)
                 found = dot_rows(part[...], away[tile : tile + lanes, :])
-                for lane in range(0, lanes, 128):
-                    row = (index * away_rows + tile + lane) // 128
+                column = columns[which][first : first + count, :]
+                for lane in range(tile, tile + lanes, 128):
+                    row = (index * away_rows + lane) // 128
                     match = column == away_tags[row : row + 1]
-                    masked = jnp.where(match, found[:, lane : lane + 128], -1.0)
+                    masked = jnp.where(match, found[:, lane - tile : lane - tile + 128], -1.0)
                     row_best = jnp.maximum(row_best, masked)
-                    folded = jnp.max(fold_sublanes(masked), axis=0, keepdims=True)
-                    place = pl.ds(row, 1)
-                    away_best[place, :] = jnp.maximum(away_best[place, :], folded)
-            place = pl.ds(start // 128, count // 128)
+                    best[lane // 128] = jnp.maximum(best[lane // 128], fold_sublanes(masked))
+            place = pl.ds(first // 128, count // 128)
             folded = fold_lanes(row_best)
             plane_best[which, place, :] = jnp.maximum(folded, plane_before[which, place, :])
+    away_best[...] = away_before[...]
+    for n, values in enumerate(best):
+        place = pl.ds(index * away_rows // 128 + n, 1)
+        away_best[place, :] = jnp.max(values, axis=0, keepdims=True)
 
 
 def small_cost():
@@ -174,14 +190,14 @@
 
 
 def plane_steps(planes):
+    if planes == 4:
+        return [[(0, 2), (2, 3), (3, 1)], [(0, 1), (1, 2), (3, 0)]]
     steps = []
     for distance in range(1, planes // 2 + 1):
         if 2 * distance < planes:
             steps.append([(z, (z + distance) % planes) for z in range(planes)])
         else:
-            steps.append(
-                [(z, z + distance) if z % 2 == 0 else (z + distance, z) for z in range(distance)]
-            )
+            steps.append([(z, z + distance) for z in range(distance)])
     return steps
 
 
@@ -196,21 +212,20 @@
     me = lax.axis_index("dp")
     lanes = lanes_shape(rows)
 
-    def in_lanes(values):
-        space = lanes.shape[0] * 128 - values.shape[0]
-        return jnp.pad(values, (0, space)).reshape(lanes.shape)
-
+    space = -(2 * rows + peers) % 2048
+    ints = jnp.concatenate([owner_index, sub_label, run_start, jnp.zeros((space,), jnp.int32)])
+    ints = ints.reshape(-1, 128)
     ways = ((1,), AWAY_CUT, MATE_CUT, NEAR_CUT)
     sizes = sum((cuts(rows, way) for way in ways), [])
     packed = pl.pallas_call(
         functools.partial(pack_kernel, rows),
         out_shape=tuple(jax.ShapeDtypeStruct((size, width), jnp.bfloat16) for size in sizes),
-        in_specs=whole(4),
+        in_specs=whole(2),
         out_specs=tuple(whole(len(sizes))),
         compiler_params=params(),
         cost_estimate=small_cost(),
         name="pack",
-    )(embeddings, in_lanes(owner_index), in_lanes(sub_label), in_lanes(run_start))
+    )(embeddings, ints)
     own, to_away, to_mate, to_near = take(packed, [len(way) for way in ways])[0]
 
     def mate(value, distance):
@@ -251,7 +266,9 @@
     plane_columns = (own_columns, near_columns, beside_columns, across_columns)
     plane_best = jnp.full((PLANE,) + lanes.shape, -1.0, jnp.float32)
     counts = (1, len(near), len(beside), len(across))
-    for pairs, received in away:
+    for step, (pairs, received) in enumerate(away):
+        if step:
+            plane_best = after(plane_best, best)
         away_best = jnp.full(lanes.shape, -1.0, jnp.float32)
         for n, part in enumerate(received):
             away_best, plane_best = pl.pallas_call(
@@ -265,9 +282,9 @@
             )(received[0], part, *plane, *plane_columns, away_best, plane_best)
         back = lax.ppermute(away_best, "dp", [(t, s) for s, t in pairs])
         if len(pairs) < peers:
-            z = me // PLANE
-            half = planes // 2
-            back = jnp.where((z % 2 == 0) == (z < half), back, -1.0)
+            sources = sum(1 << z for z in {s // PLANE for s, _ in pairs})
+            sent = (jnp.uint32(sources) >> (me // PLANE).astype(jnp.uint32)) & 1
+            back = jnp.where(sent == 1, back, -1.0)
         best = jnp.maximum(best, back)
     best = best.reshape(-1)[:rows]
     best = jnp.maximum(best, plane_best[0].reshape(-1)[:rows])

time: 59.6 us -> 64.7 us (1.086)
  local copies, waits for them, and re-layouts: 2.81 us -> 8.1 us
  Pallas kernels: 12.8 us -> 9.76 us
  starting transfers between devices: 15.9 us -> 18.2 us
    unnamed x2 -> x26, local copies, waits for them, and re-layouts: 1.41 us -> 7.31 us
    pallas_call x2, Pallas kernels: 8.34 us -> 5.6 us  [local(): pl.pallas_call(functools.partial(cross_kernel, rows, n, counts), out_shap...]
    ppermute x2, waiting for transfers between devices: 9.91 us -> 7.73 us  [local(): away.append((pairs, [lax.ppermute(part, 'dp', pairs) for part in parts]))]
    ppermute x2, starting transfers between devices: 3.61 us -> 5.69 us  [local(): back = lax.ppermute(away_best, 'dp', [(t, s) for s, t in pairs])]
    ppermute x8 -> x9, waiting for transfers between devices: 12.2 us -> 13.7 us  [mate(): return lax.ppermute(value, 'dp', [(i, i ^ distance) for i in range(peers)])]
    reshape x2 -> x0, local copies, waits for them, and re-layouts: 1.39 us -> none  [in_lanes(): return jnp.pad(values, (0, space)).reshape(lanes.shape)]
    ppermute x2, waiting for transfers between devices: 5.03 us -> 5.9 us  [local(): back = lax.ppermute(away_best, 'dp', [(t, s) for s, t in pairs])]
    ppermute x8 -> x9, starting transfers between devices: 5.34 us -> 6.12 us  [mate(): return lax.ppermute(value, 'dp', [(i, i ^ distance) for i in range(peers)])]
  transfers between devices with their start and end apart: 12 -> 13, of which waited for: 5 -> 7; matrix products, arithmetic and copies ran while one was open for 0% -> 0% of each run, Pallas kernels for 12% -> 9%
where the time goes in v5:
time: 64.7 us; the launch traced here: 64.2 us
  waiting for transfers between devices  27.3 us (42%)
  starting transfers between devices  18.2 us (28%)
  Pallas kernels  9.76 us (15%)
  local copies, waits for them, and re-layouts  8.1 us (13%)
    ppermute x9, waiting for transfers between devices, mate(): return lax.ppermute(value, 'dp', [(i, i ^ distance) for i in range(peers)])  13.7 us
    ppermute x2, waiting for transfers between devices, local(): away.append((pairs, [lax.ppermute(part, 'dp', pairs) for part in parts]))  7.73 us
    unnamed x26, local copies, waits for them, and re-layouts  7.31 us
    ppermute x2, starting transfers between devices, local(): away.append((pairs, [lax.ppermute(part, 'dp', pairs) for part in parts]))  6.44 us
    ppermute x9, starting transfers between devices, mate(): return lax.ppermute(value, 'dp', [(i, i ^ distance) for i in range(peers)])  6.12 us
    ppermute x2, waiting for transfers between devices, local(): back = lax.ppermute(away_best, 'dp', [(t, s) for s, t in pairs])  5.9 us
    ppermute x2, starting transfers between devices, local(): back = lax.ppermute(away_best, 'dp', [(t, s) for s, t in pairs])  5.69 us
    pallas_call x2, Pallas kernels, local(): pl.pallas_call(functools.partial(cross_kernel, rows, n, counts), out_shap...  5.6 us
  transfers between devices with their start and end apart: 13, of which 7 were waited for; matrix products, arithmetic and copies ran while one was open for 0% of the time, Pallas kernels for 9%

profile of v5, /device:TPU:0, one launch (start us, length us, event | category | flops | bytes accessed | tf_op | source)
XLA Modules:
  0.0 64.2 jit_solution(13125927317119471186)
XLA Ops:
  0.8 1.4 %copy-done.4 = f32[768,512]{1,0:T(8,128)S(1)} copy-done((f32[768,512]{1,0:T(8,128)S(1)}, f32[768,512]{1,0:T(8,128)}, u32[]{:S(2)}) %copy-start.4) | copy-done | bytes 1572888
  2.2 1.2 %pack.1 = (bf16[784,512]{1,0:T(8,128)(2,1)S(1)}, bf16[784,512]{1,0:T(8,128)(2,1)}, bf16[528,512]{1,0:T(8,128)(2,1)S(1)}, bf16[256,512]{1,0:T(8,128)(2,1)S(1)}, b...) custom-call(f32[768,512]{1,0:T(8,128)S(1)} %copy-done.4, s32[16,128]{1,0:T(8,128)S(1)} %bitcast.23), custom_call_target="tpu_custom_call" | custom-call | flops 1 | bytes 1 | tf_op jit(solution)/shard_map/pack/pallas_call | solution.py:220
  3.4 3.0 %collective-permute-start.2 = (bf16[528,512]{1,0:T(8,128)(2,1)S(1)}, bf16[528,512]{1,0:T(8,128)(2,1)S(1)}, u32[]{:S(2)}, u32[]{:S(2)}) collective-permute-start(bf16[528,512]{1,0:T(8,128)(2,1)S(1)} %get-tuple-element.25), channel_id=1, source_target_pairs={{0,2},{1,3},{2,0},{3,1},{4,6},{5,7},{6,4},{7,5},{8,10},{9,11},{10,... | collective-permute-start | bytes 1622024 | tf_op jit(solution)/shard_map/ppermute | solution.py:232
  6.3 4.5 %collective-permute-start.6 = (bf16[784,512]{1,0:T(8,128)(2,1)S(1)}, bf16[784,512]{1,0:T(8,128)(2,1)S(1)}, u32[]{:S(2)}, u32[]{:S(2)}) collective-permute-start(bf16[784,512]{1,0:T(8,128)(2,1)S(1)} %get-tuple-element.22.own_ref.refs_0_), channel_id=1, source_target_pairs={{0,8},{1,9},{2,10},{3,11},{8,12},{9,13},{10,14},{11,15},{12,4},{13... | collective-permute-start | bytes 2408456 | tf_op jit(solution)/shard_map/ppermute | solution.py:240
  11.5 1.9 %collective-permute-start.8 = (bf16[784,512]{1,0:T(8,128)(2,1)}, bf16[784,512]{1,0:T(8,128)(2,1)S(1)}, u32[]{:S(2)}, u32[]{:S(2)}) collective-permute-start(bf16[784,512]{1,0:T(8,128)(2,1)} %get-tuple-element.34), channel_id=1, source_target_pairs={{0,4},{1,5},{2,6},{3,7},{4,8},{5,9},{6,10},{7,11},{12,0},{13,1},{1... | collective-permute-start | bytes 2408456 | tf_op jit(solution)/shard_map/ppermute | solution.py:240
  13.4 6.1 %collective-permute-done.2.refs_0_.refs_3_ = bf16[528,512]{1,0:T(8,128)(2,1)S(1)} collective-permute-done((bf16[528,512]{1,0:T(8,128)(2,1)S(1)}, bf16[528,512]{1,0:T(8,128)(2,1)S(1)}, u32[]{:S(2)}, u32[]{:S(2)}) %collective-permute-start.2) | collective-permute-done | bytes 540704 | tf_op jit(solution)/shard_map/ppermute | solution.py:232
  20.0 4.3 %collective-permute-done.3.refs_1_.refs_4_ = bf16[256,512]{1,0:T(8,128)(2,1)S(1)} collective-permute-done((bf16[256,512]{1,0:T(8,128)(2,1)S(1)}, bf16[256,512]{1,0:T(8,128)(2,1)S(1)}, u32[]{:S(2)}, u32[]{:S(2)}) %collective-permute-start.3) | collective-permute-done | bytes 262176 | tf_op jit(solution)/shard_map/ppermute | solution.py:232
  24.2 1.5 %collective-permute-done.5.refs_3_.refs_6_ = bf16[256,512]{1,0:T(8,128)(2,1)S(1)} collective-permute-done((bf16[256,512]{1,0:T(8,128)(2,1)S(1)}, bf16[256,512]{1,0:T(8,128)(2,1)S(1)}, u32[]{:S(2)}, u32[]{:S(2)}) %collective-permute-start.5) | collective-permute-done | bytes 262176 | tf_op jit(solution)/shard_map/ppermute | solution.py:232
  25.9 1.5 %plane_far.1 = (f32[8,128]{1,0:T(8,128)S(1)}, f32[768,128]{1,0:T(8,128)S(1)}, f32[768,128]{1,0:T(8,128)S(1)}) custom-call(bf16[784,512]{1,0:T(8,128)(2,1)S(1)} %get-tuple-element.22.own_ref.refs_0_, bf16[528,512]{1,0:T(8,128)(2,1)S(1)} %collective-permute-done.2.refs_0_.refs_3_, bf16[256,512]{1,0:T(8,128)(2,1)S(1)} %collective-permute-done.3.refs_1_.refs_4_, ...), custom_call_target="tpu_custom_call" | custom-call | flops 1 | bytes 1 | tf_op jit(solution)/shard_map/plane_far/pallas_call | solution.py:246
  27.5 1.5 %plane_near.1 = (f32[8,128]{1,0:T(8,128)S(1)}, f32[768,128]{1,0:T(8,128)S(1)}, f32[768,128]{1,0:T(8,128)S(1)}) custom-call(bf16[784,512]{1,0:T(8,128)(2,1)S(1)} %get-tuple-element.22.own_ref.refs_0_, bf16[784,512]{1,0:T(8,128)(2,1)S(1)} %get-tuple-element.22.own_ref.refs_0_, bf16[528,512]{1,0:T(8,128)(2,1)S(1)} %collective-permute-done.refs_1_, ...), custom_call_target="tpu_custom_call" | custom-call | flops 1 | bytes 1 | tf_op jit(solution)/shard_map/plane_near/pallas_call | solution.py:255
  29.2 2.8 %cross.2 = (f32[8,128]{1,0:T(8,128)S(1)}, f32[4,8,128]{2,1,0:T(8,128)S(1)}) custom-call(bf16[784,512]{1,0:T(8,128)(2,1)S(1)} %collective-permute-done.6.tags_ref.away_ref, bf16[784,512]{1,0:T(8,128)(2,1)S(1)} %collective-permute-done.6.tags_ref.away_ref, bf16[784,512]{1,0:T(8,128)(2,1)S(1)} %get-tuple-element.22.own_ref.refs_0_, ...), custom_call_target="tpu_custom_call" | custom-call | flops 1 | bytes 1 | tf_op jit(solution)/shard_map/cross/pallas_call | solution.py:274
  32.1 1.3 %collective-permute-start.7 = (f32[8,128]{1,0:T(8,128)S(1)}, f32[8,128]{1,0:T(8,128)S(1)}, u32[]{:S(2)}, u32[]{:S(2)}) collective-permute-start(f32[8,128]{1,0:T(8,128)S(1)} %get-tuple-element.33), channel_id=1, source_target_pairs={{8,0},{9,1},{10,2},{11,3},{12,8},{13,9},{14,10},{15,11},{4,12},{5,... | collective-permute-start | bytes 12296 | tf_op jit(solution)/shard_map/ppermute | solution.py:283
  33.4 5.9 %collective-permute-done.7 = f32[8,128]{1,0:T(8,128)S(1)} collective-permute-done((f32[8,128]{1,0:T(8,128)S(1)}, f32[8,128]{1,0:T(8,128)S(1)}, u32[]{:S(2)}, u32[]{:S(2)}) %collective-permute-start.7) | collective-permute-done | bytes 4128 | tf_op jit(solution)/shard_map/ppermute | solution.py:283
  39.3 7.5 %collective-permute-done.8.tags_ref.away_ref = bf16[784,512]{1,0:T(8,128)(2,1)S(1)} collective-permute-done((bf16[784,512]{1,0:T(8,128)(2,1)}, bf16[784,512]{1,0:T(8,128)(2,1)S(1)}, u32[]{:S(2)}, u32[]{:S(2)}) %collective-permute-start.8) | collective-permute-done | bytes 802848 | tf_op jit(solution)/shard_map/ppermute | solution.py:240
  46.8 0.9 %copy-done.1 = bf16[256,512]{1,0:T(8,128)(2,1)S(1)} copy-done((bf16[256,512]{1,0:T(8,128)(2,1)S(1)}, bf16[256,512]{1,0:T(8,128)(2,1)}, u32[]{:S(2)}) %copy-start.1) | copy-done | bytes 262168
  47.7 0.9 %copy-done.3 = bf16[256,512]{1,0:T(8,128)(2,1)S(1)} copy-done((bf16[256,512]{1,0:T(8,128)(2,1)S(1)}, bf16[256,512]{1,0:T(8,128)(2,1)}, u32[]{:S(2)}) %copy-start.3) | copy-done | bytes 262168
  48.7 1.0 %copy-done.6 = f32[768,128]{1,0:T(8,128)S(1)} copy-done((f32[768,128]{1,0:T(8,128)S(1)}, f32[768,128]{1,0:T(8,128)}, u32[]{:S(2)}) %copy-start.6) | copy-done | bytes 393240
  49.7 1.0 %copy-done.8 = f32[768,128]{1,0:T(8,128)S(1)} copy-done((f32[768,128]{1,0:T(8,128)S(1)}, f32[768,128]{1,0:T(8,128)}, u32[]{:S(2)}) %copy-start.8) | copy-done | bytes 393240
  50.7 1.0 %copy-done.10 = f32[768,128]{1,0:T(8,128)S(1)} copy-done((f32[768,128]{1,0:T(8,128)S(1)}, f32[768,128]{1,0:T(8,128)}, u32[]{:S(2)}) %copy-start.10) | copy-done | bytes 393240
  51.7 1.0 %copy-done.12 = f32[768,128]{1,0:T(8,128)S(1)} copy-done((f32[768,128]{1,0:T(8,128)S(1)}, f32[768,128]{1,0:T(8,128)}, u32[]{:S(2)}) %copy-start.12) | copy-done | bytes 393240
  52.7 2.8 %cross.3 = (f32[8,128]{1,0:T(8,128)S(1)}, f32[4,8,128]{2,1,0:T(8,128)S(1)}) custom-call(bf16[784,512]{1,0:T(8,128)(2,1)S(1)} %collective-permute-done.8.tags_ref.away_ref, bf16[784,512]{1,0:T(8,128)(2,1)S(1)} %collective-permute-done.8.tags_ref.away_ref, bf16[784,512]{1,0:T(8,128)(2,1)S(1)} %get-tuple-element.22.own_ref.refs_0_, ...), custom_call_target="tpu_custom_call" | custom-call | flops 1 | bytes 1 | tf_op jit(solution)/shard_map/cross/pallas_call | solution.py:274
  55.5 4.4 %collective-permute-start.9 = (f32[8,128]{1,0:T(8,128)S(1)}, f32[8,128]{1,0:T(8,128)S(1)}, u32[]{:S(2)}, u32[]{:S(2)}) collective-permute-start(f32[8,128]{1,0:T(8,128)S(1)} %get-tuple-element.37), channel_id=1, source_target_pairs={{4,0},{5,1},{6,2},{7,3},{8,4},{9,5},{10,6},{11,7},{0,12},{1,13},{2... | collective-permute-start | bytes 12296 | tf_op jit(solution)/shard_map/ppermute | solution.py:283
  60.5 1.3 %collective-permute-start.10 = (f32[8,128]{1,0:T(8,128)S(1)}, f32[8,128]{1,0:T(8,128)S(1)}, u32[]{:S(2)}, u32[]{:S(2)}) collective-permute-start(f32[8,128]{1,0:T(8,128)S(1)} %get-tuple-element.39), channel_id=1, source_target_pairs={{0,3},{1,2},{2,1},{3,0},{4,7},{5,6},{6,5},{7,4},{8,11},{9,10},{10,... | collective-permute-start | bytes 12296 | tf_op jit(solution)/shard_map/ppermute | solution.py:232
  61.8 1.8 %collective-permute-done.11 = f32[8,128]{1,0:T(8,128)S(1)} collective-permute-done((f32[8,128]{1,0:T(8,128)S(1)}, f32[8,128]{1,0:T(8,128)S(1)}, u32[]{:S(2)}, u32[]{:S(2)}) %collective-permute-start.11) | collective-permute-done | bytes 4128 | tf_op jit(solution)/shard_map/ppermute | solution.py:232
  (41 shorter events, 3.5 us)
Async XLA Ops:
  0.8 1.4 %copy-start.4 = (f32[768,512]{1,0:T(8,128)S(1)}, f32[768,512]{1,0:T(8,128)}, u32[]{:S(2)}) copy-start(f32[768,512]{1,0:T(8,128)} %embeddings_ref.1) | copy-start | bytes 4718596
  3.4 16.1 %collective-permute-start.2 = (bf16[528,512]{1,0:T(8,128)(2,1)S(1)}, bf16[528,512]{1,0:T(8,128)(2,1)S(1)}, u32[]{:S(2)}, u32[]{:S(2)}) collective-permute-start(bf16[528,512]{1,0:T(8,128)(2,1)S(1)} %get-tuple-element.25), channel_id=1, source_target_pairs={{0,2},{1,3},{2,0},{3,1},{4,6},{5,7},{6,4},{7,5},{8,10},{9,11},{10,... | collective-permute-start | bytes 1622024 | tf_op jit(solution)/shard_map/ppermute | solution.py:232
  6.3 22.8 %collective-permute-start.6 = (bf16[784,512]{1,0:T(8,128)(2,1)S(1)}, bf16[784,512]{1,0:T(8,128)(2,1)S(1)}, u32[]{:S(2)}, u32[]{:S(2)}) collective-permute-start(bf16[784,512]{1,0:T(8,128)(2,1)S(1)} %get-tuple-element.22.own_ref.refs_0_), channel_id=1, source_target_pairs={{0,8},{1,9},{2,10},{3,11},{8,12},{9,13},{10,14},{11,15},{12,4},{13... | collective-permute-start | bytes 2408456 | tf_op jit(solution)/shard_map/ppermute | solution.py:240
  10.9 13.3 %collective-permute-start.3 = (bf16[256,512]{1,0:T(8,128)(2,1)S(1)}, bf16[256,512]{1,0:T(8,128)(2,1)S(1)}, u32[]{:S(2)}, u32[]{:S(2)}) collective-permute-start(bf16[256,512]{1,0:T(8,128)(2,1)S(1)} %get-tuple-element.26), channel_id=1, source_target_pairs={{0,2},{1,3},{2,0},{3,1},{4,6},{5,7},{6,4},{7,5},{8,10},{9,11},{10,... | collective-permute-start | bytes 786440 | tf_op jit(solution)/shard_map/ppermute | solution.py:232
  11.5 35.3 %collective-permute-start.8 = (bf16[784,512]{1,0:T(8,128)(2,1)}, bf16[784,512]{1,0:T(8,128)(2,1)S(1)}, u32[]{:S(2)}, u32[]{:S(2)}) collective-permute-start(bf16[784,512]{1,0:T(8,128)(2,1)} %get-tuple-element.34), channel_id=1, source_target_pairs={{0,4},{1,5},{2,6},{3,7},{4,8},{5,9},{6,10},{7,11},{12,0},{13,1},{1... | collective-permute-start | bytes 2408456 | tf_op jit(solution)/shard_map/ppermute | solution.py:240
  19.4 6.5 %collective-permute-start.4 = (bf16[528,512]{1,0:T(8,128)(2,1)S(1)}, bf16[528,512]{1,0:T(8,128)(2,1)S(1)}, u32[]{:S(2)}, u32[]{:S(2)}) collective-permute-start(bf16[528,512]{1,0:T(8,128)(2,1)S(1)} %collective-permute-done.2.refs_0_.refs_3_), channel_id=1, source_target_pairs={{0,1},{1,0},{2,3},{3,2},{4,5},{5,4},{6,7},{7,6},{8,9},{9,8},{10,11... | collective-permute-start | bytes 1622024 | tf_op jit(solution)/shard_map/ppermute | solution.py:232
  19.5 8.0 %collective-permute-start = (bf16[528,512]{1,0:T(8,128)(2,1)S(1)}, bf16[528,512]{1,0:T(8,128)(2,1)S(1)}, u32[]{:S(2)}, u32[]{:S(2)}) collective-permute-start(bf16[528,512]{1,0:T(8,128)(2,1)S(1)} %get-tuple-element.23), channel_id=1, source_target_pairs={{0,1},{1,0},{2,3},{3,2},{4,5},{5,4},{6,7},{7,6},{8,9},{9,8},{10,11... | collective-permute-start | bytes 1622024 | tf_op jit(solution)/shard_map/ppermute | solution.py:232
  24.2 1.5 %collective-permute-start.5 = (bf16[256,512]{1,0:T(8,128)(2,1)S(1)}, bf16[256,512]{1,0:T(8,128)(2,1)S(1)}, u32[]{:S(2)}, u32[]{:S(2)}) collective-permute-start(bf16[256,512]{1,0:T(8,128)(2,1)S(1)} %collective-permute-done.3.refs_1_.refs_4_), channel_id=1, source_target_pairs={{0,1},{1,0},{2,3},{3,2},{4,5},{5,4},{6,7},{7,6},{8,9},{9,8},{10,11... | collective-permute-start | bytes 786440 | tf_op jit(solution)/shard_map/ppermute | solution.py:232
  25.8 3.4 %copy-start = (bf16[256,512]{1,0:T(8,128)(2,1)}, bf16[256,512]{1,0:T(8,128)(2,1)S(1)}, u32[]{:S(2)}) copy-start(bf16[256,512]{1,0:T(8,128)(2,1)S(1)} %collective-permute-done.5.refs_3_.refs_6_) | copy-start | bytes 786436
  25.8 1.6 %collective-permute-start.1 = (bf16[256,512]{1,0:T(8,128)(2,1)S(1)}, bf16[256,512]{1,0:T(8,128)(2,1)S(1)}, u32[]{:S(2)}, u32[]{:S(2)}) collective-permute-start(bf16[256,512]{1,0:T(8,128)(2,1)S(1)} %get-tuple-element.24), channel_id=1, source_target_pairs={{0,1},{1,0},{2,3},{3,2},{4,5},{5,4},{6,7},{7,6},{8,9},{9,8},{10,11... | collective-permute-start | bytes 786440 | tf_op jit(solution)/shard_map/ppermute | solution.py:232
  27.4 4.6 %copy-start.5 = (f32[768,128]{1,0:T(8,128)}, f32[768,128]{1,0:T(8,128)S(1)}, u32[]{:S(2)}) copy-start(f32[768,128]{1,0:T(8,128)S(1)} %get-tuple-element.31.refs_9_) | copy-start | bytes 1179652
  27.4 4.6 %copy-start.7 = (f32[768,128]{1,0:T(8,128)}, f32[768,128]{1,0:T(8,128)S(1)}, u32[]{:S(2)}) copy-start(f32[768,128]{1,0:T(8,128)S(1)} %get-tuple-element.32.refs_10_) | copy-start | bytes 1179652
  27.4 4.6 %copy-start.2 = (bf16[256,512]{1,0:T(8,128)(2,1)}, bf16[256,512]{1,0:T(8,128)(2,1)S(1)}, u32[]{:S(2)}) copy-start(bf16[256,512]{1,0:T(8,128)(2,1)S(1)} %collective-permute-done.1.refs_2_) | copy-start | bytes 786436
  28.9 3.1 %copy-start.9 = (f32[768,128]{1,0:T(8,128)}, f32[768,128]{1,0:T(8,128)S(1)}, u32[]{:S(2)}) copy-start(f32[768,128]{1,0:T(8,128)S(1)} %get-tuple-element.29.refs_7_) | copy-start | bytes 1179652
  29.0 3.1 %copy-start.11 = (f32[768,128]{1,0:T(8,128)}, f32[768,128]{1,0:T(8,128)S(1)}, u32[]{:S(2)}) copy-start(f32[768,128]{1,0:T(8,128)S(1)} %get-tuple-element.30.refs_8_) | copy-start | bytes 1179652
  32.1 7.2 %collective-permute-start.7 = (f32[8,128]{1,0:T(8,128)S(1)}, f32[8,128]{1,0:T(8,128)S(1)}, u32[]{:S(2)}, u32[]{:S(2)}) collective-permute-start(f32[8,128]{1,0:T(8,128)S(1)} %get-tuple-element.33), channel_id=1, source_target_pairs={{8,0},{9,1},{10,2},{11,3},{12,8},{13,9},{14,10},{15,11},{4,12},{5,... | collective-permute-start | bytes 12296 | tf_op jit(solution)/shard_map/ppermute | solution.py:283
  48.7 1.0 %copy-start.6 = (f32[768,128]{1,0:T(8,128)S(1)}, f32[768,128]{1,0:T(8,128)}, u32[]{:S(2)}) copy-start(f32[768,128]{1,0:T(8,128)} %copy-done.5) | copy-start | bytes 1179652
  49.7 1.0 %copy-start.8 = (f32[768,128]{1,0:T(8,128)S(1)}, f32[768,128]{1,0:T(8,128)}, u32[]{:S(2)}) copy-start(f32[768,128]{1,0:T(8,128)} %copy-done.7) | copy-start | bytes 1179652
  50.7 1.0 %copy-start.10 = (f32[768,128]{1,0:T(8,128)S(1)}, f32[768,128]{1,0:T(8,128)}, u32[]{:S(2)}) copy-start(f32[768,128]{1,0:T(8,128)} %copy-done.9) | copy-start | bytes 1179652
  51.7 1.0 %copy-start.12 = (f32[768,128]{1,0:T(8,128)S(1)}, f32[768,128]{1,0:T(8,128)}, u32[]{:S(2)}) copy-start(f32[768,128]{1,0:T(8,128)} %copy-done.11) | copy-start | bytes 1179652
  55.5 6.4 %collective-permute-start.9 = (f32[8,128]{1,0:T(8,128)S(1)}, f32[8,128]{1,0:T(8,128)S(1)}, u32[]{:S(2)}, u32[]{:S(2)}) collective-permute-start(f32[8,128]{1,0:T(8,128)S(1)} %get-tuple-element.37), channel_id=1, source_target_pairs={{4,0},{5,1},{6,2},{7,3},{8,4},{9,5},{10,6},{11,7},{0,12},{1,13},{2... | collective-permute-start | bytes 12296 | tf_op jit(solution)/shard_map/ppermute | solution.py:283
  59.9 2.0 %collective-permute-start.12 = (f32[8,128]{1,0:T(8,128)S(1)}, f32[8,128]{1,0:T(8,128)S(1)}, u32[]{:S(2)}, u32[]{:S(2)}) collective-permute-start(f32[8,128]{1,0:T(8,128)S(1)} %get-tuple-element.40), channel_id=1, source_target_pairs={{0,1},{1,0},{2,3},{3,2},{4,5},{5,4},{6,7},{7,6},{8,9},{9,8},{10,11... | collective-permute-start | bytes 12296 | tf_op jit(solution)/shard_map/ppermute | solution.py:232
  60.0 3.7 %collective-permute-start.11 = (f32[8,128]{1,0:T(8,128)S(1)}, f32[8,128]{1,0:T(8,128)S(1)}, u32[]{:S(2)}, u32[]{:S(2)}) collective-permute-start(f32[8,128]{1,0:T(8,128)S(1)} %get-tuple-element.41), channel_id=1, source_target_pairs={{0,2},{1,3},{2,0},{3,1},{4,6},{5,7},{6,4},{7,5},{8,10},{9,11},{10,... | collective-permute-start | bytes 12296 | tf_op jit(solution)/shard_map/ppermute | solution.py:232
  60.5 3.1 %collective-permute-start.10 = (f32[8,128]{1,0:T(8,128)S(1)}, f32[8,128]{1,0:T(8,128)S(1)}, u32[]{:S(2)}, u32[]{:S(2)}) collective-permute-start(f32[8,128]{1,0:T(8,128)S(1)} %get-tuple-element.39), channel_id=1, source_target_pairs={{0,3},{1,2},{2,1},{3,0},{4,7},{5,6},{6,5},{7,4},{8,11},{9,10},{10,... | collective-permute-start | bytes 12296 | tf_op jit(solution)/shard_map/ppermute | solution.py:232
  (2 other events, 1.9 us)

commit v6 on v5

--- a/solution.py
+++ b/solution.py
@@ -12,9 +12,8 @@
 PAD = 16
 BASE = 64.0
 TILE = 256
-AWAY_CUT = (3,)
+AWAY_CUT = (2, 1)
 MATE_CUT = (2, 1)
-NEAR_CUT = (2, 1)
 VMEM_LIMIT = 24 * 2**20
 
 
@@ -154,12 +153,12 @@
             best_ref[place, :] = folded
 
 
-def cross_kernel(rows, index, counts, tags_ref, away_ref, *refs):
+def cross_kernel(rows, start, counts, tags_ref, away_ref, *refs):
     blocks, refs = take(refs, counts)
     columns, refs = refs[:PLANE], refs[PLANE:]
     away_before, plane_before, away_best, plane_best = refs
     away_tags = tag_rows(tags_ref)
-    away = away_ref if index else away_ref.at[PAD:]
+    away = away_ref if start else away_ref.at[PAD:]
     away_rows = away.shape[0]
     best = [jnp.full((8, 128), -1.0, jnp.float32) for _ in range(0, away_rows, 128)]
     for which in range(PLANE):
@@ -171,7 +170,7 @@
                 found = dot_rows(part[...], away[tile : tile + lanes, :])
                 column = columns[which][first : first + count, :]
                 for lane in range(tile, tile + lanes, 128):
-                    row = (index * away_rows + lane) // 128
+                    row = (start + lane) // 128
                     match = column == away_tags[row : row + 1]
                     masked = jnp.where(match, found[:, lane - tile : lane - tile + 128], -1.0)
                     row_best = jnp.maximum(row_best, masked)
@@ -181,7 +180,7 @@
             plane_best[which, place, :] = jnp.maximum(folded, plane_before[which, place, :])
     away_best[...] = away_before[...]
     for n, values in enumerate(best):
-        place = pl.ds(index * away_rows // 128 + n, 1)
+        place = pl.ds(start // 128 + n, 1)
         away_best[place, :] = jnp.max(values, axis=0, keepdims=True)
 
 
@@ -191,14 +190,11 @@
 
 def plane_steps(planes):
     if planes == 4:
-        return [[(0, 2), (2, 3), (3, 1)], [(0, 1), (1, 2), (3, 0)]]
-    steps = []
-    for distance in range(1, planes // 2 + 1):
-        if 2 * distance < planes:
-            steps.append([(z, (z + distance) % planes) for z in range(planes)])
-        else:
-            steps.append([(z, z + distance) for z in range(distance)])
-    return steps
+        return [(2, 0, 3, 1), (1, 2, 3, 0)]
+    return [
+        [(z + distance) % planes for z in range(planes)]
+        for distance in range(1, planes // 2 + 1)
+    ]
 
 
 def after(value, *others):
@@ -209,13 +205,12 @@
     rows, width = embeddings.shape
     peers = lax.axis_size("dp")
     planes = peers // PLANE
-    me = lax.axis_index("dp")
     lanes = lanes_shape(rows)
 
     space = -(2 * rows + peers) % 2048
     ints = jnp.concatenate([owner_index, sub_label, run_start, jnp.zeros((space,), jnp.int32)])
     ints = ints.reshape(-1, 128)
-    ways = ((1,), AWAY_CUT, MATE_CUT, NEAR_CUT)
+    ways = ((1,), AWAY_CUT, MATE_CUT)
     sizes = sum((cuts(rows, way) for way in ways), [])
     packed = pl.pallas_call(
         functools.partial(pack_kernel, rows),
@@ -226,20 +221,20 @@
         cost_estimate=small_cost(),
         name="pack",
     )(embeddings, ints)
-    own, to_away, to_mate, to_near = take(packed, [len(way) for way in ways])[0]
+    own, to_away, to_mate = take(packed, [len(way) for way in ways])[0]
 
     def mate(value, distance):
         return lax.ppermute(value, "dp", [(i, i ^ distance) for i in range(peers)])
 
     away = []
     for n, step in enumerate(plane_steps(planes)):
-        pairs = [(s * PLANE + j, t * PLANE + j) for s, t in step for j in range(PLANE)]
+        pairs = [(z * PLANE + j, t * PLANE + j) for z, t in enumerate(step) for j in range(PLANE)]
         parts = to_away if n else own
         if n > 1:
             parts = [after(part, away[-1][1][-1]) for part in parts]
         away.append((pairs, [lax.ppermute(part, "dp", pairs) for part in parts]))
     beside = [mate(part, 2) for part in to_mate]
-    near = [mate(part, 1) for part in to_near]
+    near = [mate(part, 1) for part in to_mate]
     across = [mate(part, 1) for part in beside]
 
     columns = jax.ShapeDtypeStruct((rows, 128), jnp.float32)
@@ -266,13 +261,15 @@
     plane_columns = (own_columns, near_columns, beside_columns, across_columns)
     plane_best = jnp.full((PLANE,) + lanes.shape, -1.0, jnp.float32)
     counts = (1, len(near), len(beside), len(across))
-    for step, (pairs, received) in enumerate(away):
-        if step:
-            plane_best = after(plane_best, best)
+    backs = []
+    for pairs, received in away:
         away_best = jnp.full(lanes.shape, -1.0, jnp.float32)
-        for n, part in enumerate(received):
+        start = 0
+        for part in received:
+            if backs and part is received[-1]:
+                plane_best = after(plane_best, backs[-1])
             away_best, plane_best = pl.pallas_call(
-                functools.partial(cross_kernel, rows, n, counts),
+                functools.partial(cross_kernel, rows, start, counts),
                 out_shape=(lanes, jax.ShapeDtypeStruct(plane_best.shape, jnp.float32)),
                 in_specs=whole(len(plane) + PLANE + 4),
                 out_specs=tuple(whole(2)),
@@ -280,14 +277,12 @@
                 cost_estimate=small_cost(),
                 name="cross",
             )(received[0], part, *plane, *plane_columns, away_best, plane_best)
+            start += part.shape[0] - (0 if start else PAD)
         back = lax.ppermute(away_best, "dp", [(t, s) for s, t in pairs])
-        if len(pairs) < peers:
-            sources = sum(1 << z for z in {s // PLANE for s, _ in pairs})
-            sent = (jnp.uint32(sources) >> (me // PLANE).astype(jnp.uint32)) & 1
-            back = jnp.where(sent == 1, back, -1.0)
-        best = jnp.maximum(best, back)
-    best = best.reshape(-1)[:rows]
-    best = jnp.maximum(best, plane_best[0].reshape(-1)[:rows])
+        backs.append(back)
+    best = jnp.maximum(best, plane_best[0]).reshape(-1)[:rows]
+    for back in backs:
+        best = jnp.maximum(best, back.reshape(-1)[:rows])
     for n, distance in ((3, 3), (2, 2), (1, 1)):
         back = mate(plane_best[n], distance)
         best = jnp.maximum(best, back.reshape(-1)[:rows])

time: 64.7 us -> 52 us (0.80)
  local copies, waits for them, and re-layouts: 8.1 us -> 2.2 us
  waiting for transfers between devices: 27.3 us -> 22.3 us
  starting transfers between devices: 18.2 us -> 17.5 us
    unnamed x26 -> x2, local copies, waits for them, and re-layouts: 7.31 us -> 1.41 us
    ppermute x2, waiting for transfers between devices: 5.9 us -> 1.77 us  [local(): back = lax.ppermute(away_best, 'dp', [(t, s) for s, t in pairs])]
    ppermute x2 -> x3, waiting for transfers between devices: 7.73 us -> 4.14 us  [local(): away.append((pairs, [lax.ppermute(part, 'dp', pairs) for part in parts]))]
    ppermute x9, waiting for transfers between devices: 13.7 us -> 16.4 us  [mate(): return lax.ppermute(value, 'dp', [(i, i ^ distance) for i in range(peers)])]
    ppermute x2, starting transfers between devices: 5.69 us -> 4.13 us  [local(): back = lax.ppermute(away_best, 'dp', [(t, s) for s, t in pairs])]
    ppermute x9, starting transfers between devices: 6.12 us -> 7.34 us  [mate(): return lax.ppermute(value, 'dp', [(i, i ^ distance) for i in range(peers)])]
    pallas_call x1, Pallas kernels: 1.19 us -> 0.25 us  [local(): pl.pallas_call(functools.partial(pack_kernel, rows), out_shape=tuple((jax...]
    ppermute x2 -> x3, starting transfers between devices: 6.44 us -> 5.98 us  [local(): away.append((pairs, [lax.ppermute(part, 'dp', pairs) for part in parts]))]
  transfers between devices with their start and end apart: 13 -> 14, of which waited for: 7 -> 7; matrix products, arithmetic and copies ran while one was open for 0% -> 0% of each run, Pallas kernels for 9% -> 15%
where the time goes in v6:
time: 52 us; the launch traced here: 51.8 us
  waiting for transfers between devices  22.3 us (43%)
  starting transfers between devices  17.5 us (34%)
  Pallas kernels  9.15 us (18%)
  local copies, waits for them, and re-layouts  2.2 us (4%)
  other arithmetic  0.6 us (1%)
    ppermute x9, waiting for transfers between devices, mate(): return lax.ppermute(value, 'dp', [(i, i ^ distance) for i in range(peers)])  16.4 us
    ppermute x9, starting transfers between devices, mate(): return lax.ppermute(value, 'dp', [(i, i ^ distance) for i in range(peers)])  7.34 us
    ppermute x3, starting transfers between devices, local(): away.append((pairs, [lax.ppermute(part, 'dp', pairs) for part in parts]))  5.98 us
    pallas_call x3, Pallas kernels, local(): pl.pallas_call(functools.partial(cross_kernel, rows, start, counts), out_...  5.96 us
    ppermute x3, waiting for transfers between devices, local(): away.append((pairs, [lax.ppermute(part, 'dp', pairs) for part in parts]))  4.14 us
    ppermute x2, starting transfers between devices, local(): back = lax.ppermute(away_best, 'dp', [(t, s) for s, t in pairs])  4.13 us
    ppermute x2, waiting for transfers between devices, local(): back = lax.ppermute(away_best, 'dp', [(t, s) for s, t in pairs])  1.77 us
    pallas_call x1, Pallas kernels, local(): pl.pallas_call(functools.partial(plane_kernel, rows, (len(beside), len(ac...  1.48 us
  transfers between devices with their start and end apart: 14, of which 7 were waited for; matrix products, arithmetic and copies ran while one was open for 0% of the time, Pallas kernels for 15%

profile of v6, /device:TPU:0, one launch (start us, length us, event | category | flops | bytes accessed | tf_op | source)
XLA Modules:
  0.0 51.8 jit_solution(17281620764819295836)
XLA Ops:
  0.0 0.8 %concatenate.3 = s32[2048]{0:T(1024)S(1)} concatenate(s32[768]{0:T(1024)} %param.5, s32[768]{0:T(1024)} %param.6, s32[16]{0:T(128)} %param.7, s32[496]{0:T(512)S(1)} %broadcast_in_dim.6), dimensions={0} | concatenate | bytes 16384 | tf_op jit(solution)/shard_map/concatenate | solution.py:211
  0.8 1.4 %copy-done = f32[768,512]{1,0:T(8,128)S(1)} copy-done((f32[768,512]{1,0:T(8,128)S(1)}, f32[768,512]{1,0:T(8,128)}, u32[]{:S(2)}) %copy-start) | copy-done | bytes 1572888
  2.4 3.0 %collective-permute-start.2 = (bf16[528,512]{1,0:T(8,128)(2,1)S(1)}, bf16[528,512]{1,0:T(8,128)(2,1)S(1)}, u32[]{:S(2)}, u32[]{:S(2)}) collective-permute-start(bf16[528,512]{1,0:T(8,128)(2,1)S(1)} %get-tuple-element.24), channel_id=1, source_target_pairs={{0,2},{1,3},{2,0},{3,1},{4,6},{5,7},{6,4},{7,5},{8,10},{9,11},{10,... | collective-permute-start | bytes 1622024 | tf_op jit(solution)/shard_map/ppermute | solution.py:227
  5.5 2.6 %collective-permute-start.8 = (bf16[784,512]{1,0:T(8,128)(2,1)S(1)}, bf16[784,512]{1,0:T(8,128)(2,1)S(1)}, u32[]{:S(2)}, u32[]{:S(2)}) collective-permute-start(bf16[784,512]{1,0:T(8,128)(2,1)S(1)} %get-tuple-element.23.own_ref.refs_0_), channel_id=1, source_target_pairs={{0,8},{1,9},{2,10},{3,11},{4,0},{5,1},{6,2},{7,3},{8,12},{9,13},{1... | collective-permute-start | bytes 2408456 | tf_op jit(solution)/shard_map/ppermute | solution.py:235
  8.1 9.7 %collective-permute-done.2.refs_0_.refs_3_ = bf16[528,512]{1,0:T(8,128)(2,1)S(1)} collective-permute-done((bf16[528,512]{1,0:T(8,128)(2,1)S(1)}, bf16[528,512]{1,0:T(8,128)(2,1)S(1)}, u32[]{:S(2)}, u32[]{:S(2)}) %collective-permute-start.2) | collective-permute-done | bytes 540704 | tf_op jit(solution)/shard_map/ppermute | solution.py:227
  17.7 1.7 %collective-permute-start.3 = (bf16[256,512]{1,0:T(8,128)(2,1)S(1)}, bf16[256,512]{1,0:T(8,128)(2,1)S(1)}, u32[]{:S(2)}, u32[]{:S(2)}) collective-permute-start(bf16[256,512]{1,0:T(8,128)(2,1)S(1)} %get-tuple-element.25), channel_id=1, source_target_pairs={{0,2},{1,3},{2,0},{3,1},{4,6},{5,7},{6,4},{7,5},{8,10},{9,11},{10,... | collective-permute-start | bytes 786440 | tf_op jit(solution)/shard_map/ppermute | solution.py:227
  19.7 1.6 %collective-permute-start.6 = (bf16[528,512]{1,0:T(8,128)(2,1)S(1)}, bf16[528,512]{1,0:T(8,128)(2,1)S(1)}, u32[]{:S(2)}, u32[]{:S(2)}) collective-permute-start(bf16[528,512]{1,0:T(8,128)(2,1)S(1)} %get-tuple-element.28), channel_id=1, source_target_pairs={{0,4},{1,5},{2,6},{3,7},{4,8},{5,9},{6,10},{7,11},{8,12},{9,13},{1... | collective-permute-start | bytes 1622024 | tf_op jit(solution)/shard_map/ppermute | solution.py:235
  21.3 5.2 %collective-permute-done.3.refs_1_.refs_4_ = bf16[256,512]{1,0:T(8,128)(2,1)S(1)} collective-permute-done((bf16[256,512]{1,0:T(8,128)(2,1)S(1)}, bf16[256,512]{1,0:T(8,128)(2,1)S(1)}, u32[]{:S(2)}, u32[]{:S(2)}) %collective-permute-start.3) | collective-permute-done | bytes 262176 | tf_op jit(solution)/shard_map/ppermute | solution.py:227
  26.5 1.5 %collective-permute-done.5.refs_3_.refs_6_ = bf16[256,512]{1,0:T(8,128)(2,1)S(1)} collective-permute-done((bf16[256,512]{1,0:T(8,128)(2,1)S(1)}, bf16[256,512]{1,0:T(8,128)(2,1)S(1)}, u32[]{:S(2)}, u32[]{:S(2)}) %collective-permute-start.5) | collective-permute-done | bytes 262176 | tf_op jit(solution)/shard_map/ppermute | solution.py:227
  28.1 1.8 %collective-permute-start.7 = (bf16[256,512]{1,0:T(8,128)(2,1)S(1)}, bf16[256,512]{1,0:T(8,128)(2,1)S(1)}, u32[]{:S(2)}, u32[]{:S(2)}) collective-permute-start(bf16[256,512]{1,0:T(8,128)(2,1)S(1)} %get-tuple-element.29), channel_id=1, source_target_pairs={{0,4},{1,5},{2,6},{3,7},{4,8},{5,9},{6,10},{7,11},{8,12},{9,13},{1... | collective-permute-start | bytes 786440 | tf_op jit(solution)/shard_map/ppermute | solution.py:235
  30.0 1.5 %plane_far.1 = (f32[8,128]{1,0:T(8,128)S(1)}, f32[768,128]{1,0:T(8,128)S(1)}, f32[768,128]{1,0:T(8,128)S(1)}) custom-call(bf16[784,512]{1,0:T(8,128)(2,1)S(1)} %get-tuple-element.23.own_ref.refs_0_, bf16[528,512]{1,0:T(8,128)(2,1)S(1)} %collective-permute-done.2.refs_0_.refs_3_, bf16[256,512]{1,0:T(8,128)(2,1)S(1)} %collective-permute-done.3.refs_1_.refs_4_, ...), custom_call_target="tpu_custom_call" | custom-call | flops 1 | bytes 1 | tf_op jit(solution)/shard_map/plane_far/pallas_call | solution.py:241
  31.5 1.5 %plane_near.1 = (f32[8,128]{1,0:T(8,128)S(1)}, f32[768,128]{1,0:T(8,128)S(1)}, f32[768,128]{1,0:T(8,128)S(1)}) custom-call(bf16[784,512]{1,0:T(8,128)(2,1)S(1)} %get-tuple-element.23.own_ref.refs_0_, bf16[784,512]{1,0:T(8,128)(2,1)S(1)} %get-tuple-element.23.own_ref.refs_0_, bf16[528,512]{1,0:T(8,128)(2,1)S(1)} %collective-permute-done.refs_1_, ...), custom_call_target="tpu_custom_call" | custom-call | flops 1 | bytes 1 | tf_op jit(solution)/shard_map/plane_near/pallas_call | solution.py:250
  33.0 2.8 %cross.3 = (f32[8,128]{1,0:T(8,128)S(1)}, f32[4,8,128]{2,1,0:T(8,128)S(1)}) custom-call(bf16[784,512]{1,0:T(8,128)(2,1)S(1)} %collective-permute-done.8.tags_ref.away_ref, bf16[784,512]{1,0:T(8,128)(2,1)S(1)} %collective-permute-done.8.tags_ref.away_ref, bf16[784,512]{1,0:T(8,128)(2,1)S(1)} %get-tuple-element.23.own_ref.refs_0_, ...), custom_call_target="tpu_custom_call" | custom-call | flops 1 | bytes 1 | tf_op jit(solution)/shard_map/cross/pallas_call | solution.py:271
  35.8 1.7 %collective-permute-start.9 = (f32[8,128]{1,0:T(8,128)S(1)}, f32[8,128]{1,0:T(8,128)S(1)}, u32[]{:S(2)}, u32[]{:S(2)}) collective-permute-start(f32[8,128]{1,0:T(8,128)S(1)} %get-tuple-element.37), channel_id=1, source_target_pairs={{8,0},{9,1},{10,2},{11,3},{0,4},{1,5},{2,6},{3,7},{12,8},{13,9},{1... | collective-permute-start | bytes 12296 | tf_op jit(solution)/shard_map/ppermute | solution.py:281
  37.5 2.4 %collective-permute-done.6.tags_ref.away_ref = bf16[528,512]{1,0:T(8,128)(2,1)S(1)} collective-permute-done((bf16[528,512]{1,0:T(8,128)(2,1)S(1)}, bf16[528,512]{1,0:T(8,128)(2,1)S(1)}, u32[]{:S(2)}, u32[]{:S(2)}) %collective-permute-start.6) | collective-permute-done | bytes 540704 | tf_op jit(solution)/shard_map/ppermute | solution.py:235
  39.8 2.0 %cross.4 = (f32[8,128]{1,0:T(8,128)S(1)}, f32[4,8,128]{2,1,0:T(8,128)S(1)}) custom-call(bf16[528,512]{1,0:T(8,128)(2,1)S(1)} %collective-permute-done.6.tags_ref.away_ref, bf16[528,512]{1,0:T(8,128)(2,1)S(1)} %collective-permute-done.6.tags_ref.away_ref, bf16[784,512]{1,0:T(8,128)(2,1)S(1)} %get-tuple-element.23.own_ref.refs_0_, ...), custom_call_target="tpu_custom_call" | custom-call | flops 1 | bytes 1 | tf_op jit(solution)/shard_map/cross/pallas_call | solution.py:271
  41.8 0.5 collective-permute-done.9
  42.2 1.8 %collective-permute-done.7.away_ref = bf16[256,512]{1,0:T(8,128)(2,1)S(1)} collective-permute-done((bf16[256,512]{1,0:T(8,128)(2,1)S(1)}, bf16[256,512]{1,0:T(8,128)(2,1)S(1)}, u32[]{:S(2)}, u32[]{:S(2)}) %collective-permute-start.7) | collective-permute-done | bytes 262176 | tf_op jit(solution)/shard_map/ppermute | solution.py:235
  44.0 1.2 %cross.5 = (f32[8,128]{1,0:T(8,128)S(1)}, f32[4,8,128]{2,1,0:T(8,128)S(1)}) custom-call(bf16[528,512]{1,0:T(8,128)(2,1)S(1)} %collective-permute-done.6.tags_ref.away_ref, bf16[256,512]{1,0:T(8,128)(2,1)S(1)} %collective-permute-done.7.away_ref, bf16[784,512]{1,0:T(8,128)(2,1)S(1)} %get-tuple-element.23.own_ref.refs_0_, ...), custom_call_target="tpu_custom_call" | custom-call | flops 1 | bytes 1 | tf_op jit(solution)/shard_map/cross/pallas_call | solution.py:271
  45.3 0.6 %collective-permute-start.13 = (f32[8,128]{1,0:T(8,128)S(1)}, f32[8,128]{1,0:T(8,128)S(1)}, u32[]{:S(2)}, u32[]{:S(2)}) collective-permute-start(f32[8,128]{1,0:T(8,128)S(1)} %get-tuple-element.42), channel_id=1, source_target_pairs={{0,1},{1,0},{2,3},{3,2},{4,5},{5,4},{6,7},{7,6},{8,9},{9,8},{10,11... | collective-permute-start | bytes 12296 | tf_op jit(solution)/shard_map/ppermute | solution.py:227
  45.9 1.5 %collective-permute-start.12 = (f32[8,128]{1,0:T(8,128)S(1)}, f32[8,128]{1,0:T(8,128)S(1)}, u32[]{:S(2)}, u32[]{:S(2)}) collective-permute-start(f32[8,128]{1,0:T(8,128)S(1)} %get-tuple-element.43), channel_id=1, source_target_pairs={{0,2},{1,3},{2,0},{3,1},{4,6},{5,7},{6,4},{7,5},{8,10},{9,11},{10,... | collective-permute-start | bytes 12296 | tf_op jit(solution)/shard_map/ppermute | solution.py:227
  47.4 2.5 %collective-permute-start.10 = (f32[8,128]{1,0:T(8,128)S(1)}, f32[8,128]{1,0:T(8,128)S(1)}, u32[]{:S(2)}, u32[]{:S(2)}) collective-permute-start(f32[8,128]{1,0:T(8,128)S(1)} %get-tuple-element.40), channel_id=1, source_target_pairs={{4,0},{5,1},{6,2},{7,3},{8,4},{9,5},{10,6},{11,7},{12,8},{13,9},{1... | collective-permute-start | bytes 12296 | tf_op jit(solution)/shard_map/ppermute | solution.py:281
  49.9 1.3 %collective-permute-done.10 = f32[8,128]{1,0:T(8,128)S(1)} collective-permute-done((f32[8,128]{1,0:T(8,128)S(1)}, f32[8,128]{1,0:T(8,128)S(1)}, u32[]{:S(2)}, u32[]{:S(2)}) %collective-permute-start.10) | collective-permute-done | bytes 4128 | tf_op jit(solution)/shard_map/ppermute | solution.py:281
  51.2 0.6 %maximum_bitcast_fusion = f32[768]{0:T(1024)} fusion(f32[8,128]{1,0:T(8,128)S(1)} %collective-permute-done.13, f32[8,128]{1,0:T(8,128)S(1)} %collective-permute-done.12, f32[8,128]{1,0:T(8,128)S(1)} %collective-permute-done.11, f32[8,128]{1,0:T(8,128)S(1)} %collective-permute-done.10, f32[8,128]{1,0:T(8,128)S(1)} %collective-permute-done.9, ...), kind=kLoop, calls=%fused_computation.1 | loop fusion | flops 3840 | bytes 21504 | tf_op jit(solution)/shard_map/max | solution.py:288
  (19 shorter events, 0.7 us)
Async XLA Ops:
  0.8 1.4 %copy-start = (f32[768,512]{1,0:T(8,128)S(1)}, f32[768,512]{1,0:T(8,128)}, u32[]{:S(2)}) copy-start(f32[768,512]{1,0:T(8,128)} %embeddings_ref.1) | copy-start | bytes 4718596
  2.4 15.3 %collective-permute-start.2 = (bf16[528,512]{1,0:T(8,128)(2,1)S(1)}, bf16[528,512]{1,0:T(8,128)(2,1)S(1)}, u32[]{:S(2)}, u32[]{:S(2)}) collective-permute-start(bf16[528,512]{1,0:T(8,128)(2,1)S(1)} %get-tuple-element.24), channel_id=1, source_target_pairs={{0,2},{1,3},{2,0},{3,1},{4,6},{5,7},{6,4},{7,5},{8,10},{9,11},{10,... | collective-permute-start | bytes 1622024 | tf_op jit(solution)/shard_map/ppermute | solution.py:227
  5.5 27.5 %collective-permute-start.8 = (bf16[784,512]{1,0:T(8,128)(2,1)S(1)}, bf16[784,512]{1,0:T(8,128)(2,1)S(1)}, u32[]{:S(2)}, u32[]{:S(2)}) collective-permute-start(bf16[784,512]{1,0:T(8,128)(2,1)S(1)} %get-tuple-element.23.own_ref.refs_0_), channel_id=1, source_target_pairs={{0,8},{1,9},{2,10},{3,11},{4,0},{5,1},{6,2},{7,3},{8,12},{9,13},{1... | collective-permute-start | bytes 2408456 | tf_op jit(solution)/shard_map/ppermute | solution.py:235
  17.7 10.4 %collective-permute-start.4 = (bf16[528,512]{1,0:T(8,128)(2,1)S(1)}, bf16[528,512]{1,0:T(8,128)(2,1)S(1)}, u32[]{:S(2)}, u32[]{:S(2)}) collective-permute-start(bf16[528,512]{1,0:T(8,128)(2,1)S(1)} %collective-permute-done.2.refs_0_.refs_3_), channel_id=1, source_target_pairs={{0,1},{1,0},{2,3},{3,2},{4,5},{5,4},{6,7},{7,6},{8,9},{9,8},{10,11... | collective-permute-start | bytes 1622024 | tf_op jit(solution)/shard_map/ppermute | solution.py:227
  17.7 8.7 %collective-permute-start.3 = (bf16[256,512]{1,0:T(8,128)(2,1)S(1)}, bf16[256,512]{1,0:T(8,128)(2,1)S(1)}, u32[]{:S(2)}, u32[]{:S(2)}) collective-permute-start(bf16[256,512]{1,0:T(8,128)(2,1)S(1)} %get-tuple-element.25), channel_id=1, source_target_pairs={{0,2},{1,3},{2,0},{3,1},{4,6},{5,7},{6,4},{7,5},{8,10},{9,11},{10,... | collective-permute-start | bytes 786440 | tf_op jit(solution)/shard_map/ppermute | solution.py:227
  19.5 12.0 %collective-permute-start = (bf16[528,512]{1,0:T(8,128)(2,1)S(1)}, bf16[528,512]{1,0:T(8,128)(2,1)S(1)}, u32[]{:S(2)}, u32[]{:S(2)}) collective-permute-start(bf16[528,512]{1,0:T(8,128)(2,1)S(1)} %get-tuple-element.24), channel_id=1, source_target_pairs={{0,1},{1,0},{2,3},{3,2},{4,5},{5,4},{6,7},{7,6},{8,9},{9,8},{10,11... | collective-permute-start | bytes 1622024 | tf_op jit(solution)/shard_map/ppermute | solution.py:227
  19.7 20.1 %collective-permute-start.6 = (bf16[528,512]{1,0:T(8,128)(2,1)S(1)}, bf16[528,512]{1,0:T(8,128)(2,1)S(1)}, u32[]{:S(2)}, u32[]{:S(2)}) collective-permute-start(bf16[528,512]{1,0:T(8,128)(2,1)S(1)} %get-tuple-element.28), channel_id=1, source_target_pairs={{0,4},{1,5},{2,6},{3,7},{4,8},{5,9},{6,10},{7,11},{8,12},{9,13},{1... | collective-permute-start | bytes 1622024 | tf_op jit(solution)/shard_map/ppermute | solution.py:235
  26.5 1.5 %collective-permute-start.5 = (bf16[256,512]{1,0:T(8,128)(2,1)S(1)}, bf16[256,512]{1,0:T(8,128)(2,1)S(1)}, u32[]{:S(2)}, u32[]{:S(2)}) collective-permute-start(bf16[256,512]{1,0:T(8,128)(2,1)S(1)} %collective-permute-done.3.refs_1_.refs_4_), channel_id=1, source_target_pairs={{0,1},{1,0},{2,3},{3,2},{4,5},{5,4},{6,7},{7,6},{8,9},{9,8},{10,11... | collective-permute-start | bytes 786440 | tf_op jit(solution)/shard_map/ppermute | solution.py:227
  28.0 3.4 %collective-permute-start.1 = (bf16[256,512]{1,0:T(8,128)(2,1)S(1)}, bf16[256,512]{1,0:T(8,128)(2,1)S(1)}, u32[]{:S(2)}, u32[]{:S(2)}) collective-permute-start(bf16[256,512]{1,0:T(8,128)(2,1)S(1)} %get-tuple-element.25), channel_id=1, source_target_pairs={{0,1},{1,0},{2,3},{3,2},{4,5},{5,4},{6,7},{7,6},{8,9},{9,8},{10,11... | collective-permute-start | bytes 786440 | tf_op jit(solution)/shard_map/ppermute | solution.py:227
  28.1 15.9 %collective-permute-start.7 = (bf16[256,512]{1,0:T(8,128)(2,1)S(1)}, bf16[256,512]{1,0:T(8,128)(2,1)S(1)}, u32[]{:S(2)}, u32[]{:S(2)}) collective-permute-start(bf16[256,512]{1,0:T(8,128)(2,1)S(1)} %get-tuple-element.29), channel_id=1, source_target_pairs={{0,4},{1,5},{2,6},{3,7},{4,8},{5,9},{6,10},{7,11},{8,12},{9,13},{1... | collective-permute-start | bytes 786440 | tf_op jit(solution)/shard_map/ppermute | solution.py:235
  35.8 6.4 %collective-permute-start.9 = (f32[8,128]{1,0:T(8,128)S(1)}, f32[8,128]{1,0:T(8,128)S(1)}, u32[]{:S(2)}, u32[]{:S(2)}) collective-permute-start(f32[8,128]{1,0:T(8,128)S(1)} %get-tuple-element.37), channel_id=1, source_target_pairs={{8,0},{9,1},{10,2},{11,3},{0,4},{1,5},{2,6},{3,7},{12,8},{13,9},{1... | collective-permute-start | bytes 12296 | tf_op jit(solution)/shard_map/ppermute | solution.py:281
  45.2 4.7 %collective-permute-start.11 = (f32[8,128]{1,0:T(8,128)S(1)}, f32[8,128]{1,0:T(8,128)S(1)}, u32[]{:S(2)}, u32[]{:S(2)}) collective-permute-start(f32[8,128]{1,0:T(8,128)S(1)} %get-tuple-element.41), channel_id=1, source_target_pairs={{0,3},{1,2},{2,1},{3,0},{4,7},{5,6},{6,5},{7,4},{8,11},{9,10},{10,... | collective-permute-start | bytes 12296 | tf_op jit(solution)/shard_map/ppermute | solution.py:227
  45.3 4.6 %collective-permute-start.13 = (f32[8,128]{1,0:T(8,128)S(1)}, f32[8,128]{1,0:T(8,128)S(1)}, u32[]{:S(2)}, u32[]{:S(2)}) collective-permute-start(f32[8,128]{1,0:T(8,128)S(1)} %get-tuple-element.42), channel_id=1, source_target_pairs={{0,1},{1,0},{2,3},{3,2},{4,5},{5,4},{6,7},{7,6},{8,9},{9,8},{10,11... | collective-permute-start | bytes 12296 | tf_op jit(solution)/shard_map/ppermute | solution.py:227
  45.9 4.0 %collective-permute-start.12 = (f32[8,128]{1,0:T(8,128)S(1)}, f32[8,128]{1,0:T(8,128)S(1)}, u32[]{:S(2)}, u32[]{:S(2)}) collective-permute-start(f32[8,128]{1,0:T(8,128)S(1)} %get-tuple-element.43), channel_id=1, source_target_pairs={{0,2},{1,3},{2,0},{3,1},{4,6},{5,7},{6,4},{7,5},{8,10},{9,11},{10,... | collective-permute-start | bytes 12296 | tf_op jit(solution)/shard_map/ppermute | solution.py:227
  47.4 3.8 %collective-permute-start.10 = (f32[8,128]{1,0:T(8,128)S(1)}, f32[8,128]{1,0:T(8,128)S(1)}, u32[]{:S(2)}, u32[]{:S(2)}) collective-permute-start(f32[8,128]{1,0:T(8,128)S(1)} %get-tuple-element.40), channel_id=1, source_target_pairs={{4,0},{5,1},{6,2},{7,3},{8,4},{9,5},{10,6},{11,7},{12,8},{13,9},{1... | collective-permute-start | bytes 12296 | tf_op jit(solution)/shard_map/ppermute | solution.py:281

commit v7 on v6

--- a/solution.py
+++ b/solution.py
@@ -12,7 +12,7 @@
 PAD = 16
 BASE = 64.0
 TILE = 256
-AWAY_CUT = (2, 1)
+AWAY_CUT = (5, 1)
 MATE_CUT = (2, 1)
 VMEM_LIMIT = 24 * 2**20
 
@@ -156,7 +156,8 @@
 def cross_kernel(rows, start, counts, tags_ref, away_ref, *refs):
     blocks, refs = take(refs, counts)
     columns, refs = refs[:PLANE], refs[PLANE:]
-    away_before, plane_before, away_best, plane_best = refs
+    away_before, away_best = refs[0], refs[PLANE + 1]
+    plane_before, plane_best = refs[1 : PLANE + 1], refs[PLANE + 2 :]
     away_tags = tag_rows(tags_ref)
     away = away_ref if start else away_ref.at[PAD:]
     away_rows = away.shape[0]
@@ -177,7 +178,7 @@
                     best[lane // 128] = jnp.maximum(best[lane // 128], fold_sublanes(masked))
             place = pl.ds(first // 128, count // 128)
             folded = fold_lanes(row_best)
-            plane_best[which, place, :] = jnp.maximum(folded, plane_before[which, place, :])
+            plane_best[which][place, :] = jnp.maximum(folded, plane_before[which][place, :])
     away_best[...] = away_before[...]
     for n, values in enumerate(best):
         place = pl.ds(start // 128 + n, 1)
@@ -235,7 +236,7 @@
         away.append((pairs, [lax.ppermute(part, "dp", pairs) for part in parts]))
     beside = [mate(part, 2) for part in to_mate]
     near = [mate(part, 1) for part in to_mate]
-    across = [mate(part, 1) for part in beside]
+    across = [mate(after(part, away[0][1][0]), 1) for part in beside]
 
     columns = jax.ShapeDtypeStruct((rows, 128), jnp.float32)
     best, beside_columns, across_columns = pl.pallas_call(
@@ -259,7 +260,7 @@
 
     plane = (own[0], *near, *beside, *across)
     plane_columns = (own_columns, near_columns, beside_columns, across_columns)
-    plane_best = jnp.full((PLANE,) + lanes.shape, -1.0, jnp.float32)
+    plane_best = [jnp.full(lanes.shape, -1.0, jnp.float32)] * PLANE
     counts = (1, len(near), len(beside), len(across))
     backs = []
     for pairs, received in away:
@@ -267,16 +268,16 @@
         start = 0
         for part in received:
             if backs and part is received[-1]:
-                plane_best = after(plane_best, backs[-1])
-            away_best, plane_best = pl.pallas_call(
+                away_best = after(away_best, backs[-1])
+            away_best, *plane_best = pl.pallas_call(
                 functools.partial(cross_kernel, rows, start, counts),
-                out_shape=(lanes, jax.ShapeDtypeStruct(plane_best.shape, jnp.float32)),
-                in_specs=whole(len(plane) + PLANE + 4),
-                out_specs=tuple(whole(2)),
+                out_shape=(lanes,) * (PLANE + 1),
+                in_specs=whole(len(plane) + 2 * PLANE + 3),
+                out_specs=tuple(whole(PLANE + 1)),
                 compiler_params=params(),
                 cost_estimate=small_cost(),
                 name="cross",
-            )(received[0], part, *plane, *plane_columns, away_best, plane_best)
+            )(received[0], part, *plane, *plane_columns, away_best, *plane_best)
             start += part.shape[0] - (0 if start else PAD)
         back = lax.ppermute(away_best, "dp", [(t, s) for s, t in pairs])
         backs.append(back)

time: 52 us -> 51.4 us (0.988)
  starting transfers between devices: 17.5 us -> 14.7 us
  waiting for transfers between devices: 22.3 us -> 23.7 us
  Pallas kernels: 9.15 us -> 9.95 us
    ppermute x9, starting transfers between devices: 7.34 us -> 4.91 us  [mate(): return lax.ppermute(value, 'dp', [(i, i ^ distance) for i in range(peers)])]
    ppermute x3, waiting for transfers between devices: 4.14 us -> 6.47 us  [local(): away.append((pairs, [lax.ppermute(part, 'dp', pairs) for part in parts]))]
    ppermute x2, waiting for transfers between devices: 1.77 us -> 0.13 us  [local(): back = lax.ppermute(away_best, 'dp', [(t, s) for s, t in pairs])]
    pallas_call x3, Pallas kernels: 5.96 us -> 6.76 us  [local(): pl.pallas_call(functools.partial(cross_kernel, rows, start, counts), out_...]
    ppermute x2, starting transfers between devices: 4.13 us -> 3.33 us  [local(): back = lax.ppermute(away_best, 'dp', [(t, s) for s, t in pairs])]
    ppermute x9, waiting for transfers between devices: 16.4 us -> 17.1 us  [mate(): return lax.ppermute(value, 'dp', [(i, i ^ distance) for i in range(peers)])]
  transfers between devices with their start and end apart: 14 -> 14, of which waited for: 7 -> 8; matrix products, arithmetic and copies ran while one was open for 0% -> 0% of each run, Pallas kernels for 15% -> 17%
where the time goes in v7:
time: 51.4 us; the launch traced here: 51.2 us
  waiting for transfers between devices  23.7 us (46%)
  starting transfers between devices  14.7 us (29%)
  Pallas kernels  9.95 us (19%)
  local copies, waits for them, and re-layouts  2.19 us (4%)
  other arithmetic  0.6 us (1%)
    ppermute x9, waiting for transfers between devices, mate(): return lax.ppermute(value, 'dp', [(i, i ^ distance) for i in range(peers)])  17.1 us
    pallas_call x3, Pallas kernels, local(): pl.pallas_call(functools.partial(cross_kernel, rows, start, counts), out_...  6.76 us
    ppermute x3, waiting for transfers between devices, local(): away.append((pairs, [lax.ppermute(part, 'dp', pairs) for part in parts]))  6.47 us
    ppermute x3, starting transfers between devices, local(): away.append((pairs, [lax.ppermute(part, 'dp', pairs) for part in parts]))  6.42 us
    ppermute x9, starting transfers between devices, mate(): return lax.ppermute(value, 'dp', [(i, i ^ distance) for i in range(peers)])  4.91 us
    ppermute x2, starting transfers between devices, local(): back = lax.ppermute(away_best, 'dp', [(t, s) for s, t in pairs])  3.33 us
    pallas_call x1, Pallas kernels, local(): pl.pallas_call(functools.partial(plane_kernel, rows, (len(beside), len(ac...  1.48 us
    pallas_call x1, Pallas kernels, local(): pl.pallas_call(functools.partial(plane_kernel, rows, (1, len(near)), True...  1.47 us
  transfers between devices with their start and end apart: 14, of which 8 were waited for; matrix products, arithmetic and copies ran while one was open for 0% of the time, Pallas kernels for 17%

profile of v7, /device:TPU:0, one launch (start us, length us, event | category | flops | bytes accessed | tf_op | source)
XLA Modules:
  0.0 51.2 jit_solution(12222530653326143102)
XLA Ops:
  0.0 0.8 %concatenate.3 = s32[2048]{0:T(1024)S(1)} concatenate(s32[768]{0:T(1024)} %param.5, s32[768]{0:T(1024)} %param.6, s32[16]{0:T(128)} %param.7, s32[496]{0:T(512)S(1)} %broadcast_in_dim.3), dimensions={0} | concatenate | bytes 16384 | tf_op jit(solution)/shard_map/concatenate | solution.py:212
  0.8 1.4 %copy-done = f32[768,512]{1,0:T(8,128)S(1)} copy-done((f32[768,512]{1,0:T(8,128)S(1)}, f32[768,512]{1,0:T(8,128)}, u32[]{:S(2)}) %copy-start) | copy-done | bytes 1572888
  2.4 4.1 %collective-permute-start.4 = (bf16[784,512]{1,0:T(8,128)(2,1)S(1)}, bf16[784,512]{1,0:T(8,128)(2,1)S(1)}, u32[]{:S(2)}, u32[]{:S(2)}) collective-permute-start(bf16[784,512]{1,0:T(8,128)(2,1)S(1)} %get-tuple-element.34.own_ref.refs_0_), channel_id=1, source_target_pairs={{0,8},{1,9},{2,10},{3,11},{4,0},{5,1},{6,2},{7,3},{8,12},{9,13},{1... | collective-permute-start | bytes 2408456 | tf_op jit(solution)/shard_map/ppermute | solution.py:236
  6.5 1.5 %collective-permute-start.2 = (bf16[528,512]{1,0:T(8,128)(2,1)S(1)}, bf16[528,512]{1,0:T(8,128)(2,1)S(1)}, u32[]{:S(2)}, u32[]{:S(2)}) collective-permute-start(bf16[528,512]{1,0:T(8,128)(2,1)S(1)} %get-tuple-element.35), channel_id=1, source_target_pairs={{0,2},{1,3},{2,0},{3,1},{4,6},{5,7},{6,4},{7,5},{8,10},{9,11},{10,... | collective-permute-start | bytes 1622024 | tf_op jit(solution)/shard_map/ppermute | solution.py:228
  8.1 0.5 collective-permute-start.3
  8.6 13.2 %collective-permute-done.2.refs_0_.refs_3_ = bf16[528,512]{1,0:T(8,128)(2,1)S(1)} collective-permute-done((bf16[528,512]{1,0:T(8,128)(2,1)S(1)}, bf16[528,512]{1,0:T(8,128)(2,1)S(1)}, u32[]{:S(2)}, u32[]{:S(2)}) %collective-permute-start.2) | collective-permute-done | bytes 540704 | tf_op jit(solution)/shard_map/ppermute | solution.py:228
  21.7 3.1 %collective-permute-done.4.tags_ref.away_ref = bf16[784,512]{1,0:T(8,128)(2,1)S(1)} collective-permute-done((bf16[784,512]{1,0:T(8,128)(2,1)S(1)}, bf16[784,512]{1,0:T(8,128)(2,1)S(1)}, u32[]{:S(2)}, u32[]{:S(2)}) %collective-permute-start.4) | collective-permute-done | bytes 802848 | tf_op jit(solution)/shard_map/ppermute | solution.py:236
  24.9 0.5 collective-permute-start
  25.4 0.5 collective-permute-done.3.refs_1_.refs_4_
  25.9 0.5 collective-permute-start.1
  26.4 1.6 %collective-permute-done.6.refs_3_.refs_6_ = bf16[256,512]{1,0:T(8,128)(2,1)S(1)} collective-permute-done((bf16[256,512]{1,0:T(8,128)(2,1)S(1)}, bf16[256,512]{1,0:T(8,128)(2,1)S(1)}, u32[]{:S(2)}, u32[]{:S(2)}) %collective-permute-start.6) | collective-permute-done | bytes 262176 | tf_op jit(solution)/shard_map/ppermute | solution.py:228
  28.0 2.3 %collective-permute-start.8 = (bf16[128,512]{1,0:T(8,128)(2,1)S(1)}, bf16[128,512]{1,0:T(8,128)(2,1)S(1)}, u32[]{:S(2)}, u32[]{:S(2)}) collective-permute-start(bf16[128,512]{1,0:T(8,128)(2,1)S(1)} %get-tuple-element.42), channel_id=1, source_target_pairs={{0,4},{1,5},{2,6},{3,7},{4,8},{5,9},{6,10},{7,11},{8,12},{9,13},{1... | collective-permute-start | bytes 393224 | tf_op jit(solution)/shard_map/ppermute | solution.py:236
  30.3 1.5 %plane_far.1 = (f32[8,128]{1,0:T(8,128)S(1)}, f32[768,128]{1,0:T(8,128)S(1)}, f32[768,128]{1,0:T(8,128)S(1)}) custom-call(bf16[784,512]{1,0:T(8,128)(2,1)S(1)} %get-tuple-element.34.own_ref.refs_0_, bf16[528,512]{1,0:T(8,128)(2,1)S(1)} %collective-permute-done.2.refs_0_.refs_3_, bf16[256,512]{1,0:T(8,128)(2,1)S(1)} %collective-permute-done.3.refs_1_.refs_4_, ...), custom_call_target="tpu_custom_call" | custom-call | flops 1 | bytes 1 | tf_op jit(solution)/shard_map/plane_far/pallas_call | solution.py:242
  31.8 1.5 %plane_near.1 = (f32[8,128]{1,0:T(8,128)S(1)}, f32[768,128]{1,0:T(8,128)S(1)}, f32[768,128]{1,0:T(8,128)S(1)}) custom-call(bf16[784,512]{1,0:T(8,128)(2,1)S(1)} %get-tuple-element.34.own_ref.refs_0_, bf16[784,512]{1,0:T(8,128)(2,1)S(1)} %get-tuple-element.34.own_ref.refs_0_, bf16[528,512]{1,0:T(8,128)(2,1)S(1)} %collective-permute-done.refs_1_, ...), custom_call_target="tpu_custom_call" | custom-call | flops 1 | bytes 1 | tf_op jit(solution)/shard_map/plane_near/pallas_call | solution.py:251
  33.3 2.8 %cross.3 = (f32[8,128]{1,0:T(8,128)S(1)}, f32[8,128]{1,0:T(8,128)S(1)}, f32[8,128]{1,0:T(8,128)S(1)}, f32[8,128]{1,0:T(8,128)S(1)}, f32[8,128]{1,0:T(8,128)S(1)}) custom-call(bf16[784,512]{1,0:T(8,128)(2,1)S(1)} %collective-permute-done.4.tags_ref.away_ref, bf16[784,512]{1,0:T(8,128)(2,1)S(1)} %collective-permute-done.4.tags_ref.away_ref, ...), custom_call_target="tpu_custom_call" | custom-call | flops 1 | bytes 1 | tf_op jit(solution)/shard_map/cross/pallas_call | solution.py:272
  36.1 1.7 %collective-permute-start.9 = (f32[8,128]{1,0:T(8,128)S(1)}, f32[8,128]{1,0:T(8,128)S(1)}, u32[]{:S(2)}, u32[]{:S(2)}) collective-permute-start(f32[8,128]{1,0:T(8,128)S(1)} %get-tuple-element.52), channel_id=1, source_target_pairs={{8,0},{9,1},{10,2},{11,3},{0,4},{1,5},{2,6},{3,7},{12,8},{13,9},{1... | collective-permute-start | bytes 12296 | tf_op jit(solution)/shard_map/ppermute | solution.py:282
  37.8 3.3 %collective-permute-done.7.tags_ref.away_ref = bf16[656,512]{1,0:T(8,128)(2,1)S(1)} collective-permute-done((bf16[656,512]{1,0:T(8,128)(2,1)S(1)}, bf16[656,512]{1,0:T(8,128)(2,1)S(1)}, u32[]{:S(2)}, u32[]{:S(2)}) %collective-permute-start.7) | collective-permute-done | bytes 671776 | tf_op jit(solution)/shard_map/ppermute | solution.py:236
  41.1 2.8 %cross.4 = (f32[8,128]{1,0:T(8,128)S(1)}, f32[8,128]{1,0:T(8,128)S(1)}, f32[8,128]{1,0:T(8,128)S(1)}, f32[8,128]{1,0:T(8,128)S(1)}, f32[8,128]{1,0:T(8,128)S(1)}) custom-call(bf16[656,512]{1,0:T(8,128)(2,1)S(1)} %collective-permute-done.7.tags_ref.away_ref, bf16[656,512]{1,0:T(8,128)(2,1)S(1)} %collective-permute-done.7.tags_ref.away_ref, ...), custom_call_target="tpu_custom_call" | custom-call | flops 1 | bytes 1 | tf_op jit(solution)/shard_map/cross/pallas_call | solution.py:272
  43.9 1.1 %cross.5 = (f32[8,128]{1,0:T(8,128)S(1)}, f32[8,128]{1,0:T(8,128)S(1)}, f32[8,128]{1,0:T(8,128)S(1)}, f32[8,128]{1,0:T(8,128)S(1)}, f32[8,128]{1,0:T(8,128)S(1)}) custom-call(bf16[656,512]{1,0:T(8,128)(2,1)S(1)} %collective-permute-done.7.tags_ref.away_ref, bf16[128,512]{1,0:T(8,128)(2,1)S(1)} %collective-permute-done.8.away_ref, ...), custom_call_target="tpu_custom_call" | custom-call | flops 1 | bytes 1 | tf_op jit(solution)/shard_map/cross/pallas_call | solution.py:272
  45.1 1.7 %collective-permute-start.10 = (f32[8,128]{1,0:T(8,128)S(1)}, f32[8,128]{1,0:T(8,128)S(1)}, u32[]{:S(2)}, u32[]{:S(2)}) collective-permute-start(f32[8,128]{1,0:T(8,128)S(1)} %get-tuple-element.59), channel_id=1, source_target_pairs={{4,0},{5,1},{6,2},{7,3},{8,4},{9,5},{10,6},{11,7},{12,8},{13,9},{1... | collective-permute-start | bytes 12296 | tf_op jit(solution)/shard_map/ppermute | solution.py:282
  47.0 1.3 %collective-permute-start.12 = (f32[8,128]{1,0:T(8,128)S(1)}, f32[8,128]{1,0:T(8,128)S(1)}, u32[]{:S(2)}, u32[]{:S(2)}) collective-permute-start(f32[8,128]{1,0:T(8,128)S(1)} %get-tuple-element.61), channel_id=1, source_target_pairs={{0,2},{1,3},{2,0},{3,1},{4,6},{5,7},{6,4},{7,5},{8,10},{9,11},{10,... | collective-permute-start | bytes 12296 | tf_op jit(solution)/shard_map/ppermute | solution.py:228
  48.7 1.0 %collective-permute-done.11 = f32[8,128]{1,0:T(8,128)S(1)} collective-permute-done((f32[8,128]{1,0:T(8,128)S(1)}, f32[8,128]{1,0:T(8,128)S(1)}, u32[]{:S(2)}, u32[]{:S(2)}) %collective-permute-start.11) | collective-permute-done | bytes 4128 | tf_op jit(solution)/shard_map/ppermute | solution.py:228
  49.8 0.8 %collective-permute-done.12 = f32[8,128]{1,0:T(8,128)S(1)} collective-permute-done((f32[8,128]{1,0:T(8,128)S(1)}, f32[8,128]{1,0:T(8,128)S(1)}, u32[]{:S(2)}, u32[]{:S(2)}) %collective-permute-start.12) | collective-permute-done | bytes 4128 | tf_op jit(solution)/shard_map/ppermute | solution.py:228
  50.6 0.6 %maximum_bitcast_fusion = f32[768]{0:T(1024)} fusion(f32[8,128]{1,0:T(8,128)S(1)} %collective-permute-done.13, f32[8,128]{1,0:T(8,128)S(1)} %collective-permute-done.12, f32[8,128]{1,0:T(8,128)S(1)} %collective-permute-done.11, f32[8,128]{1,0:T(8,128)S(1)} %collective-permute-done.10, f32[8,128]{1,0:T(8,128)S(1)} %collective-permute-done.9, f32[8,128]{1,0:T(8,128)S(1)} %max.24), kind=kLoop, calls=%fused_computation | loop fusion | flops 3840 | bytes 21504 | tf_op jit(solution)/shard_map/max | solution.py:289
  (17 shorter events, 1.0 us)
Async XLA Ops:
  0.8 1.4 %copy-start = (f32[768,512]{1,0:T(8,128)S(1)}, f32[768,512]{1,0:T(8,128)}, u32[]{:S(2)}) copy-start(f32[768,512]{1,0:T(8,128)} %embeddings_ref.1) | copy-start | bytes 4718596
  2.4 22.4 %collective-permute-start.4 = (bf16[784,512]{1,0:T(8,128)(2,1)S(1)}, bf16[784,512]{1,0:T(8,128)(2,1)S(1)}, u32[]{:S(2)}, u32[]{:S(2)}) collective-permute-start(bf16[784,512]{1,0:T(8,128)(2,1)S(1)} %get-tuple-element.34.own_ref.refs_0_), channel_id=1, source_target_pairs={{0,8},{1,9},{2,10},{3,11},{4,0},{5,1},{6,2},{7,3},{8,12},{9,13},{1... | collective-permute-start | bytes 2408456 | tf_op jit(solution)/shard_map/ppermute | solution.py:236
  6.5 15.2 %collective-permute-start.2 = (bf16[528,512]{1,0:T(8,128)(2,1)S(1)}, bf16[528,512]{1,0:T(8,128)(2,1)S(1)}, u32[]{:S(2)}, u32[]{:S(2)}) collective-permute-start(bf16[528,512]{1,0:T(8,128)(2,1)S(1)} %get-tuple-element.35), channel_id=1, source_target_pairs={{0,2},{1,3},{2,0},{3,1},{4,6},{5,7},{6,4},{7,5},{8,10},{9,11},{10,... | collective-permute-start | bytes 1622024 | tf_op jit(solution)/shard_map/ppermute | solution.py:228
  8.0 33.1 %collective-permute-start.7 = (bf16[656,512]{1,0:T(8,128)(2,1)S(1)}, bf16[656,512]{1,0:T(8,128)(2,1)S(1)}, u32[]{:S(2)}, u32[]{:S(2)}) collective-permute-start(bf16[656,512]{1,0:T(8,128)(2,1)S(1)} %get-tuple-element.41), channel_id=1, source_target_pairs={{0,4},{1,5},{2,6},{3,7},{4,8},{5,9},{6,10},{7,11},{8,12},{9,13},{1... | collective-permute-start | bytes 2015240 | tf_op jit(solution)/shard_map/ppermute | solution.py:236
  8.1 17.8 %collective-permute-start.3 = (bf16[256,512]{1,0:T(8,128)(2,1)S(1)}, bf16[256,512]{1,0:T(8,128)(2,1)S(1)}, u32[]{:S(2)}, u32[]{:S(2)}) collective-permute-start(bf16[256,512]{1,0:T(8,128)(2,1)S(1)} %get-tuple-element.36), channel_id=1, source_target_pairs={{0,2},{1,3},{2,0},{3,1},{4,6},{5,7},{6,4},{7,5},{8,10},{9,11},{10,... | collective-permute-start | bytes 786440 | tf_op jit(solution)/shard_map/ppermute | solution.py:228
  24.9 5.4 %collective-permute-start.5 = (bf16[528,512]{1,0:T(8,128)(2,1)S(1)}, bf16[528,512]{1,0:T(8,128)(2,1)S(1)}, u32[]{:S(2)}, u32[]{:S(2)}) collective-permute-start(bf16[528,512]{1,0:T(8,128)(2,1)S(1)} %collective-permute-done.2.refs_0_.refs_3_), channel_id=1, source_target_pairs={{0,1},{1,0},{2,3},{3,2},{4,5},{5,4},{6,7},{7,6},{8,9},{9,8},{10,11... | collective-permute-start | bytes 1622024 | tf_op jit(solution)/shard_map/ppermute | solution.py:228
  24.9 6.9 %collective-permute-start = (bf16[528,512]{1,0:T(8,128)(2,1)S(1)}, bf16[528,512]{1,0:T(8,128)(2,1)S(1)}, u32[]{:S(2)}, u32[]{:S(2)}) collective-permute-start(bf16[528,512]{1,0:T(8,128)(2,1)S(1)} %get-tuple-element.35), channel_id=1, source_target_pairs={{0,1},{1,0},{2,3},{3,2},{4,5},{5,4},{6,7},{7,6},{8,9},{9,8},{10,11... | collective-permute-start | bytes 1622024 | tf_op jit(solution)/shard_map/ppermute | solution.py:228
  25.9 2.1 %collective-permute-start.6 = (bf16[256,512]{1,0:T(8,128)(2,1)S(1)}, bf16[256,512]{1,0:T(8,128)(2,1)S(1)}, u32[]{:S(2)}, u32[]{:S(2)}) collective-permute-start(bf16[256,512]{1,0:T(8,128)(2,1)S(1)} %collective-permute-done.3.refs_1_.refs_4_), channel_id=1, source_target_pairs={{0,1},{1,0},{2,3},{3,2},{4,5},{5,4},{6,7},{7,6},{8,9},{9,8},{10,11... | collective-permute-start | bytes 786440 | tf_op jit(solution)/shard_map/ppermute | solution.py:228
  25.9 5.9 %collective-permute-start.1 = (bf16[256,512]{1,0:T(8,128)(2,1)S(1)}, bf16[256,512]{1,0:T(8,128)(2,1)S(1)}, u32[]{:S(2)}, u32[]{:S(2)}) collective-permute-start(bf16[256,512]{1,0:T(8,128)(2,1)S(1)} %get-tuple-element.36), channel_id=1, source_target_pairs={{0,1},{1,0},{2,3},{3,2},{4,5},{5,4},{6,7},{7,6},{8,9},{9,8},{10,11... | collective-permute-start | bytes 786440 | tf_op jit(solution)/shard_map/ppermute | solution.py:228
  28.0 16.0 %collective-permute-start.8 = (bf16[128,512]{1,0:T(8,128)(2,1)S(1)}, bf16[128,512]{1,0:T(8,128)(2,1)S(1)}, u32[]{:S(2)}, u32[]{:S(2)}) collective-permute-start(bf16[128,512]{1,0:T(8,128)(2,1)S(1)} %get-tuple-element.42), channel_id=1, source_target_pairs={{0,4},{1,5},{2,6},{3,7},{4,8},{5,9},{6,10},{7,11},{8,12},{9,13},{1... | collective-permute-start | bytes 393224 | tf_op jit(solution)/shard_map/ppermute | solution.py:236
  36.1 7.8 %collective-permute-start.9 = (f32[8,128]{1,0:T(8,128)S(1)}, f32[8,128]{1,0:T(8,128)S(1)}, u32[]{:S(2)}, u32[]{:S(2)}) collective-permute-start(f32[8,128]{1,0:T(8,128)S(1)} %get-tuple-element.52), channel_id=1, source_target_pairs={{8,0},{9,1},{10,2},{11,3},{0,4},{1,5},{2,6},{3,7},{12,8},{13,9},{1... | collective-permute-start | bytes 12296 | tf_op jit(solution)/shard_map/ppermute | solution.py:282
  45.1 3.7 %collective-permute-start.10 = (f32[8,128]{1,0:T(8,128)S(1)}, f32[8,128]{1,0:T(8,128)S(1)}, u32[]{:S(2)}, u32[]{:S(2)}) collective-permute-start(f32[8,128]{1,0:T(8,128)S(1)} %get-tuple-element.59), channel_id=1, source_target_pairs={{4,0},{5,1},{6,2},{7,3},{8,4},{9,5},{10,6},{11,7},{12,8},{13,9},{1... | collective-permute-start | bytes 12296 | tf_op jit(solution)/shard_map/ppermute | solution.py:282
  46.7 3.0 %collective-permute-start.11 = (f32[8,128]{1,0:T(8,128)S(1)}, f32[8,128]{1,0:T(8,128)S(1)}, u32[]{:S(2)}, u32[]{:S(2)}) collective-permute-start(f32[8,128]{1,0:T(8,128)S(1)} %get-tuple-element.60), channel_id=1, source_target_pairs={{0,3},{1,2},{2,1},{3,0},{4,7},{5,6},{6,5},{7,4},{8,11},{9,10},{10,... | collective-permute-start | bytes 12296 | tf_op jit(solution)/shard_map/ppermute | solution.py:228
  47.0 3.6 %collective-permute-start.12 = (f32[8,128]{1,0:T(8,128)S(1)}, f32[8,128]{1,0:T(8,128)S(1)}, u32[]{:S(2)}, u32[]{:S(2)}) collective-permute-start(f32[8,128]{1,0:T(8,128)S(1)} %get-tuple-element.61), channel_id=1, source_target_pairs={{0,2},{1,3},{2,0},{3,1},{4,6},{5,7},{6,4},{7,5},{8,10},{9,11},{10,... | collective-permute-start | bytes 12296 | tf_op jit(solution)/shard_map/ppermute | solution.py:228
  48.3 2.3 %collective-permute-start.13 = (f32[8,128]{1,0:T(8,128)S(1)}, f32[8,128]{1,0:T(8,128)S(1)}, u32[]{:S(2)}, u32[]{:S(2)}) collective-permute-start(f32[8,128]{1,0:T(8,128)S(1)} %get-tuple-element.62), channel_id=1, source_target_pairs={{0,1},{1,0},{2,3},{3,2},{4,5},{5,4},{6,7},{7,6},{8,9},{9,8},{10,11... | collective-permute-start | bytes 12296 | tf_op jit(solution)/shard_map/ppermute | solution.py:228

commit v8 on v7

--- a/solution.py
+++ b/solution.py
@@ -12,8 +12,8 @@
 PAD = 16
 BASE = 64.0
 TILE = 256
-AWAY_CUT = (5, 1)
-MATE_CUT = (2, 1)
+AWAY_CUT = (4, 2)
+MATE_CUT = (1, 1, 1)
 VMEM_LIMIT = 24 * 2**20
 
 

time: 51.4 us -> 51.4 us (level)
  starting transfers between devices: 14.7 us -> 16.2 us
  Pallas kernels: 9.95 us -> 9.19 us
  waiting for transfers between devices: 23.7 us -> 23 us
    ppermute x9 -> x12, waiting for transfers between devices: 17.1 us -> 10.6 us  [mate(): return lax.ppermute(value, 'dp', [(i, i ^ distance) for i in range(peers)])]
    ppermute x3, waiting for transfers between devices: 6.47 us -> 11.5 us  [local(): away.append((pairs, [lax.ppermute(part, 'dp', pairs) for part in parts]))]
    ppermute x9 -> x12, starting transfers between devices: 4.91 us -> 6.2 us  [mate(): return lax.ppermute(value, 'dp', [(i, i ^ distance) for i in range(peers)])]
    ppermute x2, starting transfers between devices: 3.33 us -> 4.2 us  [local(): back = lax.ppermute(away_best, 'dp', [(t, s) for s, t in pairs])]
    pallas_call x3, Pallas kernels: 6.76 us -> 5.99 us  [local(): pl.pallas_call(functools.partial(cross_kernel, rows, start, counts), out_...]
    ppermute x2, waiting for transfers between devices: 0.13 us -> 0.83 us  [local(): back = lax.ppermute(away_best, 'dp', [(t, s) for s, t in pairs])]
    ppermute x3, starting transfers between devices: 6.42 us -> 5.82 us  [local(): away.append((pairs, [lax.ppermute(part, 'dp', pairs) for part in parts]))]
  transfers between devices with their start and end apart: 14 -> 17, of which waited for: 8 -> 10; matrix products, arithmetic and copies ran while one was open for 0% -> 0% of each run, Pallas kernels for 17% -> 15%
where the time goes in v8:
time: 51.4 us; the launch traced here: 51.3 us
  waiting for transfers between devices  23 us (45%)
  starting transfers between devices  16.2 us (32%)
  Pallas kernels  9.19 us (18%)
  local copies, waits for them, and re-layouts  2.19 us (4%)
  other arithmetic  0.6 us (1%)
    ppermute x3, waiting for transfers between devices, local(): away.append((pairs, [lax.ppermute(part, 'dp', pairs) for part in parts]))  11.5 us
    ppermute x12, waiting for transfers between devices, mate(): return lax.ppermute(value, 'dp', [(i, i ^ distance) for i in range(peers)])  10.6 us
    ppermute x12, starting transfers between devices, mate(): return lax.ppermute(value, 'dp', [(i, i ^ distance) for i in range(peers)])  6.2 us
    pallas_call x3, Pallas kernels, local(): pl.pallas_call(functools.partial(cross_kernel, rows, start, counts), out_...  5.99 us
    ppermute x3, starting transfers between devices, local(): away.append((pairs, [lax.ppermute(part, 'dp', pairs) for part in parts]))  5.82 us
    ppermute x2, starting transfers between devices, local(): back = lax.ppermute(away_best, 'dp', [(t, s) for s, t in pairs])  4.2 us
    pallas_call x1, Pallas kernels, local(): pl.pallas_call(functools.partial(plane_kernel, rows, (len(beside), len(ac...  1.48 us
    pallas_call x1, Pallas kernels, local(): pl.pallas_call(functools.partial(plane_kernel, rows, (1, len(near)), True...  1.48 us
  transfers between devices with their start and end apart: 17, of which 10 were waited for; matrix products, arithmetic and copies ran while one was open for 0% of the time, Pallas kernels for 15%

profile of v8, /device:TPU:0, one launch (start us, length us, event | category | flops | bytes accessed | tf_op | source)
XLA Modules:
  0.0 51.3 jit_solution(14349752220544073835)
XLA Ops:
  0.0 0.8 %concatenate.3 = s32[2048]{0:T(1024)S(1)} concatenate(s32[768]{0:T(1024)} %param.5, s32[768]{0:T(1024)} %param.6, s32[16]{0:T(128)} %param.7, s32[496]{0:T(512)S(1)} %broadcast_in_dim.3), dimensions={0} | concatenate | bytes 16384 | tf_op jit(solution)/shard_map/concatenate | solution.py:212
  0.8 1.4 %copy-done = f32[768,512]{1,0:T(8,128)S(1)} copy-done((f32[768,512]{1,0:T(8,128)S(1)}, f32[768,512]{1,0:T(8,128)}, u32[]{:S(2)}) %copy-start) | copy-done | bytes 1572888
  2.4 4.1 %collective-permute-start.6 = (bf16[784,512]{1,0:T(8,128)(2,1)S(1)}, bf16[784,512]{1,0:T(8,128)(2,1)S(1)}, u32[]{:S(2)}, u32[]{:S(2)}) collective-permute-start(bf16[784,512]{1,0:T(8,128)(2,1)S(1)} %get-tuple-element.36.own_ref.refs_0_), channel_id=1, source_target_pairs={{0,8},{1,9},{2,10},{3,11},{4,0},{5,1},{6,2},{7,3},{8,12},{9,13},{1... | collective-permute-start | bytes 2408456 | tf_op jit(solution)/shard_map/ppermute | solution.py:236
  6.5 1.5 %collective-permute-start.3 = (bf16[272,512]{1,0:T(8,128)(2,1)S(1)}, bf16[272,512]{1,0:T(8,128)(2,1)S(1)}, u32[]{:S(2)}, u32[]{:S(2)}) collective-permute-start(bf16[272,512]{1,0:T(8,128)(2,1)S(1)} %get-tuple-element.37), channel_id=1, source_target_pairs={{0,2},{1,3},{2,0},{3,1},{4,6},{5,7},{6,4},{7,5},{8,10},{9,11},{10,... | collective-permute-start | bytes 835592 | tf_op jit(solution)/shard_map/ppermute | solution.py:228
  8.6 1.5 %collective-permute-start.4 = (bf16[256,512]{1,0:T(8,128)(2,1)S(1)}, bf16[256,512]{1,0:T(8,128)(2,1)S(1)}, u32[]{:S(2)}, u32[]{:S(2)}) collective-permute-start(bf16[256,512]{1,0:T(8,128)(2,1)S(1)} %get-tuple-element.38), channel_id=1, source_target_pairs={{0,2},{1,3},{2,0},{3,1},{4,6},{5,7},{6,4},{7,5},{8,10},{9,11},{10,... | collective-permute-start | bytes 786440 | tf_op jit(solution)/shard_map/ppermute | solution.py:228
  10.1 6.0 %collective-permute-done.3.refs_0_.refs_4_ = bf16[272,512]{1,0:T(8,128)(2,1)S(1)} collective-permute-done((bf16[272,512]{1,0:T(8,128)(2,1)S(1)}, bf16[272,512]{1,0:T(8,128)(2,1)S(1)}, u32[]{:S(2)}, u32[]{:S(2)}) %collective-permute-start.3) | collective-permute-done | bytes 278560 | tf_op jit(solution)/shard_map/ppermute | solution.py:228
  16.1 8.8 %collective-permute-done.6.tags_ref.away_ref = bf16[784,512]{1,0:T(8,128)(2,1)S(1)} collective-permute-done((bf16[784,512]{1,0:T(8,128)(2,1)S(1)}, bf16[784,512]{1,0:T(8,128)(2,1)S(1)}, u32[]{:S(2)}, u32[]{:S(2)}) %collective-permute-start.6) | collective-permute-done | bytes 802848 | tf_op jit(solution)/shard_map/ppermute | solution.py:236
  24.9 1.0 %collective-permute-done.4.refs_1_.refs_5_ = bf16[256,512]{1,0:T(8,128)(2,1)S(1)} collective-permute-done((bf16[256,512]{1,0:T(8,128)(2,1)S(1)}, bf16[256,512]{1,0:T(8,128)(2,1)S(1)}, u32[]{:S(2)}, u32[]{:S(2)}) %collective-permute-start.4) | collective-permute-done | bytes 262176 | tf_op jit(solution)/shard_map/ppermute | solution.py:228
  26.4 1.0 %collective-permute-done.8.refs_4_.refs_8_ = bf16[256,512]{1,0:T(8,128)(2,1)S(1)} collective-permute-done((bf16[256,512]{1,0:T(8,128)(2,1)S(1)}, bf16[256,512]{1,0:T(8,128)(2,1)S(1)}, u32[]{:S(2)}, u32[]{:S(2)}) %collective-permute-start.8) | collective-permute-done | bytes 262176 | tf_op jit(solution)/shard_map/ppermute | solution.py:228
  27.9 1.7 %collective-permute-start.11 = (bf16[256,512]{1,0:T(8,128)(2,1)S(1)}, bf16[256,512]{1,0:T(8,128)(2,1)S(1)}, u32[]{:S(2)}, u32[]{:S(2)}) collective-permute-start(bf16[256,512]{1,0:T(8,128)(2,1)S(1)} %get-tuple-element.46), channel_id=1, source_target_pairs={{0,4},{1,5},{2,6},{3,7},{4,8},{5,9},{6,10},{7,11},{8,12},{9,13},{1... | collective-permute-start | bytes 786440 | tf_op jit(solution)/shard_map/ppermute | solution.py:236
  29.7 1.5 %plane_far.1 = (f32[8,128]{1,0:T(8,128)S(1)}, f32[768,128]{1,0:T(8,128)S(1)}, f32[768,128]{1,0:T(8,128)S(1)}) custom-call(bf16[784,512]{1,0:T(8,128)(2,1)S(1)} %get-tuple-element.36.own_ref.refs_0_, bf16[272,512]{1,0:T(8,128)(2,1)S(1)} %collective-permute-done.3.refs_0_.refs_4_, bf16[256,512]{1,0:T(8,128)(2,1)S(1)} %collective-permute-done.4.refs_1_.refs_5_, ...), custom_call_target="tpu_custom_call" | custom-call | flops 1 | bytes 1 | tf_op jit(solution)/shard_map/plane_far/pallas_call | solution.py:242
  31.2 1.5 %plane_near.1 = (f32[8,128]{1,0:T(8,128)S(1)}, f32[768,128]{1,0:T(8,128)S(1)}, f32[768,128]{1,0:T(8,128)S(1)}) custom-call(bf16[784,512]{1,0:T(8,128)(2,1)S(1)} %get-tuple-element.36.own_ref.refs_0_, bf16[784,512]{1,0:T(8,128)(2,1)S(1)} %get-tuple-element.36.own_ref.refs_0_, bf16[272,512]{1,0:T(8,128)(2,1)S(1)} %collective-permute-done.refs_1_, ...), custom_call_target="tpu_custom_call" | custom-call | flops 1 | bytes 1 | tf_op jit(solution)/shard_map/plane_near/pallas_call | solution.py:251
  32.7 2.8 %cross.3 = (f32[8,128]{1,0:T(8,128)S(1)}, f32[8,128]{1,0:T(8,128)S(1)}, f32[8,128]{1,0:T(8,128)S(1)}, f32[8,128]{1,0:T(8,128)S(1)}, f32[8,128]{1,0:T(8,128)S(1)}) custom-call(bf16[784,512]{1,0:T(8,128)(2,1)S(1)} %collective-permute-done.6.tags_ref.away_ref, bf16[784,512]{1,0:T(8,128)(2,1)S(1)} %collective-permute-done.6.tags_ref.away_ref, ...), custom_call_target="tpu_custom_call" | custom-call | flops 1 | bytes 1 | tf_op jit(solution)/shard_map/cross/pallas_call | solution.py:272
  35.5 1.7 %collective-permute-start.12 = (f32[8,128]{1,0:T(8,128)S(1)}, f32[8,128]{1,0:T(8,128)S(1)}, u32[]{:S(2)}, u32[]{:S(2)}) collective-permute-start(f32[8,128]{1,0:T(8,128)S(1)} %get-tuple-element.56), channel_id=1, source_target_pairs={{8,0},{9,1},{10,2},{11,3},{0,4},{1,5},{2,6},{3,7},{12,8},{13,9},{1... | collective-permute-start | bytes 12296 | tf_op jit(solution)/shard_map/ppermute | solution.py:282
  37.2 1.0 %collective-permute-done.10.tags_ref.away_ref = bf16[528,512]{1,0:T(8,128)(2,1)S(1)} collective-permute-done((bf16[528,512]{1,0:T(8,128)(2,1)S(1)}, bf16[528,512]{1,0:T(8,128)(2,1)S(1)}, u32[]{:S(2)}, u32[]{:S(2)}) %collective-permute-start.10) | collective-permute-done | bytes 540704 | tf_op jit(solution)/shard_map/ppermute | solution.py:236
  38.2 2.0 %cross.4 = (f32[8,128]{1,0:T(8,128)S(1)}, f32[8,128]{1,0:T(8,128)S(1)}, f32[8,128]{1,0:T(8,128)S(1)}, f32[8,128]{1,0:T(8,128)S(1)}, f32[8,128]{1,0:T(8,128)S(1)}) custom-call(bf16[528,512]{1,0:T(8,128)(2,1)S(1)} %collective-permute-done.10.tags_ref.away_ref, bf16[528,512]{1,0:T(8,128)(2,1)S(1)} %collective-permute-done.10.tags_ref.away_ref, ...), custom_call_target="tpu_custom_call" | custom-call | flops 1 | bytes 1 | tf_op jit(solution)/shard_map/cross/pallas_call | solution.py:272
  40.2 0.8 %collective-permute-done.12 = f32[8,128]{1,0:T(8,128)S(1)} collective-permute-done((f32[8,128]{1,0:T(8,128)S(1)}, f32[8,128]{1,0:T(8,128)S(1)}, u32[]{:S(2)}, u32[]{:S(2)}) %collective-permute-start.12) | collective-permute-done | bytes 4128 | tf_op jit(solution)/shard_map/ppermute | solution.py:282
  41.0 1.8 %collective-permute-done.11.away_ref = bf16[256,512]{1,0:T(8,128)(2,1)S(1)} collective-permute-done((bf16[256,512]{1,0:T(8,128)(2,1)S(1)}, bf16[256,512]{1,0:T(8,128)(2,1)S(1)}, u32[]{:S(2)}, u32[]{:S(2)}) %collective-permute-start.11) | collective-permute-done | bytes 262176 | tf_op jit(solution)/shard_map/ppermute | solution.py:236
  42.8 1.2 %cross.5 = (f32[8,128]{1,0:T(8,128)S(1)}, f32[8,128]{1,0:T(8,128)S(1)}, f32[8,128]{1,0:T(8,128)S(1)}, f32[8,128]{1,0:T(8,128)S(1)}, f32[8,128]{1,0:T(8,128)S(1)}) custom-call(bf16[528,512]{1,0:T(8,128)(2,1)S(1)} %collective-permute-done.10.tags_ref.away_ref, bf16[256,512]{1,0:T(8,128)(2,1)S(1)} %collective-permute-done.11.away_ref, ...), custom_call_target="tpu_custom_call" | custom-call | flops 1 | bytes 1 | tf_op jit(solution)/shard_map/cross/pallas_call | solution.py:272
  44.0 2.5 %collective-permute-start.13 = (f32[8,128]{1,0:T(8,128)S(1)}, f32[8,128]{1,0:T(8,128)S(1)}, u32[]{:S(2)}, u32[]{:S(2)}) collective-permute-start(f32[8,128]{1,0:T(8,128)S(1)} %get-tuple-element.63), channel_id=1, source_target_pairs={{4,0},{5,1},{6,2},{7,3},{8,4},{9,5},{10,6},{11,7},{12,8},{13,9},{1... | collective-permute-start | bytes 12296 | tf_op jit(solution)/shard_map/ppermute | solution.py:282
  47.0 1.0 %collective-permute-start.15 = (f32[8,128]{1,0:T(8,128)S(1)}, f32[8,128]{1,0:T(8,128)S(1)}, u32[]{:S(2)}, u32[]{:S(2)}) collective-permute-start(f32[8,128]{1,0:T(8,128)S(1)} %get-tuple-element.65), channel_id=1, source_target_pairs={{0,2},{1,3},{2,0},{3,1},{4,6},{5,7},{6,4},{7,5},{8,10},{9,11},{10,... | collective-permute-start | bytes 12296 | tf_op jit(solution)/shard_map/ppermute | solution.py:228
  48.4 1.2 %collective-permute-done.14 = f32[8,128]{1,0:T(8,128)S(1)} collective-permute-done((f32[8,128]{1,0:T(8,128)S(1)}, f32[8,128]{1,0:T(8,128)S(1)}, u32[]{:S(2)}, u32[]{:S(2)}) %collective-permute-start.14) | collective-permute-done | bytes 4128 | tf_op jit(solution)/shard_map/ppermute | solution.py:228
  49.5 1.1 %collective-permute-done.15 = f32[8,128]{1,0:T(8,128)S(1)} collective-permute-done((f32[8,128]{1,0:T(8,128)S(1)}, f32[8,128]{1,0:T(8,128)S(1)}, u32[]{:S(2)}, u32[]{:S(2)}) %collective-permute-start.15) | collective-permute-done | bytes 4128 | tf_op jit(solution)/shard_map/ppermute | solution.py:228
  50.7 0.6 %maximum_bitcast_fusion = f32[768]{0:T(1024)} fusion(f32[8,128]{1,0:T(8,128)S(1)} %collective-permute-done.16, f32[8,128]{1,0:T(8,128)S(1)} %collective-permute-done.15, f32[8,128]{1,0:T(8,128)S(1)} %collective-permute-done.14, f32[8,128]{1,0:T(8,128)S(1)} %collective-permute-done.13, f32[8,128]{1,0:T(8,128)S(1)} %collective-permute-done.12, f32[8,128]{1,0:T(8,128)S(1)} %max.24), kind=kLoop, calls=%fused_computation | loop fusion | flops 3840 | bytes 21504 | tf_op jit(solution)/shard_map/max | solution.py:289
  (23 shorter events, 2.7 us)
Async XLA Ops:
  0.8 1.4 %copy-start = (f32[768,512]{1,0:T(8,128)S(1)}, f32[768,512]{1,0:T(8,128)}, u32[]{:S(2)}) copy-start(f32[768,512]{1,0:T(8,128)} %embeddings_ref.1) | copy-start | bytes 4718596
  2.4 22.4 %collective-permute-start.6 = (bf16[784,512]{1,0:T(8,128)(2,1)S(1)}, bf16[784,512]{1,0:T(8,128)(2,1)S(1)}, u32[]{:S(2)}, u32[]{:S(2)}) collective-permute-start(bf16[784,512]{1,0:T(8,128)(2,1)S(1)} %get-tuple-element.36.own_ref.refs_0_), channel_id=1, source_target_pairs={{0,8},{1,9},{2,10},{3,11},{4,0},{5,1},{6,2},{7,3},{8,12},{9,13},{1... | collective-permute-start | bytes 2408456 | tf_op jit(solution)/shard_map/ppermute | solution.py:236
  6.5 9.6 %collective-permute-start.3 = (bf16[272,512]{1,0:T(8,128)(2,1)S(1)}, bf16[272,512]{1,0:T(8,128)(2,1)S(1)}, u32[]{:S(2)}, u32[]{:S(2)}) collective-permute-start(bf16[272,512]{1,0:T(8,128)(2,1)S(1)} %get-tuple-element.37), channel_id=1, source_target_pairs={{0,2},{1,3},{2,0},{3,1},{4,6},{5,7},{6,4},{7,5},{8,10},{9,11},{10,... | collective-permute-start | bytes 835592 | tf_op jit(solution)/shard_map/ppermute | solution.py:228
  8.0 16.8 %collective-permute-start.5 = (bf16[256,512]{1,0:T(8,128)(2,1)S(1)}, bf16[256,512]{1,0:T(8,128)(2,1)S(1)}, u32[]{:S(2)}, u32[]{:S(2)}) collective-permute-start(bf16[256,512]{1,0:T(8,128)(2,1)S(1)} %get-tuple-element.39), channel_id=1, source_target_pairs={{0,2},{1,3},{2,0},{3,1},{4,6},{5,7},{6,4},{7,5},{8,10},{9,11},{10,... | collective-permute-start | bytes 786440 | tf_op jit(solution)/shard_map/ppermute | solution.py:228
  8.6 17.3 %collective-permute-start.4 = (bf16[256,512]{1,0:T(8,128)(2,1)S(1)}, bf16[256,512]{1,0:T(8,128)(2,1)S(1)}, u32[]{:S(2)}, u32[]{:S(2)}) collective-permute-start(bf16[256,512]{1,0:T(8,128)(2,1)S(1)} %get-tuple-element.38), channel_id=1, source_target_pairs={{0,2},{1,3},{2,0},{3,1},{4,6},{5,7},{6,4},{7,5},{8,10},{9,11},{10,... | collective-permute-start | bytes 786440 | tf_op jit(solution)/shard_map/ppermute | solution.py:228
  10.1 28.1 %collective-permute-start.10 = (bf16[528,512]{1,0:T(8,128)(2,1)S(1)}, bf16[528,512]{1,0:T(8,128)(2,1)S(1)}, u32[]{:S(2)}, u32[]{:S(2)}) collective-permute-start(bf16[528,512]{1,0:T(8,128)(2,1)S(1)} %get-tuple-element.45), channel_id=1, source_target_pairs={{0,4},{1,5},{2,6},{3,7},{4,8},{5,9},{6,10},{7,11},{8,12},{9,13},{1... | collective-permute-start | bytes 1622024 | tf_op jit(solution)/shard_map/ppermute | solution.py:236
  24.9 3.1 %collective-permute-start.7 = (bf16[272,512]{1,0:T(8,128)(2,1)S(1)}, bf16[272,512]{1,0:T(8,128)(2,1)S(1)}, u32[]{:S(2)}, u32[]{:S(2)}) collective-permute-start(bf16[272,512]{1,0:T(8,128)(2,1)S(1)} %collective-permute-done.3.refs_0_.refs_4_), channel_id=1, source_target_pairs={{0,1},{1,0},{2,3},{3,2},{4,5},{5,4},{6,7},{7,6},{8,9},{9,8},{10,11... | collective-permute-start | bytes 835592 | tf_op jit(solution)/shard_map/ppermute | solution.py:228
  25.9 1.5 %collective-permute-start.8 = (bf16[256,512]{1,0:T(8,128)(2,1)S(1)}, bf16[256,512]{1,0:T(8,128)(2,1)S(1)}, u32[]{:S(2)}, u32[]{:S(2)}) collective-permute-start(bf16[256,512]{1,0:T(8,128)(2,1)S(1)} %collective-permute-done.4.refs_1_.refs_5_), channel_id=1, source_target_pairs={{0,1},{1,0},{2,3},{3,2},{4,5},{5,4},{6,7},{7,6},{8,9},{9,8},{10,11... | collective-permute-start | bytes 786440 | tf_op jit(solution)/shard_map/ppermute | solution.py:228
  25.9 1.9 %collective-permute-start.9 = (bf16[256,512]{1,0:T(8,128)(2,1)S(1)}, bf16[256,512]{1,0:T(8,128)(2,1)S(1)}, u32[]{:S(2)}, u32[]{:S(2)}) collective-permute-start(bf16[256,512]{1,0:T(8,128)(2,1)S(1)} %collective-permute-done.5.refs_2_.refs_6_), channel_id=1, source_target_pairs={{0,1},{1,0},{2,3},{3,2},{4,5},{5,4},{6,7},{7,6},{8,9},{9,8},{10,11... | collective-permute-start | bytes 786440 | tf_op jit(solution)/shard_map/ppermute | solution.py:228
  26.4 4.8 %collective-permute-start = (bf16[272,512]{1,0:T(8,128)(2,1)S(1)}, bf16[272,512]{1,0:T(8,128)(2,1)S(1)}, u32[]{:S(2)}, u32[]{:S(2)}) collective-permute-start(bf16[272,512]{1,0:T(8,128)(2,1)S(1)} %get-tuple-element.37), channel_id=1, source_target_pairs={{0,1},{1,0},{2,3},{3,2},{4,5},{5,4},{6,7},{7,6},{8,9},{9,8},{10,11... | collective-permute-start | bytes 835592 | tf_op jit(solution)/shard_map/ppermute | solution.py:228
  27.4 3.7 %collective-permute-start.1 = (bf16[256,512]{1,0:T(8,128)(2,1)S(1)}, bf16[256,512]{1,0:T(8,128)(2,1)S(1)}, u32[]{:S(2)}, u32[]{:S(2)}) collective-permute-start(bf16[256,512]{1,0:T(8,128)(2,1)S(1)} %get-tuple-element.38), channel_id=1, source_target_pairs={{0,1},{1,0},{2,3},{3,2},{4,5},{5,4},{6,7},{7,6},{8,9},{9,8},{10,11... | collective-permute-start | bytes 786440 | tf_op jit(solution)/shard_map/ppermute | solution.py:228
  27.8 3.4 %collective-permute-start.2 = (bf16[256,512]{1,0:T(8,128)(2,1)S(1)}, bf16[256,512]{1,0:T(8,128)(2,1)S(1)}, u32[]{:S(2)}, u32[]{:S(2)}) collective-permute-start(bf16[256,512]{1,0:T(8,128)(2,1)S(1)} %get-tuple-element.39), channel_id=1, source_target_pairs={{0,1},{1,0},{2,3},{3,2},{4,5},{5,4},{6,7},{7,6},{8,9},{9,8},{10,11... | collective-permute-start | bytes 786440 | tf_op jit(solution)/shard_map/ppermute | solution.py:228
  27.9 14.8 %collective-permute-start.11 = (bf16[256,512]{1,0:T(8,128)(2,1)S(1)}, bf16[256,512]{1,0:T(8,128)(2,1)S(1)}, u32[]{:S(2)}, u32[]{:S(2)}) collective-permute-start(bf16[256,512]{1,0:T(8,128)(2,1)S(1)} %get-tuple-element.46), channel_id=1, source_target_pairs={{0,4},{1,5},{2,6},{3,7},{4,8},{5,9},{6,10},{7,11},{8,12},{9,13},{1... | collective-permute-start | bytes 786440 | tf_op jit(solution)/shard_map/ppermute | solution.py:236
  35.5 5.5 %collective-permute-start.12 = (f32[8,128]{1,0:T(8,128)S(1)}, f32[8,128]{1,0:T(8,128)S(1)}, u32[]{:S(2)}, u32[]{:S(2)}) collective-permute-start(f32[8,128]{1,0:T(8,128)S(1)} %get-tuple-element.56), channel_id=1, source_target_pairs={{8,0},{9,1},{10,2},{11,3},{0,4},{1,5},{2,6},{3,7},{12,8},{13,9},{1... | collective-permute-start | bytes 12296 | tf_op jit(solution)/shard_map/ppermute | solution.py:282
  44.0 4.4 %collective-permute-start.13 = (f32[8,128]{1,0:T(8,128)S(1)}, f32[8,128]{1,0:T(8,128)S(1)}, u32[]{:S(2)}, u32[]{:S(2)}) collective-permute-start(f32[8,128]{1,0:T(8,128)S(1)} %get-tuple-element.63), channel_id=1, source_target_pairs={{4,0},{5,1},{6,2},{7,3},{8,4},{9,5},{10,6},{11,7},{12,8},{13,9},{1... | collective-permute-start | bytes 12296 | tf_op jit(solution)/shard_map/ppermute | solution.py:282
  46.5 3.0 %collective-permute-start.14 = (f32[8,128]{1,0:T(8,128)S(1)}, f32[8,128]{1,0:T(8,128)S(1)}, u32[]{:S(2)}, u32[]{:S(2)}) collective-permute-start(f32[8,128]{1,0:T(8,128)S(1)} %get-tuple-element.64), channel_id=1, source_target_pairs={{0,3},{1,2},{2,1},{3,0},{4,7},{5,6},{6,5},{7,4},{8,11},{9,10},{10,... | collective-permute-start | bytes 12296 | tf_op jit(solution)/shard_map/ppermute | solution.py:228
  47.0 3.6 %collective-permute-start.15 = (f32[8,128]{1,0:T(8,128)S(1)}, f32[8,128]{1,0:T(8,128)S(1)}, u32[]{:S(2)}, u32[]{:S(2)}) collective-permute-start(f32[8,128]{1,0:T(8,128)S(1)} %get-tuple-element.65), channel_id=1, source_target_pairs={{0,2},{1,3},{2,0},{3,1},{4,6},{5,7},{6,4},{7,5},{8,10},{9,11},{10,... | collective-permute-start | bytes 12296 | tf_op jit(solution)/shard_map/ppermute | solution.py:228
  48.0 2.6 %collective-permute-start.16 = (f32[8,128]{1,0:T(8,128)S(1)}, f32[8,128]{1,0:T(8,128)S(1)}, u32[]{:S(2)}, u32[]{:S(2)}) collective-permute-start(f32[8,128]{1,0:T(8,128)S(1)} %get-tuple-element.66), channel_id=1, source_target_pairs={{0,1},{1,0},{2,3},{3,2},{4,5},{5,4},{6,7},{7,6},{8,9},{9,8},{10,11... | collective-permute-start | bytes 12296 | tf_op jit(solution)/shard_map/ppermute | solution.py:228

commit v9 on v8

v9 whole, which is shorter than its diff:
```python
import functools

import jax
import jax.numpy as jnp
from jax import lax
from jax.experimental import pallas as pl
from jax.experimental.pallas import tpu as pltpu
from jax.sharding import PartitionSpec as P

LABELS = 3
PLANE = 4
PAD = 16
BASE = 64.0
TILE = 256
FIRST = 512
VMEM_LIMIT = 24 * 2**20


def whole(count):
    return [pl.BlockSpec(memory_space=pltpu.VMEM)] * count


def params():
    return pltpu.CompilerParams(vmem_limit_bytes=VMEM_LIMIT)


def lanes_shape(rows):
    return jax.ShapeDtypeStruct((-(-rows // 1024) * 8, 128), jnp.float32)


def unit_rows(values):
    squares = jnp.sum(values * values, axis=1, keepdims=True)
    return (values * lax.rsqrt(squares + 1e-06)).astype(jnp.bfloat16)


def first_kernel(embeddings_ref, first_ref):
    for row in range(0, first_ref.shape[0], 128):
        first_ref[row : row + 128, :] = unit_rows(embeddings_ref[row : row + 128, :])


def rest_kernel(rows, embeddings_ref, ints_ref, first_ref, last_ref, head_ref, tail_ref):
    label_row = rows // 128
    owner, label = ints_ref[0:8, :], ints_ref[label_row : label_row + 8, :]
    runs = ints_ref[2 * label_row : 2 * label_row + 1, :]
    first_owner = jnp.take_along_axis(jnp.broadcast_to(runs, owner.shape), owner, axis=1)
    tags = 1 + jnp.where(label == 0, first_owner * LABELS, owner * LABELS + label)
    tags = tags.astype(jnp.float32)
    high = jnp.floor(tags * (1.0 / BASE))
    digits = jnp.concatenate([high, tags - high * BASE], axis=0).astype(jnp.bfloat16)
    width = embeddings_ref.shape[1]
    digits = jnp.concatenate([digits, jnp.zeros((PAD, width - 128), jnp.bfloat16)], axis=1)
    last_ref[0:PAD, :] = digits
    head_ref[0:PAD, :] = digits
    head_ref[PAD:, :] = first_ref[...]
    first = first_ref.shape[0]
    for row in range(0, rows - first, 128):
        unit = unit_rows(embeddings_ref[first + row : first + row + 128, :])
        last_ref[PAD + row : PAD + row + 128, :] = unit
        tail_ref[row : row + 128, :] = unit


def tag_rows(block_ref):
    digits = block_ref[0:PAD, 0:128].astype(jnp.float32)
    return digits[0:8] * BASE + digits[8:16]


def tag_columns(block_ref, rows):
    tags = tag_rows(block_ref)
    return jnp.concatenate(
        [jnp.transpose(jnp.broadcast_to(tags[n : n + 1], (128, 128))) for n in range(rows // 128)],
        axis=0,
    )


def dot_rows(values, lanes):
    return lax.dot_general(
        values, lanes, (((1,), (1,)), ((), ())), preferred_element_type=jnp.float32
    )


def unit_parts(refs):
    parts, first = [], 0
    for n, ref in enumerate(refs):
        part = ref if n + 1 < len(refs) else ref.at[PAD:]
        parts.append((first, part))
        first += part.shape[0]
    return parts


def take(refs, counts):
    groups = []
    for count in counts:
        groups.append(refs[:count])
        refs = refs[count:]
    return groups, refs


def fold_sublanes(values):
    rows, lanes = values.shape
    return jnp.max(values.reshape(rows // 8, 8, lanes), axis=0)


def fold_lanes(values):
    return jnp.concatenate(
        [
            jnp.max(jnp.transpose(values[first : first + 128]), axis=0, keepdims=True)
            for first in range(0, values.shape[0], 128)
        ],
        axis=0,
    )


def row_slices(block):
    slices = []
    for first, part in unit_parts(block):
        count = part.shape[0]
        for row in range(0, count, TILE):
            size = min(TILE, count - row)
            slices.append((first + row, part.at[row : row + size]))
    return slices


def plane_kernel(rows, with_self, *refs):
    (own, one, two), refs = take(refs, (2, 2, 2))
    best_ref, column_refs = refs[-3], refs[-2:]
    own_tags = tag_rows(own[-1])
    for block, column_ref in zip((one, two), column_refs):
        column_ref[...] = tag_columns(block[-1], rows)
    for tile, own_part in row_slices(own):
        lanes = own_part[...]
        best = [jnp.full((8, 128), -1.0, jnp.float32) for _ in range(0, TILE, 128)]
        for which, (block, column_ref) in enumerate(zip((one, two), column_refs)):
            for first, part in row_slices(block):
                count = part.shape[0]
                found = dot_rows(part[...], lanes)
                column = column_ref[first : first + count, :]
                for n in range(TILE // 128):
                    lane = tile + n * 128
                    match = column == own_tags[lane // 128 : lane // 128 + 1]
                    if with_self and which == 0 and first < lane + 128 and lane < first + count:
                        row_id = lax.broadcasted_iota(jnp.int32, (count, 128), 0) + first
                        lane_id = lax.broadcasted_iota(jnp.int32, (count, 128), 1) + lane
                        match = match & (row_id != lane_id)
                    masked = jnp.where(match, found[:, n * 128 : n * 128 + 128], -1.0)
                    best[n] = jnp.maximum(best[n], fold_sublanes(masked))
        for n in range(TILE // 128):
            place = pl.ds(tile // 128 + n, 1)
            folded = jnp.max(best[n], axis=0, keepdims=True)
            if with_self:
                folded = jnp.maximum(folded, refs[0][place, :])
            best_ref[place, :] = folded


def cross_kernel(starts, bases, *refs):
    (tags, aways), refs = take(refs, (1, len(starts)))
    blocks, refs = take(refs, (2,) * PLANE)
    columns, refs = refs[:PLANE], refs[PLANE:]
    away_before, away_best = refs[0], refs[PLANE + 1]
    plane_before, plane_best = refs[1 : PLANE + 1], refs[PLANE + 2 :]
    away_tags = tag_rows(tags[0])
    tiles = []
    for start, base, away in zip(starts, bases, aways):
        for row in range(0, away.shape[0] - base, TILE):
            tiles.append((start + row, away.at[base + row : base + row + TILE]))
    best = {}
    for which in range(PLANE):
        for first, part in row_slices(blocks[which]):
            count = part.shape[0]
            row_best = jnp.full((count, 128), -1.0, jnp.float32)
            for tile, away in tiles:
                found = dot_rows(part[...], away[...])
                column = columns[which][first : first + count, :]
                for lane in range(0, TILE, 128):
                    row = (tile + lane) // 128
                    match = column == away_tags[row : row + 1]
                    masked = jnp.where(match, found[:, lane : lane + 128], -1.0)
                    row_best = jnp.maximum(row_best, masked)
                    folded = fold_sublanes(masked)
                    best[row] = jnp.maximum(best[row], folded) if row in best else folded
            place = pl.ds(first // 128, count // 128)
            folded = fold_lanes(row_best)
            plane_best[which][place, :] = jnp.maximum(folded, plane_before[which][place, :])
    away_best[...] = away_before[...]
    for row, values in best.items():
        away_best[row : row + 1, :] = jnp.max(values, axis=0, keepdims=True)


def small_cost():
    return pl.CostEstimate(flops=1, bytes_accessed=1, transcendentals=0)


def plane_steps(planes):
    if planes == 4:
        return [(2, 0, 3, 1), (1, 2, 3, 0)]
    return [
        [(z + distance) % planes for z in range(planes)]
        for distance in range(1, planes // 2 + 1)
    ]


def after(value, *others):
    return lax.optimization_barrier((value,) + others)[0]


def local(embeddings, owner_index, sub_label, run_start):
    rows, width = embeddings.shape
    peers = lax.axis_size("dp")
    planes = peers // PLANE
    lanes = lanes_shape(rows)

    space = -(2 * rows + peers) % 2048
    ints = jnp.concatenate([owner_index, sub_label, run_start, jnp.zeros((space,), jnp.int32)])
    ints = ints.reshape(-1, 128)
    def kernel(body, inputs, outputs, name):
        return pl.pallas_call(
            body,
            out_shape=tuple(outputs),
            in_specs=whole(len(inputs)),
            out_specs=tuple(whole(len(outputs))),
            compiler_params=params(),
            cost_estimate=small_cost(),
            name=name,
        )(*inputs)

    def part_shape(count):
        return jax.ShapeDtypeStruct((count, width), jnp.bfloat16)

    rest = rows - FIRST
    (first,) = kernel(first_kernel, (embeddings,), (part_shape(FIRST),), "first")
    last, head, tail = kernel(
        functools.partial(rest_kernel, rows),
        (embeddings, ints, first),
        (part_shape(PAD + rest), part_shape(PAD + FIRST), part_shape(rest)),
        "rest",
    )
    own = (first, last)

    def mate(value, distance):
        return lax.ppermute(value, "dp", [(i, i ^ distance) for i in range(peers)])

    away = []
    for n, step in enumerate(plane_steps(planes)):
        pairs = [(z * PLANE + j, t * PLANE + j) for z, t in enumerate(step) for j in range(PLANE)]
        parts = (head, tail) if n else own
        if n > 1:
            parts = [after(part, away[-1][1][-1]) for part in parts]
        away.append((pairs, [lax.ppermute(part, "dp", pairs) for part in parts]))
    beside = [mate(part, 2) for part in own]
    near = [mate(part, 1) for part in own]
    across = [mate(after(part, *away[0][1]), 1) for part in beside]

    columns = jax.ShapeDtypeStruct((rows, 128), jnp.float32)
    best, beside_columns, across_columns = kernel(
        functools.partial(plane_kernel, rows, False),
        (*own, *beside, *across),
        (lanes, columns, columns),
        "plane_far",
    )
    best, own_columns, near_columns = kernel(
        functools.partial(plane_kernel, rows, True),
        (*own, *own, *near, best),
        (lanes, columns, columns),
        "plane_near",
    )
    plane = (*own, *near, *beside, *across)
    plane += (own_columns, near_columns, beside_columns, across_columns)
    plane_best = [jnp.full(lanes.shape, -1.0, jnp.float32)] * PLANE
    backs = []
    for n, (pairs, received) in enumerate(away):
        away_best = jnp.full(lanes.shape, -1.0, jnp.float32)
        if n:
            calls = (((0,), (PAD,), received[:1]), ((FIRST,), (0,), received[1:]))
        else:
            calls = (((0, FIRST), (0, PAD), received),)
        tags = received[0] if n else received[-1]
        for starts, bases, parts in calls:
            if n and starts[0]:
                away_best = after(away_best, backs[-1])
            away_best, *plane_best = kernel(
                functools.partial(cross_kernel, starts, bases),
                (tags, *parts, *plane, away_best, *plane_best),
                (lanes,) * (PLANE + 1),
                "cross",
            )
        backs.append(lax.ppermute(away_best, "dp", [(t, s) for s, t in pairs]))
    best = jnp.maximum(best, plane_best[0]).reshape(-1)[:rows]
    for distance, values in ((3, plane_best[3]), (2, plane_best[2]), (1, plane_best[1])):
        backs.insert(-1, mate(values, distance))
    for back in backs:
        best = jnp.maximum(best, back.reshape(-1)[:rows])
    return best


def solution(mesh):
    in_specs = (P(("groups", "dp"), None), P(("groups", "dp")), P(("groups", "dp")), P("groups"))
    out_specs = P(("groups", "dp"))
    return jax.shard_map(local, mesh=mesh, in_specs=in_specs, out_specs=out_specs, check_vma=False)
```

time: 51.4 us -> 49.6 us (0.965)
  waiting for transfers between devices: 23 us -> 21.4 us
  local copies, waits for them, and re-layouts: 2.19 us -> 1.51 us
    ppermute x12 -> x9, waiting for transfers between devices: 10.6 us -> 1.56 us  [mate(): return lax.ppermute(value, 'dp', [(i, i ^ distance) for i in range(peers)])]
    ppermute x3 -> x4, waiting for transfers between devices: 11.5 us -> 17.7 us  [local(): away.append((pairs, [lax.ppermute(part, 'dp', pairs) for part in parts]))]
    ppermute x3 -> x4, starting transfers between devices: 5.82 us -> 7.48 us  [local(): away.append((pairs, [lax.ppermute(part, 'dp', pairs) for part in parts]))]
    ppermute x2, waiting for transfers between devices: 0.83 us -> 2.13 us  [local(): backs.append(lax.ppermute(away_best, 'dp', [(t, s) for s, t in pairs]))]
    ppermute x12 -> x9, starting transfers between devices: 6.2 us -> 4.97 us  [mate(): return lax.ppermute(value, 'dp', [(i, i ^ distance) for i in range(peers)])]
    concatenate x1, local copies, waits for them, and re-layouts: 0.78 us -> 0.08 us  [local(): jnp.concatenate([owner_index, sub_label, run_start, jnp.zeros((space,), j...]
    pallas_call x6 -> x7, Pallas kernels: 9.19 us -> 9.25 us  [kernel(): pl.pallas_call(body, out_shape=tuple(outputs), in_specs=whole(len(inputs)...]
    unnamed x2 -> x10, local copies, waits for them, and re-layouts: 1.41 us -> 1.42 us
  transfers between devices with their start and end apart: 17 -> 15, of which waited for: 10 -> 7; matrix products, arithmetic and copies ran while one was open for 0% -> 0% of each run, Pallas kernels for 15% -> 16%
where the time goes in v9:
time: 49.6 us; the launch traced here: 49.4 us
  waiting for transfers between devices  21.4 us (43%)
  starting transfers between devices  16.6 us (33%)
  Pallas kernels  9.25 us (19%)
  local copies, waits for them, and re-layouts  1.51 us (3%)
  other arithmetic  0.6 us (1%)
    ppermute x4, waiting for transfers between devices, local(): away.append((pairs, [lax.ppermute(part, 'dp', pairs) for part in parts]))  17.7 us
    pallas_call x7, Pallas kernels, kernel(): pl.pallas_call(body, out_shape=tuple(outputs), in_specs=whole(len(inputs)...  9.25 us
    ppermute x4, starting transfers between devices, local(): away.append((pairs, [lax.ppermute(part, 'dp', pairs) for part in parts]))  7.48 us
    ppermute x9, starting transfers between devices, mate(): return lax.ppermute(value, 'dp', [(i, i ^ distance) for i in range(peers)])  4.97 us
    ppermute x2, starting transfers between devices, local(): backs.append(lax.ppermute(away_best, 'dp', [(t, s) for s, t in pairs]))  4.15 us
    ppermute x2, waiting for transfers between devices, local(): backs.append(lax.ppermute(away_best, 'dp', [(t, s) for s, t in pairs]))  2.13 us
    ppermute x9, waiting for transfers between devices, mate(): return lax.ppermute(value, 'dp', [(i, i ^ distance) for i in range(peers)])  1.56 us
    unnamed x10, local copies, waits for them, and re-layouts  1.42 us
  transfers between devices with their start and end apart: 15, of which 7 were waited for; matrix products, arithmetic and copies ran while one was open for 0% of the time, Pallas kernels for 16%

profile of v9, /device:TPU:0, one launch (start us, length us, event | category | flops | bytes accessed | tf_op | source)
XLA Modules:
  0.0 49.4 jit_solution(17357978328671673789)
XLA Ops:
  0.0 1.4 %copy-done = f32[768,512]{1,0:T(8,128)S(1)} copy-done((f32[768,512]{1,0:T(8,128)S(1)}, f32[768,512]{1,0:T(8,128)}, u32[]{:S(2)}) %copy-start) | copy-done | bytes 1572888
  1.6 4.1 %collective-permute-start.4 = (bf16[512,512]{1,0:T(8,128)(2,1)S(1)}, bf16[512,512]{1,0:T(8,128)(2,1)S(1)}, u32[]{:S(2)}, u32[]{:S(2)}) collective-permute-start(bf16[512,512]{1,0:T(8,128)(2,1)S(1)} %first.1.first_ref.refs_0_.refs_2_.refs_3_), channel_id=1, source_target_pairs={{0,8},{1,9},{2,10},{3,11},{4,0},{5,1},{6,2},{7,3},{8,12},{9,13},{1... | collective-permute-start | bytes 1572872 | tf_op jit(solution)/shard_map/ppermute | solution.py:247
  5.7 1.5 %collective-permute-start.2 = (bf16[512,512]{1,0:T(8,128)(2,1)S(1)}, bf16[512,512]{1,0:T(8,128)(2,1)S(1)}, u32[]{:S(2)}, u32[]{:S(2)}) collective-permute-start(bf16[512,512]{1,0:T(8,128)(2,1)S(1)} %first.1.first_ref.refs_0_.refs_2_.refs_3_), channel_id=1, source_target_pairs={{0,2},{1,3},{2,0},{3,1},{4,6},{5,7},{6,4},{7,5},{8,10},{9,11},{10,... | collective-permute-start | bytes 1572872 | tf_op jit(solution)/shard_map/ppermute | solution.py:239
  7.4 1.6 %collective-permute-start.5 = (bf16[272,512]{1,0:T(8,128)(2,1)S(1)}, bf16[272,512]{1,0:T(8,128)(2,1)S(1)}, u32[]{:S(2)}, u32[]{:S(2)}) collective-permute-start(bf16[272,512]{1,0:T(8,128)(2,1)S(1)} %get-tuple-element.32.refs_1_.refs_3_.refs_4_), channel_id=1, source_target_pairs={{0,8},{1,9},{2,10},{3,11},{4,0},{5,1},{6,2},{7,3},{8,12},{9,13},{1... | collective-permute-start | bytes 835592 | tf_op jit(solution)/shard_map/ppermute | solution.py:247
  9.1 0.5 %collective-permute-start.3 = (bf16[272,512]{1,0:T(8,128)(2,1)S(1)}, bf16[272,512]{1,0:T(8,128)(2,1)S(1)}, u32[]{:S(2)}, u32[]{:S(2)}) collective-permute-start(bf16[272,512]{1,0:T(8,128)(2,1)S(1)} %get-tuple-element.32.refs_1_.refs_3_.refs_4_), channel_id=1, source_target_pairs={{0,2},{1,3},{2,0},{3,1},{4,6},{5,7},{6,4},{7,5},{8,10},{9,11},{10,... | collective-permute-start | bytes 835592 | tf_op jit(solution)/shard_map/ppermute | solution.py:239
  9.6 0.4 collective-permute-start.8
  10.0 14.0 %collective-permute-done.5.refs_0_.refs_2_ = bf16[272,512]{1,0:T(8,128)(2,1)S(1)} collective-permute-done((bf16[272,512]{1,0:T(8,128)(2,1)S(1)}, bf16[272,512]{1,0:T(8,128)(2,1)S(1)}, u32[]{:S(2)}, u32[]{:S(2)}) %collective-permute-start.5) | collective-permute-done | bytes 278560 | tf_op jit(solution)/shard_map/ppermute | solution.py:247
  24.0 1.0 %collective-permute-done.3.refs_3_.refs_8_.refs_7_ = bf16[272,512]{1,0:T(8,128)(2,1)S(1)} collective-permute-done((bf16[272,512]{1,0:T(8,128)(2,1)S(1)}, bf16[272,512]{1,0:T(8,128)(2,1)S(1)}, u32[]{:S(2)}, u32[]{:S(2)}) %collective-permute-start.3) | collective-permute-done | bytes 278560 | tf_op jit(solution)/shard_map/ppermute | solution.py:239
  25.0 0.5 %collective-permute-start.6 = (bf16[512,512]{1,0:T(8,128)(2,1)S(1)}, bf16[512,512]{1,0:T(8,128)(2,1)S(1)}, u32[]{:S(2)}, u32[]{:S(2)}) collective-permute-start(bf16[512,512]{1,0:T(8,128)(2,1)S(1)} %collective-permute-done.2.refs_2_.refs_7_.refs_6_), channel_id=1, source_target_pairs={{0,1},{1,0},{2,3},{3,2},{4,5},{5,4},{6,7},{7,6},{8,9},{9,8},{10,11... | collective-permute-start | bytes 1572872 | tf_op jit(solution)/shard_map/ppermute | solution.py:239
  26.1 0.5 %collective-permute-done.7.refs_5_.refs_10_.refs_9_ = bf16[272,512]{1,0:T(8,128)(2,1)S(1)} collective-permute-done((bf16[272,512]{1,0:T(8,128)(2,1)S(1)}, bf16[272,512]{1,0:T(8,128)(2,1)S(1)}, u32[]{:S(2)}, u32[]{:S(2)}) %collective-permute-start.7) | collective-permute-done | bytes 278560 | tf_op jit(solution)/shard_map/ppermute | solution.py:239
  26.6 1.3 %collective-permute-start.9 = (bf16[256,512]{1,0:T(8,128)(2,1)S(1)}, bf16[256,512]{1,0:T(8,128)(2,1)S(1)}, u32[]{:S(2)}, u32[]{:S(2)}) collective-permute-start(bf16[256,512]{1,0:T(8,128)(2,1)S(1)} %get-tuple-element.38), channel_id=1, source_target_pairs={{0,4},{1,5},{2,6},{3,7},{4,8},{5,9},{6,10},{7,11},{8,12},{9,13},{1... | collective-permute-start | bytes 786440 | tf_op jit(solution)/shard_map/ppermute | solution.py:247
  27.9 1.5 %plane_far.1 = (f32[8,128]{1,0:T(8,128)S(1)}, f32[768,128]{1,0:T(8,128)S(1)}, f32[768,128]{1,0:T(8,128)S(1)}) custom-call(bf16[512,512]{1,0:T(8,128)(2,1)S(1)} %first.1.first_ref.refs_0_.refs_2_.refs_3_, bf16[272,512]{1,0:T(8,128)(2,1)S(1)} %get-tuple-element.32.refs_1_.refs_3_.refs_4_, bf16[512,512]{1,0:T(8,128)(2,1)S(1)} %collective-permute-done.2.refs_2_.refs_7_.refs_6_, ...), custom_call_target="tpu_custom_call" | custom-call | flops 1 | bytes 1 | tf_op jit(solution)/shard_map/plane_far/pallas_call | solution.py:215
  29.4 1.5 %plane_near.1 = (f32[8,128]{1,0:T(8,128)S(1)}, f32[768,128]{1,0:T(8,128)S(1)}, f32[768,128]{1,0:T(8,128)S(1)}) custom-call(bf16[512,512]{1,0:T(8,128)(2,1)S(1)} %first.1.first_ref.refs_0_.refs_2_.refs_3_, bf16[272,512]{1,0:T(8,128)(2,1)S(1)} %get-tuple-element.32.refs_1_.refs_3_.refs_4_, bf16[512,512]{1,0:T(8,128)(2,1)S(1)} %first.1.first_ref.refs_0_.refs_2_.refs_3_, ...), custom_call_target="tpu_custom_call" | custom-call | flops 1 | bytes 1 | tf_op jit(solution)/shard_map/plane_near/pallas_call | solution.py:215
  30.9 2.8 %cross.3 = (f32[8,128]{1,0:T(8,128)S(1)}, f32[8,128]{1,0:T(8,128)S(1)}, f32[8,128]{1,0:T(8,128)S(1)}, f32[8,128]{1,0:T(8,128)S(1)}, f32[8,128]{1,0:T(8,128)S(1)}) custom-call(bf16[272,512]{1,0:T(8,128)(2,1)S(1)} %collective-permute-done.5.refs_0_.refs_2_, bf16[512,512]{1,0:T(8,128)(2,1)S(1)} %collective-permute-done.4.refs_1_, ...), custom_call_target="tpu_custom_call" | custom-call | flops 1 | bytes 1 | tf_op jit(solution)/shard_map/cross/pallas_call | solution.py:215
  33.8 1.7 %collective-permute-start.10 = (f32[8,128]{1,0:T(8,128)S(1)}, f32[8,128]{1,0:T(8,128)S(1)}, u32[]{:S(2)}, u32[]{:S(2)}) collective-permute-start(f32[8,128]{1,0:T(8,128)S(1)} %get-tuple-element.48), channel_id=1, source_target_pairs={{8,0},{9,1},{10,2},{11,3},{0,4},{1,5},{2,6},{3,7},{12,8},{13,9},{1... | collective-permute-start | bytes 12296 | tf_op jit(solution)/shard_map/ppermute | solution.py:285
  35.4 2.0 %collective-permute-done.8.refs_0_.refs_1_ = bf16[528,512]{1,0:T(8,128)(2,1)S(1)} collective-permute-done((bf16[528,512]{1,0:T(8,128)(2,1)S(1)}, bf16[528,512]{1,0:T(8,128)(2,1)S(1)}, u32[]{:S(2)}, u32[]{:S(2)}) %collective-permute-start.8) | collective-permute-done | bytes 540704 | tf_op jit(solution)/shard_map/ppermute | solution.py:247
  37.4 2.0 %cross.4 = (f32[8,128]{1,0:T(8,128)S(1)}, f32[8,128]{1,0:T(8,128)S(1)}, f32[8,128]{1,0:T(8,128)S(1)}, f32[8,128]{1,0:T(8,128)S(1)}, f32[8,128]{1,0:T(8,128)S(1)}) custom-call(bf16[528,512]{1,0:T(8,128)(2,1)S(1)} %collective-permute-done.8.refs_0_.refs_1_, bf16[528,512]{1,0:T(8,128)(2,1)S(1)} %collective-permute-done.8.refs_0_.refs_1_, ...), custom_call_target="tpu_custom_call" | custom-call | flops 1 | bytes 1 | tf_op jit(solution)/shard_map/cross/pallas_call | solution.py:215
  39.3 0.8 %collective-permute-done.10 = f32[8,128]{1,0:T(8,128)S(1)} collective-permute-done((f32[8,128]{1,0:T(8,128)S(1)}, f32[8,128]{1,0:T(8,128)S(1)}, u32[]{:S(2)}, u32[]{:S(2)}) %collective-permute-start.10) | collective-permute-done | bytes 4128 | tf_op jit(solution)/shard_map/ppermute | solution.py:285
  40.2 1.8 %collective-permute-done.9.refs_1_ = bf16[256,512]{1,0:T(8,128)(2,1)S(1)} collective-permute-done((bf16[256,512]{1,0:T(8,128)(2,1)S(1)}, bf16[256,512]{1,0:T(8,128)(2,1)S(1)}, u32[]{:S(2)}, u32[]{:S(2)}) %collective-permute-start.9) | collective-permute-done | bytes 262176 | tf_op jit(solution)/shard_map/ppermute | solution.py:247
  41.9 1.2 %cross.5 = (f32[8,128]{1,0:T(8,128)S(1)}, f32[8,128]{1,0:T(8,128)S(1)}, f32[8,128]{1,0:T(8,128)S(1)}, f32[8,128]{1,0:T(8,128)S(1)}, f32[8,128]{1,0:T(8,128)S(1)}) custom-call(bf16[528,512]{1,0:T(8,128)(2,1)S(1)} %collective-permute-done.8.refs_0_.refs_1_, bf16[256,512]{1,0:T(8,128)(2,1)S(1)} %collective-permute-done.9.refs_1_, ...), custom_call_target="tpu_custom_call" | custom-call | flops 1 | bytes 1 | tf_op jit(solution)/shard_map/cross/pallas_call | solution.py:215
  43.2 1.6 %collective-permute-start.12 = (f32[8,128]{1,0:T(8,128)S(1)}, f32[8,128]{1,0:T(8,128)S(1)}, u32[]{:S(2)}, u32[]{:S(2)}) collective-permute-start(f32[8,128]{1,0:T(8,128)S(1)} %get-tuple-element.56), channel_id=1, source_target_pairs={{0,2},{1,3},{2,0},{3,1},{4,6},{5,7},{6,4},{7,5},{8,10},{9,11},{10,... | collective-permute-start | bytes 12296 | tf_op jit(solution)/shard_map/ppermute | solution.py:239
  45.0 2.5 %collective-permute-start.14 = (f32[8,128]{1,0:T(8,128)S(1)}, f32[8,128]{1,0:T(8,128)S(1)}, u32[]{:S(2)}, u32[]{:S(2)}) collective-permute-start(f32[8,128]{1,0:T(8,128)S(1)} %get-tuple-element.58), channel_id=1, source_target_pairs={{4,0},{5,1},{6,2},{7,3},{8,4},{9,5},{10,6},{11,7},{12,8},{13,9},{1... | collective-permute-start | bytes 12296 | tf_op jit(solution)/shard_map/ppermute | solution.py:285
  47.5 1.3 %collective-permute-done.14 = f32[8,128]{1,0:T(8,128)S(1)} collective-permute-done((f32[8,128]{1,0:T(8,128)S(1)}, f32[8,128]{1,0:T(8,128)S(1)}, u32[]{:S(2)}, u32[]{:S(2)}) %collective-permute-start.14) | collective-permute-done | bytes 4128 | tf_op jit(solution)/shard_map/ppermute | solution.py:285
  48.8 0.6 %maximum_bitcast_fusion = f32[768]{0:T(1024)} fusion(f32[8,128]{1,0:T(8,128)S(1)} %collective-permute-done.14, f32[8,128]{1,0:T(8,128)S(1)} %collective-permute-done.13, f32[8,128]{1,0:T(8,128)S(1)} %collective-permute-done.12, f32[8,128]{1,0:T(8,128)S(1)} %collective-permute-done.11, f32[8,128]{1,0:T(8,128)S(1)} %collective-permute-done.10, f32[8,128]{1,0:T(8,128)S(1)} %max.24), kind=kLoop, calls=%fused_computation | loop fusion | flops 3840 | bytes 21504 | tf_op jit(solution)/shard_map/max | solution.py:290
  (28 shorter events, 1.3 us)
Async XLA Ops:
  0.0 1.4 %copy-start = (f32[768,512]{1,0:T(8,128)S(1)}, f32[768,512]{1,0:T(8,128)}, u32[]{:S(2)}) copy-start(f32[768,512]{1,0:T(8,128)} %embeddings_ref.3) | copy-start | bytes 4718596
  1.4 5.8 %copy-start.2 = (s32[768]{0:T(1024)S(1)}, s32[768]{0:T(1024)}, u32[]{:S(2)}) copy-start(s32[768]{0:T(1024)} %param.5) | copy-start | bytes 9220
  1.4 5.8 %copy-start.3 = (s32[768]{0:T(1024)S(1)}, s32[768]{0:T(1024)}, u32[]{:S(2)}) copy-start(s32[768]{0:T(1024)} %param.6) | copy-start | bytes 9220
  1.4 5.8 %copy-start.4 = (s32[16]{0:T(128)S(1)}, s32[16]{0:T(128)}, u32[]{:S(2)}) copy-start(s32[16]{0:T(128)} %param.7) | copy-start | bytes 196
  1.4 5.9 %copy-start.1 = (f32[768,512]{1,0:T(8,128)S(1)}, f32[768,512]{1,0:T(8,128)}, u32[]{:S(2)}) copy-start(f32[768,512]{1,0:T(8,128)} %embeddings_ref.3) | copy-start | bytes 4718596
  1.6 23.4 %collective-permute-start.4 = (bf16[512,512]{1,0:T(8,128)(2,1)S(1)}, bf16[512,512]{1,0:T(8,128)(2,1)S(1)}, u32[]{:S(2)}, u32[]{:S(2)}) collective-permute-start(bf16[512,512]{1,0:T(8,128)(2,1)S(1)} %first.1.first_ref.refs_0_.refs_2_.refs_3_), channel_id=1, source_target_pairs={{0,8},{1,9},{2,10},{3,11},{4,0},{5,1},{6,2},{7,3},{8,12},{9,13},{1... | collective-permute-start | bytes 1572872 | tf_op jit(solution)/shard_map/ppermute | solution.py:247
  5.7 19.4 %collective-permute-start.2 = (bf16[512,512]{1,0:T(8,128)(2,1)S(1)}, bf16[512,512]{1,0:T(8,128)(2,1)S(1)}, u32[]{:S(2)}, u32[]{:S(2)}) collective-permute-start(bf16[512,512]{1,0:T(8,128)(2,1)S(1)} %first.1.first_ref.refs_0_.refs_2_.refs_3_), channel_id=1, source_target_pairs={{0,2},{1,3},{2,0},{3,1},{4,6},{5,7},{6,4},{7,5},{8,10},{9,11},{10,... | collective-permute-start | bytes 1572872 | tf_op jit(solution)/shard_map/ppermute | solution.py:239
  7.4 16.6 %collective-permute-start.5 = (bf16[272,512]{1,0:T(8,128)(2,1)S(1)}, bf16[272,512]{1,0:T(8,128)(2,1)S(1)}, u32[]{:S(2)}, u32[]{:S(2)}) collective-permute-start(bf16[272,512]{1,0:T(8,128)(2,1)S(1)} %get-tuple-element.32.refs_1_.refs_3_.refs_4_), channel_id=1, source_target_pairs={{0,8},{1,9},{2,10},{3,11},{4,0},{5,1},{6,2},{7,3},{8,12},{9,13},{1... | collective-permute-start | bytes 835592 | tf_op jit(solution)/shard_map/ppermute | solution.py:247
  9.1 15.9 %collective-permute-start.3 = (bf16[272,512]{1,0:T(8,128)(2,1)S(1)}, bf16[272,512]{1,0:T(8,128)(2,1)S(1)}, u32[]{:S(2)}, u32[]{:S(2)}) collective-permute-start(bf16[272,512]{1,0:T(8,128)(2,1)S(1)} %get-tuple-element.32.refs_1_.refs_3_.refs_4_), channel_id=1, source_target_pairs={{0,2},{1,3},{2,0},{3,1},{4,6},{5,7},{6,4},{7,5},{8,10},{9,11},{10,... | collective-permute-start | bytes 835592 | tf_op jit(solution)/shard_map/ppermute | solution.py:239
  9.6 27.8 %collective-permute-start.8 = (bf16[528,512]{1,0:T(8,128)(2,1)S(1)}, bf16[528,512]{1,0:T(8,128)(2,1)S(1)}, u32[]{:S(2)}, u32[]{:S(2)}) collective-permute-start(bf16[528,512]{1,0:T(8,128)(2,1)S(1)} %get-tuple-element.37), channel_id=1, source_target_pairs={{0,4},{1,5},{2,6},{3,7},{4,8},{5,9},{6,10},{7,11},{8,12},{9,13},{1... | collective-permute-start | bytes 1622024 | tf_op jit(solution)/shard_map/ppermute | solution.py:247
  25.0 1.6 %collective-permute-start.7 = (bf16[272,512]{1,0:T(8,128)(2,1)S(1)}, bf16[272,512]{1,0:T(8,128)(2,1)S(1)}, u32[]{:S(2)}, u32[]{:S(2)}) collective-permute-start(bf16[272,512]{1,0:T(8,128)(2,1)S(1)} %collective-permute-done.3.refs_3_.refs_8_.refs_7_), channel_id=1, source_target_pairs={{0,1},{1,0},{2,3},{3,2},{4,5},{5,4},{6,7},{7,6},{8,9},{9,8},{10,11... | collective-permute-start | bytes 835592 | tf_op jit(solution)/shard_map/ppermute | solution.py:239
  25.0 2.9 %collective-permute-start.6 = (bf16[512,512]{1,0:T(8,128)(2,1)S(1)}, bf16[512,512]{1,0:T(8,128)(2,1)S(1)}, u32[]{:S(2)}, u32[]{:S(2)}) collective-permute-start(bf16[512,512]{1,0:T(8,128)(2,1)S(1)} %collective-permute-done.2.refs_2_.refs_7_.refs_6_), channel_id=1, source_target_pairs={{0,1},{1,0},{2,3},{3,2},{4,5},{5,4},{6,7},{7,6},{8,9},{9,8},{10,11... | collective-permute-start | bytes 1572872 | tf_op jit(solution)/shard_map/ppermute | solution.py:239
  25.5 3.9 %collective-permute-start = (bf16[512,512]{1,0:T(8,128)(2,1)S(1)}, bf16[512,512]{1,0:T(8,128)(2,1)S(1)}, u32[]{:S(2)}, u32[]{:S(2)}) collective-permute-start(bf16[512,512]{1,0:T(8,128)(2,1)S(1)} %first.1.first_ref.refs_0_.refs_2_.refs_3_), channel_id=1, source_target_pairs={{0,1},{1,0},{2,3},{3,2},{4,5},{5,4},{6,7},{7,6},{8,9},{9,8},{10,11... | collective-permute-start | bytes 1572872 | tf_op jit(solution)/shard_map/ppermute | solution.py:239
  25.6 3.8 %collective-permute-start.1 = (bf16[272,512]{1,0:T(8,128)(2,1)S(1)}, bf16[272,512]{1,0:T(8,128)(2,1)S(1)}, u32[]{:S(2)}, u32[]{:S(2)}) collective-permute-start(bf16[272,512]{1,0:T(8,128)(2,1)S(1)} %get-tuple-element.32.refs_1_.refs_3_.refs_4_), channel_id=1, source_target_pairs={{0,1},{1,0},{2,3},{3,2},{4,5},{5,4},{6,7},{7,6},{8,9},{9,8},{10,11... | collective-permute-start | bytes 835592 | tf_op jit(solution)/shard_map/ppermute | solution.py:239
  26.6 15.3 %collective-permute-start.9 = (bf16[256,512]{1,0:T(8,128)(2,1)S(1)}, bf16[256,512]{1,0:T(8,128)(2,1)S(1)}, u32[]{:S(2)}, u32[]{:S(2)}) collective-permute-start(bf16[256,512]{1,0:T(8,128)(2,1)S(1)} %get-tuple-element.38), channel_id=1, source_target_pairs={{0,4},{1,5},{2,6},{3,7},{4,8},{5,9},{6,10},{7,11},{8,12},{9,13},{1... | collective-permute-start | bytes 786440 | tf_op jit(solution)/shard_map/ppermute | solution.py:247
  33.8 6.4 %collective-permute-start.10 = (f32[8,128]{1,0:T(8,128)S(1)}, f32[8,128]{1,0:T(8,128)S(1)}, u32[]{:S(2)}, u32[]{:S(2)}) collective-permute-start(f32[8,128]{1,0:T(8,128)S(1)} %get-tuple-element.48), channel_id=1, source_target_pairs={{8,0},{9,1},{10,2},{11,3},{0,4},{1,5},{2,6},{3,7},{12,8},{13,9},{1... | collective-permute-start | bytes 12296 | tf_op jit(solution)/shard_map/ppermute | solution.py:285
  43.1 4.4 %collective-permute-start.11 = (f32[8,128]{1,0:T(8,128)S(1)}, f32[8,128]{1,0:T(8,128)S(1)}, u32[]{:S(2)}, u32[]{:S(2)}) collective-permute-start(f32[8,128]{1,0:T(8,128)S(1)} %get-tuple-element.55), channel_id=1, source_target_pairs={{0,3},{1,2},{2,1},{3,0},{4,7},{5,6},{6,5},{7,4},{8,11},{9,10},{10,... | collective-permute-start | bytes 12296 | tf_op jit(solution)/shard_map/ppermute | solution.py:239
  43.2 4.3 %collective-permute-start.12 = (f32[8,128]{1,0:T(8,128)S(1)}, f32[8,128]{1,0:T(8,128)S(1)}, u32[]{:S(2)}, u32[]{:S(2)}) collective-permute-start(f32[8,128]{1,0:T(8,128)S(1)} %get-tuple-element.56), channel_id=1, source_target_pairs={{0,2},{1,3},{2,0},{3,1},{4,6},{5,7},{6,4},{7,5},{8,10},{9,11},{10,... | collective-permute-start | bytes 12296 | tf_op jit(solution)/shard_map/ppermute | solution.py:239
  44.8 2.8 %collective-permute-start.13 = (f32[8,128]{1,0:T(8,128)S(1)}, f32[8,128]{1,0:T(8,128)S(1)}, u32[]{:S(2)}, u32[]{:S(2)}) collective-permute-start(f32[8,128]{1,0:T(8,128)S(1)} %get-tuple-element.57), channel_id=1, source_target_pairs={{0,1},{1,0},{2,3},{3,2},{4,5},{5,4},{6,7},{7,6},{8,9},{9,8},{10,11... | collective-permute-start | bytes 12296 | tf_op jit(solution)/shard_map/ppermute | solution.py:239
  45.0 3.8 %collective-permute-start.14 = (f32[8,128]{1,0:T(8,128)S(1)}, f32[8,128]{1,0:T(8,128)S(1)}, u32[]{:S(2)}, u32[]{:S(2)}) collective-permute-start(f32[8,128]{1,0:T(8,128)S(1)} %get-tuple-element.58), channel_id=1, source_target_pairs={{4,0},{5,1},{6,2},{7,3},{8,4},{9,5},{10,6},{11,7},{12,8},{13,9},{1... | collective-permute-start | bytes 12296 | tf_op jit(solution)/shard_map/ppermute | solution.py:285

commit v10 on v9

--- a/solution.py
+++ b/solution.py
@@ -191,7 +191,7 @@
 
 def plane_steps(planes):
     if planes == 4:
-        return [(2, 0, 3, 1), (1, 2, 3, 0)]
+        return [(2, 0, 3, 1), (3, 0, 1, 2)]
     return [
         [(z + distance) % planes for z in range(planes)]
         for distance in range(1, planes // 2 + 1)

time: 49.6 us -> 51.2 us (1.032)
  waiting for transfers between devices: 21.4 us -> 25.6 us
  starting transfers between devices: 16.6 us -> 14 us
    ppermute x2, waiting for transfers between devices: 2.13 us -> 7.22 us  [local(): backs.append(lax.ppermute(away_best, 'dp', [(t, s) for s, t in pairs]))]
    ppermute x2, starting transfers between devices: 4.15 us -> 1.24 us  [local(): backs.append(lax.ppermute(away_best, 'dp', [(t, s) for s, t in pairs]))]
    ppermute x4, waiting for transfers between devices: 17.7 us -> 14.9 us  [local(): away.append((pairs, [lax.ppermute(part, 'dp', pairs) for part in parts]))]
    ppermute x9, waiting for transfers between devices: 1.56 us -> 3.48 us  [mate(): return lax.ppermute(value, 'dp', [(i, i ^ distance) for i in range(peers)])]
  transfers between devices with their start and end apart: 15 -> 15, of which waited for: 7 -> 8; matrix products, arithmetic and copies ran while one was open for 0% -> 0% of each run, Pallas kernels for 16% -> 15%
where the time goes in v10:
time: 51.2 us; the launch traced here: 51.1 us
  waiting for transfers between devices  25.6 us (50%)
  starting transfers between devices  14 us (27%)
  Pallas kernels  9.25 us (18%)
  local copies, waits for them, and re-layouts  1.51 us (3%)
  other arithmetic  0.6 us (1%)
    ppermute x4, waiting for transfers between devices, local(): away.append((pairs, [lax.ppermute(part, 'dp', pairs) for part in parts]))  14.9 us
    pallas_call x7, Pallas kernels, kernel(): pl.pallas_call(body, out_shape=tuple(outputs), in_specs=whole(len(inputs)...  9.25 us
    ppermute x4, starting transfers between devices, local(): away.append((pairs, [lax.ppermute(part, 'dp', pairs) for part in parts]))  7.77 us
    ppermute x2, waiting for transfers between devices, local(): backs.append(lax.ppermute(away_best, 'dp', [(t, s) for s, t in pairs]))  7.22 us
    ppermute x9, starting transfers between devices, mate(): return lax.ppermute(value, 'dp', [(i, i ^ distance) for i in range(peers)])  4.97 us
    ppermute x9, waiting for transfers between devices, mate(): return lax.ppermute(value, 'dp', [(i, i ^ distance) for i in range(peers)])  3.48 us
    unnamed x10, local copies, waits for them, and re-layouts  1.42 us
    ppermute x2, starting transfers between devices, local(): backs.append(lax.ppermute(away_best, 'dp', [(t, s) for s, t in pairs]))  1.24 us
  transfers between devices with their start and end apart: 15, of which 8 were waited for; matrix products, arithmetic and copies ran while one was open for 0% of the time, Pallas kernels for 15%

profile of v10, /device:TPU:0, one launch (start us, length us, event | category | flops | bytes accessed | tf_op | source)
XLA Modules:
  0.0 51.1 jit_solution(12050164255781755512)
XLA Ops:
  0.0 1.4 %copy-done = f32[768,512]{1,0:T(8,128)S(1)} copy-done((f32[768,512]{1,0:T(8,128)S(1)}, f32[768,512]{1,0:T(8,128)}, u32[]{:S(2)}) %copy-start) | copy-done | bytes 1572888
  1.6 4.1 %collective-permute-start.4 = (bf16[512,512]{1,0:T(8,128)(2,1)S(1)}, bf16[512,512]{1,0:T(8,128)(2,1)S(1)}, u32[]{:S(2)}, u32[]{:S(2)}) collective-permute-start(bf16[512,512]{1,0:T(8,128)(2,1)S(1)} %first.1.first_ref.refs_0_.refs_2_.refs_3_), channel_id=1, source_target_pairs={{0,8},{1,9},{2,10},{3,11},{4,0},{5,1},{6,2},{7,3},{8,12},{9,13},{1... | collective-permute-start | bytes 1572872 | tf_op jit(solution)/shard_map/ppermute | solution.py:247
  5.7 1.5 %collective-permute-start.2 = (bf16[512,512]{1,0:T(8,128)(2,1)S(1)}, bf16[512,512]{1,0:T(8,128)(2,1)S(1)}, u32[]{:S(2)}, u32[]{:S(2)}) collective-permute-start(bf16[512,512]{1,0:T(8,128)(2,1)S(1)} %first.1.first_ref.refs_0_.refs_2_.refs_3_), channel_id=1, source_target_pairs={{0,2},{1,3},{2,0},{3,1},{4,6},{5,7},{6,4},{7,5},{8,10},{9,11},{10,... | collective-permute-start | bytes 1572872 | tf_op jit(solution)/shard_map/ppermute | solution.py:239
  7.4 1.6 %collective-permute-start.5 = (bf16[272,512]{1,0:T(8,128)(2,1)S(1)}, bf16[272,512]{1,0:T(8,128)(2,1)S(1)}, u32[]{:S(2)}, u32[]{:S(2)}) collective-permute-start(bf16[272,512]{1,0:T(8,128)(2,1)S(1)} %get-tuple-element.32.refs_1_.refs_3_.refs_4_), channel_id=1, source_target_pairs={{0,8},{1,9},{2,10},{3,11},{4,0},{5,1},{6,2},{7,3},{8,12},{9,13},{1... | collective-permute-start | bytes 835592 | tf_op jit(solution)/shard_map/ppermute | solution.py:247
  9.1 0.5 collective-permute-start.3
  10.0 14.0 %collective-permute-done.5.refs_0_.refs_2_ = bf16[272,512]{1,0:T(8,128)(2,1)S(1)} collective-permute-done((bf16[272,512]{1,0:T(8,128)(2,1)S(1)}, bf16[272,512]{1,0:T(8,128)(2,1)S(1)}, u32[]{:S(2)}, u32[]{:S(2)}) %collective-permute-start.5) | collective-permute-done | bytes 278560 | tf_op jit(solution)/shard_map/ppermute | solution.py:247
  24.0 1.1 %collective-permute-done.3.refs_3_.refs_8_.refs_7_ = bf16[272,512]{1,0:T(8,128)(2,1)S(1)} collective-permute-done((bf16[272,512]{1,0:T(8,128)(2,1)S(1)}, bf16[272,512]{1,0:T(8,128)(2,1)S(1)}, u32[]{:S(2)}, u32[]{:S(2)}) %collective-permute-start.3) | collective-permute-done | bytes 278560 | tf_op jit(solution)/shard_map/ppermute | solution.py:239
  25.0 0.5 collective-permute-start.6
  26.1 0.5 %collective-permute-done.7.refs_5_.refs_10_.refs_9_ = bf16[272,512]{1,0:T(8,128)(2,1)S(1)} collective-permute-done((bf16[272,512]{1,0:T(8,128)(2,1)S(1)}, bf16[272,512]{1,0:T(8,128)(2,1)S(1)}, u32[]{:S(2)}, u32[]{:S(2)}) %collective-permute-start.7) | collective-permute-done | bytes 278560 | tf_op jit(solution)/shard_map/ppermute | solution.py:239
  26.6 1.7 %collective-permute-start.9 = (bf16[256,512]{1,0:T(8,128)(2,1)S(1)}, bf16[256,512]{1,0:T(8,128)(2,1)S(1)}, u32[]{:S(2)}, u32[]{:S(2)}) collective-permute-start(bf16[256,512]{1,0:T(8,128)(2,1)S(1)} %get-tuple-element.38), channel_id=1, source_target_pairs={{0,12},{1,13},{2,14},{3,15},{4,0},{5,1},{6,2},{7,3},{8,4},{9,5},{1... | collective-permute-start | bytes 786440 | tf_op jit(solution)/shard_map/ppermute | solution.py:247
  28.2 1.5 %plane_far.1 = (f32[8,128]{1,0:T(8,128)S(1)}, f32[768,128]{1,0:T(8,128)S(1)}, f32[768,128]{1,0:T(8,128)S(1)}) custom-call(bf16[512,512]{1,0:T(8,128)(2,1)S(1)} %first.1.first_ref.refs_0_.refs_2_.refs_3_, bf16[272,512]{1,0:T(8,128)(2,1)S(1)} %get-tuple-element.32.refs_1_.refs_3_.refs_4_, bf16[512,512]{1,0:T(8,128)(2,1)S(1)} %collective-permute-done.2.refs_2_.refs_7_.refs_6_, ...), custom_call_target="tpu_custom_call" | custom-call | flops 1 | bytes 1 | tf_op jit(solution)/shard_map/plane_far/pallas_call | solution.py:215
  29.8 1.5 %plane_near.1 = (f32[8,128]{1,0:T(8,128)S(1)}, f32[768,128]{1,0:T(8,128)S(1)}, f32[768,128]{1,0:T(8,128)S(1)}) custom-call(bf16[512,512]{1,0:T(8,128)(2,1)S(1)} %first.1.first_ref.refs_0_.refs_2_.refs_3_, bf16[272,512]{1,0:T(8,128)(2,1)S(1)} %get-tuple-element.32.refs_1_.refs_3_.refs_4_, bf16[512,512]{1,0:T(8,128)(2,1)S(1)} %first.1.first_ref.refs_0_.refs_2_.refs_3_, ...), custom_call_target="tpu_custom_call" | custom-call | flops 1 | bytes 1 | tf_op jit(solution)/shard_map/plane_near/pallas_call | solution.py:215
  31.2 2.8 %cross.3 = (f32[8,128]{1,0:T(8,128)S(1)}, f32[8,128]{1,0:T(8,128)S(1)}, f32[8,128]{1,0:T(8,128)S(1)}, f32[8,128]{1,0:T(8,128)S(1)}, f32[8,128]{1,0:T(8,128)S(1)}) custom-call(bf16[272,512]{1,0:T(8,128)(2,1)S(1)} %collective-permute-done.5.refs_0_.refs_2_, bf16[512,512]{1,0:T(8,128)(2,1)S(1)} %collective-permute-done.4.refs_1_, ...), custom_call_target="tpu_custom_call" | custom-call | flops 1 | bytes 1 | tf_op jit(solution)/shard_map/cross/pallas_call | solution.py:215
  34.1 0.5 %collective-permute-start.10 = (f32[8,128]{1,0:T(8,128)S(1)}, f32[8,128]{1,0:T(8,128)S(1)}, u32[]{:S(2)}, u32[]{:S(2)}) collective-permute-start(f32[8,128]{1,0:T(8,128)S(1)} %get-tuple-element.48), channel_id=1, source_target_pairs={{8,0},{9,1},{10,2},{11,3},{0,4},{1,5},{2,6},{3,7},{12,8},{13,9},{1... | collective-permute-start | bytes 12296 | tf_op jit(solution)/shard_map/ppermute | solution.py:285
  34.6 0.9 %collective-permute-done.8.refs_0_.refs_1_ = bf16[528,512]{1,0:T(8,128)(2,1)S(1)} collective-permute-done((bf16[528,512]{1,0:T(8,128)(2,1)S(1)}, bf16[528,512]{1,0:T(8,128)(2,1)S(1)}, u32[]{:S(2)}, u32[]{:S(2)}) %collective-permute-start.8) | collective-permute-done | bytes 540704 | tf_op jit(solution)/shard_map/ppermute | solution.py:247
  35.6 2.0 %cross.4 = (f32[8,128]{1,0:T(8,128)S(1)}, f32[8,128]{1,0:T(8,128)S(1)}, f32[8,128]{1,0:T(8,128)S(1)}, f32[8,128]{1,0:T(8,128)S(1)}, f32[8,128]{1,0:T(8,128)S(1)}) custom-call(bf16[528,512]{1,0:T(8,128)(2,1)S(1)} %collective-permute-done.8.refs_0_.refs_1_, bf16[528,512]{1,0:T(8,128)(2,1)S(1)} %collective-permute-done.8.refs_0_.refs_1_, ...), custom_call_target="tpu_custom_call" | custom-call | flops 1 | bytes 1 | tf_op jit(solution)/shard_map/cross/pallas_call | solution.py:215
  37.5 4.4 %collective-permute-done.10 = f32[8,128]{1,0:T(8,128)S(1)} collective-permute-done((f32[8,128]{1,0:T(8,128)S(1)}, f32[8,128]{1,0:T(8,128)S(1)}, u32[]{:S(2)}, u32[]{:S(2)}) %collective-permute-start.10) | collective-permute-done | bytes 4128 | tf_op jit(solution)/shard_map/ppermute | solution.py:285
  41.9 1.2 %cross.5 = (f32[8,128]{1,0:T(8,128)S(1)}, f32[8,128]{1,0:T(8,128)S(1)}, f32[8,128]{1,0:T(8,128)S(1)}, f32[8,128]{1,0:T(8,128)S(1)}, f32[8,128]{1,0:T(8,128)S(1)}) custom-call(bf16[528,512]{1,0:T(8,128)(2,1)S(1)} %collective-permute-done.8.refs_0_.refs_1_, bf16[256,512]{1,0:T(8,128)(2,1)S(1)} %collective-permute-done.9.refs_1_, ...), custom_call_target="tpu_custom_call" | custom-call | flops 1 | bytes 1 | tf_op jit(solution)/shard_map/cross/pallas_call | solution.py:215
  43.1 0.9 %collective-permute-start.11 = (f32[8,128]{1,0:T(8,128)S(1)}, f32[8,128]{1,0:T(8,128)S(1)}, u32[]{:S(2)}, u32[]{:S(2)}) collective-permute-start(f32[8,128]{1,0:T(8,128)S(1)} %get-tuple-element.55), channel_id=1, source_target_pairs={{0,3},{1,2},{2,1},{3,0},{4,7},{5,6},{6,5},{7,4},{8,11},{9,10},{10,... | collective-permute-start | bytes 12296 | tf_op jit(solution)/shard_map/ppermute | solution.py:239
  44.0 0.8 %collective-permute-start.12 = (f32[8,128]{1,0:T(8,128)S(1)}, f32[8,128]{1,0:T(8,128)S(1)}, u32[]{:S(2)}, u32[]{:S(2)}) collective-permute-start(f32[8,128]{1,0:T(8,128)S(1)} %get-tuple-element.56), channel_id=1, source_target_pairs={{0,2},{1,3},{2,0},{3,1},{4,6},{5,7},{6,4},{7,5},{8,10},{9,11},{10,... | collective-permute-start | bytes 12296 | tf_op jit(solution)/shard_map/ppermute | solution.py:239
  45.0 0.7 %collective-permute-start.14 = (f32[8,128]{1,0:T(8,128)S(1)}, f32[8,128]{1,0:T(8,128)S(1)}, u32[]{:S(2)}, u32[]{:S(2)}) collective-permute-start(f32[8,128]{1,0:T(8,128)S(1)} %get-tuple-element.58), channel_id=1, source_target_pairs={{12,0},{13,1},{14,2},{15,3},{0,4},{1,5},{2,6},{3,7},{4,8},{5,9},{6... | collective-permute-start | bytes 12296 | tf_op jit(solution)/shard_map/ppermute | solution.py:285
  46.2 1.4 %collective-permute-done.12 = f32[8,128]{1,0:T(8,128)S(1)} collective-permute-done((f32[8,128]{1,0:T(8,128)S(1)}, f32[8,128]{1,0:T(8,128)S(1)}, u32[]{:S(2)}, u32[]{:S(2)}) %collective-permute-start.12) | collective-permute-done | bytes 4128 | tf_op jit(solution)/shard_map/ppermute | solution.py:239
  47.6 2.8 %collective-permute-done.14 = f32[8,128]{1,0:T(8,128)S(1)} collective-permute-done((f32[8,128]{1,0:T(8,128)S(1)}, f32[8,128]{1,0:T(8,128)S(1)}, u32[]{:S(2)}, u32[]{:S(2)}) %collective-permute-start.14) | collective-permute-done | bytes 4128 | tf_op jit(solution)/shard_map/ppermute | solution.py:285
  50.5 0.6 %maximum_bitcast_fusion = f32[768]{0:T(1024)} fusion(f32[8,128]{1,0:T(8,128)S(1)} %collective-permute-done.14, f32[8,128]{1,0:T(8,128)S(1)} %collective-permute-done.13, f32[8,128]{1,0:T(8,128)S(1)} %collective-permute-done.12, f32[8,128]{1,0:T(8,128)S(1)} %collective-permute-done.11, f32[8,128]{1,0:T(8,128)S(1)} %collective-permute-done.10, f32[8,128]{1,0:T(8,128)S(1)} %max.24), kind=kLoop, calls=%fused_computation | loop fusion | flops 3840 | bytes 21504 | tf_op jit(solution)/shard_map/max | solution.py:290
  (28 shorter events, 2.1 us)
Async XLA Ops:
  0.0 1.4 %copy-start = (f32[768,512]{1,0:T(8,128)S(1)}, f32[768,512]{1,0:T(8,128)}, u32[]{:S(2)}) copy-start(f32[768,512]{1,0:T(8,128)} %embeddings_ref.3) | copy-start | bytes 4718596
  1.4 5.8 %copy-start.2 = (s32[768]{0:T(1024)S(1)}, s32[768]{0:T(1024)}, u32[]{:S(2)}) copy-start(s32[768]{0:T(1024)} %param.5) | copy-start | bytes 9220
  1.4 5.8 %copy-start.3 = (s32[768]{0:T(1024)S(1)}, s32[768]{0:T(1024)}, u32[]{:S(2)}) copy-start(s32[768]{0:T(1024)} %param.6) | copy-start | bytes 9220
  1.4 5.8 %copy-start.4 = (s32[16]{0:T(128)S(1)}, s32[16]{0:T(128)}, u32[]{:S(2)}) copy-start(s32[16]{0:T(128)} %param.7) | copy-start | bytes 196
  1.4 5.9 %copy-start.1 = (f32[768,512]{1,0:T(8,128)S(1)}, f32[768,512]{1,0:T(8,128)}, u32[]{:S(2)}) copy-start(f32[768,512]{1,0:T(8,128)} %embeddings_ref.3) | copy-start | bytes 4718596
  1.6 23.4 %collective-permute-start.4 = (bf16[512,512]{1,0:T(8,128)(2,1)S(1)}, bf16[512,512]{1,0:T(8,128)(2,1)S(1)}, u32[]{:S(2)}, u32[]{:S(2)}) collective-permute-start(bf16[512,512]{1,0:T(8,128)(2,1)S(1)} %first.1.first_ref.refs_0_.refs_2_.refs_3_), channel_id=1, source_target_pairs={{0,8},{1,9},{2,10},{3,11},{4,0},{5,1},{6,2},{7,3},{8,12},{9,13},{1... | collective-permute-start | bytes 1572872 | tf_op jit(solution)/shard_map/ppermute | solution.py:247
  5.7 19.4 %collective-permute-start.2 = (bf16[512,512]{1,0:T(8,128)(2,1)S(1)}, bf16[512,512]{1,0:T(8,128)(2,1)S(1)}, u32[]{:S(2)}, u32[]{:S(2)}) collective-permute-start(bf16[512,512]{1,0:T(8,128)(2,1)S(1)} %first.1.first_ref.refs_0_.refs_2_.refs_3_), channel_id=1, source_target_pairs={{0,2},{1,3},{2,0},{3,1},{4,6},{5,7},{6,4},{7,5},{8,10},{9,11},{10,... | collective-permute-start | bytes 1572872 | tf_op jit(solution)/shard_map/ppermute | solution.py:239
  7.4 16.5 %collective-permute-start.5 = (bf16[272,512]{1,0:T(8,128)(2,1)S(1)}, bf16[272,512]{1,0:T(8,128)(2,1)S(1)}, u32[]{:S(2)}, u32[]{:S(2)}) collective-permute-start(bf16[272,512]{1,0:T(8,128)(2,1)S(1)} %get-tuple-element.32.refs_1_.refs_3_.refs_4_), channel_id=1, source_target_pairs={{0,8},{1,9},{2,10},{3,11},{4,0},{5,1},{6,2},{7,3},{8,12},{9,13},{1... | collective-permute-start | bytes 835592 | tf_op jit(solution)/shard_map/ppermute | solution.py:247
  9.1 15.9 %collective-permute-start.3 = (bf16[272,512]{1,0:T(8,128)(2,1)S(1)}, bf16[272,512]{1,0:T(8,128)(2,1)S(1)}, u32[]{:S(2)}, u32[]{:S(2)}) collective-permute-start(bf16[272,512]{1,0:T(8,128)(2,1)S(1)} %get-tuple-element.32.refs_1_.refs_3_.refs_4_), channel_id=1, source_target_pairs={{0,2},{1,3},{2,0},{3,1},{4,6},{5,7},{6,4},{7,5},{8,10},{9,11},{10,... | collective-permute-start | bytes 835592 | tf_op jit(solution)/shard_map/ppermute | solution.py:239
  9.6 26.0 %collective-permute-start.8 = (bf16[528,512]{1,0:T(8,128)(2,1)S(1)}, bf16[528,512]{1,0:T(8,128)(2,1)S(1)}, u32[]{:S(2)}, u32[]{:S(2)}) collective-permute-start(bf16[528,512]{1,0:T(8,128)(2,1)S(1)} %get-tuple-element.37), channel_id=1, source_target_pairs={{0,12},{1,13},{2,14},{3,15},{4,0},{5,1},{6,2},{7,3},{8,4},{9,5},{1... | collective-permute-start | bytes 1622024 | tf_op jit(solution)/shard_map/ppermute | solution.py:247
  25.0 1.6 %collective-permute-start.7 = (bf16[272,512]{1,0:T(8,128)(2,1)S(1)}, bf16[272,512]{1,0:T(8,128)(2,1)S(1)}, u32[]{:S(2)}, u32[]{:S(2)}) collective-permute-start(bf16[272,512]{1,0:T(8,128)(2,1)S(1)} %collective-permute-done.3.refs_3_.refs_8_.refs_7_), channel_id=1, source_target_pairs={{0,1},{1,0},{2,3},{3,2},{4,5},{5,4},{6,7},{7,6},{8,9},{9,8},{10,11... | collective-permute-start | bytes 835592 | tf_op jit(solution)/shard_map/ppermute | solution.py:239
  25.0 3.2 %collective-permute-start.6 = (bf16[512,512]{1,0:T(8,128)(2,1)S(1)}, bf16[512,512]{1,0:T(8,128)(2,1)S(1)}, u32[]{:S(2)}, u32[]{:S(2)}) collective-permute-start(bf16[512,512]{1,0:T(8,128)(2,1)S(1)} %collective-permute-done.2.refs_2_.refs_7_.refs_6_), channel_id=1, source_target_pairs={{0,1},{1,0},{2,3},{3,2},{4,5},{5,4},{6,7},{7,6},{8,9},{9,8},{10,11... | collective-permute-start | bytes 1572872 | tf_op jit(solution)/shard_map/ppermute | solution.py:239
  25.5 4.2 %collective-permute-start = (bf16[512,512]{1,0:T(8,128)(2,1)S(1)}, bf16[512,512]{1,0:T(8,128)(2,1)S(1)}, u32[]{:S(2)}, u32[]{:S(2)}) collective-permute-start(bf16[512,512]{1,0:T(8,128)(2,1)S(1)} %first.1.first_ref.refs_0_.refs_2_.refs_3_), channel_id=1, source_target_pairs={{0,1},{1,0},{2,3},{3,2},{4,5},{5,4},{6,7},{7,6},{8,9},{9,8},{10,11... | collective-permute-start | bytes 1572872 | tf_op jit(solution)/shard_map/ppermute | solution.py:239
  25.6 4.1 %collective-permute-start.1 = (bf16[272,512]{1,0:T(8,128)(2,1)S(1)}, bf16[272,512]{1,0:T(8,128)(2,1)S(1)}, u32[]{:S(2)}, u32[]{:S(2)}) collective-permute-start(bf16[272,512]{1,0:T(8,128)(2,1)S(1)} %get-tuple-element.32.refs_1_.refs_3_.refs_4_), channel_id=1, source_target_pairs={{0,1},{1,0},{2,3},{3,2},{4,5},{5,4},{6,7},{7,6},{8,9},{9,8},{10,11... | collective-permute-start | bytes 835592 | tf_op jit(solution)/shard_map/ppermute | solution.py:239
  26.6 15.3 %collective-permute-start.9 = (bf16[256,512]{1,0:T(8,128)(2,1)S(1)}, bf16[256,512]{1,0:T(8,128)(2,1)S(1)}, u32[]{:S(2)}, u32[]{:S(2)}) collective-permute-start(bf16[256,512]{1,0:T(8,128)(2,1)S(1)} %get-tuple-element.38), channel_id=1, source_target_pairs={{0,12},{1,13},{2,14},{3,15},{4,0},{5,1},{6,2},{7,3},{8,4},{9,5},{1... | collective-permute-start | bytes 786440 | tf_op jit(solution)/shard_map/ppermute | solution.py:247
  34.1 7.8 %collective-permute-start.10 = (f32[8,128]{1,0:T(8,128)S(1)}, f32[8,128]{1,0:T(8,128)S(1)}, u32[]{:S(2)}, u32[]{:S(2)}) collective-permute-start(f32[8,128]{1,0:T(8,128)S(1)} %get-tuple-element.48), channel_id=1, source_target_pairs={{8,0},{9,1},{10,2},{11,3},{0,4},{1,5},{2,6},{3,7},{12,8},{13,9},{1... | collective-permute-start | bytes 12296 | tf_op jit(solution)/shard_map/ppermute | solution.py:285
  43.1 3.1 %collective-permute-start.11 = (f32[8,128]{1,0:T(8,128)S(1)}, f32[8,128]{1,0:T(8,128)S(1)}, u32[]{:S(2)}, u32[]{:S(2)}) collective-permute-start(f32[8,128]{1,0:T(8,128)S(1)} %get-tuple-element.55), channel_id=1, source_target_pairs={{0,3},{1,2},{2,1},{3,0},{4,7},{5,6},{6,5},{7,4},{8,11},{9,10},{10,... | collective-permute-start | bytes 12296 | tf_op jit(solution)/shard_map/ppermute | solution.py:239
  44.0 3.6 %collective-permute-start.12 = (f32[8,128]{1,0:T(8,128)S(1)}, f32[8,128]{1,0:T(8,128)S(1)}, u32[]{:S(2)}, u32[]{:S(2)}) collective-permute-start(f32[8,128]{1,0:T(8,128)S(1)} %get-tuple-element.56), channel_id=1, source_target_pairs={{0,2},{1,3},{2,0},{3,1},{4,6},{5,7},{6,4},{7,5},{8,10},{9,11},{10,... | collective-permute-start | bytes 12296 | tf_op jit(solution)/shard_map/ppermute | solution.py:239
  44.8 2.9 %collective-permute-start.13 = (f32[8,128]{1,0:T(8,128)S(1)}, f32[8,128]{1,0:T(8,128)S(1)}, u32[]{:S(2)}, u32[]{:S(2)}) collective-permute-start(f32[8,128]{1,0:T(8,128)S(1)} %get-tuple-element.57), channel_id=1, source_target_pairs={{0,1},{1,0},{2,3},{3,2},{4,5},{5,4},{6,7},{7,6},{8,9},{9,8},{10,11... | collective-permute-start | bytes 12296 | tf_op jit(solution)/shard_map/ppermute | solution.py:239
  45.0 5.4 %collective-permute-start.14 = (f32[8,128]{1,0:T(8,128)S(1)}, f32[8,128]{1,0:T(8,128)S(1)}, u32[]{:S(2)}, u32[]{:S(2)}) collective-permute-start(f32[8,128]{1,0:T(8,128)S(1)} %get-tuple-element.58), channel_id=1, source_target_pairs={{12,0},{13,1},{14,2},{15,3},{0,4},{1,5},{2,6},{3,7},{4,8},{5,9},{6... | collective-permute-start | bytes 12296 | tf_op jit(solution)/shard_map/ppermute | solution.py:285

commit v11 on v10

--- a/solution.py
+++ b/solution.py
@@ -191,7 +191,7 @@
 
 def plane_steps(planes):
     if planes == 4:
-        return [(2, 0, 3, 1), (3, 0, 1, 2)]
+        return [(3, 0, 1, 2), (2, 0, 3, 1)]
     return [
         [(z + distance) % planes for z in range(planes)]
         for distance in range(1, planes // 2 + 1)
@@ -199,6 +199,8 @@
 
 
 def after(value, *others):
+    if not others:
+        return value
     return lax.optimization_barrier((value,) + others)[0]
 
 
@@ -274,18 +276,17 @@
             calls = (((0, FIRST), (0, PAD), received),)
         tags = received[0] if n else received[-1]
         for starts, bases, parts in calls:
-            if n and starts[0]:
-                away_best = after(away_best, backs[-1])
             away_best, *plane_best = kernel(
                 functools.partial(cross_kernel, starts, bases),
                 (tags, *parts, *plane, away_best, *plane_best),
                 (lanes,) * (PLANE + 1),
                 "cross",
             )
-        backs.append(lax.ppermute(away_best, "dp", [(t, s) for s, t in pairs]))
+        answer = after(away_best, *backs[:1])
+        backs.append(lax.ppermute(answer, "dp", [(t, s) for s, t in pairs]))
     best = jnp.maximum(best, plane_best[0]).reshape(-1)[:rows]
-    for distance, values in ((3, plane_best[3]), (2, plane_best[2]), (1, plane_best[1])):
-        backs.insert(-1, mate(values, distance))
+    for distance in (3, 2, 1):
+        backs.insert(-1, mate(after(plane_best[distance], *backs[:1]), distance))
     for back in backs:
         best = jnp.maximum(best, back.reshape(-1)[:rows])
     return best

time: 51.2 us -> 50 us (0.977)
  waiting for transfers between devices: 25.6 us -> 24.5 us
    ppermute x4, waiting for transfers between devices: 14.9 us -> 19 us  [local(): away.append((pairs, [lax.ppermute(part, 'dp', pairs) for part in parts]))]
    ppermute x2, waiting for transfers between devices: 7.22 us -> 3.15 us  [local(): backs.append(lax.ppermute(answer, 'dp', [(t, s) for s, t in pairs]))]
    ppermute x4, starting transfers between devices: 7.77 us -> 6.02 us  [local(): away.append((pairs, [lax.ppermute(part, 'dp', pairs) for part in parts]))]
    ppermute x2, starting transfers between devices: 1.24 us -> 2.69 us  [local(): backs.append(lax.ppermute(answer, 'dp', [(t, s) for s, t in pairs]))]
    ppermute x9, waiting for transfers between devices: 3.48 us -> 2.36 us  [mate(): return lax.ppermute(value, 'dp', [(i, i ^ distance) for i in range(peers)])]
  transfers between devices with their start and end apart: 15 -> 15, of which waited for: 8 -> 8; matrix products, arithmetic and copies ran while one was open for 0% -> 0% of each run, Pallas kernels for 15% -> 18%
where the time goes in v11:
time: 50 us; the launch traced here: 49.9 us
  waiting for transfers between devices  24.5 us (49%)
  starting transfers between devices  13.9 us (28%)
  Pallas kernels  9.28 us (19%)
  local copies, waits for them, and re-layouts  1.51 us (3%)
  other arithmetic  0.6 us (1%)
    ppermute x4, waiting for transfers between devices, local(): away.append((pairs, [lax.ppermute(part, 'dp', pairs) for part in parts]))  19 us
    pallas_call x7, Pallas kernels, kernel(): pl.pallas_call(body, out_shape=tuple(outputs), in_specs=whole(len(inputs)...  9.28 us
    ppermute x4, starting transfers between devices, local(): away.append((pairs, [lax.ppermute(part, 'dp', pairs) for part in parts]))  6.02 us
    ppermute x9, starting transfers between devices, mate(): return lax.ppermute(value, 'dp', [(i, i ^ distance) for i in range(peers)])  5.14 us
    ppermute x2, waiting for transfers between devices, local(): backs.append(lax.ppermute(answer, 'dp', [(t, s) for s, t in pairs]))  3.15 us
    ppermute x2, starting transfers between devices, local(): backs.append(lax.ppermute(answer, 'dp', [(t, s) for s, t in pairs]))  2.69 us
    ppermute x9, waiting for transfers between devices, mate(): return lax.ppermute(value, 'dp', [(i, i ^ distance) for i in range(peers)])  2.36 us
    unnamed x10, local copies, waits for them, and re-layouts  1.42 us
  transfers between devices with their start and end apart: 15, of which 8 were waited for; matrix products, arithmetic and copies ran while one was open for 0% of the time, Pallas kernels for 18%

profile of v11, /device:TPU:0, one launch (start us, length us, event | category | flops | bytes accessed | tf_op | source)
XLA Modules:
  0.0 49.9 jit_solution(16351711463425688224)
XLA Ops:
  0.0 1.4 %copy-done = f32[768,512]{1,0:T(8,128)S(1)} copy-done((f32[768,512]{1,0:T(8,128)S(1)}, f32[768,512]{1,0:T(8,128)}, u32[]{:S(2)}) %copy-start) | copy-done | bytes 1572888
  1.6 5.1 %collective-permute-start.4 = (bf16[512,512]{1,0:T(8,128)(2,1)S(1)}, bf16[512,512]{1,0:T(8,128)(2,1)S(1)}, u32[]{:S(2)}, u32[]{:S(2)}) collective-permute-start(bf16[512,512]{1,0:T(8,128)(2,1)S(1)} %first.1.first_ref.refs_0_.refs_2_.refs_3_), channel_id=1, source_target_pairs={{0,12},{1,13},{2,14},{3,15},{4,0},{5,1},{6,2},{7,3},{8,4},{9,5},{1... | collective-permute-start | bytes 1572872 | tf_op jit(solution)/shard_map/ppermute | solution.py:249
  6.7 1.5 %collective-permute-start.2 = (bf16[512,512]{1,0:T(8,128)(2,1)S(1)}, bf16[512,512]{1,0:T(8,128)(2,1)S(1)}, u32[]{:S(2)}, u32[]{:S(2)}) collective-permute-start(bf16[512,512]{1,0:T(8,128)(2,1)S(1)} %first.1.first_ref.refs_0_.refs_2_.refs_3_), channel_id=1, source_target_pairs={{0,2},{1,3},{2,0},{3,1},{4,6},{5,7},{6,4},{7,5},{8,10},{9,11},{10,... | collective-permute-start | bytes 1572872 | tf_op jit(solution)/shard_map/ppermute | solution.py:241
  8.5 0.5 %collective-permute-start.5 = (bf16[272,512]{1,0:T(8,128)(2,1)S(1)}, bf16[272,512]{1,0:T(8,128)(2,1)S(1)}, u32[]{:S(2)}, u32[]{:S(2)}) collective-permute-start(bf16[272,512]{1,0:T(8,128)(2,1)S(1)} %get-tuple-element.35.refs_1_.refs_3_.refs_4_), channel_id=1, source_target_pairs={{0,12},{1,13},{2,14},{3,15},{4,0},{5,1},{6,2},{7,3},{8,4},{9,5},{1... | collective-permute-start | bytes 835592 | tf_op jit(solution)/shard_map/ppermute | solution.py:249
  9.0 0.7 %collective-permute-start.3 = (bf16[272,512]{1,0:T(8,128)(2,1)S(1)}, bf16[272,512]{1,0:T(8,128)(2,1)S(1)}, u32[]{:S(2)}, u32[]{:S(2)}) collective-permute-start(bf16[272,512]{1,0:T(8,128)(2,1)S(1)} %get-tuple-element.35.refs_1_.refs_3_.refs_4_), channel_id=1, source_target_pairs={{0,2},{1,3},{2,0},{3,1},{4,6},{5,7},{6,4},{7,5},{8,10},{9,11},{10,... | collective-permute-start | bytes 835592 | tf_op jit(solution)/shard_map/ppermute | solution.py:241
  9.6 15.3 %collective-permute-done.5.refs_0_.refs_2_ = bf16[272,512]{1,0:T(8,128)(2,1)S(1)} collective-permute-done((bf16[272,512]{1,0:T(8,128)(2,1)S(1)}, bf16[272,512]{1,0:T(8,128)(2,1)S(1)}, u32[]{:S(2)}, u32[]{:S(2)}) %collective-permute-start.5) | collective-permute-done | bytes 278560 | tf_op jit(solution)/shard_map/ppermute | solution.py:249
  25.0 1.1 %collective-permute-done.3.refs_3_.refs_8_.refs_7_ = bf16[272,512]{1,0:T(8,128)(2,1)S(1)} collective-permute-done((bf16[272,512]{1,0:T(8,128)(2,1)S(1)}, bf16[272,512]{1,0:T(8,128)(2,1)S(1)}, u32[]{:S(2)}, u32[]{:S(2)}) %collective-permute-start.3) | collective-permute-done | bytes 278560 | tf_op jit(solution)/shard_map/ppermute | solution.py:241
  26.1 0.5 %collective-permute-start.6 = (bf16[512,512]{1,0:T(8,128)(2,1)S(1)}, bf16[512,512]{1,0:T(8,128)(2,1)S(1)}, u32[]{:S(2)}, u32[]{:S(2)}) collective-permute-start(bf16[512,512]{1,0:T(8,128)(2,1)S(1)} %collective-permute-done.2.refs_2_.refs_7_.refs_6_), channel_id=1, source_target_pairs={{0,1},{1,0},{2,3},{3,2},{4,5},{5,4},{6,7},{7,6},{8,9},{9,8},{10,11... | collective-permute-start | bytes 1572872 | tf_op jit(solution)/shard_map/ppermute | solution.py:241
  26.6 0.4 collective-permute-start.1
  27.1 0.5 %collective-permute-done.7.refs_5_.refs_10_.refs_9_ = bf16[272,512]{1,0:T(8,128)(2,1)S(1)} collective-permute-done((bf16[272,512]{1,0:T(8,128)(2,1)S(1)}, bf16[272,512]{1,0:T(8,128)(2,1)S(1)}, u32[]{:S(2)}, u32[]{:S(2)}) %collective-permute-start.7) | collective-permute-done | bytes 278560 | tf_op jit(solution)/shard_map/ppermute | solution.py:241
  27.6 0.4 collective-permute-start.9
  28.4 1.5 %plane_far.1 = (f32[8,128]{1,0:T(8,128)S(1)}, f32[768,128]{1,0:T(8,128)S(1)}, f32[768,128]{1,0:T(8,128)S(1)}) custom-call(bf16[512,512]{1,0:T(8,128)(2,1)S(1)} %first.1.first_ref.refs_0_.refs_2_.refs_3_, bf16[272,512]{1,0:T(8,128)(2,1)S(1)} %get-tuple-element.35.refs_1_.refs_3_.refs_4_, bf16[512,512]{1,0:T(8,128)(2,1)S(1)} %collective-permute-done.2.refs_2_.refs_7_.refs_6_, ...), custom_call_target="tpu_custom_call" | custom-call | flops 1 | bytes 1 | tf_op jit(solution)/shard_map/plane_far/pallas_call | solution.py:217
  29.9 1.5 %plane_near.1 = (f32[8,128]{1,0:T(8,128)S(1)}, f32[768,128]{1,0:T(8,128)S(1)}, f32[768,128]{1,0:T(8,128)S(1)}) custom-call(bf16[512,512]{1,0:T(8,128)(2,1)S(1)} %first.1.first_ref.refs_0_.refs_2_.refs_3_, bf16[272,512]{1,0:T(8,128)(2,1)S(1)} %get-tuple-element.35.refs_1_.refs_3_.refs_4_, bf16[512,512]{1,0:T(8,128)(2,1)S(1)} %first.1.first_ref.refs_0_.refs_2_.refs_3_, ...), custom_call_target="tpu_custom_call" | custom-call | flops 1 | bytes 1 | tf_op jit(solution)/shard_map/plane_near/pallas_call | solution.py:217
  31.4 2.8 %cross.3 = (f32[8,128]{1,0:T(8,128)S(1)}, f32[8,128]{1,0:T(8,128)S(1)}, f32[8,128]{1,0:T(8,128)S(1)}, f32[8,128]{1,0:T(8,128)S(1)}, f32[8,128]{1,0:T(8,128)S(1)}) custom-call(bf16[272,512]{1,0:T(8,128)(2,1)S(1)} %collective-permute-done.5.refs_0_.refs_2_, bf16[512,512]{1,0:T(8,128)(2,1)S(1)} %collective-permute-done.4.refs_1_, ...), custom_call_target="tpu_custom_call" | custom-call | flops 1 | bytes 1 | tf_op jit(solution)/shard_map/cross/pallas_call | solution.py:217
  34.2 1.3 %collective-permute-start.10 = (f32[8,128]{1,0:T(8,128)S(1)}, f32[8,128]{1,0:T(8,128)S(1)}, u32[]{:S(2)}, u32[]{:S(2)}) collective-permute-start(f32[8,128]{1,0:T(8,128)S(1)} %get-tuple-element.56), channel_id=1, source_target_pairs={{12,0},{13,1},{14,2},{15,3},{0,4},{1,5},{2,6},{3,7},{4,8},{5,9},{6... | collective-permute-start | bytes 12296 | tf_op jit(solution)/shard_map/ppermute | solution.py:286
  35.5 1.0 %collective-permute-done.8.refs_0_.refs_1_ = bf16[528,512]{1,0:T(8,128)(2,1)S(1)} collective-permute-done((bf16[528,512]{1,0:T(8,128)(2,1)S(1)}, bf16[528,512]{1,0:T(8,128)(2,1)S(1)}, u32[]{:S(2)}, u32[]{:S(2)}) %collective-permute-start.8) | collective-permute-done | bytes 540704 | tf_op jit(solution)/shard_map/ppermute | solution.py:249
  36.6 2.0 %cross.4 = (f32[8,128]{1,0:T(8,128)S(1)}, f32[8,128]{1,0:T(8,128)S(1)}, f32[8,128]{1,0:T(8,128)S(1)}, f32[8,128]{1,0:T(8,128)S(1)}, f32[8,128]{1,0:T(8,128)S(1)}) custom-call(bf16[528,512]{1,0:T(8,128)(2,1)S(1)} %collective-permute-done.8.refs_0_.refs_1_, bf16[528,512]{1,0:T(8,128)(2,1)S(1)} %collective-permute-done.8.refs_0_.refs_1_, ...), custom_call_target="tpu_custom_call" | custom-call | flops 1 | bytes 1 | tf_op jit(solution)/shard_map/cross/pallas_call | solution.py:217
  38.5 2.6 %collective-permute-done.9.refs_1_ = bf16[256,512]{1,0:T(8,128)(2,1)S(1)} collective-permute-done((bf16[256,512]{1,0:T(8,128)(2,1)S(1)}, bf16[256,512]{1,0:T(8,128)(2,1)S(1)}, u32[]{:S(2)}, u32[]{:S(2)}) %collective-permute-start.9) | collective-permute-done | bytes 262176 | tf_op jit(solution)/shard_map/ppermute | solution.py:249
  41.2 1.2 %cross.5 = (f32[8,128]{1,0:T(8,128)S(1)}, f32[8,128]{1,0:T(8,128)S(1)}, f32[8,128]{1,0:T(8,128)S(1)}, f32[8,128]{1,0:T(8,128)S(1)}, f32[8,128]{1,0:T(8,128)S(1)}) custom-call(bf16[528,512]{1,0:T(8,128)(2,1)S(1)} %collective-permute-done.8.refs_0_.refs_1_, bf16[256,512]{1,0:T(8,128)(2,1)S(1)} %collective-permute-done.9.refs_1_, ...), custom_call_target="tpu_custom_call" | custom-call | flops 1 | bytes 1 | tf_op jit(solution)/shard_map/cross/pallas_call | solution.py:217
  42.5 1.6 %collective-permute-start.12 = (f32[8,128]{1,0:T(8,128)S(1)}, f32[8,128]{1,0:T(8,128)S(1)}, u32[]{:S(2)}, u32[]{:S(2)}) collective-permute-start(f32[8,128]{1,0:T(8,128)S(1)} %get-tuple-element.60), channel_id=1, source_target_pairs={{0,2},{1,3},{2,0},{3,1},{4,6},{5,7},{6,4},{7,5},{8,10},{9,11},{10,... | collective-permute-start | bytes 12296 | tf_op jit(solution)/shard_map/ppermute | solution.py:241
  44.3 1.4 %collective-permute-start.14 = (f32[8,128]{1,0:T(8,128)S(1)}, f32[8,128]{1,0:T(8,128)S(1)}, u32[]{:S(2)}, u32[]{:S(2)}) collective-permute-start(f32[8,128]{1,0:T(8,128)S(1)} %get-tuple-element.64), channel_id=1, source_target_pairs={{8,0},{9,1},{10,2},{11,3},{0,4},{1,5},{2,6},{3,7},{12,8},{13,9},{1... | collective-permute-start | bytes 12296 | tf_op jit(solution)/shard_map/ppermute | solution.py:286
  45.7 0.4 collective-permute-done.12
  46.1 3.1 %collective-permute-done.14 = f32[8,128]{1,0:T(8,128)S(1)} collective-permute-done((f32[8,128]{1,0:T(8,128)S(1)}, f32[8,128]{1,0:T(8,128)S(1)}, u32[]{:S(2)}, u32[]{:S(2)}) %collective-permute-start.14) | collective-permute-done | bytes 4128 | tf_op jit(solution)/shard_map/ppermute | solution.py:286
  49.3 0.6 %maximum_bitcast_fusion = f32[768]{0:T(1024)} fusion(f32[8,128]{1,0:T(8,128)S(1)} %collective-permute-done.14, f32[8,128]{1,0:T(8,128)S(1)} %collective-permute-done.13, f32[8,128]{1,0:T(8,128)S(1)} %collective-permute-done.12, f32[8,128]{1,0:T(8,128)S(1)} %collective-permute-done.11, f32[8,128]{1,0:T(8,128)S(1)} %collective-permute-done.10, f32[8,128]{1,0:T(8,128)S(1)} %max.24), kind=kLoop, calls=%fused_computation | loop fusion | flops 3840 | bytes 21504 | tf_op jit(solution)/shard_map/max | solution.py:291
  (28 shorter events, 1.2 us)
Async XLA Ops:
  0.0 1.4 %copy-start = (f32[768,512]{1,0:T(8,128)S(1)}, f32[768,512]{1,0:T(8,128)}, u32[]{:S(2)}) copy-start(f32[768,512]{1,0:T(8,128)} %embeddings_ref.3) | copy-start | bytes 4718596
  1.4 6.8 %copy-start.2 = (s32[768]{0:T(1024)S(1)}, s32[768]{0:T(1024)}, u32[]{:S(2)}) copy-start(s32[768]{0:T(1024)} %param.5) | copy-start | bytes 9220
  1.4 6.8 %copy-start.3 = (s32[768]{0:T(1024)S(1)}, s32[768]{0:T(1024)}, u32[]{:S(2)}) copy-start(s32[768]{0:T(1024)} %param.6) | copy-start | bytes 9220
  1.4 6.8 %copy-start.4 = (s32[16]{0:T(128)S(1)}, s32[16]{0:T(128)}, u32[]{:S(2)}) copy-start(s32[16]{0:T(128)} %param.7) | copy-start | bytes 196
  1.4 6.9 %copy-start.1 = (f32[768,512]{1,0:T(8,128)S(1)}, f32[768,512]{1,0:T(8,128)}, u32[]{:S(2)}) copy-start(f32[768,512]{1,0:T(8,128)} %embeddings_ref.3) | copy-start | bytes 4718596
  1.6 24.5 %collective-permute-start.4 = (bf16[512,512]{1,0:T(8,128)(2,1)S(1)}, bf16[512,512]{1,0:T(8,128)(2,1)S(1)}, u32[]{:S(2)}, u32[]{:S(2)}) collective-permute-start(bf16[512,512]{1,0:T(8,128)(2,1)S(1)} %first.1.first_ref.refs_0_.refs_2_.refs_3_), channel_id=1, source_target_pairs={{0,12},{1,13},{2,14},{3,15},{4,0},{5,1},{6,2},{7,3},{8,4},{9,5},{1... | collective-permute-start | bytes 1572872 | tf_op jit(solution)/shard_map/ppermute | solution.py:249
  6.7 19.4 %collective-permute-start.2 = (bf16[512,512]{1,0:T(8,128)(2,1)S(1)}, bf16[512,512]{1,0:T(8,128)(2,1)S(1)}, u32[]{:S(2)}, u32[]{:S(2)}) collective-permute-start(bf16[512,512]{1,0:T(8,128)(2,1)S(1)} %first.1.first_ref.refs_0_.refs_2_.refs_3_), channel_id=1, source_target_pairs={{0,2},{1,3},{2,0},{3,1},{4,6},{5,7},{6,4},{7,5},{8,10},{9,11},{10,... | collective-permute-start | bytes 1572872 | tf_op jit(solution)/shard_map/ppermute | solution.py:241
  8.5 16.5 %collective-permute-start.5 = (bf16[272,512]{1,0:T(8,128)(2,1)S(1)}, bf16[272,512]{1,0:T(8,128)(2,1)S(1)}, u32[]{:S(2)}, u32[]{:S(2)}) collective-permute-start(bf16[272,512]{1,0:T(8,128)(2,1)S(1)} %get-tuple-element.35.refs_1_.refs_3_.refs_4_), channel_id=1, source_target_pairs={{0,12},{1,13},{2,14},{3,15},{4,0},{5,1},{6,2},{7,3},{8,4},{9,5},{1... | collective-permute-start | bytes 835592 | tf_op jit(solution)/shard_map/ppermute | solution.py:249
  9.0 17.1 %collective-permute-start.3 = (bf16[272,512]{1,0:T(8,128)(2,1)S(1)}, bf16[272,512]{1,0:T(8,128)(2,1)S(1)}, u32[]{:S(2)}, u32[]{:S(2)}) collective-permute-start(bf16[272,512]{1,0:T(8,128)(2,1)S(1)} %get-tuple-element.35.refs_1_.refs_3_.refs_4_), channel_id=1, source_target_pairs={{0,2},{1,3},{2,0},{3,1},{4,6},{5,7},{6,4},{7,5},{8,10},{9,11},{10,... | collective-permute-start | bytes 835592 | tf_op jit(solution)/shard_map/ppermute | solution.py:241
  9.6 26.9 %collective-permute-start.8 = (bf16[528,512]{1,0:T(8,128)(2,1)S(1)}, bf16[528,512]{1,0:T(8,128)(2,1)S(1)}, u32[]{:S(2)}, u32[]{:S(2)}) collective-permute-start(bf16[528,512]{1,0:T(8,128)(2,1)S(1)} %get-tuple-element.40), channel_id=1, source_target_pairs={{0,8},{1,9},{2,10},{3,11},{4,0},{5,1},{6,2},{7,3},{8,12},{9,13},{1... | collective-permute-start | bytes 1622024 | tf_op jit(solution)/shard_map/ppermute | solution.py:249
  26.0 1.6 %collective-permute-start.7 = (bf16[272,512]{1,0:T(8,128)(2,1)S(1)}, bf16[272,512]{1,0:T(8,128)(2,1)S(1)}, u32[]{:S(2)}, u32[]{:S(2)}) collective-permute-start(bf16[272,512]{1,0:T(8,128)(2,1)S(1)} %collective-permute-done.3.refs_3_.refs_8_.refs_7_), channel_id=1, source_target_pairs={{0,1},{1,0},{2,3},{3,2},{4,5},{5,4},{6,7},{7,6},{8,9},{9,8},{10,11... | collective-permute-start | bytes 835592 | tf_op jit(solution)/shard_map/ppermute | solution.py:241
  26.1 2.3 %collective-permute-start.6 = (bf16[512,512]{1,0:T(8,128)(2,1)S(1)}, bf16[512,512]{1,0:T(8,128)(2,1)S(1)}, u32[]{:S(2)}, u32[]{:S(2)}) collective-permute-start(bf16[512,512]{1,0:T(8,128)(2,1)S(1)} %collective-permute-done.2.refs_2_.refs_7_.refs_6_), channel_id=1, source_target_pairs={{0,1},{1,0},{2,3},{3,2},{4,5},{5,4},{6,7},{7,6},{8,9},{9,8},{10,11... | collective-permute-start | bytes 1572872 | tf_op jit(solution)/shard_map/ppermute | solution.py:241
  26.6 3.3 %collective-permute-start = (bf16[512,512]{1,0:T(8,128)(2,1)S(1)}, bf16[512,512]{1,0:T(8,128)(2,1)S(1)}, u32[]{:S(2)}, u32[]{:S(2)}) collective-permute-start(bf16[512,512]{1,0:T(8,128)(2,1)S(1)} %first.1.first_ref.refs_0_.refs_2_.refs_3_), channel_id=1, source_target_pairs={{0,1},{1,0},{2,3},{3,2},{4,5},{5,4},{6,7},{7,6},{8,9},{9,8},{10,11... | collective-permute-start | bytes 1572872 | tf_op jit(solution)/shard_map/ppermute | solution.py:241
  26.6 3.2 %collective-permute-start.1 = (bf16[272,512]{1,0:T(8,128)(2,1)S(1)}, bf16[272,512]{1,0:T(8,128)(2,1)S(1)}, u32[]{:S(2)}, u32[]{:S(2)}) collective-permute-start(bf16[272,512]{1,0:T(8,128)(2,1)S(1)} %get-tuple-element.35.refs_1_.refs_3_.refs_4_), channel_id=1, source_target_pairs={{0,1},{1,0},{2,3},{3,2},{4,5},{5,4},{6,7},{7,6},{8,9},{9,8},{10,11... | collective-permute-start | bytes 835592 | tf_op jit(solution)/shard_map/ppermute | solution.py:241
  27.6 13.6 %collective-permute-start.9 = (bf16[256,512]{1,0:T(8,128)(2,1)S(1)}, bf16[256,512]{1,0:T(8,128)(2,1)S(1)}, u32[]{:S(2)}, u32[]{:S(2)}) collective-permute-start(bf16[256,512]{1,0:T(8,128)(2,1)S(1)} %get-tuple-element.41), channel_id=1, source_target_pairs={{0,8},{1,9},{2,10},{3,11},{4,0},{5,1},{6,2},{7,3},{8,12},{9,13},{1... | collective-permute-start | bytes 786440 | tf_op jit(solution)/shard_map/ppermute | solution.py:249
  34.2 8.1 %collective-permute-start.10 = (f32[8,128]{1,0:T(8,128)S(1)}, f32[8,128]{1,0:T(8,128)S(1)}, u32[]{:S(2)}, u32[]{:S(2)}) collective-permute-start(f32[8,128]{1,0:T(8,128)S(1)} %get-tuple-element.56), channel_id=1, source_target_pairs={{12,0},{13,1},{14,2},{15,3},{0,4},{1,5},{2,6},{3,7},{4,8},{5,9},{6... | collective-permute-start | bytes 12296 | tf_op jit(solution)/shard_map/ppermute | solution.py:286
  42.4 3.3 %collective-permute-start.11 = (f32[8,128]{1,0:T(8,128)S(1)}, f32[8,128]{1,0:T(8,128)S(1)}, u32[]{:S(2)}, u32[]{:S(2)}) collective-permute-start(f32[8,128]{1,0:T(8,128)S(1)} %get-tuple-element.58), channel_id=1, source_target_pairs={{0,3},{1,2},{2,1},{3,0},{4,7},{5,6},{6,5},{7,4},{8,11},{9,10},{10,... | collective-permute-start | bytes 12296 | tf_op jit(solution)/shard_map/ppermute | solution.py:241
  42.5 3.6 %collective-permute-start.12 = (f32[8,128]{1,0:T(8,128)S(1)}, f32[8,128]{1,0:T(8,128)S(1)}, u32[]{:S(2)}, u32[]{:S(2)}) collective-permute-start(f32[8,128]{1,0:T(8,128)S(1)} %get-tuple-element.60), channel_id=1, source_target_pairs={{0,2},{1,3},{2,0},{3,1},{4,6},{5,7},{6,4},{7,5},{8,10},{9,11},{10,... | collective-permute-start | bytes 12296 | tf_op jit(solution)/shard_map/ppermute | solution.py:241
  44.0 2.1 %collective-permute-start.13 = (f32[8,128]{1,0:T(8,128)S(1)}, f32[8,128]{1,0:T(8,128)S(1)}, u32[]{:S(2)}, u32[]{:S(2)}) collective-permute-start(f32[8,128]{1,0:T(8,128)S(1)} %get-tuple-element.62), channel_id=1, source_target_pairs={{0,1},{1,0},{2,3},{3,2},{4,5},{5,4},{6,7},{7,6},{8,9},{9,8},{10,11... | collective-permute-start | bytes 12296 | tf_op jit(solution)/shard_map/ppermute | solution.py:241
  44.3 5.0 %collective-permute-start.14 = (f32[8,128]{1,0:T(8,128)S(1)}, f32[8,128]{1,0:T(8,128)S(1)}, u32[]{:S(2)}, u32[]{:S(2)}) collective-permute-start(f32[8,128]{1,0:T(8,128)S(1)} %get-tuple-element.64), channel_id=1, source_target_pairs={{8,0},{9,1},{10,2},{11,3},{0,4},{1,5},{2,6},{3,7},{12,8},{13,9},{1... | collective-permute-start | bytes 12296 | tf_op jit(solution)/shard_map/ppermute | solution.py:286

commit v12 on v11

--- a/solution.py
+++ b/solution.py
@@ -191,7 +191,7 @@
 
 def plane_steps(planes):
     if planes == 4:
-        return [(3, 0, 1, 2), (2, 0, 3, 1)]
+        return [(1, 2, 3, 0), (2, 0, 3, 1)]
     return [
         [(z + distance) % planes for z in range(planes)]
         for distance in range(1, planes // 2 + 1)
@@ -286,7 +286,7 @@
         backs.append(lax.ppermute(answer, "dp", [(t, s) for s, t in pairs]))
     best = jnp.maximum(best, plane_best[0]).reshape(-1)[:rows]
     for distance in (3, 2, 1):
-        backs.insert(-1, mate(after(plane_best[distance], *backs[:1]), distance))
+        backs.append(mate(after(plane_best[distance], *backs[:1]), distance))
     for back in backs:
         best = jnp.maximum(best, back.reshape(-1)[:rows])
     return best

time: 50 us -> 54.4 us (1.088)
  starting transfers between devices: 13.9 us -> 24.4 us
  waiting for transfers between devices: 24.5 us -> 18.4 us
    ppermute x4, starting transfers between devices: 6.02 us -> 17.8 us  [local(): away.append((pairs, [lax.ppermute(part, 'dp', pairs) for part in parts]))]
    ppermute x4, waiting for transfers between devices: 19 us -> 15.3 us  [local(): away.append((pairs, [lax.ppermute(part, 'dp', pairs) for part in parts]))]
    ppermute x2, waiting for transfers between devices: 3.15 us -> 1.39 us  [local(): backs.append(lax.ppermute(answer, 'dp', [(t, s) for s, t in pairs]))]
    ppermute x2, starting transfers between devices: 2.69 us -> 1.72 us  [local(): backs.append(lax.ppermute(answer, 'dp', [(t, s) for s, t in pairs]))]
    ppermute x9, waiting for transfers between devices: 2.36 us -> 1.73 us  [mate(): return lax.ppermute(value, 'dp', [(i, i ^ distance) for i in range(peers)])]
  transfers between devices with their start and end apart: 15 -> 15, of which waited for: 8 -> 6; matrix products, arithmetic and copies ran while one was open for 0% -> 0% of each run, Pallas kernels for 18% -> 17%
where the time goes in v12:
time: 54.4 us; the launch traced here: 54.3 us
  starting transfers between devices  24.4 us (45%)
  waiting for transfers between devices  18.4 us (34%)
  Pallas kernels  9.26 us (17%)
  local copies, waits for them, and re-layouts  1.51 us (3%)
  other arithmetic  0.6 us (1%)
    ppermute x4, starting transfers between devices, local(): away.append((pairs, [lax.ppermute(part, 'dp', pairs) for part in parts]))  17.8 us
    ppermute x4, waiting for transfers between devices, local(): away.append((pairs, [lax.ppermute(part, 'dp', pairs) for part in parts]))  15.3 us
    pallas_call x7, Pallas kernels, kernel(): pl.pallas_call(body, out_shape=tuple(outputs), in_specs=whole(len(inputs)...  9.26 us
    ppermute x9, starting transfers between devices, mate(): return lax.ppermute(value, 'dp', [(i, i ^ distance) for i in range(peers)])  4.9 us
    ppermute x9, waiting for transfers between devices, mate(): return lax.ppermute(value, 'dp', [(i, i ^ distance) for i in range(peers)])  1.73 us
    ppermute x2, starting transfers between devices, local(): backs.append(lax.ppermute(answer, 'dp', [(t, s) for s, t in pairs]))  1.72 us
    unnamed x10, local copies, waits for them, and re-layouts  1.42 us
    ppermute x2, waiting for transfers between devices, local(): backs.append(lax.ppermute(answer, 'dp', [(t, s) for s, t in pairs]))  1.39 us
  transfers between devices with their start and end apart: 15, of which 6 were waited for; matrix products, arithmetic and copies ran while one was open for 0% of the time, Pallas kernels for 17%

profile of v12, /device:TPU:0, one launch (start us, length us, event | category | flops | bytes accessed | tf_op | source)
XLA Modules:
  0.0 54.3 jit_solution(3800956515677412448)
XLA Ops:
  0.0 1.4 %copy-done = f32[768,512]{1,0:T(8,128)S(1)} copy-done((f32[768,512]{1,0:T(8,128)S(1)}, f32[768,512]{1,0:T(8,128)}, u32[]{:S(2)}) %copy-start) | copy-done | bytes 1572888
  1.6 3.1 %collective-permute-start.4 = (bf16[512,512]{1,0:T(8,128)(2,1)S(1)}, bf16[512,512]{1,0:T(8,128)(2,1)S(1)}, u32[]{:S(2)}, u32[]{:S(2)}) collective-permute-start(bf16[512,512]{1,0:T(8,128)(2,1)S(1)} %first.1.first_ref.refs_0_.refs_2_.refs_3_), channel_id=1, source_target_pairs={{0,4},{1,5},{2,6},{3,7},{4,8},{5,9},{6,10},{7,11},{8,12},{9,13},{1... | collective-permute-start | bytes 1572872 | tf_op jit(solution)/shard_map/ppermute | solution.py:249
  4.7 1.5 %collective-permute-start.2 = (bf16[512,512]{1,0:T(8,128)(2,1)S(1)}, bf16[512,512]{1,0:T(8,128)(2,1)S(1)}, u32[]{:S(2)}, u32[]{:S(2)}) collective-permute-start(bf16[512,512]{1,0:T(8,128)(2,1)S(1)} %first.1.first_ref.refs_0_.refs_2_.refs_3_), channel_id=1, source_target_pairs={{0,2},{1,3},{2,0},{3,1},{4,6},{5,7},{6,4},{7,5},{8,10},{9,11},{10,... | collective-permute-start | bytes 1572872 | tf_op jit(solution)/shard_map/ppermute | solution.py:241
  6.4 1.6 %collective-permute-start.5 = (bf16[272,512]{1,0:T(8,128)(2,1)S(1)}, bf16[272,512]{1,0:T(8,128)(2,1)S(1)}, u32[]{:S(2)}, u32[]{:S(2)}) collective-permute-start(bf16[272,512]{1,0:T(8,128)(2,1)S(1)} %get-tuple-element.35.refs_1_.refs_3_.refs_4_), channel_id=1, source_target_pairs={{0,4},{1,5},{2,6},{3,7},{4,8},{5,9},{6,10},{7,11},{8,12},{9,13},{1... | collective-permute-start | bytes 835592 | tf_op jit(solution)/shard_map/ppermute | solution.py:249
  8.1 0.5 collective-permute-start.3
  8.6 1.6 %collective-permute-start.8 = (bf16[528,512]{1,0:T(8,128)(2,1)S(1)}, bf16[528,512]{1,0:T(8,128)(2,1)S(1)}, u32[]{:S(2)}, u32[]{:S(2)}) collective-permute-start(bf16[528,512]{1,0:T(8,128)(2,1)S(1)} %get-tuple-element.40), channel_id=1, source_target_pairs={{0,8},{1,9},{2,10},{3,11},{4,0},{5,1},{6,2},{7,3},{8,12},{9,13},{1... | collective-permute-start | bytes 1622024 | tf_op jit(solution)/shard_map/ppermute | solution.py:249
  10.2 15.2 %collective-permute-done.5.refs_0_.refs_2_ = bf16[272,512]{1,0:T(8,128)(2,1)S(1)} collective-permute-done((bf16[272,512]{1,0:T(8,128)(2,1)S(1)}, bf16[272,512]{1,0:T(8,128)(2,1)S(1)}, u32[]{:S(2)}, u32[]{:S(2)}) %collective-permute-start.5) | collective-permute-done | bytes 278560 | tf_op jit(solution)/shard_map/ppermute | solution.py:249
  25.5 0.5 collective-permute-start.6
  26.1 0.4 collective-permute-start.1
  26.5 0.5 collective-permute-done.7.refs_5_.refs_10_.refs_9_
  27.0 11.4 %collective-permute-start.9 = (bf16[256,512]{1,0:T(8,128)(2,1)S(1)}, bf16[256,512]{1,0:T(8,128)(2,1)S(1)}, u32[]{:S(2)}, u32[]{:S(2)}) collective-permute-start(bf16[256,512]{1,0:T(8,128)(2,1)S(1)} %get-tuple-element.41), channel_id=1, source_target_pairs={{0,8},{1,9},{2,10},{3,11},{4,0},{5,1},{6,2},{7,3},{8,12},{9,13},{1... | collective-permute-start | bytes 786440 | tf_op jit(solution)/shard_map/ppermute | solution.py:249
  38.5 1.5 %plane_far.1 = (f32[8,128]{1,0:T(8,128)S(1)}, f32[768,128]{1,0:T(8,128)S(1)}, f32[768,128]{1,0:T(8,128)S(1)}) custom-call(bf16[512,512]{1,0:T(8,128)(2,1)S(1)} %first.1.first_ref.refs_0_.refs_2_.refs_3_, bf16[272,512]{1,0:T(8,128)(2,1)S(1)} %get-tuple-element.35.refs_1_.refs_3_.refs_4_, bf16[512,512]{1,0:T(8,128)(2,1)S(1)} %collective-permute-done.2.refs_2_.refs_7_.refs_6_, ...), custom_call_target="tpu_custom_call" | custom-call | flops 1 | bytes 1 | tf_op jit(solution)/shard_map/plane_far/pallas_call | solution.py:217
  40.0 1.5 %plane_near.1 = (f32[8,128]{1,0:T(8,128)S(1)}, f32[768,128]{1,0:T(8,128)S(1)}, f32[768,128]{1,0:T(8,128)S(1)}) custom-call(bf16[512,512]{1,0:T(8,128)(2,1)S(1)} %first.1.first_ref.refs_0_.refs_2_.refs_3_, bf16[272,512]{1,0:T(8,128)(2,1)S(1)} %get-tuple-element.35.refs_1_.refs_3_.refs_4_, bf16[512,512]{1,0:T(8,128)(2,1)S(1)} %first.1.first_ref.refs_0_.refs_2_.refs_3_, ...), custom_call_target="tpu_custom_call" | custom-call | flops 1 | bytes 1 | tf_op jit(solution)/shard_map/plane_near/pallas_call | solution.py:217
  41.5 2.8 %cross.3 = (f32[8,128]{1,0:T(8,128)S(1)}, f32[8,128]{1,0:T(8,128)S(1)}, f32[8,128]{1,0:T(8,128)S(1)}, f32[8,128]{1,0:T(8,128)S(1)}, f32[8,128]{1,0:T(8,128)S(1)}) custom-call(bf16[272,512]{1,0:T(8,128)(2,1)S(1)} %collective-permute-done.5.refs_0_.refs_2_, bf16[512,512]{1,0:T(8,128)(2,1)S(1)} %collective-permute-done.4.refs_1_, ...), custom_call_target="tpu_custom_call" | custom-call | flops 1 | bytes 1 | tf_op jit(solution)/shard_map/cross/pallas_call | solution.py:217
  44.4 2.0 %cross.4 = (f32[8,128]{1,0:T(8,128)S(1)}, f32[8,128]{1,0:T(8,128)S(1)}, f32[8,128]{1,0:T(8,128)S(1)}, f32[8,128]{1,0:T(8,128)S(1)}, f32[8,128]{1,0:T(8,128)S(1)}) custom-call(bf16[528,512]{1,0:T(8,128)(2,1)S(1)} %collective-permute-done.8.refs_0_.refs_1_, bf16[528,512]{1,0:T(8,128)(2,1)S(1)} %collective-permute-done.8.refs_0_.refs_1_, ...), custom_call_target="tpu_custom_call" | custom-call | flops 1 | bytes 1 | tf_op jit(solution)/shard_map/cross/pallas_call | solution.py:217
  46.4 1.2 %cross.5 = (f32[8,128]{1,0:T(8,128)S(1)}, f32[8,128]{1,0:T(8,128)S(1)}, f32[8,128]{1,0:T(8,128)S(1)}, f32[8,128]{1,0:T(8,128)S(1)}, f32[8,128]{1,0:T(8,128)S(1)}) custom-call(bf16[528,512]{1,0:T(8,128)(2,1)S(1)} %collective-permute-done.8.refs_0_.refs_1_, bf16[256,512]{1,0:T(8,128)(2,1)S(1)} %collective-permute-done.9.refs_1_, ...), custom_call_target="tpu_custom_call" | custom-call | flops 1 | bytes 1 | tf_op jit(solution)/shard_map/cross/pallas_call | solution.py:217
  47.6 0.4 collective-permute-done.10
  48.0 1.7 %collective-permute-start.11 = (f32[8,128]{1,0:T(8,128)S(1)}, f32[8,128]{1,0:T(8,128)S(1)}, u32[]{:S(2)}, u32[]{:S(2)}) collective-permute-start(f32[8,128]{1,0:T(8,128)S(1)} %get-tuple-element.58), channel_id=1, source_target_pairs={{8,0},{9,1},{10,2},{11,3},{0,4},{1,5},{2,6},{3,7},{12,8},{13,9},{1... | collective-permute-start | bytes 12296 | tf_op jit(solution)/shard_map/ppermute | solution.py:286
  49.6 0.4 collective-permute-start.12
  50.1 1.1 %collective-permute-start.13 = (f32[8,128]{1,0:T(8,128)S(1)}, f32[8,128]{1,0:T(8,128)S(1)}, u32[]{:S(2)}, u32[]{:S(2)}) collective-permute-start(f32[8,128]{1,0:T(8,128)S(1)} %get-tuple-element.62), channel_id=1, source_target_pairs={{0,2},{1,3},{2,0},{3,1},{4,6},{5,7},{6,4},{7,5},{8,10},{9,11},{10,... | collective-permute-start | bytes 12296 | tf_op jit(solution)/shard_map/ppermute | solution.py:241
  51.2 0.3 collective-permute-start.14
  51.5 1.0 %collective-permute-done.11 = f32[8,128]{1,0:T(8,128)S(1)} collective-permute-done((f32[8,128]{1,0:T(8,128)S(1)}, f32[8,128]{1,0:T(8,128)S(1)}, u32[]{:S(2)}, u32[]{:S(2)}) %collective-permute-start.11) | collective-permute-done | bytes 4128 | tf_op jit(solution)/shard_map/ppermute | solution.py:286
  52.7 1.0 %collective-permute-done.13 = f32[8,128]{1,0:T(8,128)S(1)} collective-permute-done((f32[8,128]{1,0:T(8,128)S(1)}, f32[8,128]{1,0:T(8,128)S(1)}, u32[]{:S(2)}, u32[]{:S(2)}) %collective-permute-start.13) | collective-permute-done | bytes 4128 | tf_op jit(solution)/shard_map/ppermute | solution.py:241
  53.7 0.6 %maximum_bitcast_fusion = f32[768]{0:T(1024)} fusion(f32[8,128]{1,0:T(8,128)S(1)} %collective-permute-done.14, f32[8,128]{1,0:T(8,128)S(1)} %collective-permute-done.13, f32[8,128]{1,0:T(8,128)S(1)} %collective-permute-done.12, f32[8,128]{1,0:T(8,128)S(1)} %collective-permute-done.11, f32[8,128]{1,0:T(8,128)S(1)} %collective-permute-done.10, f32[8,128]{1,0:T(8,128)S(1)} %max.24), kind=kLoop, calls=%fused_computation | loop fusion | flops 3840 | bytes 21504 | tf_op jit(solution)/shard_map/max | solution.py:291
  (28 shorter events, 0.8 us)
Async XLA Ops:
  0.0 1.4 %copy-start = (f32[768,512]{1,0:T(8,128)S(1)}, f32[768,512]{1,0:T(8,128)}, u32[]{:S(2)}) copy-start(f32[768,512]{1,0:T(8,128)} %embeddings_ref.3) | copy-start | bytes 4718596
  1.4 4.8 %copy-start.2 = (s32[768]{0:T(1024)S(1)}, s32[768]{0:T(1024)}, u32[]{:S(2)}) copy-start(s32[768]{0:T(1024)} %param.5) | copy-start | bytes 9220
  1.4 4.8 %copy-start.3 = (s32[768]{0:T(1024)S(1)}, s32[768]{0:T(1024)}, u32[]{:S(2)}) copy-start(s32[768]{0:T(1024)} %param.6) | copy-start | bytes 9220
  1.4 4.8 %copy-start.4 = (s32[16]{0:T(128)S(1)}, s32[16]{0:T(128)}, u32[]{:S(2)}) copy-start(s32[16]{0:T(128)} %param.7) | copy-start | bytes 196
  1.4 4.9 %copy-start.1 = (f32[768,512]{1,0:T(8,128)S(1)}, f32[768,512]{1,0:T(8,128)}, u32[]{:S(2)}) copy-start(f32[768,512]{1,0:T(8,128)} %embeddings_ref.3) | copy-start | bytes 4718596
  1.6 23.9 %collective-permute-start.4 = (bf16[512,512]{1,0:T(8,128)(2,1)S(1)}, bf16[512,512]{1,0:T(8,128)(2,1)S(1)}, u32[]{:S(2)}, u32[]{:S(2)}) collective-permute-start(bf16[512,512]{1,0:T(8,128)(2,1)S(1)} %first.1.first_ref.refs_0_.refs_2_.refs_3_), channel_id=1, source_target_pairs={{0,4},{1,5},{2,6},{3,7},{4,8},{5,9},{6,10},{7,11},{8,12},{9,13},{1... | collective-permute-start | bytes 1572872 | tf_op jit(solution)/shard_map/ppermute | solution.py:249
  4.7 20.8 %collective-permute-start.2 = (bf16[512,512]{1,0:T(8,128)(2,1)S(1)}, bf16[512,512]{1,0:T(8,128)(2,1)S(1)}, u32[]{:S(2)}, u32[]{:S(2)}) collective-permute-start(bf16[512,512]{1,0:T(8,128)(2,1)S(1)} %first.1.first_ref.refs_0_.refs_2_.refs_3_), channel_id=1, source_target_pairs={{0,2},{1,3},{2,0},{3,1},{4,6},{5,7},{6,4},{7,5},{8,10},{9,11},{10,... | collective-permute-start | bytes 1572872 | tf_op jit(solution)/shard_map/ppermute | solution.py:241
  6.4 19.0 %collective-permute-start.5 = (bf16[272,512]{1,0:T(8,128)(2,1)S(1)}, bf16[272,512]{1,0:T(8,128)(2,1)S(1)}, u32[]{:S(2)}, u32[]{:S(2)}) collective-permute-start(bf16[272,512]{1,0:T(8,128)(2,1)S(1)} %get-tuple-element.35.refs_1_.refs_3_.refs_4_), channel_id=1, source_target_pairs={{0,4},{1,5},{2,6},{3,7},{4,8},{5,9},{6,10},{7,11},{8,12},{9,13},{1... | collective-permute-start | bytes 835592 | tf_op jit(solution)/shard_map/ppermute | solution.py:249
  8.1 17.4 %collective-permute-start.3 = (bf16[272,512]{1,0:T(8,128)(2,1)S(1)}, bf16[272,512]{1,0:T(8,128)(2,1)S(1)}, u32[]{:S(2)}, u32[]{:S(2)}) collective-permute-start(bf16[272,512]{1,0:T(8,128)(2,1)S(1)} %get-tuple-element.35.refs_1_.refs_3_.refs_4_), channel_id=1, source_target_pairs={{0,2},{1,3},{2,0},{3,1},{4,6},{5,7},{6,4},{7,5},{8,10},{9,11},{10,... | collective-permute-start | bytes 835592 | tf_op jit(solution)/shard_map/ppermute | solution.py:241
  8.6 35.8 %collective-permute-start.8 = (bf16[528,512]{1,0:T(8,128)(2,1)S(1)}, bf16[528,512]{1,0:T(8,128)(2,1)S(1)}, u32[]{:S(2)}, u32[]{:S(2)}) collective-permute-start(bf16[528,512]{1,0:T(8,128)(2,1)S(1)} %get-tuple-element.40), channel_id=1, source_target_pairs={{0,8},{1,9},{2,10},{3,11},{4,0},{5,1},{6,2},{7,3},{8,12},{9,13},{1... | collective-permute-start | bytes 1622024 | tf_op jit(solution)/shard_map/ppermute | solution.py:249
  25.5 1.6 %collective-permute-start.7 = (bf16[272,512]{1,0:T(8,128)(2,1)S(1)}, bf16[272,512]{1,0:T(8,128)(2,1)S(1)}, u32[]{:S(2)}, u32[]{:S(2)}) collective-permute-start(bf16[272,512]{1,0:T(8,128)(2,1)S(1)} %collective-permute-done.3.refs_3_.refs_8_.refs_7_), channel_id=1, source_target_pairs={{0,1},{1,0},{2,3},{3,2},{4,5},{5,4},{6,7},{7,6},{8,9},{9,8},{10,11... | collective-permute-start | bytes 835592 | tf_op jit(solution)/shard_map/ppermute | solution.py:241
  25.5 13.0 %collective-permute-start.6 = (bf16[512,512]{1,0:T(8,128)(2,1)S(1)}, bf16[512,512]{1,0:T(8,128)(2,1)S(1)}, u32[]{:S(2)}, u32[]{:S(2)}) collective-permute-start(bf16[512,512]{1,0:T(8,128)(2,1)S(1)} %collective-permute-done.2.refs_2_.refs_7_.refs_6_), channel_id=1, source_target_pairs={{0,1},{1,0},{2,3},{3,2},{4,5},{5,4},{6,7},{7,6},{8,9},{9,8},{10,11... | collective-permute-start | bytes 1572872 | tf_op jit(solution)/shard_map/ppermute | solution.py:241
  26.0 14.0 %collective-permute-start = (bf16[512,512]{1,0:T(8,128)(2,1)S(1)}, bf16[512,512]{1,0:T(8,128)(2,1)S(1)}, u32[]{:S(2)}, u32[]{:S(2)}) collective-permute-start(bf16[512,512]{1,0:T(8,128)(2,1)S(1)} %first.1.first_ref.refs_0_.refs_2_.refs_3_), channel_id=1, source_target_pairs={{0,1},{1,0},{2,3},{3,2},{4,5},{5,4},{6,7},{7,6},{8,9},{9,8},{10,11... | collective-permute-start | bytes 1572872 | tf_op jit(solution)/shard_map/ppermute | solution.py:241
  26.1 13.9 %collective-permute-start.1 = (bf16[272,512]{1,0:T(8,128)(2,1)S(1)}, bf16[272,512]{1,0:T(8,128)(2,1)S(1)}, u32[]{:S(2)}, u32[]{:S(2)}) collective-permute-start(bf16[272,512]{1,0:T(8,128)(2,1)S(1)} %get-tuple-element.35.refs_1_.refs_3_.refs_4_), channel_id=1, source_target_pairs={{0,1},{1,0},{2,3},{3,2},{4,5},{5,4},{6,7},{7,6},{8,9},{9,8},{10,11... | collective-permute-start | bytes 835592 | tf_op jit(solution)/shard_map/ppermute | solution.py:241
  27.0 19.3 %collective-permute-start.9 = (bf16[256,512]{1,0:T(8,128)(2,1)S(1)}, bf16[256,512]{1,0:T(8,128)(2,1)S(1)}, u32[]{:S(2)}, u32[]{:S(2)}) collective-permute-start(bf16[256,512]{1,0:T(8,128)(2,1)S(1)} %get-tuple-element.41), channel_id=1, source_target_pairs={{0,8},{1,9},{2,10},{3,11},{4,0},{5,1},{6,2},{7,3},{8,12},{9,13},{1... | collective-permute-start | bytes 786440 | tf_op jit(solution)/shard_map/ppermute | solution.py:249
  44.3 3.7 %collective-permute-start.10 = (f32[8,128]{1,0:T(8,128)S(1)}, f32[8,128]{1,0:T(8,128)S(1)}, u32[]{:S(2)}, u32[]{:S(2)}) collective-permute-start(f32[8,128]{1,0:T(8,128)S(1)} %get-tuple-element.56), channel_id=1, source_target_pairs={{4,0},{5,1},{6,2},{7,3},{8,4},{9,5},{10,6},{11,7},{12,8},{13,9},{1... | collective-permute-start | bytes 12296 | tf_op jit(solution)/shard_map/ppermute | solution.py:286
  48.0 4.5 %collective-permute-start.11 = (f32[8,128]{1,0:T(8,128)S(1)}, f32[8,128]{1,0:T(8,128)S(1)}, u32[]{:S(2)}, u32[]{:S(2)}) collective-permute-start(f32[8,128]{1,0:T(8,128)S(1)} %get-tuple-element.58), channel_id=1, source_target_pairs={{8,0},{9,1},{10,2},{11,3},{0,4},{1,5},{2,6},{3,7},{12,8},{13,9},{1... | collective-permute-start | bytes 12296 | tf_op jit(solution)/shard_map/ppermute | solution.py:286
  49.6 3.0 %collective-permute-start.12 = (f32[8,128]{1,0:T(8,128)S(1)}, f32[8,128]{1,0:T(8,128)S(1)}, u32[]{:S(2)}, u32[]{:S(2)}) collective-permute-start(f32[8,128]{1,0:T(8,128)S(1)} %get-tuple-element.60), channel_id=1, source_target_pairs={{0,3},{1,2},{2,1},{3,0},{4,7},{5,6},{6,5},{7,4},{8,11},{9,10},{10,... | collective-permute-start | bytes 12296 | tf_op jit(solution)/shard_map/ppermute | solution.py:241
  50.1 3.6 %collective-permute-start.13 = (f32[8,128]{1,0:T(8,128)S(1)}, f32[8,128]{1,0:T(8,128)S(1)}, u32[]{:S(2)}, u32[]{:S(2)}) collective-permute-start(f32[8,128]{1,0:T(8,128)S(1)} %get-tuple-element.62), channel_id=1, source_target_pairs={{0,2},{1,3},{2,0},{3,1},{4,6},{5,7},{6,4},{7,5},{8,10},{9,11},{10,... | collective-permute-start | bytes 12296 | tf_op jit(solution)/shard_map/ppermute | solution.py:241
  51.2 2.5 %collective-permute-start.14 = (f32[8,128]{1,0:T(8,128)S(1)}, f32[8,128]{1,0:T(8,128)S(1)}, u32[]{:S(2)}, u32[]{:S(2)}) collective-permute-start(f32[8,128]{1,0:T(8,128)S(1)} %get-tuple-element.64), channel_id=1, source_target_pairs={{0,1},{1,0},{2,3},{3,2},{4,5},{5,4},{6,7},{7,6},{8,9},{9,8},{10,11... | collective-permute-start | bytes 12296 | tf_op jit(solution)/shard_map/ppermute | solution.py:241

commit v13 on v12

--- a/solution.py
+++ b/solution.py
@@ -13,6 +13,7 @@
 BASE = 64.0
 TILE = 256
 FIRST = 512
+HEAD = 512
 VMEM_LIMIT = 24 * 2**20
 
 
@@ -51,12 +52,16 @@
     digits = jnp.concatenate([digits, jnp.zeros((PAD, width - 128), jnp.bfloat16)], axis=1)
     last_ref[0:PAD, :] = digits
     head_ref[0:PAD, :] = digits
-    head_ref[PAD:, :] = first_ref[...]
     first = first_ref.shape[0]
-    for row in range(0, rows - first, 128):
-        unit = unit_rows(embeddings_ref[first + row : first + row + 128, :])
-        last_ref[PAD + row : PAD + row + 128, :] = unit
-        tail_ref[row : row + 128, :] = unit
+    head = head_ref.shape[0] - PAD
+    head_ref[PAD : PAD + first, :] = first_ref[...]
+    for row in range(first, rows, 128):
+        unit = unit_rows(embeddings_ref[row : row + 128, :])
+        last_ref[PAD + row - first : PAD + row - first + 128, :] = unit
+        if row < head:
+            head_ref[PAD + row : PAD + row + 128, :] = unit
+        else:
+            tail_ref[row - head : row - head + 128, :] = unit
 
 
 def tag_rows(block_ref):
@@ -64,12 +69,13 @@
     return digits[0:8] * BASE + digits[8:16]
 
 
-def tag_columns(block_ref, rows):
+def tag_columns(block_ref, first, count):
     tags = tag_rows(block_ref)
-    return jnp.concatenate(
-        [jnp.transpose(jnp.broadcast_to(tags[n : n + 1], (128, 128))) for n in range(rows // 128)],
-        axis=0,
-    )
+    parts = [
+        jnp.transpose(jnp.broadcast_to(tags[n : n + 1], (128, 128)))
+        for n in range(first // 128, (first + count) // 128)
+    ]
+    return jnp.concatenate(parts, axis=0)
 
 
 def dot_rows(values, lanes):
@@ -122,18 +128,17 @@
 
 def plane_kernel(rows, with_self, *refs):
     (own, one, two), refs = take(refs, (2, 2, 2))
-    best_ref, column_refs = refs[-3], refs[-2:]
+    best_ref = refs[-1]
     own_tags = tag_rows(own[-1])
-    for block, column_ref in zip((one, two), column_refs):
-        column_ref[...] = tag_columns(block[-1], rows)
+    columns = [tag_columns(block[-1], 0, rows) for block in (one, two)]
     for tile, own_part in row_slices(own):
         lanes = own_part[...]
         best = [jnp.full((8, 128), -1.0, jnp.float32) for _ in range(0, TILE, 128)]
-        for which, (block, column_ref) in enumerate(zip((one, two), column_refs)):
+        for which, block in enumerate((one, two)):
             for first, part in row_slices(block):
                 count = part.shape[0]
                 found = dot_rows(part[...], lanes)
-                column = column_ref[first : first + count, :]
+                column = columns[which][first : first + count]
                 for n in range(TILE // 128):
                     lane = tile + n * 128
                     match = column == own_tags[lane // 128 : lane // 128 + 1]
@@ -154,35 +159,35 @@
 def cross_kernel(starts, bases, *refs):
     (tags, aways), refs = take(refs, (1, len(starts)))
     blocks, refs = take(refs, (2,) * PLANE)
-    columns, refs = refs[:PLANE], refs[PLANE:]
     away_before, away_best = refs[0], refs[PLANE + 1]
     plane_before, plane_best = refs[1 : PLANE + 1], refs[PLANE + 2 :]
-    away_tags = tag_rows(tags[0])
-    tiles = []
+    plane_tags = [tag_rows(block[-1]) for block in blocks]
+    away_best[...] = away_before[...]
+    best = {}
     for start, base, away in zip(starts, bases, aways):
-        for row in range(0, away.shape[0] - base, TILE):
-            tiles.append((start + row, away.at[base + row : base + row + TILE]))
-    best = {}
+        for tile in range(0, away.shape[0] - base, TILE):
+            values = away[base + tile : base + tile + TILE, :]
+            column = tag_columns(tags[0], start + tile, TILE)
+            row_best = jnp.full((TILE, 128), -1.0, jnp.float32)
+            for which in range(PLANE):
+                for first, part in row_slices(blocks[which]):
+                    found = dot_rows(values, part[...])
+                    for lane in range(0, part.shape[0], 128):
+                        row = (first + lane) // 128
+                        match = column == plane_tags[which][row : row + 1]
+                        masked = jnp.where(match, found[:, lane : lane + 128], -1.0)
+                        row_best = jnp.maximum(row_best, masked)
+                        folded = fold_sublanes(masked)
+                        place = which, row
+                        best[place] = jnp.maximum(best[place], folded) if place in best else folded
+            place = pl.ds((start + tile) // 128, TILE // 128)
+            away_best[place, :] = fold_lanes(row_best)
     for which in range(PLANE):
-        for first, part in row_slices(blocks[which]):
-            count = part.shape[0]
-            row_best = jnp.full((count, 128), -1.0, jnp.float32)
-            for tile, away in tiles:
-                found = dot_rows(part[...], away[...])
-                column = columns[which][first : first + count, :]
-                for lane in range(0, TILE, 128):
-                    row = (tile + lane) // 128
-                    match = column == away_tags[row : row + 1]
-                    masked = jnp.where(match, found[:, lane : lane + 128], -1.0)
-                    row_best = jnp.maximum(row_best, masked)
-                    folded = fold_sublanes(masked)
-                    best[row] = jnp.maximum(best[row], folded) if row in best else folded
-            place = pl.ds(first // 128, count // 128)
-            folded = fold_lanes(row_best)
-            plane_best[which][place, :] = jnp.maximum(folded, plane_before[which][place, :])
-    away_best[...] = away_before[...]
-    for row, values in best.items():
-        away_best[row : row + 1, :] = jnp.max(values, axis=0, keepdims=True)
+        plane_best[which][...] = plane_before[which][...]
+    for (which, row), values in best.items():
+        folded = jnp.max(values, axis=0, keepdims=True)
+        place = pl.ds(row, 1)
+        plane_best[which][place, :] = jnp.maximum(folded, plane_before[which][place, :])
 
 
 def small_cost():
@@ -191,7 +196,7 @@
 
 def plane_steps(planes):
     if planes == 4:
-        return [(1, 2, 3, 0), (2, 0, 3, 1)]
+        return [(3, 0, 1, 2), (2, 0, 3, 1)]
     return [
         [(z + distance) % planes for z in range(planes)]
         for distance in range(1, planes // 2 + 1)
@@ -227,12 +232,11 @@
     def part_shape(count):
         return jax.ShapeDtypeStruct((count, width), jnp.bfloat16)
 
-    rest = rows - FIRST
-    (first,) = kernel(first_kernel, (embeddings,), (part_shape(FIRST),), "first")
+    (first,) = kernel(first_kernel, (embeddings[:FIRST],), (part_shape(FIRST),), "first")
     last, head, tail = kernel(
         functools.partial(rest_kernel, rows),
         (embeddings, ints, first),
-        (part_shape(PAD + rest), part_shape(PAD + FIRST), part_shape(rest)),
+        (part_shape(PAD + rows - FIRST), part_shape(PAD + HEAD), part_shape(rows - HEAD)),
         "rest",
     )
     own = (first, last)
@@ -251,27 +255,25 @@
     near = [mate(part, 1) for part in own]
     across = [mate(after(part, *away[0][1]), 1) for part in beside]
 
-    columns = jax.ShapeDtypeStruct((rows, 128), jnp.float32)
-    best, beside_columns, across_columns = kernel(
+    (best,) = kernel(
         functools.partial(plane_kernel, rows, False),
         (*own, *beside, *across),
-        (lanes, columns, columns),
+        (lanes,),
         "plane_far",
     )
-    best, own_columns, near_columns = kernel(
+    (best,) = kernel(
         functools.partial(plane_kernel, rows, True),
         (*own, *own, *near, best),
-        (lanes, columns, columns),
+        (lanes,),
         "plane_near",
     )
     plane = (*own, *near, *beside, *across)
-    plane += (own_columns, near_columns, beside_columns, across_columns)
-    plane_best = [jnp.full(lanes.shape, -1.0, jnp.float32)] * PLANE
+    plane_best = [best] + [jnp.full(lanes.shape, -1.0, jnp.float32)] * (PLANE - 1)
     backs = []
     for n, (pairs, received) in enumerate(away):
         away_best = jnp.full(lanes.shape, -1.0, jnp.float32)
         if n:
-            calls = (((0,), (PAD,), received[:1]), ((FIRST,), (0,), received[1:]))
+            calls = (((0,), (PAD,), received[:1]), ((HEAD,), (0,), received[1:]))
         else:
             calls = (((0, FIRST), (0, PAD), received),)
         tags = received[0] if n else received[-1]
@@ -282,9 +284,8 @@
                 (lanes,) * (PLANE + 1),
                 "cross",
             )
-        answer = after(away_best, *backs[:1])
-        backs.append(lax.ppermute(answer, "dp", [(t, s) for s, t in pairs]))
-    best = jnp.maximum(best, plane_best[0]).reshape(-1)[:rows]
+        backs.append(lax.ppermute(away_best, "dp", [(t, s) for s, t in pairs]))
+    best = plane_best[0].reshape(-1)[:rows]
     for distance in (3, 2, 1):
         backs.append(mate(after(plane_best[distance], *backs[:1]), distance))
     for back in backs:

time: 54.4 us -> 49.8 us (0.915); the launches traced: 54.3 us -> 48.9 us
  starting transfers between devices: 24.4 us -> 13.7 us
  waiting for transfers between devices: 18.4 us -> 23.9 us
    ppermute x4, starting transfers between devices: 17.8 us -> 6.03 us  [local(): away.append((pairs, [lax.ppermute(part, 'dp', pairs) for part in parts]))]
    ppermute x4, waiting for transfers between devices: 15.3 us -> 19.3 us  [local(): away.append((pairs, [lax.ppermute(part, 'dp', pairs) for part in parts]))]
    slice x0 -> x1, local copies, waits for them, and re-layouts: none -> 1.41 us  [local(): embeddings[:FIRST]]
    unnamed x10 -> x8, local copies, waits for them, and re-layouts: 1.42 us -> 0.01 us
    ppermute x9, waiting for transfers between devices: 1.73 us -> 2.89 us  [mate(): return lax.ppermute(value, 'dp', [(i, i ^ distance) for i in range(peers)])]
    ppermute x2, starting transfers between devices: 1.72 us -> 2.79 us  [local(): backs.append(lax.ppermute(away_best, 'dp', [(t, s) for s, t in pairs]))]
  transfers between devices with their start and end apart: 15 -> 15, of which waited for: 6 -> 8; matrix products, arithmetic and copies ran while one was open for 0% -> 0% of each run, Pallas kernels for 17% -> 18%
where the time goes in v13:
time: 49.8 us; the launch traced here: 48.9 us
  waiting for transfers between devices  23.9 us (48%)
  starting transfers between devices  13.7 us (28%)
  Pallas kernels  9.12 us (18%)
  local copies, waits for them, and re-layouts  1.51 us (3%)
  other arithmetic  0.6 us (1%)
    ppermute x4, waiting for transfers between devices, local(): away.append((pairs, [lax.ppermute(part, 'dp', pairs) for part in parts]))  19.3 us
    pallas_call x7, Pallas kernels, kernel(): pl.pallas_call(body, out_shape=tuple(outputs), in_specs=whole(len(inputs)...  9.12 us
    ppermute x4, starting transfers between devices, local(): away.append((pairs, [lax.ppermute(part, 'dp', pairs) for part in parts]))  6.03 us
    ppermute x9, starting transfers between devices, mate(): return lax.ppermute(value, 'dp', [(i, i ^ distance) for i in range(peers)])  4.91 us
    ppermute x9, waiting for transfers between devices, mate(): return lax.ppermute(value, 'dp', [(i, i ^ distance) for i in range(peers)])  2.89 us
    ppermute x2, starting transfers between devices, local(): backs.append(lax.ppermute(away_best, 'dp', [(t, s) for s, t in pairs]))  2.79 us
    ppermute x2, waiting for transfers between devices, local(): backs.append(lax.ppermute(away_best, 'dp', [(t, s) for s, t in pairs]))  1.72 us
    slice x1, local copies, waits for them, and re-layouts, local(): embeddings[:FIRST]  1.41 us
  transfers between devices with their start and end apart: 15, of which 8 were waited for; matrix products, arithmetic and copies ran while one was open for 0% of the time, Pallas kernels for 18%

profile of v13, /device:TPU:0, one launch (start us, length us, event | category | flops | bytes accessed | tf_op | source)
XLA Modules:
  0.0 48.9 jit_solution(17867609141767719389)
XLA Ops:
  0.0 1.4 %slice.29.embeddings_ref = f32[512,512]{1,0:T(8,128)S(1)} slice(f32[768,512]{1,0:T(8,128)} %embeddings_ref.1), slice={[0:512], [0:512]} | slice | bytes 2097152 | tf_op jit(solution)/shard_map/slice | solution.py:235
  1.6 5.1 %collective-permute-start.6 = (bf16[512,512]{1,0:T(8,128)(2,1)S(1)}, bf16[512,512]{1,0:T(8,128)(2,1)S(1)}, u32[]{:S(2)}, u32[]{:S(2)}) collective-permute-start(bf16[512,512]{1,0:T(8,128)(2,1)S(1)} %first.1.first_ref.refs_0_.refs_2_.refs_3_), channel_id=1, source_target_pairs={{0,12},{1,13},{2,14},{3,15},{4,0},{5,1},{6,2},{7,3},{8,4},{9,5},{1... | collective-permute-start | bytes 1572872 | tf_op jit(solution)/shard_map/ppermute | solution.py:253
  6.7 1.5 %collective-permute-start.4 = (bf16[512,512]{1,0:T(8,128)(2,1)S(1)}, bf16[512,512]{1,0:T(8,128)(2,1)S(1)}, u32[]{:S(2)}, u32[]{:S(2)}) collective-permute-start(bf16[512,512]{1,0:T(8,128)(2,1)S(1)} %first.1.first_ref.refs_0_.refs_2_.refs_3_), channel_id=1, source_target_pairs={{0,2},{1,3},{2,0},{3,1},{4,6},{5,7},{6,4},{7,5},{8,10},{9,11},{10,... | collective-permute-start | bytes 1572872 | tf_op jit(solution)/shard_map/ppermute | solution.py:245
  8.5 0.5 %collective-permute-start.7 = (bf16[272,512]{1,0:T(8,128)(2,1)S(1)}, bf16[272,512]{1,0:T(8,128)(2,1)S(1)}, u32[]{:S(2)}, u32[]{:S(2)}) collective-permute-start(bf16[272,512]{1,0:T(8,128)(2,1)S(1)} %get-tuple-element.30.refs_1_.refs_3_.refs_4_), channel_id=1, source_target_pairs={{0,12},{1,13},{2,14},{3,15},{4,0},{5,1},{6,2},{7,3},{8,4},{9,5},{1... | collective-permute-start | bytes 835592 | tf_op jit(solution)/shard_map/ppermute | solution.py:253
  9.0 0.5 %collective-permute-start.5 = (bf16[272,512]{1,0:T(8,128)(2,1)S(1)}, bf16[272,512]{1,0:T(8,128)(2,1)S(1)}, u32[]{:S(2)}, u32[]{:S(2)}) collective-permute-start(bf16[272,512]{1,0:T(8,128)(2,1)S(1)} %get-tuple-element.30.refs_1_.refs_3_.refs_4_), channel_id=1, source_target_pairs={{0,2},{1,3},{2,0},{3,1},{4,6},{5,7},{6,4},{7,5},{8,10},{9,11},{10,... | collective-permute-start | bytes 835592 | tf_op jit(solution)/shard_map/ppermute | solution.py:245
  9.5 15.5 %collective-permute-done.7.refs_0_.refs_2_ = bf16[272,512]{1,0:T(8,128)(2,1)S(1)} collective-permute-done((bf16[272,512]{1,0:T(8,128)(2,1)S(1)}, bf16[272,512]{1,0:T(8,128)(2,1)S(1)}, u32[]{:S(2)}, u32[]{:S(2)}) %collective-permute-start.7) | collective-permute-done | bytes 278560 | tf_op jit(solution)/shard_map/ppermute | solution.py:253
  25.0 1.1 %collective-permute-done.5.refs_3_.refs_8_.refs_7_ = bf16[272,512]{1,0:T(8,128)(2,1)S(1)} collective-permute-done((bf16[272,512]{1,0:T(8,128)(2,1)S(1)}, bf16[272,512]{1,0:T(8,128)(2,1)S(1)}, u32[]{:S(2)}, u32[]{:S(2)}) %collective-permute-start.5) | collective-permute-done | bytes 278560 | tf_op jit(solution)/shard_map/ppermute | solution.py:245
  26.1 0.5 %collective-permute-start.8 = (bf16[512,512]{1,0:T(8,128)(2,1)S(1)}, bf16[512,512]{1,0:T(8,128)(2,1)S(1)}, u32[]{:S(2)}, u32[]{:S(2)}) collective-permute-start(bf16[512,512]{1,0:T(8,128)(2,1)S(1)} %collective-permute-done.4.refs_2_.refs_7_.refs_6_), channel_id=1, source_target_pairs={{0,1},{1,0},{2,3},{3,2},{4,5},{5,4},{6,7},{7,6},{8,9},{9,8},{10,11... | collective-permute-start | bytes 1572872 | tf_op jit(solution)/shard_map/ppermute | solution.py:245
  26.6 0.4 collective-permute-start.3
  27.1 0.5 %collective-permute-done.9.refs_5_.refs_10_.refs_9_ = bf16[272,512]{1,0:T(8,128)(2,1)S(1)} collective-permute-done((bf16[272,512]{1,0:T(8,128)(2,1)S(1)}, bf16[272,512]{1,0:T(8,128)(2,1)S(1)}, u32[]{:S(2)}, u32[]{:S(2)}) %collective-permute-start.9) | collective-permute-done | bytes 278560 | tf_op jit(solution)/shard_map/ppermute | solution.py:245
  27.6 0.4 collective-permute-start.1
  28.4 1.4 %plane_far.1.refs_6_ = f32[8,128]{1,0:T(8,128)S(1)} custom-call(bf16[512,512]{1,0:T(8,128)(2,1)S(1)} %first.1.first_ref.refs_0_.refs_2_.refs_3_, bf16[272,512]{1,0:T(8,128)(2,1)S(1)} %get-tuple-element.30.refs_1_.refs_3_.refs_4_, bf16[512,512]{1,0:T(8,128)(2,1)S(1)} %collective-permute-done.4.refs_2_.refs_7_.refs_6_, ...), custom_call_target="tpu_custom_call" | custom-call | flops 1 | bytes 1 | tf_op jit(solution)/shard_map/plane_far/pallas_call | solution.py:222
  29.8 1.4 %plane_near.1.refs_12_ = f32[8,128]{1,0:T(8,128)S(1)} custom-call(bf16[512,512]{1,0:T(8,128)(2,1)S(1)} %first.1.first_ref.refs_0_.refs_2_.refs_3_, bf16[272,512]{1,0:T(8,128)(2,1)S(1)} %get-tuple-element.30.refs_1_.refs_3_.refs_4_, bf16[512,512]{1,0:T(8,128)(2,1)S(1)} %first.1.first_ref.refs_0_.refs_2_.refs_3_, ...), custom_call_target="tpu_custom_call" | custom-call | flops 1 | bytes 1 | tf_op jit(solution)/shard_map/plane_near/pallas_call | solution.py:222
  31.3 2.8 %cross.3 = (f32[8,128]{1,0:T(8,128)S(1)}, f32[8,128]{1,0:T(8,128)S(1)}, f32[8,128]{1,0:T(8,128)S(1)}, f32[8,128]{1,0:T(8,128)S(1)}, f32[8,128]{1,0:T(8,128)S(1)}) custom-call(bf16[272,512]{1,0:T(8,128)(2,1)S(1)} %collective-permute-done.7.refs_0_.refs_2_, bf16[512,512]{1,0:T(8,128)(2,1)S(1)} %collective-permute-done.6.refs_1_, ...), custom_call_target="tpu_custom_call" | custom-call | flops 1 | bytes 1 | tf_op jit(solution)/shard_map/cross/pallas_call | solution.py:222
  34.1 1.3 %collective-permute-start.10 = (f32[8,128]{1,0:T(8,128)S(1)}, f32[8,128]{1,0:T(8,128)S(1)}, u32[]{:S(2)}, u32[]{:S(2)}) collective-permute-start(f32[8,128]{1,0:T(8,128)S(1)} %get-tuple-element.43), channel_id=1, source_target_pairs={{12,0},{13,1},{14,2},{15,3},{0,4},{1,5},{2,6},{3,7},{4,8},{5,9},{6... | collective-permute-start | bytes 12296 | tf_op jit(solution)/shard_map/ppermute | solution.py:287
  35.5 1.1 %collective-permute-done.refs_0_.refs_1_ = bf16[528,512]{1,0:T(8,128)(2,1)S(1)} collective-permute-done((bf16[528,512]{1,0:T(8,128)(2,1)S(1)}, bf16[528,512]{1,0:T(8,128)(2,1)S(1)}, u32[]{:S(2)}, u32[]{:S(2)}) %collective-permute-start) | collective-permute-done | bytes 540704 | tf_op jit(solution)/shard_map/ppermute | solution.py:253
  36.6 1.9 %cross.4 = (f32[8,128]{1,0:T(8,128)S(1)}, f32[8,128]{1,0:T(8,128)S(1)}, f32[8,128]{1,0:T(8,128)S(1)}, f32[8,128]{1,0:T(8,128)S(1)}, f32[8,128]{1,0:T(8,128)S(1)}) custom-call(bf16[528,512]{1,0:T(8,128)(2,1)S(1)} %collective-permute-done.refs_0_.refs_1_, bf16[528,512]{1,0:T(8,128)(2,1)S(1)} %collective-permute-done.refs_0_.refs_1_, ...), custom_call_target="tpu_custom_call" | custom-call | flops 1 | bytes 1 | tf_op jit(solution)/shard_map/cross/pallas_call | solution.py:222
  38.5 2.6 %collective-permute-done.1.refs_1_ = bf16[256,512]{1,0:T(8,128)(2,1)S(1)} collective-permute-done((bf16[256,512]{1,0:T(8,128)(2,1)S(1)}, bf16[256,512]{1,0:T(8,128)(2,1)S(1)}, u32[]{:S(2)}, u32[]{:S(2)}) %collective-permute-start.1) | collective-permute-done | bytes 262176 | tf_op jit(solution)/shard_map/ppermute | solution.py:253
  41.2 1.1 %cross.5 = (f32[8,128]{1,0:T(8,128)S(1)}, f32[8,128]{1,0:T(8,128)S(1)}, f32[8,128]{1,0:T(8,128)S(1)}, f32[8,128]{1,0:T(8,128)S(1)}, f32[8,128]{1,0:T(8,128)S(1)}) custom-call(bf16[528,512]{1,0:T(8,128)(2,1)S(1)} %collective-permute-done.refs_0_.refs_1_, bf16[256,512]{1,0:T(8,128)(2,1)S(1)} %collective-permute-done.1.refs_1_, ...), custom_call_target="tpu_custom_call" | custom-call | flops 1 | bytes 1 | tf_op jit(solution)/shard_map/cross/pallas_call | solution.py:222
  42.3 1.5 %collective-permute-start.11 = (f32[8,128]{1,0:T(8,128)S(1)}, f32[8,128]{1,0:T(8,128)S(1)}, u32[]{:S(2)}, u32[]{:S(2)}) collective-permute-start(f32[8,128]{1,0:T(8,128)S(1)} %get-tuple-element.44), channel_id=1, source_target_pairs={{8,0},{9,1},{10,2},{11,3},{0,4},{1,5},{2,6},{3,7},{12,8},{13,9},{1... | collective-permute-start | bytes 12296 | tf_op jit(solution)/shard_map/ppermute | solution.py:287
  43.8 1.5 %collective-permute-start.13 = (f32[8,128]{1,0:T(8,128)S(1)}, f32[8,128]{1,0:T(8,128)S(1)}, u32[]{:S(2)}, u32[]{:S(2)}) collective-permute-start(f32[8,128]{1,0:T(8,128)S(1)} %get-tuple-element.48), channel_id=1, source_target_pairs={{0,2},{1,3},{2,0},{3,1},{4,6},{5,7},{6,4},{7,5},{8,10},{9,11},{10,... | collective-permute-start | bytes 12296 | tf_op jit(solution)/shard_map/ppermute | solution.py:245
  45.6 1.7 %collective-permute-done.11 = f32[8,128]{1,0:T(8,128)S(1)} collective-permute-done((f32[8,128]{1,0:T(8,128)S(1)}, f32[8,128]{1,0:T(8,128)S(1)}, u32[]{:S(2)}, u32[]{:S(2)}) %collective-permute-start.11) | collective-permute-done | bytes 4128 | tf_op jit(solution)/shard_map/ppermute | solution.py:287
  47.4 0.9 %collective-permute-done.12 = f32[8,128]{1,0:T(8,128)S(1)} collective-permute-done((f32[8,128]{1,0:T(8,128)S(1)}, f32[8,128]{1,0:T(8,128)S(1)}, u32[]{:S(2)}, u32[]{:S(2)}) %collective-permute-start.12) | collective-permute-done | bytes 4128 | tf_op jit(solution)/shard_map/ppermute | solution.py:245
  48.3 0.6 %maximum_bitcast_fusion = f32[768]{0:T(1024)} fusion(f32[8,128]{1,0:T(8,128)S(1)} %collective-permute-done.14, f32[8,128]{1,0:T(8,128)S(1)} %collective-permute-done.13, f32[8,128]{1,0:T(8,128)S(1)} %collective-permute-done.12, f32[8,128]{1,0:T(8,128)S(1)} %collective-permute-done.11, f32[8,128]{1,0:T(8,128)S(1)} %collective-permute-done.10, ...), kind=kLoop, calls=%fused_computation | loop fusion | flops 3840 | bytes 21504 | tf_op jit(solution)/shard_map/max | solution.py:292
  (26 shorter events, 1.2 us)
Async XLA Ops:
  0.0 8.3 %copy-start = (f32[768,512]{1,0:T(8,128)S(1)}, f32[768,512]{1,0:T(8,128)}, u32[]{:S(2)}) copy-start(f32[768,512]{1,0:T(8,128)} %embeddings_ref.1) | copy-start | bytes 4718596
  0.0 8.2 %copy-start.3 = (s32[16]{0:T(128)S(1)}, s32[16]{0:T(128)}, u32[]{:S(2)}) copy-start(s32[16]{0:T(128)} %param.7) | copy-start | bytes 196
  0.0 8.2 %copy-start.2 = (s32[768]{0:T(1024)S(1)}, s32[768]{0:T(1024)}, u32[]{:S(2)}) copy-start(s32[768]{0:T(1024)} %param.6) | copy-start | bytes 9220
  0.0 8.2 %copy-start.1 = (s32[768]{0:T(1024)S(1)}, s32[768]{0:T(1024)}, u32[]{:S(2)}) copy-start(s32[768]{0:T(1024)} %param.5) | copy-start | bytes 9220
  1.6 24.5 %collective-permute-start.6 = (bf16[512,512]{1,0:T(8,128)(2,1)S(1)}, bf16[512,512]{1,0:T(8,128)(2,1)S(1)}, u32[]{:S(2)}, u32[]{:S(2)}) collective-permute-start(bf16[512,512]{1,0:T(8,128)(2,1)S(1)} %first.1.first_ref.refs_0_.refs_2_.refs_3_), channel_id=1, source_target_pairs={{0,12},{1,13},{2,14},{3,15},{4,0},{5,1},{6,2},{7,3},{8,4},{9,5},{1... | collective-permute-start | bytes 1572872 | tf_op jit(solution)/shard_map/ppermute | solution.py:253
  6.7 19.4 %collective-permute-start.4 = (bf16[512,512]{1,0:T(8,128)(2,1)S(1)}, bf16[512,512]{1,0:T(8,128)(2,1)S(1)}, u32[]{:S(2)}, u32[]{:S(2)}) collective-permute-start(bf16[512,512]{1,0:T(8,128)(2,1)S(1)} %first.1.first_ref.refs_0_.refs_2_.refs_3_), channel_id=1, source_target_pairs={{0,2},{1,3},{2,0},{3,1},{4,6},{5,7},{6,4},{7,5},{8,10},{9,11},{10,... | collective-permute-start | bytes 1572872 | tf_op jit(solution)/shard_map/ppermute | solution.py:245
  8.5 16.5 %collective-permute-start.7 = (bf16[272,512]{1,0:T(8,128)(2,1)S(1)}, bf16[272,512]{1,0:T(8,128)(2,1)S(1)}, u32[]{:S(2)}, u32[]{:S(2)}) collective-permute-start(bf16[272,512]{1,0:T(8,128)(2,1)S(1)} %get-tuple-element.30.refs_1_.refs_3_.refs_4_), channel_id=1, source_target_pairs={{0,12},{1,13},{2,14},{3,15},{4,0},{5,1},{6,2},{7,3},{8,4},{9,5},{1... | collective-permute-start | bytes 835592 | tf_op jit(solution)/shard_map/ppermute | solution.py:253
  9.0 17.1 %collective-permute-start.5 = (bf16[272,512]{1,0:T(8,128)(2,1)S(1)}, bf16[272,512]{1,0:T(8,128)(2,1)S(1)}, u32[]{:S(2)}, u32[]{:S(2)}) collective-permute-start(bf16[272,512]{1,0:T(8,128)(2,1)S(1)} %get-tuple-element.30.refs_1_.refs_3_.refs_4_), channel_id=1, source_target_pairs={{0,2},{1,3},{2,0},{3,1},{4,6},{5,7},{6,4},{7,5},{8,10},{9,11},{10,... | collective-permute-start | bytes 835592 | tf_op jit(solution)/shard_map/ppermute | solution.py:245
  9.5 27.1 %collective-permute-start = (bf16[528,512]{1,0:T(8,128)(2,1)S(1)}, bf16[528,512]{1,0:T(8,128)(2,1)S(1)}, u32[]{:S(2)}, u32[]{:S(2)}) collective-permute-start(bf16[528,512]{1,0:T(8,128)(2,1)S(1)} %get-tuple-element.28), channel_id=1, source_target_pairs={{0,8},{1,9},{2,10},{3,11},{4,0},{5,1},{6,2},{7,3},{8,12},{9,13},{1... | collective-permute-start | bytes 1622024 | tf_op jit(solution)/shard_map/ppermute | solution.py:253
  26.1 1.6 %collective-permute-start.9 = (bf16[272,512]{1,0:T(8,128)(2,1)S(1)}, bf16[272,512]{1,0:T(8,128)(2,1)S(1)}, u32[]{:S(2)}, u32[]{:S(2)}) collective-permute-start(bf16[272,512]{1,0:T(8,128)(2,1)S(1)} %collective-permute-done.5.refs_3_.refs_8_.refs_7_), channel_id=1, source_target_pairs={{0,1},{1,0},{2,3},{3,2},{4,5},{5,4},{6,7},{7,6},{8,9},{9,8},{10,11... | collective-permute-start | bytes 835592 | tf_op jit(solution)/shard_map/ppermute | solution.py:245
  26.1 2.3 %collective-permute-start.8 = (bf16[512,512]{1,0:T(8,128)(2,1)S(1)}, bf16[512,512]{1,0:T(8,128)(2,1)S(1)}, u32[]{:S(2)}, u32[]{:S(2)}) collective-permute-start(bf16[512,512]{1,0:T(8,128)(2,1)S(1)} %collective-permute-done.4.refs_2_.refs_7_.refs_6_), channel_id=1, source_target_pairs={{0,1},{1,0},{2,3},{3,2},{4,5},{5,4},{6,7},{7,6},{8,9},{9,8},{10,11... | collective-permute-start | bytes 1572872 | tf_op jit(solution)/shard_map/ppermute | solution.py:245
  26.6 3.3 %collective-permute-start.2 = (bf16[512,512]{1,0:T(8,128)(2,1)S(1)}, bf16[512,512]{1,0:T(8,128)(2,1)S(1)}, u32[]{:S(2)}, u32[]{:S(2)}) collective-permute-start(bf16[512,512]{1,0:T(8,128)(2,1)S(1)} %first.1.first_ref.refs_0_.refs_2_.refs_3_), channel_id=1, source_target_pairs={{0,1},{1,0},{2,3},{3,2},{4,5},{5,4},{6,7},{7,6},{8,9},{9,8},{10,11... | collective-permute-start | bytes 1572872 | tf_op jit(solution)/shard_map/ppermute | solution.py:245
  26.6 3.2 %collective-permute-start.3 = (bf16[272,512]{1,0:T(8,128)(2,1)S(1)}, bf16[272,512]{1,0:T(8,128)(2,1)S(1)}, u32[]{:S(2)}, u32[]{:S(2)}) collective-permute-start(bf16[272,512]{1,0:T(8,128)(2,1)S(1)} %get-tuple-element.30.refs_1_.refs_3_.refs_4_), channel_id=1, source_target_pairs={{0,1},{1,0},{2,3},{3,2},{4,5},{5,4},{6,7},{7,6},{8,9},{9,8},{10,11... | collective-permute-start | bytes 835592 | tf_op jit(solution)/shard_map/ppermute | solution.py:245
  27.6 13.6 %collective-permute-start.1 = (bf16[256,512]{1,0:T(8,128)(2,1)S(1)}, bf16[256,512]{1,0:T(8,128)(2,1)S(1)}, u32[]{:S(2)}, u32[]{:S(2)}) collective-permute-start(bf16[256,512]{1,0:T(8,128)(2,1)S(1)} %get-tuple-element.29), channel_id=1, source_target_pairs={{0,8},{1,9},{2,10},{3,11},{4,0},{5,1},{6,2},{7,3},{8,12},{9,13},{1... | collective-permute-start | bytes 786440 | tf_op jit(solution)/shard_map/ppermute | solution.py:253
  34.1 9.6 %collective-permute-start.10 = (f32[8,128]{1,0:T(8,128)S(1)}, f32[8,128]{1,0:T(8,128)S(1)}, u32[]{:S(2)}, u32[]{:S(2)}) collective-permute-start(f32[8,128]{1,0:T(8,128)S(1)} %get-tuple-element.43), channel_id=1, source_target_pairs={{12,0},{13,1},{14,2},{15,3},{0,4},{1,5},{2,6},{3,7},{4,8},{5,9},{6... | collective-permute-start | bytes 12296 | tf_op jit(solution)/shard_map/ppermute | solution.py:287
  42.3 5.0 %collective-permute-start.11 = (f32[8,128]{1,0:T(8,128)S(1)}, f32[8,128]{1,0:T(8,128)S(1)}, u32[]{:S(2)}, u32[]{:S(2)}) collective-permute-start(f32[8,128]{1,0:T(8,128)S(1)} %get-tuple-element.44), channel_id=1, source_target_pairs={{8,0},{9,1},{10,2},{11,3},{0,4},{1,5},{2,6},{3,7},{12,8},{13,9},{1... | collective-permute-start | bytes 12296 | tf_op jit(solution)/shard_map/ppermute | solution.py:287
  43.8 3.6 %collective-permute-start.14 = (f32[8,128]{1,0:T(8,128)S(1)}, f32[8,128]{1,0:T(8,128)S(1)}, u32[]{:S(2)}, u32[]{:S(2)}) collective-permute-start(f32[8,128]{1,0:T(8,128)S(1)} %get-tuple-element.50), channel_id=1, source_target_pairs={{0,1},{1,0},{2,3},{3,2},{4,5},{5,4},{6,7},{7,6},{8,9},{9,8},{10,11... | collective-permute-start | bytes 12296 | tf_op jit(solution)/shard_map/ppermute | solution.py:245
  43.8 3.6 %collective-permute-start.13 = (f32[8,128]{1,0:T(8,128)S(1)}, f32[8,128]{1,0:T(8,128)S(1)}, u32[]{:S(2)}, u32[]{:S(2)}) collective-permute-start(f32[8,128]{1,0:T(8,128)S(1)} %get-tuple-element.48), channel_id=1, source_target_pairs={{0,2},{1,3},{2,0},{3,1},{4,6},{5,7},{6,4},{7,5},{8,10},{9,11},{10,... | collective-permute-start | bytes 12296 | tf_op jit(solution)/shard_map/ppermute | solution.py:245
  45.3 3.0 %collective-permute-start.12 = (f32[8,128]{1,0:T(8,128)S(1)}, f32[8,128]{1,0:T(8,128)S(1)}, u32[]{:S(2)}, u32[]{:S(2)}) collective-permute-start(f32[8,128]{1,0:T(8,128)S(1)} %get-tuple-element.46), channel_id=1, source_target_pairs={{0,3},{1,2},{2,1},{3,0},{4,7},{5,6},{6,5},{7,4},{8,11},{9,10},{10,... | collective-permute-start | bytes 12296 | tf_op jit(solution)/shard_map/ppermute | solution.py:245

commit v14 on v13

--- a/solution.py
+++ b/solution.py
@@ -196,9 +196,9 @@
 
 def plane_steps(planes):
     if planes == 4:
-        return [(3, 0, 1, 2), (2, 0, 3, 1)]
+        return [[(0, 2), (1, 0), (2, 3), (3, 1)], [(0, 3), (2, 1)]]
     return [
-        [(z + distance) % planes for z in range(planes)]
+        [(z, (z + distance) % planes) for z in range(planes)]
         for distance in range(1, planes // 2 + 1)
     ]
 
@@ -232,7 +232,7 @@
     def part_shape(count):
         return jax.ShapeDtypeStruct((count, width), jnp.bfloat16)
 
-    (first,) = kernel(first_kernel, (embeddings[:FIRST],), (part_shape(FIRST),), "first")
+    (first,) = kernel(first_kernel, (embeddings,), (part_shape(FIRST),), "first")
     last, head, tail = kernel(
         functools.partial(rest_kernel, rows),
         (embeddings, ints, first),
@@ -246,7 +246,7 @@
 
     away = []
     for n, step in enumerate(plane_steps(planes)):
-        pairs = [(z * PLANE + j, t * PLANE + j) for z, t in enumerate(step) for j in range(PLANE)]
+        pairs = [(z * PLANE + j, t * PLANE + j) for z, t in step for j in range(PLANE)]
         parts = (head, tail) if n else own
         if n > 1:
             parts = [after(part, away[-1][1][-1]) for part in parts]
@@ -269,7 +269,7 @@
     )
     plane = (*own, *near, *beside, *across)
     plane_best = [best] + [jnp.full(lanes.shape, -1.0, jnp.float32)] * (PLANE - 1)
-    backs = []
+    backs, masks = [], {}
     for n, (pairs, received) in enumerate(away):
         away_best = jnp.full(lanes.shape, -1.0, jnp.float32)
         if n:
@@ -285,11 +285,16 @@
                 "cross",
             )
         backs.append(lax.ppermute(away_best, "dp", [(t, s) for s, t in pairs]))
+        if len(pairs) < peers:
+            sources = sum(1 << z for z in {s // PLANE for s, _ in pairs})
+            sent = (jnp.int32(sources) >> (lax.axis_index("dp") // PLANE)) & 1
+            masks[n] = jnp.broadcast_to(sent == 1, (rows,))
     best = plane_best[0].reshape(-1)[:rows]
     for distance in (3, 2, 1):
         backs.append(mate(after(plane_best[distance], *backs[:1]), distance))
-    for back in backs:
-        best = jnp.maximum(best, back.reshape(-1)[:rows])
+    for n, back in enumerate(backs):
+        back = back.reshape(-1)[:rows]
+        best = jnp.maximum(best, jnp.where(masks[n], back, -1.0) if n in masks else back)
     return best
 
 

time: 49.8 us -> 49.4 us (level); the launches traced: 48.9 us -> 49.2 us
  starting transfers between devices: 13.7 us -> 17.9 us
  waiting for transfers between devices: 23.9 us -> 19.9 us
    ppermute x4, waiting for transfers between devices: 19.3 us -> 2.19 us  [local(): away.append((pairs, [lax.ppermute(part, 'dp', pairs) for part in parts]))]
    ppermute x9, waiting for transfers between devices: 2.89 us -> 13.7 us  [mate(): return lax.ppermute(value, 'dp', [(i, i ^ distance) for i in range(peers)])]
    ppermute x4, starting transfers between devices: 6.03 us -> 11.5 us  [local(): away.append((pairs, [lax.ppermute(part, 'dp', pairs) for part in parts]))]
    ppermute x2, waiting for transfers between devices: 1.72 us -> 4.05 us  [local(): backs.append(lax.ppermute(away_best, 'dp', [(t, s) for s, t in pairs]))]
    ppermute x2, starting transfers between devices: 2.79 us -> 1.35 us  [local(): backs.append(lax.ppermute(away_best, 'dp', [(t, s) for s, t in pairs]))]
    slice x1 -> x0, local copies, waits for them, and re-layouts: 1.41 us -> none  [local(): embeddings[:FIRST]]
    unnamed x8 -> x10, local copies, waits for them, and re-layouts: 0.01 us -> 1.42 us
  transfers between devices with their start and end apart: 15 -> 15, of which waited for: 8 -> 4; matrix products, arithmetic and copies ran while one was open for 0% -> 0% of each run, Pallas kernels for 18% -> 18%
where the time goes in v14:
time: 49.4 us; the launch traced here: 49.2 us
  waiting for transfers between devices  19.9 us (40%)
  starting transfers between devices  17.9 us (36%)
  Pallas kernels  9.08 us (18%)
  local copies, waits for them, and re-layouts  1.51 us (3%)
  other arithmetic  0.6 us (1%)
    ppermute x9, waiting for transfers between devices, mate(): return lax.ppermute(value, 'dp', [(i, i ^ distance) for i in range(peers)])  13.7 us
    ppermute x4, starting transfers between devices, local(): away.append((pairs, [lax.ppermute(part, 'dp', pairs) for part in parts]))  11.5 us
    pallas_call x7, Pallas kernels, kernel(): pl.pallas_call(body, out_shape=tuple(outputs), in_specs=whole(len(inputs)...  9.08 us
    ppermute x9, starting transfers between devices, mate(): return lax.ppermute(value, 'dp', [(i, i ^ distance) for i in range(peers)])  5.03 us
    ppermute x2, waiting for transfers between devices, local(): backs.append(lax.ppermute(away_best, 'dp', [(t, s) for s, t in pairs]))  4.05 us
    ppermute x4, waiting for transfers between devices, local(): away.append((pairs, [lax.ppermute(part, 'dp', pairs) for part in parts]))  2.19 us
    unnamed x10, local copies, waits for them, and re-layouts  1.42 us
    ppermute x2, starting transfers between devices, local(): backs.append(lax.ppermute(away_best, 'dp', [(t, s) for s, t in pairs]))  1.35 us
  transfers between devices with their start and end apart: 15, of which 4 were waited for; matrix products, arithmetic and copies ran while one was open for 0% of the time, Pallas kernels for 18%

profile of v14, /device:TPU:0, one launch (start us, length us, event | category | flops | bytes accessed | tf_op | source)
XLA Modules:
  0.0 49.2 jit_solution(15507450772854181917)
XLA Ops:
  0.0 1.4 %copy-done = f32[768,512]{1,0:T(8,128)S(1)} copy-done((f32[768,512]{1,0:T(8,128)S(1)}, f32[768,512]{1,0:T(8,128)}, u32[]{:S(2)}) %copy-start) | copy-done | bytes 1572888
  1.4 0.2 first.1.first_ref.refs_0_.refs_2_.refs_3_
  1.6 4.1 %collective-permute-start.6 = (bf16[512,512]{1,0:T(8,128)(2,1)S(1)}, bf16[512,512]{1,0:T(8,128)(2,1)S(1)}, u32[]{:S(2)}, u32[]{:S(2)}) collective-permute-start(bf16[512,512]{1,0:T(8,128)(2,1)S(1)} %first.1.first_ref.refs_0_.refs_2_.refs_3_), channel_id=1, source_target_pairs={{0,8},{1,9},{2,10},{3,11},{4,0},{5,1},{6,2},{7,3},{8,12},{9,13},{1... | collective-permute-start | bytes 1572872 | tf_op jit(solution)/shard_map/ppermute | solution.py:253
  5.7 1.5 %collective-permute-start.4 = (bf16[512,512]{1,0:T(8,128)(2,1)S(1)}, bf16[512,512]{1,0:T(8,128)(2,1)S(1)}, u32[]{:S(2)}, u32[]{:S(2)}) collective-permute-start(bf16[512,512]{1,0:T(8,128)(2,1)S(1)} %first.1.first_ref.refs_0_.refs_2_.refs_3_), channel_id=1, source_target_pairs={{0,2},{1,3},{2,0},{3,1},{4,6},{5,7},{6,4},{7,5},{8,10},{9,11},{10,... | collective-permute-start | bytes 1572872 | tf_op jit(solution)/shard_map/ppermute | solution.py:245
  7.3 0.2 rest.1
  7.4 0.6 %collective-permute-start.5 = (bf16[272,512]{1,0:T(8,128)(2,1)S(1)}, bf16[272,512]{1,0:T(8,128)(2,1)S(1)}, u32[]{:S(2)}, u32[]{:S(2)}) collective-permute-start(bf16[272,512]{1,0:T(8,128)(2,1)S(1)} %get-tuple-element.30.refs_1_.refs_3_.refs_4_), channel_id=1, source_target_pairs={{0,2},{1,3},{2,0},{3,1},{4,6},{5,7},{6,4},{7,5},{8,10},{9,11},{10,... | collective-permute-start | bytes 835592 | tf_op jit(solution)/shard_map/ppermute | solution.py:245
  8.0 1.6 %collective-permute-start.7 = (bf16[272,512]{1,0:T(8,128)(2,1)S(1)}, bf16[272,512]{1,0:T(8,128)(2,1)S(1)}, u32[]{:S(2)}, u32[]{:S(2)}) collective-permute-start(bf16[272,512]{1,0:T(8,128)(2,1)S(1)} %get-tuple-element.30.refs_1_.refs_3_.refs_4_), channel_id=1, source_target_pairs={{0,8},{1,9},{2,10},{3,11},{4,0},{5,1},{6,2},{7,3},{8,12},{9,13},{1... | collective-permute-start | bytes 835592 | tf_op jit(solution)/shard_map/ppermute | solution.py:253
  9.6 2.3 %collective-permute-start = (bf16[528,512]{1,0:T(8,128)(2,1)S(1)}, bf16[528,512]{1,0:T(8,128)(2,1)S(1)}, u32[]{:S(2)}, u32[]{:S(2)}) collective-permute-start(bf16[528,512]{1,0:T(8,128)(2,1)S(1)} %get-tuple-element.28), channel_id=1, source_target_pairs={{0,12},{1,13},{2,14},{3,15},{8,4},{9,5},{10,6},{11,7},{16,28},{17,... | collective-permute-start | bytes 1622024 | tf_op jit(solution)/shard_map/ppermute | solution.py:253
  11.9 13.1 %collective-permute-done.5.refs_3_.refs_8_.refs_7_ = bf16[272,512]{1,0:T(8,128)(2,1)S(1)} collective-permute-done((bf16[272,512]{1,0:T(8,128)(2,1)S(1)}, bf16[272,512]{1,0:T(8,128)(2,1)S(1)}, u32[]{:S(2)}, u32[]{:S(2)}) %collective-permute-start.5) | collective-permute-done | bytes 278560 | tf_op jit(solution)/shard_map/ppermute | solution.py:245
  25.1 0.5 %collective-permute-start.8 = (bf16[512,512]{1,0:T(8,128)(2,1)S(1)}, bf16[512,512]{1,0:T(8,128)(2,1)S(1)}, u32[]{:S(2)}, u32[]{:S(2)}) collective-permute-start(bf16[512,512]{1,0:T(8,128)(2,1)S(1)} %collective-permute-done.4.refs_2_.refs_7_.refs_6_), channel_id=1, source_target_pairs={{0,1},{1,0},{2,3},{3,2},{4,5},{5,4},{6,7},{7,6},{8,9},{9,8},{10,11... | collective-permute-start | bytes 1572872 | tf_op jit(solution)/shard_map/ppermute | solution.py:245
  25.6 0.4 collective-permute-start.3
  26.1 0.5 %collective-permute-done.9.refs_5_.refs_10_.refs_9_ = bf16[272,512]{1,0:T(8,128)(2,1)S(1)} collective-permute-done((bf16[272,512]{1,0:T(8,128)(2,1)S(1)}, bf16[272,512]{1,0:T(8,128)(2,1)S(1)}, u32[]{:S(2)}, u32[]{:S(2)}) %collective-permute-start.9) | collective-permute-done | bytes 278560 | tf_op jit(solution)/shard_map/ppermute | solution.py:245
  26.6 3.6 %collective-permute-start.1 = (bf16[256,512]{1,0:T(8,128)(2,1)S(1)}, bf16[256,512]{1,0:T(8,128)(2,1)S(1)}, u32[]{:S(2)}, u32[]{:S(2)}) collective-permute-start(bf16[256,512]{1,0:T(8,128)(2,1)S(1)} %get-tuple-element.29), channel_id=1, source_target_pairs={{0,12},{1,13},{2,14},{3,15},{8,4},{9,5},{10,6},{11,7},{16,28},{17,... | collective-permute-start | bytes 786440 | tf_op jit(solution)/shard_map/ppermute | solution.py:253
  30.2 1.4 %plane_far.1.refs_6_ = f32[8,128]{1,0:T(8,128)S(1)} custom-call(bf16[512,512]{1,0:T(8,128)(2,1)S(1)} %first.1.first_ref.refs_0_.refs_2_.refs_3_, bf16[272,512]{1,0:T(8,128)(2,1)S(1)} %get-tuple-element.30.refs_1_.refs_3_.refs_4_, bf16[512,512]{1,0:T(8,128)(2,1)S(1)} %collective-permute-done.4.refs_2_.refs_7_.refs_6_, ...), custom_call_target="tpu_custom_call" | custom-call | flops 1 | bytes 1 | tf_op jit(solution)/shard_map/plane_far/pallas_call | solution.py:222
  31.6 1.4 %plane_near.1.refs_12_ = f32[8,128]{1,0:T(8,128)S(1)} custom-call(bf16[512,512]{1,0:T(8,128)(2,1)S(1)} %first.1.first_ref.refs_0_.refs_2_.refs_3_, bf16[272,512]{1,0:T(8,128)(2,1)S(1)} %get-tuple-element.30.refs_1_.refs_3_.refs_4_, bf16[512,512]{1,0:T(8,128)(2,1)S(1)} %first.1.first_ref.refs_0_.refs_2_.refs_3_, ...), custom_call_target="tpu_custom_call" | custom-call | flops 1 | bytes 1 | tf_op jit(solution)/shard_map/plane_near/pallas_call | solution.py:222
  33.1 2.8 %cross.3 = (f32[8,128]{1,0:T(8,128)S(1)}, f32[8,128]{1,0:T(8,128)S(1)}, f32[8,128]{1,0:T(8,128)S(1)}, f32[8,128]{1,0:T(8,128)S(1)}, f32[8,128]{1,0:T(8,128)S(1)}) custom-call(bf16[272,512]{1,0:T(8,128)(2,1)S(1)} %collective-permute-done.7.refs_0_.refs_2_, bf16[512,512]{1,0:T(8,128)(2,1)S(1)} %collective-permute-done.6.refs_1_, ...), custom_call_target="tpu_custom_call" | custom-call | flops 1 | bytes 1 | tf_op jit(solution)/shard_map/cross/pallas_call | solution.py:222
  36.0 1.9 %cross.4 = (f32[8,128]{1,0:T(8,128)S(1)}, f32[8,128]{1,0:T(8,128)S(1)}, f32[8,128]{1,0:T(8,128)S(1)}, f32[8,128]{1,0:T(8,128)S(1)}, f32[8,128]{1,0:T(8,128)S(1)}) custom-call(bf16[528,512]{1,0:T(8,128)(2,1)S(1)} %collective-permute-done.refs_0_.refs_1_, bf16[528,512]{1,0:T(8,128)(2,1)S(1)} %collective-permute-done.refs_0_.refs_1_, ...), custom_call_target="tpu_custom_call" | custom-call | flops 1 | bytes 1 | tf_op jit(solution)/shard_map/cross/pallas_call | solution.py:222
  37.9 2.2 %collective-permute-done.1.refs_1_ = bf16[256,512]{1,0:T(8,128)(2,1)S(1)} collective-permute-done((bf16[256,512]{1,0:T(8,128)(2,1)S(1)}, bf16[256,512]{1,0:T(8,128)(2,1)S(1)}, u32[]{:S(2)}, u32[]{:S(2)}) %collective-permute-start.1) | collective-permute-done | bytes 262176 | tf_op jit(solution)/shard_map/ppermute | solution.py:253
  40.1 1.2 %cross.5 = (f32[8,128]{1,0:T(8,128)S(1)}, f32[8,128]{1,0:T(8,128)S(1)}, f32[8,128]{1,0:T(8,128)S(1)}, f32[8,128]{1,0:T(8,128)S(1)}, f32[8,128]{1,0:T(8,128)S(1)}) custom-call(bf16[528,512]{1,0:T(8,128)(2,1)S(1)} %collective-permute-done.refs_0_.refs_1_, bf16[256,512]{1,0:T(8,128)(2,1)S(1)} %collective-permute-done.1.refs_1_, ...), custom_call_target="tpu_custom_call" | custom-call | flops 1 | bytes 1 | tf_op jit(solution)/shard_map/cross/pallas_call | solution.py:222
  41.3 1.3 %collective-permute-start.11 = (f32[8,128]{1,0:T(8,128)S(1)}, f32[8,128]{1,0:T(8,128)S(1)}, u32[]{:S(2)}, u32[]{:S(2)}) collective-permute-start(f32[8,128]{1,0:T(8,128)S(1)} %get-tuple-element.44), channel_id=1, source_target_pairs={{12,0},{13,1},{14,2},{15,3},{4,8},{5,9},{6,10},{7,11},{28,16},{29,... | collective-permute-start | bytes 12296 | tf_op jit(solution)/shard_map/ppermute | solution.py:287
  42.7 1.6 %collective-permute-start.13 = (f32[8,128]{1,0:T(8,128)S(1)}, f32[8,128]{1,0:T(8,128)S(1)}, u32[]{:S(2)}, u32[]{:S(2)}) collective-permute-start(f32[8,128]{1,0:T(8,128)S(1)} %get-tuple-element.48), channel_id=1, source_target_pairs={{0,2},{1,3},{2,0},{3,1},{4,6},{5,7},{6,4},{7,5},{8,10},{9,11},{10,... | collective-permute-start | bytes 12296 | tf_op jit(solution)/shard_map/ppermute | solution.py:245
  44.2 0.3 collective-permute-start.12
  44.5 4.0 %collective-permute-done.11 = f32[8,128]{1,0:T(8,128)S(1)} collective-permute-done((f32[8,128]{1,0:T(8,128)S(1)}, f32[8,128]{1,0:T(8,128)S(1)}, u32[]{:S(2)}, u32[]{:S(2)}) %collective-permute-start.11) | collective-permute-done | bytes 4128 | tf_op jit(solution)/shard_map/ppermute | solution.py:287
  48.6 0.6 %maximum_bitcast_fusion = f32[768]{0:T(1024)} fusion(f32[8,128]{1,0:T(8,128)S(1)} %collective-permute-done.14, f32[8,128]{1,0:T(8,128)S(1)} %collective-permute-done.13, f32[8,128]{1,0:T(8,128)S(1)} %collective-permute-done.12, f32[8,128]{1,0:T(8,128)S(1)} %collective-permute-done.11, f32[8,128]{1,0:T(8,128)S(1)} %collective-permute-done.10, ...), kind=kLoop, calls=%fused_computation | loop fusion | flops 4608 | bytes 21505 | tf_op jit(solution)/shard_map/max | solution.py:297
  (27 shorter events, 0.3 us)
Async XLA Ops:
  0.0 1.4 %copy-start = (f32[768,512]{1,0:T(8,128)S(1)}, f32[768,512]{1,0:T(8,128)}, u32[]{:S(2)}) copy-start(f32[768,512]{1,0:T(8,128)} %embeddings_ref.3) | copy-start | bytes 4718596
  1.4 5.8 %copy-start.2 = (s32[768]{0:T(1024)S(1)}, s32[768]{0:T(1024)}, u32[]{:S(2)}) copy-start(s32[768]{0:T(1024)} %param.5) | copy-start | bytes 9220
  1.4 5.8 %copy-start.3 = (s32[768]{0:T(1024)S(1)}, s32[768]{0:T(1024)}, u32[]{:S(2)}) copy-start(s32[768]{0:T(1024)} %param.6) | copy-start | bytes 9220
  1.4 5.8 %copy-start.4 = (s32[16]{0:T(128)S(1)}, s32[16]{0:T(128)}, u32[]{:S(2)}) copy-start(s32[16]{0:T(128)} %param.7) | copy-start | bytes 196
  1.4 5.9 %copy-start.1 = (f32[768,512]{1,0:T(8,128)S(1)}, f32[768,512]{1,0:T(8,128)}, u32[]{:S(2)}) copy-start(f32[768,512]{1,0:T(8,128)} %embeddings_ref.3) | copy-start | bytes 4718596
  1.6 23.4 %collective-permute-start.6 = (bf16[512,512]{1,0:T(8,128)(2,1)S(1)}, bf16[512,512]{1,0:T(8,128)(2,1)S(1)}, u32[]{:S(2)}, u32[]{:S(2)}) collective-permute-start(bf16[512,512]{1,0:T(8,128)(2,1)S(1)} %first.1.first_ref.refs_0_.refs_2_.refs_3_), channel_id=1, source_target_pairs={{0,8},{1,9},{2,10},{3,11},{4,0},{5,1},{6,2},{7,3},{8,12},{9,13},{1... | collective-permute-start | bytes 1572872 | tf_op jit(solution)/shard_map/ppermute | solution.py:253
  5.7 19.4 %collective-permute-start.4 = (bf16[512,512]{1,0:T(8,128)(2,1)S(1)}, bf16[512,512]{1,0:T(8,128)(2,1)S(1)}, u32[]{:S(2)}, u32[]{:S(2)}) collective-permute-start(bf16[512,512]{1,0:T(8,128)(2,1)S(1)} %first.1.first_ref.refs_0_.refs_2_.refs_3_), channel_id=1, source_target_pairs={{0,2},{1,3},{2,0},{3,1},{4,6},{5,7},{6,4},{7,5},{8,10},{9,11},{10,... | collective-permute-start | bytes 1572872 | tf_op jit(solution)/shard_map/ppermute | solution.py:245
  7.4 17.6 %collective-permute-start.5 = (bf16[272,512]{1,0:T(8,128)(2,1)S(1)}, bf16[272,512]{1,0:T(8,128)(2,1)S(1)}, u32[]{:S(2)}, u32[]{:S(2)}) collective-permute-start(bf16[272,512]{1,0:T(8,128)(2,1)S(1)} %get-tuple-element.30.refs_1_.refs_3_.refs_4_), channel_id=1, source_target_pairs={{0,2},{1,3},{2,0},{3,1},{4,6},{5,7},{6,4},{7,5},{8,10},{9,11},{10,... | collective-permute-start | bytes 835592 | tf_op jit(solution)/shard_map/ppermute | solution.py:245
  8.0 17.0 %collective-permute-start.7 = (bf16[272,512]{1,0:T(8,128)(2,1)S(1)}, bf16[272,512]{1,0:T(8,128)(2,1)S(1)}, u32[]{:S(2)}, u32[]{:S(2)}) collective-permute-start(bf16[272,512]{1,0:T(8,128)(2,1)S(1)} %get-tuple-element.30.refs_1_.refs_3_.refs_4_), channel_id=1, source_target_pairs={{0,8},{1,9},{2,10},{3,11},{4,0},{5,1},{6,2},{7,3},{8,12},{9,13},{1... | collective-permute-start | bytes 835592 | tf_op jit(solution)/shard_map/ppermute | solution.py:253
  9.6 26.4 %collective-permute-start = (bf16[528,512]{1,0:T(8,128)(2,1)S(1)}, bf16[528,512]{1,0:T(8,128)(2,1)S(1)}, u32[]{:S(2)}, u32[]{:S(2)}) collective-permute-start(bf16[528,512]{1,0:T(8,128)(2,1)S(1)} %get-tuple-element.28), channel_id=1, source_target_pairs={{0,12},{1,13},{2,14},{3,15},{8,4},{9,5},{10,6},{11,7},{16,28},{17,... | collective-permute-start | bytes 1622024 | tf_op jit(solution)/shard_map/ppermute | solution.py:253
  25.0 1.6 %collective-permute-start.9 = (bf16[272,512]{1,0:T(8,128)(2,1)S(1)}, bf16[272,512]{1,0:T(8,128)(2,1)S(1)}, u32[]{:S(2)}, u32[]{:S(2)}) collective-permute-start(bf16[272,512]{1,0:T(8,128)(2,1)S(1)} %collective-permute-done.5.refs_3_.refs_8_.refs_7_), channel_id=1, source_target_pairs={{0,1},{1,0},{2,3},{3,2},{4,5},{5,4},{6,7},{7,6},{8,9},{9,8},{10,11... | collective-permute-start | bytes 835592 | tf_op jit(solution)/shard_map/ppermute | solution.py:245
  25.1 5.1 %collective-permute-start.8 = (bf16[512,512]{1,0:T(8,128)(2,1)S(1)}, bf16[512,512]{1,0:T(8,128)(2,1)S(1)}, u32[]{:S(2)}, u32[]{:S(2)}) collective-permute-start(bf16[512,512]{1,0:T(8,128)(2,1)S(1)} %collective-permute-done.4.refs_2_.refs_7_.refs_6_), channel_id=1, source_target_pairs={{0,1},{1,0},{2,3},{3,2},{4,5},{5,4},{6,7},{7,6},{8,9},{9,8},{10,11... | collective-permute-start | bytes 1572872 | tf_op jit(solution)/shard_map/ppermute | solution.py:245
  25.6 6.1 %collective-permute-start.2 = (bf16[512,512]{1,0:T(8,128)(2,1)S(1)}, bf16[512,512]{1,0:T(8,128)(2,1)S(1)}, u32[]{:S(2)}, u32[]{:S(2)}) collective-permute-start(bf16[512,512]{1,0:T(8,128)(2,1)S(1)} %first.1.first_ref.refs_0_.refs_2_.refs_3_), channel_id=1, source_target_pairs={{0,1},{1,0},{2,3},{3,2},{4,5},{5,4},{6,7},{7,6},{8,9},{9,8},{10,11... | collective-permute-start | bytes 1572872 | tf_op jit(solution)/shard_map/ppermute | solution.py:245
  25.6 6.0 %collective-permute-start.3 = (bf16[272,512]{1,0:T(8,128)(2,1)S(1)}, bf16[272,512]{1,0:T(8,128)(2,1)S(1)}, u32[]{:S(2)}, u32[]{:S(2)}) collective-permute-start(bf16[272,512]{1,0:T(8,128)(2,1)S(1)} %get-tuple-element.30.refs_1_.refs_3_.refs_4_), channel_id=1, source_target_pairs={{0,1},{1,0},{2,3},{3,2},{4,5},{5,4},{6,7},{7,6},{8,9},{9,8},{10,11... | collective-permute-start | bytes 835592 | tf_op jit(solution)/shard_map/ppermute | solution.py:245
  26.6 13.5 %collective-permute-start.1 = (bf16[256,512]{1,0:T(8,128)(2,1)S(1)}, bf16[256,512]{1,0:T(8,128)(2,1)S(1)}, u32[]{:S(2)}, u32[]{:S(2)}) collective-permute-start(bf16[256,512]{1,0:T(8,128)(2,1)S(1)} %get-tuple-element.29), channel_id=1, source_target_pairs={{0,12},{1,13},{2,14},{3,15},{8,4},{9,5},{10,6},{11,7},{16,28},{17,... | collective-permute-start | bytes 786440 | tf_op jit(solution)/shard_map/ppermute | solution.py:253
  35.9 6.7 %collective-permute-start.10 = (f32[8,128]{1,0:T(8,128)S(1)}, f32[8,128]{1,0:T(8,128)S(1)}, u32[]{:S(2)}, u32[]{:S(2)}) collective-permute-start(f32[8,128]{1,0:T(8,128)S(1)} %get-tuple-element.43), channel_id=1, source_target_pairs={{8,0},{9,1},{10,2},{11,3},{0,4},{1,5},{2,6},{3,7},{12,8},{13,9},{1... | collective-permute-start | bytes 12296 | tf_op jit(solution)/shard_map/ppermute | solution.py:287
  41.3 7.3 %collective-permute-start.11 = (f32[8,128]{1,0:T(8,128)S(1)}, f32[8,128]{1,0:T(8,128)S(1)}, u32[]{:S(2)}, u32[]{:S(2)}) collective-permute-start(f32[8,128]{1,0:T(8,128)S(1)} %get-tuple-element.44), channel_id=1, source_target_pairs={{12,0},{13,1},{14,2},{15,3},{4,8},{5,9},{6,10},{7,11},{28,16},{29,... | collective-permute-start | bytes 12296 | tf_op jit(solution)/shard_map/ppermute | solution.py:287
  42.6 6.0 %collective-permute-start.14 = (f32[8,128]{1,0:T(8,128)S(1)}, f32[8,128]{1,0:T(8,128)S(1)}, u32[]{:S(2)}, u32[]{:S(2)}) collective-permute-start(f32[8,128]{1,0:T(8,128)S(1)} %get-tuple-element.50), channel_id=1, source_target_pairs={{0,1},{1,0},{2,3},{3,2},{4,5},{5,4},{6,7},{7,6},{8,9},{9,8},{10,11... | collective-permute-start | bytes 12296 | tf_op jit(solution)/shard_map/ppermute | solution.py:245
  42.7 5.9 %collective-permute-start.13 = (f32[8,128]{1,0:T(8,128)S(1)}, f32[8,128]{1,0:T(8,128)S(1)}, u32[]{:S(2)}, u32[]{:S(2)}) collective-permute-start(f32[8,128]{1,0:T(8,128)S(1)} %get-tuple-element.48), channel_id=1, source_target_pairs={{0,2},{1,3},{2,0},{3,1},{4,6},{5,7},{6,4},{7,5},{8,10},{9,11},{10,... | collective-permute-start | bytes 12296 | tf_op jit(solution)/shard_map/ppermute | solution.py:245
  44.2 4.3 %collective-permute-start.12 = (f32[8,128]{1,0:T(8,128)S(1)}, f32[8,128]{1,0:T(8,128)S(1)}, u32[]{:S(2)}, u32[]{:S(2)}) collective-permute-start(f32[8,128]{1,0:T(8,128)S(1)} %get-tuple-element.46), channel_id=1, source_target_pairs={{0,3},{1,2},{2,1},{3,0},{4,7},{5,6},{6,5},{7,4},{8,11},{9,10},{10,... | collective-permute-start | bytes 12296 | tf_op jit(solution)/shard_map/ppermute | solution.py:245

commit v15 on v14

--- a/solution.py
+++ b/solution.py
@@ -196,7 +196,7 @@
 
 def plane_steps(planes):
     if planes == 4:
-        return [[(0, 2), (1, 0), (2, 3), (3, 1)], [(0, 3), (2, 1)]]
+        return [[(0, 2), (1, 0), (2, 3), (3, 1)], [(3, 0), (1, 2)]]
     return [
         [(z, (z + distance) % planes) for z in range(planes)]
         for distance in range(1, planes // 2 + 1)

time: 49.4 us -> 50 us (1.012)
  waiting for transfers between devices: 19.9 us -> 21 us
    ppermute x2, waiting for transfers between devices: 4.05 us -> 0.01 us  [local(): backs.append(lax.ppermute(away_best, 'dp', [(t, s) for s, t in pairs]))]
    ppermute x9, waiting for transfers between devices: 13.7 us -> 17.4 us  [mate(): return lax.ppermute(value, 'dp', [(i, i ^ distance) for i in range(peers)])]
    ppermute x4, starting transfers between devices: 11.5 us -> 8.23 us  [local(): away.append((pairs, [lax.ppermute(part, 'dp', pairs) for part in parts]))]
    ppermute x2, starting transfers between devices: 1.35 us -> 4.26 us  [local(): backs.append(lax.ppermute(away_best, 'dp', [(t, s) for s, t in pairs]))]
    ppermute x4, waiting for transfers between devices: 2.19 us -> 3.54 us  [local(): away.append((pairs, [lax.ppermute(part, 'dp', pairs) for part in parts]))]
  transfers between devices with their start and end apart: 15 -> 15, of which waited for: 4 -> 6; matrix products, arithmetic and copies ran while one was open for 0% -> 0% of each run, Pallas kernels for 18% -> 18%
where the time goes in v15:
time: 50 us; the launch traced here: 49.8 us
  waiting for transfers between devices  21 us (42%)
  starting transfers between devices  17.5 us (35%)
  Pallas kernels  9.08 us (18%)
  local copies, waits for them, and re-layouts  1.51 us (3%)
  other arithmetic  0.6 us (1%)
    ppermute x9, waiting for transfers between devices, mate(): return lax.ppermute(value, 'dp', [(i, i ^ distance) for i in range(peers)])  17.4 us
    pallas_call x7, Pallas kernels, kernel(): pl.pallas_call(body, out_shape=tuple(outputs), in_specs=whole(len(inputs)...  9.08 us
    ppermute x4, starting transfers between devices, local(): away.append((pairs, [lax.ppermute(part, 'dp', pairs) for part in parts]))  8.23 us
    ppermute x9, starting transfers between devices, mate(): return lax.ppermute(value, 'dp', [(i, i ^ distance) for i in range(peers)])  5.03 us
    ppermute x2, starting transfers between devices, local(): backs.append(lax.ppermute(away_best, 'dp', [(t, s) for s, t in pairs]))  4.26 us
    ppermute x4, waiting for transfers between devices, local(): away.append((pairs, [lax.ppermute(part, 'dp', pairs) for part in parts]))  3.54 us
    unnamed x10, local copies, waits for them, and re-layouts  1.42 us
  transfers between devices with their start and end apart: 15, of which 6 were waited for; matrix products, arithmetic and copies ran while one was open for 0% of the time, Pallas kernels for 18%

profile of v15, /device:TPU:0, one launch (start us, length us, event | category | flops | bytes accessed | tf_op | source)
XLA Modules:
  0.0 49.8 jit_solution(8848479388843944663)
XLA Ops:
  0.0 1.4 %copy-done = f32[768,512]{1,0:T(8,128)S(1)} copy-done((f32[768,512]{1,0:T(8,128)S(1)}, f32[768,512]{1,0:T(8,128)}, u32[]{:S(2)}) %copy-start) | copy-done | bytes 1572888
  1.6 4.1 %collective-permute-start.6 = (bf16[512,512]{1,0:T(8,128)(2,1)S(1)}, bf16[512,512]{1,0:T(8,128)(2,1)S(1)}, u32[]{:S(2)}, u32[]{:S(2)}) collective-permute-start(bf16[512,512]{1,0:T(8,128)(2,1)S(1)} %first.1.first_ref.refs_0_.refs_2_.refs_3_), channel_id=1, source_target_pairs={{0,8},{1,9},{2,10},{3,11},{4,0},{5,1},{6,2},{7,3},{8,12},{9,13},{1... | collective-permute-start | bytes 1572872 | tf_op jit(solution)/shard_map/ppermute | solution.py:253
  5.7 1.5 %collective-permute-start.4 = (bf16[512,512]{1,0:T(8,128)(2,1)S(1)}, bf16[512,512]{1,0:T(8,128)(2,1)S(1)}, u32[]{:S(2)}, u32[]{:S(2)}) collective-permute-start(bf16[512,512]{1,0:T(8,128)(2,1)S(1)} %first.1.first_ref.refs_0_.refs_2_.refs_3_), channel_id=1, source_target_pairs={{0,2},{1,3},{2,0},{3,1},{4,6},{5,7},{6,4},{7,5},{8,10},{9,11},{10,... | collective-permute-start | bytes 1572872 | tf_op jit(solution)/shard_map/ppermute | solution.py:245
  7.4 0.6 %collective-permute-start.5 = (bf16[272,512]{1,0:T(8,128)(2,1)S(1)}, bf16[272,512]{1,0:T(8,128)(2,1)S(1)}, u32[]{:S(2)}, u32[]{:S(2)}) collective-permute-start(bf16[272,512]{1,0:T(8,128)(2,1)S(1)} %get-tuple-element.30.refs_1_.refs_3_.refs_4_), channel_id=1, source_target_pairs={{0,2},{1,3},{2,0},{3,1},{4,6},{5,7},{6,4},{7,5},{8,10},{9,11},{10,... | collective-permute-start | bytes 835592 | tf_op jit(solution)/shard_map/ppermute | solution.py:245
  8.0 1.6 %collective-permute-start.7 = (bf16[272,512]{1,0:T(8,128)(2,1)S(1)}, bf16[272,512]{1,0:T(8,128)(2,1)S(1)}, u32[]{:S(2)}, u32[]{:S(2)}) collective-permute-start(bf16[272,512]{1,0:T(8,128)(2,1)S(1)} %get-tuple-element.30.refs_1_.refs_3_.refs_4_), channel_id=1, source_target_pairs={{0,8},{1,9},{2,10},{3,11},{4,0},{5,1},{6,2},{7,3},{8,12},{9,13},{1... | collective-permute-start | bytes 835592 | tf_op jit(solution)/shard_map/ppermute | solution.py:253
  9.6 1.3 %collective-permute-start = (bf16[528,512]{1,0:T(8,128)(2,1)S(1)}, bf16[528,512]{1,0:T(8,128)(2,1)S(1)}, u32[]{:S(2)}, u32[]{:S(2)}) collective-permute-start(bf16[528,512]{1,0:T(8,128)(2,1)S(1)} %get-tuple-element.28), channel_id=1, source_target_pairs={{12,0},{13,1},{14,2},{15,3},{4,8},{5,9},{6,10},{7,11},{28,16},{29,... | collective-permute-start | bytes 1622024 | tf_op jit(solution)/shard_map/ppermute | solution.py:253
  10.9 14.1 %collective-permute-done.5.refs_3_.refs_8_.refs_7_ = bf16[272,512]{1,0:T(8,128)(2,1)S(1)} collective-permute-done((bf16[272,512]{1,0:T(8,128)(2,1)S(1)}, bf16[272,512]{1,0:T(8,128)(2,1)S(1)}, u32[]{:S(2)}, u32[]{:S(2)}) %collective-permute-start.5) | collective-permute-done | bytes 278560 | tf_op jit(solution)/shard_map/ppermute | solution.py:245
  25.1 0.5 collective-permute-start.8
  25.6 0.4 collective-permute-start.3
  26.1 0.5 %collective-permute-done.9.refs_5_.refs_10_.refs_9_ = bf16[272,512]{1,0:T(8,128)(2,1)S(1)} collective-permute-done((bf16[272,512]{1,0:T(8,128)(2,1)S(1)}, bf16[272,512]{1,0:T(8,128)(2,1)S(1)}, u32[]{:S(2)}, u32[]{:S(2)}) %collective-permute-start.9) | collective-permute-done | bytes 278560 | tf_op jit(solution)/shard_map/ppermute | solution.py:245
  26.6 1.3 %collective-permute-start.1 = (bf16[256,512]{1,0:T(8,128)(2,1)S(1)}, bf16[256,512]{1,0:T(8,128)(2,1)S(1)}, u32[]{:S(2)}, u32[]{:S(2)}) collective-permute-start(bf16[256,512]{1,0:T(8,128)(2,1)S(1)} %get-tuple-element.29), channel_id=1, source_target_pairs={{12,0},{13,1},{14,2},{15,3},{4,8},{5,9},{6,10},{7,11},{28,16},{29,... | collective-permute-start | bytes 786440 | tf_op jit(solution)/shard_map/ppermute | solution.py:253
  27.9 1.4 %plane_far.1.refs_6_ = f32[8,128]{1,0:T(8,128)S(1)} custom-call(bf16[512,512]{1,0:T(8,128)(2,1)S(1)} %first.1.first_ref.refs_0_.refs_2_.refs_3_, bf16[272,512]{1,0:T(8,128)(2,1)S(1)} %get-tuple-element.30.refs_1_.refs_3_.refs_4_, bf16[512,512]{1,0:T(8,128)(2,1)S(1)} %collective-permute-done.4.refs_2_.refs_7_.refs_6_, ...), custom_call_target="tpu_custom_call" | custom-call | flops 1 | bytes 1 | tf_op jit(solution)/shard_map/plane_far/pallas_call | solution.py:222
  29.4 1.4 %plane_near.1.refs_12_ = f32[8,128]{1,0:T(8,128)S(1)} custom-call(bf16[512,512]{1,0:T(8,128)(2,1)S(1)} %first.1.first_ref.refs_0_.refs_2_.refs_3_, bf16[272,512]{1,0:T(8,128)(2,1)S(1)} %get-tuple-element.30.refs_1_.refs_3_.refs_4_, bf16[512,512]{1,0:T(8,128)(2,1)S(1)} %first.1.first_ref.refs_0_.refs_2_.refs_3_, ...), custom_call_target="tpu_custom_call" | custom-call | flops 1 | bytes 1 | tf_op jit(solution)/shard_map/plane_near/pallas_call | solution.py:222
  30.8 2.8 %cross.3 = (f32[8,128]{1,0:T(8,128)S(1)}, f32[8,128]{1,0:T(8,128)S(1)}, f32[8,128]{1,0:T(8,128)S(1)}, f32[8,128]{1,0:T(8,128)S(1)}, f32[8,128]{1,0:T(8,128)S(1)}) custom-call(bf16[272,512]{1,0:T(8,128)(2,1)S(1)} %collective-permute-done.7.refs_0_.refs_2_, bf16[512,512]{1,0:T(8,128)(2,1)S(1)} %collective-permute-done.6.refs_1_, ...), custom_call_target="tpu_custom_call" | custom-call | flops 1 | bytes 1 | tf_op jit(solution)/shard_map/cross/pallas_call | solution.py:222
  33.6 2.8 %collective-permute-start.10 = (f32[8,128]{1,0:T(8,128)S(1)}, f32[8,128]{1,0:T(8,128)S(1)}, u32[]{:S(2)}, u32[]{:S(2)}) collective-permute-start(f32[8,128]{1,0:T(8,128)S(1)} %get-tuple-element.43), channel_id=1, source_target_pairs={{8,0},{9,1},{10,2},{11,3},{0,4},{1,5},{2,6},{3,7},{12,8},{13,9},{1... | collective-permute-start | bytes 12296 | tf_op jit(solution)/shard_map/ppermute | solution.py:287
  36.5 0.9 %collective-permute-done.refs_0_.refs_1_ = bf16[528,512]{1,0:T(8,128)(2,1)S(1)} collective-permute-done((bf16[528,512]{1,0:T(8,128)(2,1)S(1)}, bf16[528,512]{1,0:T(8,128)(2,1)S(1)}, u32[]{:S(2)}, u32[]{:S(2)}) %collective-permute-start) | collective-permute-done | bytes 540704 | tf_op jit(solution)/shard_map/ppermute | solution.py:253
  37.4 1.9 %cross.4 = (f32[8,128]{1,0:T(8,128)S(1)}, f32[8,128]{1,0:T(8,128)S(1)}, f32[8,128]{1,0:T(8,128)S(1)}, f32[8,128]{1,0:T(8,128)S(1)}, f32[8,128]{1,0:T(8,128)S(1)}) custom-call(bf16[528,512]{1,0:T(8,128)(2,1)S(1)} %collective-permute-done.refs_0_.refs_1_, bf16[528,512]{1,0:T(8,128)(2,1)S(1)} %collective-permute-done.refs_0_.refs_1_, ...), custom_call_target="tpu_custom_call" | custom-call | flops 1 | bytes 1 | tf_op jit(solution)/shard_map/cross/pallas_call | solution.py:222
  39.3 2.6 %collective-permute-done.1.refs_1_ = bf16[256,512]{1,0:T(8,128)(2,1)S(1)} collective-permute-done((bf16[256,512]{1,0:T(8,128)(2,1)S(1)}, bf16[256,512]{1,0:T(8,128)(2,1)S(1)}, u32[]{:S(2)}, u32[]{:S(2)}) %collective-permute-start.1) | collective-permute-done | bytes 262176 | tf_op jit(solution)/shard_map/ppermute | solution.py:253
  41.9 1.2 %cross.5 = (f32[8,128]{1,0:T(8,128)S(1)}, f32[8,128]{1,0:T(8,128)S(1)}, f32[8,128]{1,0:T(8,128)S(1)}, f32[8,128]{1,0:T(8,128)S(1)}, f32[8,128]{1,0:T(8,128)S(1)}) custom-call(bf16[528,512]{1,0:T(8,128)(2,1)S(1)} %collective-permute-done.refs_0_.refs_1_, bf16[256,512]{1,0:T(8,128)(2,1)S(1)} %collective-permute-done.1.refs_1_, ...), custom_call_target="tpu_custom_call" | custom-call | flops 1 | bytes 1 | tf_op jit(solution)/shard_map/cross/pallas_call | solution.py:222
  43.1 1.4 %collective-permute-start.11 = (f32[8,128]{1,0:T(8,128)S(1)}, f32[8,128]{1,0:T(8,128)S(1)}, u32[]{:S(2)}, u32[]{:S(2)}) collective-permute-start(f32[8,128]{1,0:T(8,128)S(1)} %get-tuple-element.44), channel_id=1, source_target_pairs={{0,12},{1,13},{2,14},{3,15},{8,4},{9,5},{10,6},{11,7},{16,28},{17,... | collective-permute-start | bytes 12296 | tf_op jit(solution)/shard_map/ppermute | solution.py:287
  44.6 1.6 %collective-permute-start.13 = (f32[8,128]{1,0:T(8,128)S(1)}, f32[8,128]{1,0:T(8,128)S(1)}, u32[]{:S(2)}, u32[]{:S(2)}) collective-permute-start(f32[8,128]{1,0:T(8,128)S(1)} %get-tuple-element.48), channel_id=1, source_target_pairs={{0,2},{1,3},{2,0},{3,1},{4,6},{5,7},{6,4},{7,5},{8,10},{9,11},{10,... | collective-permute-start | bytes 12296 | tf_op jit(solution)/shard_map/ppermute | solution.py:245
  46.5 1.8 %collective-permute-done.13 = f32[8,128]{1,0:T(8,128)S(1)} collective-permute-done((f32[8,128]{1,0:T(8,128)S(1)}, f32[8,128]{1,0:T(8,128)S(1)}, u32[]{:S(2)}, u32[]{:S(2)}) %collective-permute-start.13) | collective-permute-done | bytes 4128 | tf_op jit(solution)/shard_map/ppermute | solution.py:245
  48.3 0.9 %collective-permute-done.12 = f32[8,128]{1,0:T(8,128)S(1)} collective-permute-done((f32[8,128]{1,0:T(8,128)S(1)}, f32[8,128]{1,0:T(8,128)S(1)}, u32[]{:S(2)}, u32[]{:S(2)}) %collective-permute-start.12) | collective-permute-done | bytes 4128 | tf_op jit(solution)/shard_map/ppermute | solution.py:245
  49.2 0.6 %maximum_bitcast_fusion = f32[768]{0:T(1024)} fusion(f32[8,128]{1,0:T(8,128)S(1)} %collective-permute-done.14, f32[8,128]{1,0:T(8,128)S(1)} %collective-permute-done.13, f32[8,128]{1,0:T(8,128)S(1)} %collective-permute-done.12, f32[8,128]{1,0:T(8,128)S(1)} %collective-permute-done.11, f32[8,128]{1,0:T(8,128)S(1)} %collective-permute-done.10, ...), kind=kLoop, calls=%fused_computation | loop fusion | flops 4608 | bytes 21505 | tf_op jit(solution)/shard_map/max | solution.py:297
  (27 shorter events, 0.9 us)
Async XLA Ops:
  0.0 1.4 %copy-start = (f32[768,512]{1,0:T(8,128)S(1)}, f32[768,512]{1,0:T(8,128)}, u32[]{:S(2)}) copy-start(f32[768,512]{1,0:T(8,128)} %embeddings_ref.3) | copy-start | bytes 4718596
  1.4 5.8 %copy-start.2 = (s32[768]{0:T(1024)S(1)}, s32[768]{0:T(1024)}, u32[]{:S(2)}) copy-start(s32[768]{0:T(1024)} %param.5) | copy-start | bytes 9220
  1.4 5.8 %copy-start.3 = (s32[768]{0:T(1024)S(1)}, s32[768]{0:T(1024)}, u32[]{:S(2)}) copy-start(s32[768]{0:T(1024)} %param.6) | copy-start | bytes 9220
  1.4 5.8 %copy-start.4 = (s32[16]{0:T(128)S(1)}, s32[16]{0:T(128)}, u32[]{:S(2)}) copy-start(s32[16]{0:T(128)} %param.7) | copy-start | bytes 196
  1.4 5.9 %copy-start.1 = (f32[768,512]{1,0:T(8,128)S(1)}, f32[768,512]{1,0:T(8,128)}, u32[]{:S(2)}) copy-start(f32[768,512]{1,0:T(8,128)} %embeddings_ref.3) | copy-start | bytes 4718596
  1.6 23.4 %collective-permute-start.6 = (bf16[512,512]{1,0:T(8,128)(2,1)S(1)}, bf16[512,512]{1,0:T(8,128)(2,1)S(1)}, u32[]{:S(2)}, u32[]{:S(2)}) collective-permute-start(bf16[512,512]{1,0:T(8,128)(2,1)S(1)} %first.1.first_ref.refs_0_.refs_2_.refs_3_), channel_id=1, source_target_pairs={{0,8},{1,9},{2,10},{3,11},{4,0},{5,1},{6,2},{7,3},{8,12},{9,13},{1... | collective-permute-start | bytes 1572872 | tf_op jit(solution)/shard_map/ppermute | solution.py:253
  5.7 19.4 %collective-permute-start.4 = (bf16[512,512]{1,0:T(8,128)(2,1)S(1)}, bf16[512,512]{1,0:T(8,128)(2,1)S(1)}, u32[]{:S(2)}, u32[]{:S(2)}) collective-permute-start(bf16[512,512]{1,0:T(8,128)(2,1)S(1)} %first.1.first_ref.refs_0_.refs_2_.refs_3_), channel_id=1, source_target_pairs={{0,2},{1,3},{2,0},{3,1},{4,6},{5,7},{6,4},{7,5},{8,10},{9,11},{10,... | collective-permute-start | bytes 1572872 | tf_op jit(solution)/shard_map/ppermute | solution.py:245
  7.4 17.6 %collective-permute-start.5 = (bf16[272,512]{1,0:T(8,128)(2,1)S(1)}, bf16[272,512]{1,0:T(8,128)(2,1)S(1)}, u32[]{:S(2)}, u32[]{:S(2)}) collective-permute-start(bf16[272,512]{1,0:T(8,128)(2,1)S(1)} %get-tuple-element.30.refs_1_.refs_3_.refs_4_), channel_id=1, source_target_pairs={{0,2},{1,3},{2,0},{3,1},{4,6},{5,7},{6,4},{7,5},{8,10},{9,11},{10,... | collective-permute-start | bytes 835592 | tf_op jit(solution)/shard_map/ppermute | solution.py:245
  8.0 17.0 %collective-permute-start.7 = (bf16[272,512]{1,0:T(8,128)(2,1)S(1)}, bf16[272,512]{1,0:T(8,128)(2,1)S(1)}, u32[]{:S(2)}, u32[]{:S(2)}) collective-permute-start(bf16[272,512]{1,0:T(8,128)(2,1)S(1)} %get-tuple-element.30.refs_1_.refs_3_.refs_4_), channel_id=1, source_target_pairs={{0,8},{1,9},{2,10},{3,11},{4,0},{5,1},{6,2},{7,3},{8,12},{9,13},{1... | collective-permute-start | bytes 835592 | tf_op jit(solution)/shard_map/ppermute | solution.py:253
  9.6 27.8 %collective-permute-start = (bf16[528,512]{1,0:T(8,128)(2,1)S(1)}, bf16[528,512]{1,0:T(8,128)(2,1)S(1)}, u32[]{:S(2)}, u32[]{:S(2)}) collective-permute-start(bf16[528,512]{1,0:T(8,128)(2,1)S(1)} %get-tuple-element.28), channel_id=1, source_target_pairs={{12,0},{13,1},{14,2},{15,3},{4,8},{5,9},{6,10},{7,11},{28,16},{29,... | collective-permute-start | bytes 1622024 | tf_op jit(solution)/shard_map/ppermute | solution.py:253
  25.0 1.6 %collective-permute-start.9 = (bf16[272,512]{1,0:T(8,128)(2,1)S(1)}, bf16[272,512]{1,0:T(8,128)(2,1)S(1)}, u32[]{:S(2)}, u32[]{:S(2)}) collective-permute-start(bf16[272,512]{1,0:T(8,128)(2,1)S(1)} %collective-permute-done.5.refs_3_.refs_8_.refs_7_), channel_id=1, source_target_pairs={{0,1},{1,0},{2,3},{3,2},{4,5},{5,4},{6,7},{7,6},{8,9},{9,8},{10,11... | collective-permute-start | bytes 835592 | tf_op jit(solution)/shard_map/ppermute | solution.py:245
  25.1 2.8 %collective-permute-start.8 = (bf16[512,512]{1,0:T(8,128)(2,1)S(1)}, bf16[512,512]{1,0:T(8,128)(2,1)S(1)}, u32[]{:S(2)}, u32[]{:S(2)}) collective-permute-start(bf16[512,512]{1,0:T(8,128)(2,1)S(1)} %collective-permute-done.4.refs_2_.refs_7_.refs_6_), channel_id=1, source_target_pairs={{0,1},{1,0},{2,3},{3,2},{4,5},{5,4},{6,7},{7,6},{8,9},{9,8},{10,11... | collective-permute-start | bytes 1572872 | tf_op jit(solution)/shard_map/ppermute | solution.py:245
  25.6 3.8 %collective-permute-start.2 = (bf16[512,512]{1,0:T(8,128)(2,1)S(1)}, bf16[512,512]{1,0:T(8,128)(2,1)S(1)}, u32[]{:S(2)}, u32[]{:S(2)}) collective-permute-start(bf16[512,512]{1,0:T(8,128)(2,1)S(1)} %first.1.first_ref.refs_0_.refs_2_.refs_3_), channel_id=1, source_target_pairs={{0,1},{1,0},{2,3},{3,2},{4,5},{5,4},{6,7},{7,6},{8,9},{9,8},{10,11... | collective-permute-start | bytes 1572872 | tf_op jit(solution)/shard_map/ppermute | solution.py:245
  25.6 3.7 %collective-permute-start.3 = (bf16[272,512]{1,0:T(8,128)(2,1)S(1)}, bf16[272,512]{1,0:T(8,128)(2,1)S(1)}, u32[]{:S(2)}, u32[]{:S(2)}) collective-permute-start(bf16[272,512]{1,0:T(8,128)(2,1)S(1)} %get-tuple-element.30.refs_1_.refs_3_.refs_4_), channel_id=1, source_target_pairs={{0,1},{1,0},{2,3},{3,2},{4,5},{5,4},{6,7},{7,6},{8,9},{9,8},{10,11... | collective-permute-start | bytes 835592 | tf_op jit(solution)/shard_map/ppermute | solution.py:245
  26.6 15.3 %collective-permute-start.1 = (bf16[256,512]{1,0:T(8,128)(2,1)S(1)}, bf16[256,512]{1,0:T(8,128)(2,1)S(1)}, u32[]{:S(2)}, u32[]{:S(2)}) collective-permute-start(bf16[256,512]{1,0:T(8,128)(2,1)S(1)} %get-tuple-element.29), channel_id=1, source_target_pairs={{12,0},{13,1},{14,2},{15,3},{4,8},{5,9},{6,10},{7,11},{28,16},{29,... | collective-permute-start | bytes 786440 | tf_op jit(solution)/shard_map/ppermute | solution.py:253
  33.6 10.9 %collective-permute-start.10 = (f32[8,128]{1,0:T(8,128)S(1)}, f32[8,128]{1,0:T(8,128)S(1)}, u32[]{:S(2)}, u32[]{:S(2)}) collective-permute-start(f32[8,128]{1,0:T(8,128)S(1)} %get-tuple-element.43), channel_id=1, source_target_pairs={{8,0},{9,1},{10,2},{11,3},{0,4},{1,5},{2,6},{3,7},{12,8},{13,9},{1... | collective-permute-start | bytes 12296 | tf_op jit(solution)/shard_map/ppermute | solution.py:287
  43.1 3.4 %collective-permute-start.11 = (f32[8,128]{1,0:T(8,128)S(1)}, f32[8,128]{1,0:T(8,128)S(1)}, u32[]{:S(2)}, u32[]{:S(2)}) collective-permute-start(f32[8,128]{1,0:T(8,128)S(1)} %get-tuple-element.44), channel_id=1, source_target_pairs={{0,12},{1,13},{2,14},{3,15},{8,4},{9,5},{10,6},{11,7},{16,28},{17,... | collective-permute-start | bytes 12296 | tf_op jit(solution)/shard_map/ppermute | solution.py:287
  44.5 1.9 %collective-permute-start.14 = (f32[8,128]{1,0:T(8,128)S(1)}, f32[8,128]{1,0:T(8,128)S(1)}, u32[]{:S(2)}, u32[]{:S(2)}) collective-permute-start(f32[8,128]{1,0:T(8,128)S(1)} %get-tuple-element.50), channel_id=1, source_target_pairs={{0,1},{1,0},{2,3},{3,2},{4,5},{5,4},{6,7},{7,6},{8,9},{9,8},{10,11... | collective-permute-start | bytes 12296 | tf_op jit(solution)/shard_map/ppermute | solution.py:245
  44.6 3.7 %collective-permute-start.13 = (f32[8,128]{1,0:T(8,128)S(1)}, f32[8,128]{1,0:T(8,128)S(1)}, u32[]{:S(2)}, u32[]{:S(2)}) collective-permute-start(f32[8,128]{1,0:T(8,128)S(1)} %get-tuple-element.48), channel_id=1, source_target_pairs={{0,2},{1,3},{2,0},{3,1},{4,6},{5,7},{6,4},{7,5},{8,10},{9,11},{10,... | collective-permute-start | bytes 12296 | tf_op jit(solution)/shard_map/ppermute | solution.py:245
  46.2 3.0 %collective-permute-start.12 = (f32[8,128]{1,0:T(8,128)S(1)}, f32[8,128]{1,0:T(8,128)S(1)}, u32[]{:S(2)}, u32[]{:S(2)}) collective-permute-start(f32[8,128]{1,0:T(8,128)S(1)} %get-tuple-element.46), channel_id=1, source_target_pairs={{0,3},{1,2},{2,1},{3,0},{4,7},{5,6},{6,5},{7,4},{8,11},{9,10},{10,... | collective-permute-start | bytes 12296 | tf_op jit(solution)/shard_map/ppermute | solution.py:245

commit v16 on v15

--- a/solution.py
+++ b/solution.py
@@ -196,7 +196,7 @@
 
 def plane_steps(planes):
     if planes == 4:
-        return [[(0, 2), (1, 0), (2, 3), (3, 1)], [(3, 0), (1, 2)]]
+        return [[(0, 3), (1, 0), (2, 1), (3, 2)], [(0, 2), (3, 1)]]
     return [
         [(z, (z + distance) % planes) for z in range(planes)]
         for distance in range(1, planes // 2 + 1)

time: 50 us -> 49.5 us (0.990)
  starting transfers between devices: 17.5 us -> 15.8 us
  waiting for transfers between devices: 21 us -> 22.2 us
    ppermute x2, waiting for transfers between devices: 0.01 us -> 3.15 us  [local(): backs.append(lax.ppermute(away_best, 'dp', [(t, s) for s, t in pairs]))]
    ppermute x2, starting transfers between devices: 4.26 us -> 1.35 us  [local(): backs.append(lax.ppermute(away_best, 'dp', [(t, s) for s, t in pairs]))]
    ppermute x9, waiting for transfers between devices: 17.4 us -> 15.6 us  [mate(): return lax.ppermute(value, 'dp', [(i, i ^ distance) for i in range(peers)])]
    ppermute x4, starting transfers between devices: 8.23 us -> 9.4 us  [local(): away.append((pairs, [lax.ppermute(part, 'dp', pairs) for part in parts]))]
  transfers between devices with their start and end apart: 15 -> 15, of which waited for: 6 -> 5; matrix products, arithmetic and copies ran while one was open for 0% -> 0% of each run, Pallas kernels for 18% -> 18%
where the time goes in v16:
time: 49.5 us; the launch traced here: 49.3 us
  waiting for transfers between devices  22.2 us (45%)
  starting transfers between devices  15.8 us (32%)
  Pallas kernels  9.07 us (18%)
  local copies, waits for them, and re-layouts  1.51 us (3%)
  other arithmetic  0.6 us (1%)
    ppermute x9, waiting for transfers between devices, mate(): return lax.ppermute(value, 'dp', [(i, i ^ distance) for i in range(peers)])  15.6 us
    ppermute x4, starting transfers between devices, local(): away.append((pairs, [lax.ppermute(part, 'dp', pairs) for part in parts]))  9.4 us
    pallas_call x7, Pallas kernels, kernel(): pl.pallas_call(body, out_shape=tuple(outputs), in_specs=whole(len(inputs)...  9.07 us
    ppermute x9, starting transfers between devices, mate(): return lax.ppermute(value, 'dp', [(i, i ^ distance) for i in range(peers)])  5.03 us
    ppermute x4, waiting for transfers between devices, local(): away.append((pairs, [lax.ppermute(part, 'dp', pairs) for part in parts]))  3.44 us
    ppermute x2, waiting for transfers between devices, local(): backs.append(lax.ppermute(away_best, 'dp', [(t, s) for s, t in pairs]))  3.15 us
    unnamed x10, local copies, waits for them, and re-layouts  1.42 us
    ppermute x2, starting transfers between devices, local(): backs.append(lax.ppermute(away_best, 'dp', [(t, s) for s, t in pairs]))  1.35 us
  transfers between devices with their start and end apart: 15, of which 5 were waited for; matrix products, arithmetic and copies ran while one was open for 0% of the time, Pallas kernels for 18%

profile of v16, /device:TPU:0, one launch (start us, length us, event | category | flops | bytes accessed | tf_op | source)
XLA Modules:
  0.0 49.3 jit_solution(18067810440953786260)
XLA Ops:
  0.0 1.4 %copy-done = f32[768,512]{1,0:T(8,128)S(1)} copy-done((f32[768,512]{1,0:T(8,128)S(1)}, f32[768,512]{1,0:T(8,128)}, u32[]{:S(2)}) %copy-start) | copy-done | bytes 1572888
  1.4 0.2 first.1.first_ref.refs_0_.refs_2_.refs_3_
  1.6 5.1 %collective-permute-start.6 = (bf16[512,512]{1,0:T(8,128)(2,1)S(1)}, bf16[512,512]{1,0:T(8,128)(2,1)S(1)}, u32[]{:S(2)}, u32[]{:S(2)}) collective-permute-start(bf16[512,512]{1,0:T(8,128)(2,1)S(1)} %first.1.first_ref.refs_0_.refs_2_.refs_3_), channel_id=1, source_target_pairs={{0,12},{1,13},{2,14},{3,15},{4,0},{5,1},{6,2},{7,3},{8,4},{9,5},{1... | collective-permute-start | bytes 1572872 | tf_op jit(solution)/shard_map/ppermute | solution.py:253
  6.7 1.5 %collective-permute-start.4 = (bf16[512,512]{1,0:T(8,128)(2,1)S(1)}, bf16[512,512]{1,0:T(8,128)(2,1)S(1)}, u32[]{:S(2)}, u32[]{:S(2)}) collective-permute-start(bf16[512,512]{1,0:T(8,128)(2,1)S(1)} %first.1.first_ref.refs_0_.refs_2_.refs_3_), channel_id=1, source_target_pairs={{0,2},{1,3},{2,0},{3,1},{4,6},{5,7},{6,4},{7,5},{8,10},{9,11},{10,... | collective-permute-start | bytes 1572872 | tf_op jit(solution)/shard_map/ppermute | solution.py:245
  8.5 0.6 %collective-permute-start.5 = (bf16[272,512]{1,0:T(8,128)(2,1)S(1)}, bf16[272,512]{1,0:T(8,128)(2,1)S(1)}, u32[]{:S(2)}, u32[]{:S(2)}) collective-permute-start(bf16[272,512]{1,0:T(8,128)(2,1)S(1)} %get-tuple-element.30.refs_1_.refs_3_.refs_4_), channel_id=1, source_target_pairs={{0,2},{1,3},{2,0},{3,1},{4,6},{5,7},{6,4},{7,5},{8,10},{9,11},{10,... | collective-permute-start | bytes 835592 | tf_op jit(solution)/shard_map/ppermute | solution.py:245
  9.0 0.6 %collective-permute-start.7 = (bf16[272,512]{1,0:T(8,128)(2,1)S(1)}, bf16[272,512]{1,0:T(8,128)(2,1)S(1)}, u32[]{:S(2)}, u32[]{:S(2)}) collective-permute-start(bf16[272,512]{1,0:T(8,128)(2,1)S(1)} %get-tuple-element.30.refs_1_.refs_3_.refs_4_), channel_id=1, source_target_pairs={{0,12},{1,13},{2,14},{3,15},{4,0},{5,1},{6,2},{7,3},{8,4},{9,5},{1... | collective-permute-start | bytes 835592 | tf_op jit(solution)/shard_map/ppermute | solution.py:253
  9.7 1.4 %collective-permute-start = (bf16[528,512]{1,0:T(8,128)(2,1)S(1)}, bf16[528,512]{1,0:T(8,128)(2,1)S(1)}, u32[]{:S(2)}, u32[]{:S(2)}) collective-permute-start(bf16[528,512]{1,0:T(8,128)(2,1)S(1)} %get-tuple-element.28), channel_id=1, source_target_pairs={{0,8},{1,9},{2,10},{3,11},{12,4},{13,5},{14,6},{15,7},{16,24},{17,... | collective-permute-start | bytes 1622024 | tf_op jit(solution)/shard_map/ppermute | solution.py:253
  11.0 15.0 %collective-permute-done.5.refs_3_.refs_8_.refs_7_ = bf16[272,512]{1,0:T(8,128)(2,1)S(1)} collective-permute-done((bf16[272,512]{1,0:T(8,128)(2,1)S(1)}, bf16[272,512]{1,0:T(8,128)(2,1)S(1)}, u32[]{:S(2)}, u32[]{:S(2)}) %collective-permute-start.5) | collective-permute-done | bytes 278560 | tf_op jit(solution)/shard_map/ppermute | solution.py:245
  26.1 0.5 %collective-permute-start.8 = (bf16[512,512]{1,0:T(8,128)(2,1)S(1)}, bf16[512,512]{1,0:T(8,128)(2,1)S(1)}, u32[]{:S(2)}, u32[]{:S(2)}) collective-permute-start(bf16[512,512]{1,0:T(8,128)(2,1)S(1)} %collective-permute-done.4.refs_2_.refs_7_.refs_6_), channel_id=1, source_target_pairs={{0,1},{1,0},{2,3},{3,2},{4,5},{5,4},{6,7},{7,6},{8,9},{9,8},{10,11... | collective-permute-start | bytes 1572872 | tf_op jit(solution)/shard_map/ppermute | solution.py:245
  26.6 0.4 collective-permute-start.3
  27.1 0.5 %collective-permute-done.9.refs_5_.refs_10_.refs_9_ = bf16[272,512]{1,0:T(8,128)(2,1)S(1)} collective-permute-done((bf16[272,512]{1,0:T(8,128)(2,1)S(1)}, bf16[272,512]{1,0:T(8,128)(2,1)S(1)}, u32[]{:S(2)}, u32[]{:S(2)}) %collective-permute-start.9) | collective-permute-done | bytes 278560 | tf_op jit(solution)/shard_map/ppermute | solution.py:245
  27.6 2.3 %collective-permute-start.1 = (bf16[256,512]{1,0:T(8,128)(2,1)S(1)}, bf16[256,512]{1,0:T(8,128)(2,1)S(1)}, u32[]{:S(2)}, u32[]{:S(2)}) collective-permute-start(bf16[256,512]{1,0:T(8,128)(2,1)S(1)} %get-tuple-element.29), channel_id=1, source_target_pairs={{0,8},{1,9},{2,10},{3,11},{12,4},{13,5},{14,6},{15,7},{16,24},{17,... | collective-permute-start | bytes 786440 | tf_op jit(solution)/shard_map/ppermute | solution.py:253
  29.9 1.4 %plane_far.1.refs_6_ = f32[8,128]{1,0:T(8,128)S(1)} custom-call(bf16[512,512]{1,0:T(8,128)(2,1)S(1)} %first.1.first_ref.refs_0_.refs_2_.refs_3_, bf16[272,512]{1,0:T(8,128)(2,1)S(1)} %get-tuple-element.30.refs_1_.refs_3_.refs_4_, bf16[512,512]{1,0:T(8,128)(2,1)S(1)} %collective-permute-done.4.refs_2_.refs_7_.refs_6_, ...), custom_call_target="tpu_custom_call" | custom-call | flops 1 | bytes 1 | tf_op jit(solution)/shard_map/plane_far/pallas_call | solution.py:222
  31.4 1.4 %plane_near.1.refs_12_ = f32[8,128]{1,0:T(8,128)S(1)} custom-call(bf16[512,512]{1,0:T(8,128)(2,1)S(1)} %first.1.first_ref.refs_0_.refs_2_.refs_3_, bf16[272,512]{1,0:T(8,128)(2,1)S(1)} %get-tuple-element.30.refs_1_.refs_3_.refs_4_, bf16[512,512]{1,0:T(8,128)(2,1)S(1)} %first.1.first_ref.refs_0_.refs_2_.refs_3_, ...), custom_call_target="tpu_custom_call" | custom-call | flops 1 | bytes 1 | tf_op jit(solution)/shard_map/plane_near/pallas_call | solution.py:222
  32.9 2.8 %cross.3 = (f32[8,128]{1,0:T(8,128)S(1)}, f32[8,128]{1,0:T(8,128)S(1)}, f32[8,128]{1,0:T(8,128)S(1)}, f32[8,128]{1,0:T(8,128)S(1)}, f32[8,128]{1,0:T(8,128)S(1)}) custom-call(bf16[272,512]{1,0:T(8,128)(2,1)S(1)} %collective-permute-done.7.refs_0_.refs_2_, bf16[512,512]{1,0:T(8,128)(2,1)S(1)} %collective-permute-done.6.refs_1_, ...), custom_call_target="tpu_custom_call" | custom-call | flops 1 | bytes 1 | tf_op jit(solution)/shard_map/cross/pallas_call | solution.py:222
  35.8 0.8 %collective-permute-done.refs_0_.refs_1_ = bf16[528,512]{1,0:T(8,128)(2,1)S(1)} collective-permute-done((bf16[528,512]{1,0:T(8,128)(2,1)S(1)}, bf16[528,512]{1,0:T(8,128)(2,1)S(1)}, u32[]{:S(2)}, u32[]{:S(2)}) %collective-permute-start) | collective-permute-done | bytes 540704 | tf_op jit(solution)/shard_map/ppermute | solution.py:253
  36.6 1.9 %cross.4 = (f32[8,128]{1,0:T(8,128)S(1)}, f32[8,128]{1,0:T(8,128)S(1)}, f32[8,128]{1,0:T(8,128)S(1)}, f32[8,128]{1,0:T(8,128)S(1)}, f32[8,128]{1,0:T(8,128)S(1)}) custom-call(bf16[528,512]{1,0:T(8,128)(2,1)S(1)} %collective-permute-done.refs_0_.refs_1_, bf16[528,512]{1,0:T(8,128)(2,1)S(1)} %collective-permute-done.refs_0_.refs_1_, ...), custom_call_target="tpu_custom_call" | custom-call | flops 1 | bytes 1 | tf_op jit(solution)/shard_map/cross/pallas_call | solution.py:222
  38.5 2.6 %collective-permute-done.1.refs_1_ = bf16[256,512]{1,0:T(8,128)(2,1)S(1)} collective-permute-done((bf16[256,512]{1,0:T(8,128)(2,1)S(1)}, bf16[256,512]{1,0:T(8,128)(2,1)S(1)}, u32[]{:S(2)}, u32[]{:S(2)}) %collective-permute-start.1) | collective-permute-done | bytes 262176 | tf_op jit(solution)/shard_map/ppermute | solution.py:253
  41.1 1.1 %cross.5 = (f32[8,128]{1,0:T(8,128)S(1)}, f32[8,128]{1,0:T(8,128)S(1)}, f32[8,128]{1,0:T(8,128)S(1)}, f32[8,128]{1,0:T(8,128)S(1)}, f32[8,128]{1,0:T(8,128)S(1)}) custom-call(bf16[528,512]{1,0:T(8,128)(2,1)S(1)} %collective-permute-done.refs_0_.refs_1_, bf16[256,512]{1,0:T(8,128)(2,1)S(1)} %collective-permute-done.1.refs_1_, ...), custom_call_target="tpu_custom_call" | custom-call | flops 1 | bytes 1 | tf_op jit(solution)/shard_map/cross/pallas_call | solution.py:222
  42.3 1.3 %collective-permute-start.11 = (f32[8,128]{1,0:T(8,128)S(1)}, f32[8,128]{1,0:T(8,128)S(1)}, u32[]{:S(2)}, u32[]{:S(2)}) collective-permute-start(f32[8,128]{1,0:T(8,128)S(1)} %get-tuple-element.44), channel_id=1, source_target_pairs={{8,0},{9,1},{10,2},{11,3},{4,12},{5,13},{6,14},{7,15},{24,16},{25,... | collective-permute-start | bytes 12296 | tf_op jit(solution)/shard_map/ppermute | solution.py:287
  43.7 1.6 %collective-permute-start.13 = (f32[8,128]{1,0:T(8,128)S(1)}, f32[8,128]{1,0:T(8,128)S(1)}, u32[]{:S(2)}, u32[]{:S(2)}) collective-permute-start(f32[8,128]{1,0:T(8,128)S(1)} %get-tuple-element.48), channel_id=1, source_target_pairs={{0,2},{1,3},{2,0},{3,1},{4,6},{5,7},{6,4},{7,5},{8,10},{9,11},{10,... | collective-permute-start | bytes 12296 | tf_op jit(solution)/shard_map/ppermute | solution.py:245
  45.2 0.3 collective-permute-start.12
  45.5 3.1 %collective-permute-done.11 = f32[8,128]{1,0:T(8,128)S(1)} collective-permute-done((f32[8,128]{1,0:T(8,128)S(1)}, f32[8,128]{1,0:T(8,128)S(1)}, u32[]{:S(2)}, u32[]{:S(2)}) %collective-permute-start.11) | collective-permute-done | bytes 4128 | tf_op jit(solution)/shard_map/ppermute | solution.py:287
  48.7 0.6 %maximum_bitcast_fusion = f32[768]{0:T(1024)} fusion(f32[8,128]{1,0:T(8,128)S(1)} %collective-permute-done.14, f32[8,128]{1,0:T(8,128)S(1)} %collective-permute-done.13, f32[8,128]{1,0:T(8,128)S(1)} %collective-permute-done.12, f32[8,128]{1,0:T(8,128)S(1)} %collective-permute-done.11, f32[8,128]{1,0:T(8,128)S(1)} %collective-permute-done.10, ...), kind=kLoop, calls=%fused_computation | loop fusion | flops 4608 | bytes 21505 | tf_op jit(solution)/shard_map/max | solution.py:297
  (27 shorter events, 0.5 us)
Async XLA Ops:
  0.0 1.4 %copy-start = (f32[768,512]{1,0:T(8,128)S(1)}, f32[768,512]{1,0:T(8,128)}, u32[]{:S(2)}) copy-start(f32[768,512]{1,0:T(8,128)} %embeddings_ref.3) | copy-start | bytes 4718596
  1.4 6.8 %copy-start.2 = (s32[768]{0:T(1024)S(1)}, s32[768]{0:T(1024)}, u32[]{:S(2)}) copy-start(s32[768]{0:T(1024)} %param.5) | copy-start | bytes 9220
  1.4 6.8 %copy-start.3 = (s32[768]{0:T(1024)S(1)}, s32[768]{0:T(1024)}, u32[]{:S(2)}) copy-start(s32[768]{0:T(1024)} %param.6) | copy-start | bytes 9220
  1.4 6.8 %copy-start.4 = (s32[16]{0:T(128)S(1)}, s32[16]{0:T(128)}, u32[]{:S(2)}) copy-start(s32[16]{0:T(128)} %param.7) | copy-start | bytes 196
  1.4 6.9 %copy-start.1 = (f32[768,512]{1,0:T(8,128)S(1)}, f32[768,512]{1,0:T(8,128)}, u32[]{:S(2)}) copy-start(f32[768,512]{1,0:T(8,128)} %embeddings_ref.3) | copy-start | bytes 4718596
  1.6 24.5 %collective-permute-start.6 = (bf16[512,512]{1,0:T(8,128)(2,1)S(1)}, bf16[512,512]{1,0:T(8,128)(2,1)S(1)}, u32[]{:S(2)}, u32[]{:S(2)}) collective-permute-start(bf16[512,512]{1,0:T(8,128)(2,1)S(1)} %first.1.first_ref.refs_0_.refs_2_.refs_3_), channel_id=1, source_target_pairs={{0,12},{1,13},{2,14},{3,15},{4,0},{5,1},{6,2},{7,3},{8,4},{9,5},{1... | collective-permute-start | bytes 1572872 | tf_op jit(solution)/shard_map/ppermute | solution.py:253
  6.7 19.4 %collective-permute-start.4 = (bf16[512,512]{1,0:T(8,128)(2,1)S(1)}, bf16[512,512]{1,0:T(8,128)(2,1)S(1)}, u32[]{:S(2)}, u32[]{:S(2)}) collective-permute-start(bf16[512,512]{1,0:T(8,128)(2,1)S(1)} %first.1.first_ref.refs_0_.refs_2_.refs_3_), channel_id=1, source_target_pairs={{0,2},{1,3},{2,0},{3,1},{4,6},{5,7},{6,4},{7,5},{8,10},{9,11},{10,... | collective-permute-start | bytes 1572872 | tf_op jit(solution)/shard_map/ppermute | solution.py:245
  8.5 17.6 %collective-permute-start.5 = (bf16[272,512]{1,0:T(8,128)(2,1)S(1)}, bf16[272,512]{1,0:T(8,128)(2,1)S(1)}, u32[]{:S(2)}, u32[]{:S(2)}) collective-permute-start(bf16[272,512]{1,0:T(8,128)(2,1)S(1)} %get-tuple-element.30.refs_1_.refs_3_.refs_4_), channel_id=1, source_target_pairs={{0,2},{1,3},{2,0},{3,1},{4,6},{5,7},{6,4},{7,5},{8,10},{9,11},{10,... | collective-permute-start | bytes 835592 | tf_op jit(solution)/shard_map/ppermute | solution.py:245
  9.0 17.0 %collective-permute-start.7 = (bf16[272,512]{1,0:T(8,128)(2,1)S(1)}, bf16[272,512]{1,0:T(8,128)(2,1)S(1)}, u32[]{:S(2)}, u32[]{:S(2)}) collective-permute-start(bf16[272,512]{1,0:T(8,128)(2,1)S(1)} %get-tuple-element.30.refs_1_.refs_3_.refs_4_), channel_id=1, source_target_pairs={{0,12},{1,13},{2,14},{3,15},{4,0},{5,1},{6,2},{7,3},{8,4},{9,5},{1... | collective-permute-start | bytes 835592 | tf_op jit(solution)/shard_map/ppermute | solution.py:253
  9.7 26.9 %collective-permute-start = (bf16[528,512]{1,0:T(8,128)(2,1)S(1)}, bf16[528,512]{1,0:T(8,128)(2,1)S(1)}, u32[]{:S(2)}, u32[]{:S(2)}) collective-permute-start(bf16[528,512]{1,0:T(8,128)(2,1)S(1)} %get-tuple-element.28), channel_id=1, source_target_pairs={{0,8},{1,9},{2,10},{3,11},{12,4},{13,5},{14,6},{15,7},{16,24},{17,... | collective-permute-start | bytes 1622024 | tf_op jit(solution)/shard_map/ppermute | solution.py:253
  26.0 1.6 %collective-permute-start.9 = (bf16[272,512]{1,0:T(8,128)(2,1)S(1)}, bf16[272,512]{1,0:T(8,128)(2,1)S(1)}, u32[]{:S(2)}, u32[]{:S(2)}) collective-permute-start(bf16[272,512]{1,0:T(8,128)(2,1)S(1)} %collective-permute-done.5.refs_3_.refs_8_.refs_7_), channel_id=1, source_target_pairs={{0,1},{1,0},{2,3},{3,2},{4,5},{5,4},{6,7},{7,6},{8,9},{9,8},{10,11... | collective-permute-start | bytes 835592 | tf_op jit(solution)/shard_map/ppermute | solution.py:245
  26.1 3.9 %collective-permute-start.8 = (bf16[512,512]{1,0:T(8,128)(2,1)S(1)}, bf16[512,512]{1,0:T(8,128)(2,1)S(1)}, u32[]{:S(2)}, u32[]{:S(2)}) collective-permute-start(bf16[512,512]{1,0:T(8,128)(2,1)S(1)} %collective-permute-done.4.refs_2_.refs_7_.refs_6_), channel_id=1, source_target_pairs={{0,1},{1,0},{2,3},{3,2},{4,5},{5,4},{6,7},{7,6},{8,9},{9,8},{10,11... | collective-permute-start | bytes 1572872 | tf_op jit(solution)/shard_map/ppermute | solution.py:245
  26.6 4.8 %collective-permute-start.2 = (bf16[512,512]{1,0:T(8,128)(2,1)S(1)}, bf16[512,512]{1,0:T(8,128)(2,1)S(1)}, u32[]{:S(2)}, u32[]{:S(2)}) collective-permute-start(bf16[512,512]{1,0:T(8,128)(2,1)S(1)} %first.1.first_ref.refs_0_.refs_2_.refs_3_), channel_id=1, source_target_pairs={{0,1},{1,0},{2,3},{3,2},{4,5},{5,4},{6,7},{7,6},{8,9},{9,8},{10,11... | collective-permute-start | bytes 1572872 | tf_op jit(solution)/shard_map/ppermute | solution.py:245
  26.6 4.7 %collective-permute-start.3 = (bf16[272,512]{1,0:T(8,128)(2,1)S(1)}, bf16[272,512]{1,0:T(8,128)(2,1)S(1)}, u32[]{:S(2)}, u32[]{:S(2)}) collective-permute-start(bf16[272,512]{1,0:T(8,128)(2,1)S(1)} %get-tuple-element.30.refs_1_.refs_3_.refs_4_), channel_id=1, source_target_pairs={{0,1},{1,0},{2,3},{3,2},{4,5},{5,4},{6,7},{7,6},{8,9},{9,8},{10,11... | collective-permute-start | bytes 835592 | tf_op jit(solution)/shard_map/ppermute | solution.py:245
  27.6 13.5 %collective-permute-start.1 = (bf16[256,512]{1,0:T(8,128)(2,1)S(1)}, bf16[256,512]{1,0:T(8,128)(2,1)S(1)}, u32[]{:S(2)}, u32[]{:S(2)}) collective-permute-start(bf16[256,512]{1,0:T(8,128)(2,1)S(1)} %get-tuple-element.29), channel_id=1, source_target_pairs={{0,8},{1,9},{2,10},{3,11},{12,4},{13,5},{14,6},{15,7},{16,24},{17,... | collective-permute-start | bytes 786440 | tf_op jit(solution)/shard_map/ppermute | solution.py:253
  35.7 7.9 %collective-permute-start.10 = (f32[8,128]{1,0:T(8,128)S(1)}, f32[8,128]{1,0:T(8,128)S(1)}, u32[]{:S(2)}, u32[]{:S(2)}) collective-permute-start(f32[8,128]{1,0:T(8,128)S(1)} %get-tuple-element.43), channel_id=1, source_target_pairs={{12,0},{13,1},{14,2},{15,3},{0,4},{1,5},{2,6},{3,7},{4,8},{5,9},{6... | collective-permute-start | bytes 12296 | tf_op jit(solution)/shard_map/ppermute | solution.py:287
  42.3 6.4 %collective-permute-start.11 = (f32[8,128]{1,0:T(8,128)S(1)}, f32[8,128]{1,0:T(8,128)S(1)}, u32[]{:S(2)}, u32[]{:S(2)}) collective-permute-start(f32[8,128]{1,0:T(8,128)S(1)} %get-tuple-element.44), channel_id=1, source_target_pairs={{8,0},{9,1},{10,2},{11,3},{4,12},{5,13},{6,14},{7,15},{24,16},{25,... | collective-permute-start | bytes 12296 | tf_op jit(solution)/shard_map/ppermute | solution.py:287
  43.6 5.1 %collective-permute-start.14 = (f32[8,128]{1,0:T(8,128)S(1)}, f32[8,128]{1,0:T(8,128)S(1)}, u32[]{:S(2)}, u32[]{:S(2)}) collective-permute-start(f32[8,128]{1,0:T(8,128)S(1)} %get-tuple-element.50), channel_id=1, source_target_pairs={{0,1},{1,0},{2,3},{3,2},{4,5},{5,4},{6,7},{7,6},{8,9},{9,8},{10,11... | collective-permute-start | bytes 12296 | tf_op jit(solution)/shard_map/ppermute | solution.py:245
  43.7 5.0 %collective-permute-start.13 = (f32[8,128]{1,0:T(8,128)S(1)}, f32[8,128]{1,0:T(8,128)S(1)}, u32[]{:S(2)}, u32[]{:S(2)}) collective-permute-start(f32[8,128]{1,0:T(8,128)S(1)} %get-tuple-element.48), channel_id=1, source_target_pairs={{0,2},{1,3},{2,0},{3,1},{4,6},{5,7},{6,4},{7,5},{8,10},{9,11},{10,... | collective-permute-start | bytes 12296 | tf_op jit(solution)/shard_map/ppermute | solution.py:245
  45.2 3.4 %collective-permute-start.12 = (f32[8,128]{1,0:T(8,128)S(1)}, f32[8,128]{1,0:T(8,128)S(1)}, u32[]{:S(2)}, u32[]{:S(2)}) collective-permute-start(f32[8,128]{1,0:T(8,128)S(1)} %get-tuple-element.46), channel_id=1, source_target_pairs={{0,3},{1,2},{2,1},{3,0},{4,7},{5,6},{6,5},{7,4},{8,11},{9,10},{10,... | collective-permute-start | bytes 12296 | tf_op jit(solution)/shard_map/ppermute | solution.py:245

commit v17 on v14

--- a/solution.py
+++ b/solution.py
@@ -13,7 +13,6 @@
 BASE = 64.0
 TILE = 256
 FIRST = 512
-HEAD = 512
 VMEM_LIMIT = 24 * 2**20
 
 
@@ -39,7 +38,9 @@
         first_ref[row : row + 128, :] = unit_rows(embeddings_ref[row : row + 128, :])
 
 
-def rest_kernel(rows, embeddings_ref, ints_ref, first_ref, last_ref, head_ref, tail_ref):
+def rest_kernel(
+    rows, embeddings_ref, ints_ref, first_ref, tags_ref, last_ref, block_ref, tail_ref
+):
     label_row = rows // 128
     owner, label = ints_ref[0:8, :], ints_ref[label_row : label_row + 8, :]
     runs = ints_ref[2 * label_row : 2 * label_row + 1, :]
@@ -48,20 +49,18 @@
     tags = tags.astype(jnp.float32)
     high = jnp.floor(tags * (1.0 / BASE))
     digits = jnp.concatenate([high, tags - high * BASE], axis=0).astype(jnp.bfloat16)
+    tags_ref[...] = digits
     width = embeddings_ref.shape[1]
     digits = jnp.concatenate([digits, jnp.zeros((PAD, width - 128), jnp.bfloat16)], axis=1)
+    first = first_ref.shape[0]
     last_ref[0:PAD, :] = digits
-    head_ref[0:PAD, :] = digits
-    first = first_ref.shape[0]
-    head = head_ref.shape[0] - PAD
-    head_ref[PAD : PAD + first, :] = first_ref[...]
+    block_ref[0:PAD, :] = digits
+    block_ref[PAD : PAD + first, :] = first_ref[...]
     for row in range(first, rows, 128):
         unit = unit_rows(embeddings_ref[row : row + 128, :])
         last_ref[PAD + row - first : PAD + row - first + 128, :] = unit
-        if row < head:
-            head_ref[PAD + row : PAD + row + 128, :] = unit
-        else:
-            tail_ref[row - head : row - head + 128, :] = unit
+        block_ref[PAD + row : PAD + row + 128, :] = unit
+        tail_ref[row - first : row - first + 128, :] = unit
 
 
 def tag_rows(block_ref):
@@ -156,32 +155,31 @@
             best_ref[place, :] = folded
 
 
-def cross_kernel(starts, bases, *refs):
-    (tags, aways), refs = take(refs, (1, len(starts)))
+def cross_kernel(start, base, *refs):
+    (tags, (away,)), refs = take(refs, (1, 1))
     blocks, refs = take(refs, (2,) * PLANE)
     away_before, away_best = refs[0], refs[PLANE + 1]
     plane_before, plane_best = refs[1 : PLANE + 1], refs[PLANE + 2 :]
     plane_tags = [tag_rows(block[-1]) for block in blocks]
     away_best[...] = away_before[...]
     best = {}
-    for start, base, away in zip(starts, bases, aways):
-        for tile in range(0, away.shape[0] - base, TILE):
-            values = away[base + tile : base + tile + TILE, :]
-            column = tag_columns(tags[0], start + tile, TILE)
-            row_best = jnp.full((TILE, 128), -1.0, jnp.float32)
-            for which in range(PLANE):
-                for first, part in row_slices(blocks[which]):
-                    found = dot_rows(values, part[...])
-                    for lane in range(0, part.shape[0], 128):
-                        row = (first + lane) // 128
-                        match = column == plane_tags[which][row : row + 1]
-                        masked = jnp.where(match, found[:, lane : lane + 128], -1.0)
-                        row_best = jnp.maximum(row_best, masked)
-                        folded = fold_sublanes(masked)
-                        place = which, row
-                        best[place] = jnp.maximum(best[place], folded) if place in best else folded
-            place = pl.ds((start + tile) // 128, TILE // 128)
-            away_best[place, :] = fold_lanes(row_best)
+    for tile in range(0, away.shape[0] - base, TILE):
+        values = away[base + tile : base + tile + TILE, :]
+        column = tag_columns(tags[0], start + tile, TILE)
+        row_best = jnp.full((TILE, 128), -1.0, jnp.float32)
+        for which in range(PLANE):
+            for first, part in row_slices(blocks[which]):
+                found = dot_rows(values, part[...])
+                for lane in range(0, part.shape[0], 128):
+                    row = (first + lane) // 128
+                    match = column == plane_tags[which][row : row + 1]
+                    masked = jnp.where(match, found[:, lane : lane + 128], -1.0)
+                    row_best = jnp.maximum(row_best, masked)
+                    folded = fold_sublanes(masked)
+                    place = which, row
+                    best[place] = jnp.maximum(best[place], folded) if place in best else folded
+        place = pl.ds((start + tile) // 128, TILE // 128)
+        away_best[place, :] = fold_lanes(row_best)
     for which in range(PLANE):
         plane_best[which][...] = plane_before[which][...]
     for (which, row), values in best.items():
@@ -233,10 +231,15 @@
         return jax.ShapeDtypeStruct((count, width), jnp.bfloat16)
 
     (first,) = kernel(first_kernel, (embeddings,), (part_shape(FIRST),), "first")
-    last, head, tail = kernel(
+    tags, last, block, tail = kernel(
         functools.partial(rest_kernel, rows),
         (embeddings, ints, first),
-        (part_shape(PAD + rows - FIRST), part_shape(PAD + HEAD), part_shape(rows - HEAD)),
+        (
+            jax.ShapeDtypeStruct((PAD, 128), jnp.bfloat16),
+            part_shape(PAD + rows - FIRST),
+            part_shape(PAD + rows),
+            part_shape(rows - FIRST),
+        ),
         "rest",
     )
     own = (first, last)
@@ -244,16 +247,19 @@
     def mate(value, distance):
         return lax.ppermute(value, "dp", [(i, i ^ distance) for i in range(peers)])
 
-    away = []
-    for n, step in enumerate(plane_steps(planes)):
+    def moved(value, step, back=False):
         pairs = [(z * PLANE + j, t * PLANE + j) for z, t in step for j in range(PLANE)]
-        parts = (head, tail) if n else own
-        if n > 1:
-            parts = [after(part, away[-1][1][-1]) for part in parts]
-        away.append((pairs, [lax.ppermute(part, "dp", pairs) for part in parts]))
+        return lax.ppermute(value, "dp", [(t, s) for s, t in pairs] if back else pairs)
+
+    split, *others = plane_steps(planes)
+    away = [moved(first, split)]
+    for n, step in enumerate(others):
+        away.append(moved(after(block, away[-1]) if n else block, step))
+    away_tags = moved(tags, split)
+    away_tail = moved(tail, split)
     beside = [mate(part, 2) for part in own]
     near = [mate(part, 1) for part in own]
-    across = [mate(after(part, *away[0][1]), 1) for part in beside]
+    across = [mate(after(part, away[0], away_tags), 1) for part in beside]
 
     (best,) = kernel(
         functools.partial(plane_kernel, rows, False),
@@ -270,28 +276,32 @@
     plane = (*own, *near, *beside, *across)
     plane_best = [best] + [jnp.full(lanes.shape, -1.0, jnp.float32)] * (PLANE - 1)
     backs, masks = [], {}
-    for n, (pairs, received) in enumerate(away):
-        away_best = jnp.full(lanes.shape, -1.0, jnp.float32)
-        if n:
-            calls = (((0,), (PAD,), received[:1]), ((HEAD,), (0,), received[1:]))
-        else:
-            calls = (((0, FIRST), (0, PAD), received),)
-        tags = received[0] if n else received[-1]
-        for starts, bases, parts in calls:
-            away_best, *plane_best = kernel(
-                functools.partial(cross_kernel, starts, bases),
-                (tags, *parts, *plane, away_best, *plane_best),
-                (lanes,) * (PLANE + 1),
-                "cross",
-            )
-        backs.append(lax.ppermute(away_best, "dp", [(t, s) for s, t in pairs]))
-        if len(pairs) < peers:
-            sources = sum(1 << z for z in {s // PLANE for s, _ in pairs})
+    empty = jnp.full(lanes.shape, -1.0, jnp.float32)
+
+    def crossed(part, part_tags, start, base, away_best, plane_best):
+        away_best, *plane_best = kernel(
+            functools.partial(cross_kernel, start, base),
+            (part_tags, part, *plane, away_best, *plane_best),
+            (lanes,) * (PLANE + 1),
+            "cross",
+        )
+        return away_best, plane_best
+
+    split_best, plane_best = crossed(away[0], away_tags, 0, 0, empty, plane_best)
+    for n, step in enumerate(others):
+        part = away[n + 1]
+        away_best, plane_best = crossed(part, part, 0, PAD, empty, plane_best)
+        backs.append(moved(away_best, step, back=True))
+        if len(step) < planes:
+            sources = sum(1 << z for z, _ in step)
             sent = (jnp.int32(sources) >> (lax.axis_index("dp") // PLANE)) & 1
             masks[n] = jnp.broadcast_to(sent == 1, (rows,))
+    split_best, plane_best = crossed(away_tail, away_tags, FIRST, 0, split_best, plane_best)
+    first_backs = tuple(backs)
+    backs.append(moved(split_best, split, back=True))
     best = plane_best[0].reshape(-1)[:rows]
     for distance in (3, 2, 1):
-        backs.append(mate(after(plane_best[distance], *backs[:1]), distance))
+        backs.append(mate(after(plane_best[distance], *first_backs), distance))
     for n, back in enumerate(backs):
         back = back.reshape(-1)[:rows]
         best = jnp.maximum(best, jnp.where(masks[n], back, -1.0) if n in masks else back)

time: 49.4 us -> 59.5 us (1.20)
  waiting for transfers between devices: 19.9 us -> 28.6 us
  starting transfers between devices: 17.9 us -> 19.3 us
    ppermute x6, waiting for transfers between devices: 6.24 us -> 25.4 us  [moved(): lax.ppermute(value, 'dp', [(t, s) for s, t in pairs] if back else pairs)]
    ppermute x9, waiting for transfers between devices: 13.7 us -> 3.24 us  [mate(): return lax.ppermute(value, 'dp', [(i, i ^ distance) for i in range(peers)])]
    ppermute x6, starting transfers between devices: 12.9 us -> 14.4 us  [moved(): lax.ppermute(value, 'dp', [(t, s) for s, t in pairs] if back else pairs)]
  transfers between devices with their start and end apart: 15 -> 15, of which waited for: 4 -> 5; matrix products, arithmetic and copies ran while one was open for 0% -> 0% of each run, Pallas kernels for 18% -> 15%
where the time goes in v17:
time: 59.5 us; the launch traced here: 59.3 us
  waiting for transfers between devices  28.6 us (48%)
  starting transfers between devices  19.3 us (32%)
  Pallas kernels  9.16 us (15%)
  local copies, waits for them, and re-layouts  1.51 us (3%)
  other arithmetic  0.6 us (1%)
    ppermute x6, waiting for transfers between devices, moved(): lax.ppermute(value, 'dp', [(t, s) for s, t in pairs] if back else pairs)  25.4 us
    ppermute x6, starting transfers between devices, moved(): lax.ppermute(value, 'dp', [(t, s) for s, t in pairs] if back else pairs)  14.4 us
    pallas_call x7, Pallas kernels, kernel(): pl.pallas_call(body, out_shape=tuple(outputs), in_specs=whole(len(inputs)...  9.16 us
    ppermute x9, starting transfers between devices, mate(): return lax.ppermute(value, 'dp', [(i, i ^ distance) for i in range(peers)])  4.96 us
    ppermute x9, waiting for transfers between devices, mate(): return lax.ppermute(value, 'dp', [(i, i ^ distance) for i in range(peers)])  3.24 us
    unnamed x10, local copies, waits for them, and re-layouts  1.42 us
  transfers between devices with their start and end apart: 15, of which 5 were waited for; matrix products, arithmetic and copies ran while one was open for 0% of the time, Pallas kernels for 15%

profile of v17, /device:TPU:0, one launch (start us, length us, event | category | flops | bytes accessed | tf_op | source)
XLA Modules:
  0.0 59.3 jit_solution(17564293935930225149)
XLA Ops:
  0.0 1.4 %copy-done = f32[768,512]{1,0:T(8,128)S(1)} copy-done((f32[768,512]{1,0:T(8,128)S(1)}, f32[768,512]{1,0:T(8,128)}, u32[]{:S(2)}) %copy-start) | copy-done | bytes 1572888
  1.6 4.1 %collective-permute-start.6 = (bf16[512,512]{1,0:T(8,128)(2,1)S(1)}, bf16[512,512]{1,0:T(8,128)(2,1)S(1)}, u32[]{:S(2)}, u32[]{:S(2)}) collective-permute-start(bf16[512,512]{1,0:T(8,128)(2,1)S(1)} %first.1.first_ref.refs_0_.refs_2_), channel_id=1, source_target_pairs={{0,8},{1,9},{2,10},{3,11},{4,0},{5,1},{6,2},{7,3},{8,12},{9,13},{1... | collective-permute-start | bytes 1572872 | tf_op jit(solution)/shard_map/ppermute | solution.py:252
  5.7 1.5 %collective-permute-start.4 = (bf16[512,512]{1,0:T(8,128)(2,1)S(1)}, bf16[512,512]{1,0:T(8,128)(2,1)S(1)}, u32[]{:S(2)}, u32[]{:S(2)}) collective-permute-start(bf16[512,512]{1,0:T(8,128)(2,1)S(1)} %first.1.first_ref.refs_0_.refs_2_), channel_id=1, source_target_pairs={{0,2},{1,3},{2,0},{3,1},{4,6},{5,7},{6,4},{7,5},{8,10},{9,11},{10,... | collective-permute-start | bytes 1572872 | tf_op jit(solution)/shard_map/ppermute | solution.py:248
  7.3 0.2 rest.1
  7.5 0.6 collective-permute-start.5
  8.0 3.6 %collective-permute-start.9 = (bf16[784,512]{1,0:T(8,128)(2,1)S(1)}, bf16[784,512]{1,0:T(8,128)(2,1)S(1)}, u32[]{:S(2)}, u32[]{:S(2)}) collective-permute-start(bf16[784,512]{1,0:T(8,128)(2,1)S(1)} %get-tuple-element.35), channel_id=1, source_target_pairs={{0,12},{1,13},{2,14},{3,15},{8,4},{9,5},{10,6},{11,7},{16,28},{17,... | collective-permute-start | bytes 2408456 | tf_op jit(solution)/shard_map/ppermute | solution.py:252
  11.7 22.5 %collective-permute-done.refs_0_ = bf16[16,128]{1,0:T(8,128)(2,1)S(1)} collective-permute-done((bf16[16,128]{1,0:T(8,128)(2,1)S(1)}, bf16[16,128]{1,0:T(8,128)(2,1)S(1)}, u32[]{:S(2)}, u32[]{:S(2)}) %collective-permute-start) | collective-permute-done | bytes 4128 | tf_op jit(solution)/shard_map/ppermute | solution.py:252
  34.2 0.5 collective-permute-start.7
  34.7 0.4 collective-permute-start.3
  35.2 0.5 collective-permute-done.8.refs_5_.refs_9_
  35.7 3.4 %collective-permute-start.1 = (bf16[256,512]{1,0:T(8,128)(2,1)S(1)}, bf16[256,512]{1,0:T(8,128)(2,1)S(1)}, u32[]{:S(2)}, u32[]{:S(2)}) collective-permute-start(bf16[256,512]{1,0:T(8,128)(2,1)S(1)} %get-tuple-element.30), channel_id=1, source_target_pairs={{0,8},{1,9},{2,10},{3,11},{4,0},{5,1},{6,2},{7,3},{8,12},{9,13},{1... | collective-permute-start | bytes 786440 | tf_op jit(solution)/shard_map/ppermute | solution.py:252
  39.1 1.4 %plane_far.1.refs_6_ = f32[8,128]{1,0:T(8,128)S(1)} custom-call(bf16[512,512]{1,0:T(8,128)(2,1)S(1)} %first.1.first_ref.refs_0_.refs_2_, bf16[272,512]{1,0:T(8,128)(2,1)S(1)} %get-tuple-element.31.refs_1_.refs_3_, bf16[512,512]{1,0:T(8,128)(2,1)S(1)} %collective-permute-done.4.refs_2_.refs_6_, bf16[272,512]{1,0:T(8,128)(2,1)S(1)} %collective-permute-done.5.refs_3_.refs_7_, ...), custom_call_target="tpu_custom_call" | custom-call | flops 1 | bytes 1 | tf_op jit(solution)/shard_map/plane_far/pallas_call | solution.py:220
  40.6 1.4 %plane_near.1.refs_11_ = f32[8,128]{1,0:T(8,128)S(1)} custom-call(bf16[512,512]{1,0:T(8,128)(2,1)S(1)} %first.1.first_ref.refs_0_.refs_2_, bf16[272,512]{1,0:T(8,128)(2,1)S(1)} %get-tuple-element.31.refs_1_.refs_3_, bf16[512,512]{1,0:T(8,128)(2,1)S(1)} %first.1.first_ref.refs_0_.refs_2_, bf16[272,512]{1,0:T(8,128)(2,1)S(1)} %get-tuple-element.31.refs_1_.refs_3_, ...), custom_call_target="tpu_custom_call" | custom-call | flops 1 | bytes 1 | tf_op jit(solution)/shard_map/plane_near/pallas_call | solution.py:220
  42.0 1.9 %cross.3 = (f32[8,128]{1,0:T(8,128)S(1)}, f32[8,128]{1,0:T(8,128)S(1)}, f32[8,128]{1,0:T(8,128)S(1)}, f32[8,128]{1,0:T(8,128)S(1)}, f32[8,128]{1,0:T(8,128)S(1)}) custom-call(bf16[16,128]{1,0:T(8,128)(2,1)S(1)} %collective-permute-done.refs_0_, bf16[512,512]{1,0:T(8,128)(2,1)S(1)} %collective-permute-done.6.refs_1_, ...), custom_call_target="tpu_custom_call" | custom-call | flops 1 | bytes 1 | tf_op jit(solution)/shard_map/cross/pallas_call | solution.py:220
  44.0 2.9 %cross.4 = (f32[8,128]{1,0:T(8,128)S(1)}, f32[8,128]{1,0:T(8,128)S(1)}, f32[8,128]{1,0:T(8,128)S(1)}, f32[8,128]{1,0:T(8,128)S(1)}, f32[8,128]{1,0:T(8,128)S(1)}) custom-call(bf16[784,512]{1,0:T(8,128)(2,1)S(1)} %collective-permute-done.9.refs_0_.refs_1_, bf16[784,512]{1,0:T(8,128)(2,1)S(1)} %collective-permute-done.9.refs_0_.refs_1_, ...), custom_call_target="tpu_custom_call" | custom-call | flops 1 | bytes 1 | tf_op jit(solution)/shard_map/cross/pallas_call | solution.py:220
  46.9 1.3 %collective-permute-start.10 = (f32[8,128]{1,0:T(8,128)S(1)}, f32[8,128]{1,0:T(8,128)S(1)}, u32[]{:S(2)}, u32[]{:S(2)}) collective-permute-start(f32[8,128]{1,0:T(8,128)S(1)} %get-tuple-element.45), channel_id=1, source_target_pairs={{12,0},{13,1},{14,2},{15,3},{4,8},{5,9},{6,10},{7,11},{28,16},{29,... | collective-permute-start | bytes 12296 | tf_op jit(solution)/shard_map/ppermute | solution.py:252
  48.2 1.1 %cross.5 = (f32[8,128]{1,0:T(8,128)S(1)}, f32[8,128]{1,0:T(8,128)S(1)}, f32[8,128]{1,0:T(8,128)S(1)}, f32[8,128]{1,0:T(8,128)S(1)}, f32[8,128]{1,0:T(8,128)S(1)}) custom-call(bf16[16,128]{1,0:T(8,128)(2,1)S(1)} %collective-permute-done.refs_0_, bf16[256,512]{1,0:T(8,128)(2,1)S(1)} %collective-permute-done.1.refs_1_, ...), custom_call_target="tpu_custom_call" | custom-call | flops 1 | bytes 1 | tf_op jit(solution)/shard_map/cross/pallas_call | solution.py:220
  49.3 2.0 %collective-permute-start.11 = (f32[8,128]{1,0:T(8,128)S(1)}, f32[8,128]{1,0:T(8,128)S(1)}, u32[]{:S(2)}, u32[]{:S(2)}) collective-permute-start(f32[8,128]{1,0:T(8,128)S(1)} %get-tuple-element.46), channel_id=1, source_target_pairs={{8,0},{9,1},{10,2},{11,3},{0,4},{1,5},{2,6},{3,7},{12,8},{13,9},{1... | collective-permute-start | bytes 12296 | tf_op jit(solution)/shard_map/ppermute | solution.py:252
  51.3 2.9 %collective-permute-done.10 = f32[8,128]{1,0:T(8,128)S(1)} collective-permute-done((f32[8,128]{1,0:T(8,128)S(1)}, f32[8,128]{1,0:T(8,128)S(1)}, u32[]{:S(2)}, u32[]{:S(2)}) %collective-permute-start.10) | collective-permute-done | bytes 4128 | tf_op jit(solution)/shard_map/ppermute | solution.py:252
  54.2 1.5 %collective-permute-start.13 = (f32[8,128]{1,0:T(8,128)S(1)}, f32[8,128]{1,0:T(8,128)S(1)}, u32[]{:S(2)}, u32[]{:S(2)}) collective-permute-start(f32[8,128]{1,0:T(8,128)S(1)} %get-tuple-element.50), channel_id=1, source_target_pairs={{0,2},{1,3},{2,0},{3,1},{4,6},{5,7},{6,4},{7,5},{8,10},{9,11},{10,... | collective-permute-start | bytes 12296 | tf_op jit(solution)/shard_map/ppermute | solution.py:248
  55.7 0.3 collective-permute-start.12
  56.1 1.7 %collective-permute-done.13 = f32[8,128]{1,0:T(8,128)S(1)} collective-permute-done((f32[8,128]{1,0:T(8,128)S(1)}, f32[8,128]{1,0:T(8,128)S(1)}, u32[]{:S(2)}, u32[]{:S(2)}) %collective-permute-start.13) | collective-permute-done | bytes 4128 | tf_op jit(solution)/shard_map/ppermute | solution.py:248
  57.8 0.9 %collective-permute-done.12 = f32[8,128]{1,0:T(8,128)S(1)} collective-permute-done((f32[8,128]{1,0:T(8,128)S(1)}, f32[8,128]{1,0:T(8,128)S(1)}, u32[]{:S(2)}, u32[]{:S(2)}) %collective-permute-start.12) | collective-permute-done | bytes 4128 | tf_op jit(solution)/shard_map/ppermute | solution.py:248
  58.7 0.6 %maximum_bitcast_fusion = f32[768]{0:T(1024)} fusion(f32[8,128]{1,0:T(8,128)S(1)} %collective-permute-done.14, f32[8,128]{1,0:T(8,128)S(1)} %collective-permute-done.13, f32[8,128]{1,0:T(8,128)S(1)} %collective-permute-done.12, f32[8,128]{1,0:T(8,128)S(1)} %collective-permute-done.11, f32[8,128]{1,0:T(8,128)S(1)} %collective-permute-done.10, ...), kind=kLoop, calls=%fused_computation | loop fusion | flops 4608 | bytes 21505 | tf_op jit(solution)/shard_map/max | solution.py:307
  (27 shorter events, 0.4 us)
Async XLA Ops:
  0.0 1.4 %copy-start = (f32[768,512]{1,0:T(8,128)S(1)}, f32[768,512]{1,0:T(8,128)}, u32[]{:S(2)}) copy-start(f32[768,512]{1,0:T(8,128)} %embeddings_ref.3) | copy-start | bytes 4718596
  1.4 5.8 %copy-start.2 = (s32[768]{0:T(1024)S(1)}, s32[768]{0:T(1024)}, u32[]{:S(2)}) copy-start(s32[768]{0:T(1024)} %param.5) | copy-start | bytes 9220
  1.4 5.8 %copy-start.3 = (s32[768]{0:T(1024)S(1)}, s32[768]{0:T(1024)}, u32[]{:S(2)}) copy-start(s32[768]{0:T(1024)} %param.6) | copy-start | bytes 9220
  1.4 5.8 %copy-start.4 = (s32[16]{0:T(128)S(1)}, s32[16]{0:T(128)}, u32[]{:S(2)}) copy-start(s32[16]{0:T(128)} %param.7) | copy-start | bytes 196
  1.4 5.9 %copy-start.1 = (f32[768,512]{1,0:T(8,128)S(1)}, f32[768,512]{1,0:T(8,128)}, u32[]{:S(2)}) copy-start(f32[768,512]{1,0:T(8,128)} %embeddings_ref.3) | copy-start | bytes 4718596
  1.6 32.6 %collective-permute-start.6 = (bf16[512,512]{1,0:T(8,128)(2,1)S(1)}, bf16[512,512]{1,0:T(8,128)(2,1)S(1)}, u32[]{:S(2)}, u32[]{:S(2)}) collective-permute-start(bf16[512,512]{1,0:T(8,128)(2,1)S(1)} %first.1.first_ref.refs_0_.refs_2_), channel_id=1, source_target_pairs={{0,8},{1,9},{2,10},{3,11},{4,0},{5,1},{6,2},{7,3},{8,12},{9,13},{1... | collective-permute-start | bytes 1572872 | tf_op jit(solution)/shard_map/ppermute | solution.py:252
  5.7 28.5 %collective-permute-start.4 = (bf16[512,512]{1,0:T(8,128)(2,1)S(1)}, bf16[512,512]{1,0:T(8,128)(2,1)S(1)}, u32[]{:S(2)}, u32[]{:S(2)}) collective-permute-start(bf16[512,512]{1,0:T(8,128)(2,1)S(1)} %first.1.first_ref.refs_0_.refs_2_), channel_id=1, source_target_pairs={{0,2},{1,3},{2,0},{3,1},{4,6},{5,7},{6,4},{7,5},{8,10},{9,11},{10,... | collective-permute-start | bytes 1572872 | tf_op jit(solution)/shard_map/ppermute | solution.py:248
  7.5 26.7 %collective-permute-start.5 = (bf16[272,512]{1,0:T(8,128)(2,1)S(1)}, bf16[272,512]{1,0:T(8,128)(2,1)S(1)}, u32[]{:S(2)}, u32[]{:S(2)}) collective-permute-start(bf16[272,512]{1,0:T(8,128)(2,1)S(1)} %get-tuple-element.31.refs_1_.refs_3_), channel_id=1, source_target_pairs={{0,2},{1,3},{2,0},{3,1},{4,6},{5,7},{6,4},{7,5},{8,10},{9,11},{10,... | collective-permute-start | bytes 835592 | tf_op jit(solution)/shard_map/ppermute | solution.py:248
  8.0 35.9 %collective-permute-start.9 = (bf16[784,512]{1,0:T(8,128)(2,1)S(1)}, bf16[784,512]{1,0:T(8,128)(2,1)S(1)}, u32[]{:S(2)}, u32[]{:S(2)}) collective-permute-start(bf16[784,512]{1,0:T(8,128)(2,1)S(1)} %get-tuple-element.35), channel_id=1, source_target_pairs={{0,12},{1,13},{2,14},{3,15},{8,4},{9,5},{10,6},{11,7},{16,28},{17,... | collective-permute-start | bytes 2408456 | tf_op jit(solution)/shard_map/ppermute | solution.py:252
  11.6 22.5 %collective-permute-start = (bf16[16,128]{1,0:T(8,128)(2,1)S(1)}, bf16[16,128]{1,0:T(8,128)(2,1)S(1)}, u32[]{:S(2)}, u32[]{:S(2)}) collective-permute-start(bf16[16,128]{1,0:T(8,128)(2,1)S(1)} %get-tuple-element.29), channel_id=1, source_target_pairs={{0,8},{1,9},{2,10},{3,11},{4,0},{5,1},{6,2},{7,3},{8,12},{9,13},{1... | collective-permute-start | bytes 12296 | tf_op jit(solution)/shard_map/ppermute | solution.py:252
  34.2 1.6 %collective-permute-start.8 = (bf16[272,512]{1,0:T(8,128)(2,1)S(1)}, bf16[272,512]{1,0:T(8,128)(2,1)S(1)}, u32[]{:S(2)}, u32[]{:S(2)}) collective-permute-start(bf16[272,512]{1,0:T(8,128)(2,1)S(1)} %collective-permute-done.5.refs_3_.refs_7_), channel_id=1, source_target_pairs={{0,1},{1,0},{2,3},{3,2},{4,5},{5,4},{6,7},{7,6},{8,9},{9,8},{10,11... | collective-permute-start | bytes 835592 | tf_op jit(solution)/shard_map/ppermute | solution.py:248
  34.2 4.9 %collective-permute-start.7 = (bf16[512,512]{1,0:T(8,128)(2,1)S(1)}, bf16[512,512]{1,0:T(8,128)(2,1)S(1)}, u32[]{:S(2)}, u32[]{:S(2)}) collective-permute-start(bf16[512,512]{1,0:T(8,128)(2,1)S(1)} %collective-permute-done.4.refs_2_.refs_6_), channel_id=1, source_target_pairs={{0,1},{1,0},{2,3},{3,2},{4,5},{5,4},{6,7},{7,6},{8,9},{9,8},{10,11... | collective-permute-start | bytes 1572872 | tf_op jit(solution)/shard_map/ppermute | solution.py:248
  34.7 5.9 %collective-permute-start.2 = (bf16[512,512]{1,0:T(8,128)(2,1)S(1)}, bf16[512,512]{1,0:T(8,128)(2,1)S(1)}, u32[]{:S(2)}, u32[]{:S(2)}) collective-permute-start(bf16[512,512]{1,0:T(8,128)(2,1)S(1)} %first.1.first_ref.refs_0_.refs_2_), channel_id=1, source_target_pairs={{0,1},{1,0},{2,3},{3,2},{4,5},{5,4},{6,7},{7,6},{8,9},{9,8},{10,11... | collective-permute-start | bytes 1572872 | tf_op jit(solution)/shard_map/ppermute | solution.py:248
  34.7 5.8 %collective-permute-start.3 = (bf16[272,512]{1,0:T(8,128)(2,1)S(1)}, bf16[272,512]{1,0:T(8,128)(2,1)S(1)}, u32[]{:S(2)}, u32[]{:S(2)}) collective-permute-start(bf16[272,512]{1,0:T(8,128)(2,1)S(1)} %get-tuple-element.31.refs_1_.refs_3_), channel_id=1, source_target_pairs={{0,1},{1,0},{2,3},{3,2},{4,5},{5,4},{6,7},{7,6},{8,9},{9,8},{10,11... | collective-permute-start | bytes 835592 | tf_op jit(solution)/shard_map/ppermute | solution.py:248
  35.7 12.5 %collective-permute-start.1 = (bf16[256,512]{1,0:T(8,128)(2,1)S(1)}, bf16[256,512]{1,0:T(8,128)(2,1)S(1)}, u32[]{:S(2)}, u32[]{:S(2)}) collective-permute-start(bf16[256,512]{1,0:T(8,128)(2,1)S(1)} %get-tuple-element.30), channel_id=1, source_target_pairs={{0,8},{1,9},{2,10},{3,11},{4,0},{5,1},{6,2},{7,3},{8,12},{9,13},{1... | collective-permute-start | bytes 786440 | tf_op jit(solution)/shard_map/ppermute | solution.py:252
  46.9 7.3 %collective-permute-start.10 = (f32[8,128]{1,0:T(8,128)S(1)}, f32[8,128]{1,0:T(8,128)S(1)}, u32[]{:S(2)}, u32[]{:S(2)}) collective-permute-start(f32[8,128]{1,0:T(8,128)S(1)} %get-tuple-element.45), channel_id=1, source_target_pairs={{12,0},{13,1},{14,2},{15,3},{4,8},{5,9},{6,10},{7,11},{28,16},{29,... | collective-permute-start | bytes 12296 | tf_op jit(solution)/shard_map/ppermute | solution.py:252
  49.3 6.7 %collective-permute-start.11 = (f32[8,128]{1,0:T(8,128)S(1)}, f32[8,128]{1,0:T(8,128)S(1)}, u32[]{:S(2)}, u32[]{:S(2)}) collective-permute-start(f32[8,128]{1,0:T(8,128)S(1)} %get-tuple-element.46), channel_id=1, source_target_pairs={{8,0},{9,1},{10,2},{11,3},{0,4},{1,5},{2,6},{3,7},{12,8},{13,9},{1... | collective-permute-start | bytes 12296 | tf_op jit(solution)/shard_map/ppermute | solution.py:252
  54.2 1.9 %collective-permute-start.14 = (f32[8,128]{1,0:T(8,128)S(1)}, f32[8,128]{1,0:T(8,128)S(1)}, u32[]{:S(2)}, u32[]{:S(2)}) collective-permute-start(f32[8,128]{1,0:T(8,128)S(1)} %get-tuple-element.52), channel_id=1, source_target_pairs={{0,1},{1,0},{2,3},{3,2},{4,5},{5,4},{6,7},{7,6},{8,9},{9,8},{10,11... | collective-permute-start | bytes 12296 | tf_op jit(solution)/shard_map/ppermute | solution.py:248
  54.2 3.6 %collective-permute-start.13 = (f32[8,128]{1,0:T(8,128)S(1)}, f32[8,128]{1,0:T(8,128)S(1)}, u32[]{:S(2)}, u32[]{:S(2)}) collective-permute-start(f32[8,128]{1,0:T(8,128)S(1)} %get-tuple-element.50), channel_id=1, source_target_pairs={{0,2},{1,3},{2,0},{3,1},{4,6},{5,7},{6,4},{7,5},{8,10},{9,11},{10,... | collective-permute-start | bytes 12296 | tf_op jit(solution)/shard_map/ppermute | solution.py:248
  55.7 3.0 %collective-permute-start.12 = (f32[8,128]{1,0:T(8,128)S(1)}, f32[8,128]{1,0:T(8,128)S(1)}, u32[]{:S(2)}, u32[]{:S(2)}) collective-permute-start(f32[8,128]{1,0:T(8,128)S(1)} %get-tuple-element.48), channel_id=1, source_target_pairs={{0,3},{1,2},{2,1},{3,0},{4,7},{5,6},{6,5},{7,4},{8,11},{9,10},{10,... | collective-permute-start | bytes 12296 | tf_op jit(solution)/shard_map/ppermute | solution.py:248

commit v18 on v17

--- a/solution.py
+++ b/solution.py
@@ -13,6 +13,8 @@
 BASE = 64.0
 TILE = 256
 FIRST = 512
+LATE = 128
+HALF = 640
 VMEM_LIMIT = 24 * 2**20
 
 
@@ -39,7 +41,7 @@
 
 
 def rest_kernel(
-    rows, embeddings_ref, ints_ref, first_ref, tags_ref, last_ref, block_ref, tail_ref
+    rows, embeddings_ref, ints_ref, first_ref, next_ref, last_ref, head_ref, half_ref, tail_ref
 ):
     label_row = rows // 128
     owner, label = ints_ref[0:8, :], ints_ref[label_row : label_row + 8, :]
@@ -49,18 +51,25 @@
     tags = tags.astype(jnp.float32)
     high = jnp.floor(tags * (1.0 / BASE))
     digits = jnp.concatenate([high, tags - high * BASE], axis=0).astype(jnp.bfloat16)
-    tags_ref[...] = digits
     width = embeddings_ref.shape[1]
     digits = jnp.concatenate([digits, jnp.zeros((PAD, width - 128), jnp.bfloat16)], axis=1)
     first = first_ref.shape[0]
+    next_ref[0:PAD, :] = digits
     last_ref[0:PAD, :] = digits
-    block_ref[0:PAD, :] = digits
-    block_ref[PAD : PAD + first, :] = first_ref[...]
+    head_ref[0:PAD, :] = digits
+    head_ref[PAD : PAD + first, :] = first_ref[...]
     for row in range(first, rows, 128):
         unit = unit_rows(embeddings_ref[row : row + 128, :])
         last_ref[PAD + row - first : PAD + row - first + 128, :] = unit
-        block_ref[PAD + row : PAD + row + 128, :] = unit
-        tail_ref[row - first : row - first + 128, :] = unit
+        if row < HALF:
+            head_ref[PAD + row : PAD + row + 128, :] = unit
+        else:
+            half_ref[row - HALF : row - HALF + 128, :] = unit
+        late = row - (rows - LATE)
+        if late < 0:
+            next_ref[PAD + row - first : PAD + row - first + 128, :] = unit
+        else:
+            tail_ref[late : late + 128, :] = unit
 
 
 def tag_rows(block_ref):
@@ -164,9 +173,10 @@
     away_best[...] = away_before[...]
     best = {}
     for tile in range(0, away.shape[0] - base, TILE):
-        values = away[base + tile : base + tile + TILE, :]
-        column = tag_columns(tags[0], start + tile, TILE)
-        row_best = jnp.full((TILE, 128), -1.0, jnp.float32)
+        count = min(TILE, away.shape[0] - base - tile)
+        values = away[base + tile : base + tile + count, :]
+        column = tag_columns(tags[0], start + tile, count)
+        row_best = jnp.full((count, 128), -1.0, jnp.float32)
         for which in range(PLANE):
             for first, part in row_slices(blocks[which]):
                 found = dot_rows(values, part[...])
@@ -178,7 +188,7 @@
                     folded = fold_sublanes(masked)
                     place = which, row
                     best[place] = jnp.maximum(best[place], folded) if place in best else folded
-        place = pl.ds((start + tile) // 128, TILE // 128)
+        place = pl.ds((start + tile) // 128, count // 128)
         away_best[place, :] = fold_lanes(row_best)
     for which in range(PLANE):
         plane_best[which][...] = plane_before[which][...]
@@ -231,14 +241,15 @@
         return jax.ShapeDtypeStruct((count, width), jnp.bfloat16)
 
     (first,) = kernel(first_kernel, (embeddings,), (part_shape(FIRST),), "first")
-    tags, last, block, tail = kernel(
+    after_first, last, head, half, tail = kernel(
         functools.partial(rest_kernel, rows),
         (embeddings, ints, first),
         (
-            jax.ShapeDtypeStruct((PAD, 128), jnp.bfloat16),
+            part_shape(PAD + rows - FIRST - LATE),
             part_shape(PAD + rows - FIRST),
-            part_shape(PAD + rows),
-            part_shape(rows - FIRST),
+            part_shape(PAD + HALF),
+            part_shape(rows - HALF),
+            part_shape(LATE),
         ),
         "rest",
     )
@@ -254,12 +265,13 @@
     split, *others = plane_steps(planes)
     away = [moved(first, split)]
     for n, step in enumerate(others):
-        away.append(moved(after(block, away[-1]) if n else block, step))
-    away_tags = moved(tags, split)
+        parts = [after(part, *away[-1]) if n else part for part in (head, half)]
+        away.append([moved(part, step) for part in parts])
+    away_next = moved(after_first, split)
     away_tail = moved(tail, split)
     beside = [mate(part, 2) for part in own]
     near = [mate(part, 1) for part in own]
-    across = [mate(after(part, away[0], away_tags), 1) for part in beside]
+    across = [mate(after(part, away[0], away_next), 1) for part in beside]
 
     (best,) = kernel(
         functools.partial(plane_kernel, rows, False),
@@ -287,16 +299,18 @@
         )
         return away_best, plane_best
 
-    split_best, plane_best = crossed(away[0], away_tags, 0, 0, empty, plane_best)
+    split_best, plane_best = crossed(away[0], away_next, 0, 0, empty, plane_best)
+    split_best, plane_best = crossed(away_next, away_next, FIRST, PAD, split_best, plane_best)
     for n, step in enumerate(others):
-        part = away[n + 1]
-        away_best, plane_best = crossed(part, part, 0, PAD, empty, plane_best)
+        one, two = away[n + 1]
+        away_best, plane_best = crossed(one, one, 0, PAD, empty, plane_best)
+        away_best, plane_best = crossed(two, one, HALF, 0, away_best, plane_best)
         backs.append(moved(away_best, step, back=True))
         if len(step) < planes:
             sources = sum(1 << z for z, _ in step)
             sent = (jnp.int32(sources) >> (lax.axis_index("dp") // PLANE)) & 1
             masks[n] = jnp.broadcast_to(sent == 1, (rows,))
-    split_best, plane_best = crossed(away_tail, away_tags, FIRST, 0, split_best, plane_best)
+    split_best, plane_best = crossed(away_tail, away_next, rows - LATE, 0, split_best, plane_best)
     first_backs = tuple(backs)
     backs.append(moved(split_best, split, back=True))
     best = plane_best[0].reshape(-1)[:rows]

time: 59.5 us -> 52.1 us (0.88)
  waiting for transfers between devices: 28.6 us -> 16.4 us
  Pallas kernels: 9.16 us -> 11.8 us
  starting transfers between devices: 19.3 us -> 21.4 us
    ppermute x6 -> x7, waiting for transfers between devices: 25.4 us -> 10.2 us  [moved(): lax.ppermute(value, 'dp', [(t, s) for s, t in pairs] if back else pairs)]
    ppermute x9, waiting for transfers between devices: 3.24 us -> 6.18 us  [mate(): return lax.ppermute(value, 'dp', [(i, i ^ distance) for i in range(peers)])]
    pallas_call x7 -> x9, Pallas kernels: 9.16 us -> 11.8 us  [kernel(): pl.pallas_call(body, out_shape=tuple(outputs), in_specs=whole(len(inputs)...]
    ppermute x6 -> x7, starting transfers between devices: 14.4 us -> 16.5 us  [moved(): lax.ppermute(value, 'dp', [(t, s) for s, t in pairs] if back else pairs)]
  transfers between devices with their start and end apart: 15 -> 16, of which waited for: 5 -> 6; matrix products, arithmetic and copies ran while one was open for 0% -> 0% of each run, Pallas kernels for 15% -> 22%
where the time goes in v18:
time: 52.1 us; the launch traced here: 51.9 us
  starting transfers between devices  21.4 us (41%)
  waiting for transfers between devices  16.4 us (31%)
  Pallas kernels  11.8 us (23%)
  local copies, waits for them, and re-layouts  1.51 us (3%)
  other arithmetic  0.6 us (1%)
    ppermute x7, starting transfers between devices, moved(): lax.ppermute(value, 'dp', [(t, s) for s, t in pairs] if back else pairs)  16.5 us
    pallas_call x9, Pallas kernels, kernel(): pl.pallas_call(body, out_shape=tuple(outputs), in_specs=whole(len(inputs)...  11.8 us
    ppermute x7, waiting for transfers between devices, moved(): lax.ppermute(value, 'dp', [(t, s) for s, t in pairs] if back else pairs)  10.2 us
    ppermute x9, waiting for transfers between devices, mate(): return lax.ppermute(value, 'dp', [(i, i ^ distance) for i in range(peers)])  6.18 us
    ppermute x9, starting transfers between devices, mate(): return lax.ppermute(value, 'dp', [(i, i ^ distance) for i in range(peers)])  4.91 us
    unnamed x10, local copies, waits for them, and re-layouts  1.42 us
  transfers between devices with their start and end apart: 16, of which 6 were waited for; matrix products, arithmetic and copies ran while one was open for 0% of the time, Pallas kernels for 22%

profile of v18, /device:TPU:0, one launch (start us, length us, event | category | flops | bytes accessed | tf_op | source)
XLA Modules:
  0.0 51.9 jit_solution(3849055213489811714)
XLA Ops:
  0.0 1.4 %copy-done = f32[768,512]{1,0:T(8,128)S(1)} copy-done((f32[768,512]{1,0:T(8,128)S(1)}, f32[768,512]{1,0:T(8,128)}, u32[]{:S(2)}) %copy-start) | copy-done | bytes 1572888
  1.6 4.1 %collective-permute-start.6 = (bf16[512,512]{1,0:T(8,128)(2,1)S(1)}, bf16[512,512]{1,0:T(8,128)(2,1)S(1)}, u32[]{:S(2)}, u32[]{:S(2)}) collective-permute-start(bf16[512,512]{1,0:T(8,128)(2,1)S(1)} %first.1.first_ref.refs_0_.refs_2_), channel_id=1, source_target_pairs={{0,8},{1,9},{2,10},{3,11},{4,0},{5,1},{6,2},{7,3},{8,12},{9,13},{1... | collective-permute-start | bytes 1572872 | tf_op jit(solution)/shard_map/ppermute | solution.py:263
  5.7 1.5 %collective-permute-start.4 = (bf16[512,512]{1,0:T(8,128)(2,1)S(1)}, bf16[512,512]{1,0:T(8,128)(2,1)S(1)}, u32[]{:S(2)}, u32[]{:S(2)}) collective-permute-start(bf16[512,512]{1,0:T(8,128)(2,1)S(1)} %first.1.first_ref.refs_0_.refs_2_), channel_id=1, source_target_pairs={{0,2},{1,3},{2,0},{3,1},{4,6},{5,7},{6,4},{7,5},{8,10},{9,11},{10,... | collective-permute-start | bytes 1572872 | tf_op jit(solution)/shard_map/ppermute | solution.py:259
  7.5 1.6 %collective-permute-start = (bf16[144,512]{1,0:T(8,128)(2,1)S(1)}, bf16[144,512]{1,0:T(8,128)(2,1)S(1)}, u32[]{:S(2)}, u32[]{:S(2)}) collective-permute-start(bf16[144,512]{1,0:T(8,128)(2,1)S(1)} %get-tuple-element.40), channel_id=1, source_target_pairs={{0,8},{1,9},{2,10},{3,11},{4,0},{5,1},{6,2},{7,3},{8,12},{9,13},{1... | collective-permute-start | bytes 442376 | tf_op jit(solution)/shard_map/ppermute | solution.py:263
  9.6 2.3 %collective-permute-start.9 = (bf16[656,512]{1,0:T(8,128)(2,1)S(1)}, bf16[656,512]{1,0:T(8,128)(2,1)S(1)}, u32[]{:S(2)}, u32[]{:S(2)}) collective-permute-start(bf16[656,512]{1,0:T(8,128)(2,1)S(1)} %get-tuple-element.51), channel_id=1, source_target_pairs={{0,12},{1,13},{2,14},{3,15},{8,4},{9,5},{10,6},{11,7},{16,28},{17,... | collective-permute-start | bytes 2015240 | tf_op jit(solution)/shard_map/ppermute | solution.py:263
  11.9 9.2 %collective-permute-done.refs_0_.refs_1_ = bf16[144,512]{1,0:T(8,128)(2,1)S(1)} collective-permute-done((bf16[144,512]{1,0:T(8,128)(2,1)S(1)}, bf16[144,512]{1,0:T(8,128)(2,1)S(1)}, u32[]{:S(2)}, u32[]{:S(2)}) %collective-permute-start) | collective-permute-done | bytes 147488 | tf_op jit(solution)/shard_map/ppermute | solution.py:263
  21.7 3.3 %collective-permute-done.5.refs_3_.refs_7_ = bf16[272,512]{1,0:T(8,128)(2,1)S(1)} collective-permute-done((bf16[272,512]{1,0:T(8,128)(2,1)S(1)}, bf16[272,512]{1,0:T(8,128)(2,1)S(1)}, u32[]{:S(2)}, u32[]{:S(2)}) %collective-permute-start.5) | collective-permute-done | bytes 278560 | tf_op jit(solution)/shard_map/ppermute | solution.py:259
  25.0 0.5 collective-permute-start.3
  25.5 1.0 %collective-permute-done.8.refs_5_.refs_9_ = bf16[272,512]{1,0:T(8,128)(2,1)S(1)} collective-permute-done((bf16[272,512]{1,0:T(8,128)(2,1)S(1)}, bf16[272,512]{1,0:T(8,128)(2,1)S(1)}, u32[]{:S(2)}, u32[]{:S(2)}) %collective-permute-start.8) | collective-permute-done | bytes 278560 | tf_op jit(solution)/shard_map/ppermute | solution.py:259
  26.6 3.3 %collective-permute-start.10 = (bf16[128,512]{1,0:T(8,128)(2,1)S(1)}, bf16[128,512]{1,0:T(8,128)(2,1)S(1)}, u32[]{:S(2)}, u32[]{:S(2)}) collective-permute-start(bf16[128,512]{1,0:T(8,128)(2,1)S(1)} %get-tuple-element.52), channel_id=1, source_target_pairs={{0,12},{1,13},{2,14},{3,15},{8,4},{9,5},{10,6},{11,7},{16,28},{17,... | collective-permute-start | bytes 393224 | tf_op jit(solution)/shard_map/ppermute | solution.py:263
  29.9 1.5 %plane_far.1.refs_6_ = f32[8,128]{1,0:T(8,128)S(1)} custom-call(bf16[512,512]{1,0:T(8,128)(2,1)S(1)} %first.1.first_ref.refs_0_.refs_2_, bf16[272,512]{1,0:T(8,128)(2,1)S(1)} %get-tuple-element.42.refs_1_.refs_3_, bf16[512,512]{1,0:T(8,128)(2,1)S(1)} %collective-permute-done.4.refs_2_.refs_6_, bf16[272,512]{1,0:T(8,128)(2,1)S(1)} %collective-permute-done.5.refs_3_.refs_7_, ...), custom_call_target="tpu_custom_call" | custom-call | flops 1 | bytes 1 | tf_op jit(solution)/shard_map/plane_far/pallas_call | solution.py:230
  31.5 1.4 %plane_near.1.refs_11_ = f32[8,128]{1,0:T(8,128)S(1)} custom-call(bf16[512,512]{1,0:T(8,128)(2,1)S(1)} %first.1.first_ref.refs_0_.refs_2_, bf16[272,512]{1,0:T(8,128)(2,1)S(1)} %get-tuple-element.42.refs_1_.refs_3_, bf16[512,512]{1,0:T(8,128)(2,1)S(1)} %first.1.first_ref.refs_0_.refs_2_, bf16[272,512]{1,0:T(8,128)(2,1)S(1)} %get-tuple-element.42.refs_1_.refs_3_, ...), custom_call_target="tpu_custom_call" | custom-call | flops 1 | bytes 1 | tf_op jit(solution)/shard_map/plane_near/pallas_call | solution.py:230
  32.9 2.0 %cross.5 = (f32[8,128]{1,0:T(8,128)S(1)}, f32[8,128]{1,0:T(8,128)S(1)}, f32[8,128]{1,0:T(8,128)S(1)}, f32[8,128]{1,0:T(8,128)S(1)}, f32[8,128]{1,0:T(8,128)S(1)}) custom-call(bf16[144,512]{1,0:T(8,128)(2,1)S(1)} %collective-permute-done.refs_0_.refs_1_, bf16[512,512]{1,0:T(8,128)(2,1)S(1)} %collective-permute-done.6.refs_1_, ...), custom_call_target="tpu_custom_call" | custom-call | flops 1 | bytes 1 | tf_op jit(solution)/shard_map/cross/pallas_call | solution.py:230
  34.9 1.2 %cross.6 = (f32[8,128]{1,0:T(8,128)S(1)}, f32[8,128]{1,0:T(8,128)S(1)}, f32[8,128]{1,0:T(8,128)S(1)}, f32[8,128]{1,0:T(8,128)S(1)}, f32[8,128]{1,0:T(8,128)S(1)}) custom-call(bf16[144,512]{1,0:T(8,128)(2,1)S(1)} %collective-permute-done.refs_0_.refs_1_, bf16[144,512]{1,0:T(8,128)(2,1)S(1)} %collective-permute-done.refs_0_.refs_1_, ...), custom_call_target="tpu_custom_call" | custom-call | flops 1 | bytes 1 | tf_op jit(solution)/shard_map/cross/pallas_call | solution.py:230
  36.1 3.0 %cross.7 = (f32[8,128]{1,0:T(8,128)S(1)}, f32[8,128]{1,0:T(8,128)S(1)}, f32[8,128]{1,0:T(8,128)S(1)}, f32[8,128]{1,0:T(8,128)S(1)}, f32[8,128]{1,0:T(8,128)S(1)}) custom-call(bf16[656,512]{1,0:T(8,128)(2,1)S(1)} %collective-permute-done.9.refs_0_.refs_1_, bf16[656,512]{1,0:T(8,128)(2,1)S(1)} %collective-permute-done.9.refs_0_.refs_1_, ...), custom_call_target="tpu_custom_call" | custom-call | flops 1 | bytes 1 | tf_op jit(solution)/shard_map/cross/pallas_call | solution.py:230
  39.1 1.2 %cross.8 = (f32[8,128]{1,0:T(8,128)S(1)}, f32[8,128]{1,0:T(8,128)S(1)}, f32[8,128]{1,0:T(8,128)S(1)}, f32[8,128]{1,0:T(8,128)S(1)}, f32[8,128]{1,0:T(8,128)S(1)}) custom-call(bf16[656,512]{1,0:T(8,128)(2,1)S(1)} %collective-permute-done.9.refs_0_.refs_1_, bf16[128,512]{1,0:T(8,128)(2,1)S(1)} %collective-permute-done.10.refs_1_, ...), custom_call_target="tpu_custom_call" | custom-call | flops 1 | bytes 1 | tf_op jit(solution)/shard_map/cross/pallas_call | solution.py:230
  40.3 1.3 %collective-permute-start.11 = (f32[8,128]{1,0:T(8,128)S(1)}, f32[8,128]{1,0:T(8,128)S(1)}, u32[]{:S(2)}, u32[]{:S(2)}) collective-permute-start(f32[8,128]{1,0:T(8,128)S(1)} %get-tuple-element.67), channel_id=1, source_target_pairs={{12,0},{13,1},{14,2},{15,3},{4,8},{5,9},{6,10},{7,11},{28,16},{29,... | collective-permute-start | bytes 12296 | tf_op jit(solution)/shard_map/ppermute | solution.py:263
  41.6 1.2 %cross.9 = (f32[8,128]{1,0:T(8,128)S(1)}, f32[8,128]{1,0:T(8,128)S(1)}, f32[8,128]{1,0:T(8,128)S(1)}, f32[8,128]{1,0:T(8,128)S(1)}, f32[8,128]{1,0:T(8,128)S(1)}) custom-call(bf16[144,512]{1,0:T(8,128)(2,1)S(1)} %collective-permute-done.refs_0_.refs_1_, bf16[128,512]{1,0:T(8,128)(2,1)S(1)} %collective-permute-done.1.refs_1_, ...), custom_call_target="tpu_custom_call" | custom-call | flops 1 | bytes 1 | tf_op jit(solution)/shard_map/cross/pallas_call | solution.py:230
  42.9 3.8 %collective-permute-start.12 = (f32[8,128]{1,0:T(8,128)S(1)}, f32[8,128]{1,0:T(8,128)S(1)}, u32[]{:S(2)}, u32[]{:S(2)}) collective-permute-start(f32[8,128]{1,0:T(8,128)S(1)} %get-tuple-element.68), channel_id=1, source_target_pairs={{8,0},{9,1},{10,2},{11,3},{0,4},{1,5},{2,6},{3,7},{12,8},{13,9},{1... | collective-permute-start | bytes 12296 | tf_op jit(solution)/shard_map/ppermute | solution.py:263
  46.6 1.0 %collective-permute-done.11 = f32[8,128]{1,0:T(8,128)S(1)} collective-permute-done((f32[8,128]{1,0:T(8,128)S(1)}, f32[8,128]{1,0:T(8,128)S(1)}, u32[]{:S(2)}, u32[]{:S(2)}) %collective-permute-start.11) | collective-permute-done | bytes 4128 | tf_op jit(solution)/shard_map/ppermute | solution.py:263
  47.6 1.5 %collective-permute-start.14 = (f32[8,128]{1,0:T(8,128)S(1)}, f32[8,128]{1,0:T(8,128)S(1)}, u32[]{:S(2)}, u32[]{:S(2)}) collective-permute-start(f32[8,128]{1,0:T(8,128)S(1)} %get-tuple-element.72), channel_id=1, source_target_pairs={{0,2},{1,3},{2,0},{3,1},{4,6},{5,7},{6,4},{7,5},{8,10},{9,11},{10,... | collective-permute-start | bytes 12296 | tf_op jit(solution)/shard_map/ppermute | solution.py:259
  49.5 1.2 %collective-permute-done.13 = f32[8,128]{1,0:T(8,128)S(1)} collective-permute-done((f32[8,128]{1,0:T(8,128)S(1)}, f32[8,128]{1,0:T(8,128)S(1)}, u32[]{:S(2)}, u32[]{:S(2)}) %collective-permute-start.13) | collective-permute-done | bytes 4128 | tf_op jit(solution)/shard_map/ppermute | solution.py:259
  50.7 0.6 %collective-permute-done.14 = f32[8,128]{1,0:T(8,128)S(1)} collective-permute-done((f32[8,128]{1,0:T(8,128)S(1)}, f32[8,128]{1,0:T(8,128)S(1)}, u32[]{:S(2)}, u32[]{:S(2)}) %collective-permute-start.14) | collective-permute-done | bytes 4128 | tf_op jit(solution)/shard_map/ppermute | solution.py:259
  51.3 0.6 %maximum_bitcast_fusion = f32[768]{0:T(1024)} fusion(f32[8,128]{1,0:T(8,128)S(1)} %collective-permute-done.15, f32[8,128]{1,0:T(8,128)S(1)} %collective-permute-done.14, f32[8,128]{1,0:T(8,128)S(1)} %collective-permute-done.13, f32[8,128]{1,0:T(8,128)S(1)} %collective-permute-done.12, f32[8,128]{1,0:T(8,128)S(1)} %collective-permute-done.11, ...), kind=kLoop, calls=%fused_computation | loop fusion | flops 4608 | bytes 21505 | tf_op jit(solution)/shard_map/max | solution.py:321
  (31 shorter events, 1.9 us)
Async XLA Ops:
  0.0 1.4 %copy-start = (f32[768,512]{1,0:T(8,128)S(1)}, f32[768,512]{1,0:T(8,128)}, u32[]{:S(2)}) copy-start(f32[768,512]{1,0:T(8,128)} %embeddings_ref.3) | copy-start | bytes 4718596
  1.4 5.8 %copy-start.2 = (s32[768]{0:T(1024)S(1)}, s32[768]{0:T(1024)}, u32[]{:S(2)}) copy-start(s32[768]{0:T(1024)} %param.5) | copy-start | bytes 9220
  1.4 5.8 %copy-start.3 = (s32[768]{0:T(1024)S(1)}, s32[768]{0:T(1024)}, u32[]{:S(2)}) copy-start(s32[768]{0:T(1024)} %param.6) | copy-start | bytes 9220
  1.4 5.8 %copy-start.4 = (s32[16]{0:T(128)S(1)}, s32[16]{0:T(128)}, u32[]{:S(2)}) copy-start(s32[16]{0:T(128)} %param.7) | copy-start | bytes 196
  1.4 5.9 %copy-start.1 = (f32[768,512]{1,0:T(8,128)S(1)}, f32[768,512]{1,0:T(8,128)}, u32[]{:S(2)}) copy-start(f32[768,512]{1,0:T(8,128)} %embeddings_ref.3) | copy-start | bytes 4718596
  1.6 19.6 %collective-permute-start.6 = (bf16[512,512]{1,0:T(8,128)(2,1)S(1)}, bf16[512,512]{1,0:T(8,128)(2,1)S(1)}, u32[]{:S(2)}, u32[]{:S(2)}) collective-permute-start(bf16[512,512]{1,0:T(8,128)(2,1)S(1)} %first.1.first_ref.refs_0_.refs_2_), channel_id=1, source_target_pairs={{0,8},{1,9},{2,10},{3,11},{4,0},{5,1},{6,2},{7,3},{8,12},{9,13},{1... | collective-permute-start | bytes 1572872 | tf_op jit(solution)/shard_map/ppermute | solution.py:263
  5.7 15.5 %collective-permute-start.4 = (bf16[512,512]{1,0:T(8,128)(2,1)S(1)}, bf16[512,512]{1,0:T(8,128)(2,1)S(1)}, u32[]{:S(2)}, u32[]{:S(2)}) collective-permute-start(bf16[512,512]{1,0:T(8,128)(2,1)S(1)} %first.1.first_ref.refs_0_.refs_2_), channel_id=1, source_target_pairs={{0,2},{1,3},{2,0},{3,1},{4,6},{5,7},{6,4},{7,5},{8,10},{9,11},{10,... | collective-permute-start | bytes 1572872 | tf_op jit(solution)/shard_map/ppermute | solution.py:259
  7.5 13.7 %collective-permute-start = (bf16[144,512]{1,0:T(8,128)(2,1)S(1)}, bf16[144,512]{1,0:T(8,128)(2,1)S(1)}, u32[]{:S(2)}, u32[]{:S(2)}) collective-permute-start(bf16[144,512]{1,0:T(8,128)(2,1)S(1)} %get-tuple-element.40), channel_id=1, source_target_pairs={{0,8},{1,9},{2,10},{3,11},{4,0},{5,1},{6,2},{7,3},{8,12},{9,13},{1... | collective-permute-start | bytes 442376 | tf_op jit(solution)/shard_map/ppermute | solution.py:263
  9.1 15.9 %collective-permute-start.5 = (bf16[272,512]{1,0:T(8,128)(2,1)S(1)}, bf16[272,512]{1,0:T(8,128)(2,1)S(1)}, u32[]{:S(2)}, u32[]{:S(2)}) collective-permute-start(bf16[272,512]{1,0:T(8,128)(2,1)S(1)} %get-tuple-element.42.refs_1_.refs_3_), channel_id=1, source_target_pairs={{0,2},{1,3},{2,0},{3,1},{4,6},{5,7},{6,4},{7,5},{8,10},{9,11},{10,... | collective-permute-start | bytes 835592 | tf_op jit(solution)/shard_map/ppermute | solution.py:259
  9.6 26.5 %collective-permute-start.9 = (bf16[656,512]{1,0:T(8,128)(2,1)S(1)}, bf16[656,512]{1,0:T(8,128)(2,1)S(1)}, u32[]{:S(2)}, u32[]{:S(2)}) collective-permute-start(bf16[656,512]{1,0:T(8,128)(2,1)S(1)} %get-tuple-element.51), channel_id=1, source_target_pairs={{0,12},{1,13},{2,14},{3,15},{8,4},{9,5},{10,6},{11,7},{16,28},{17,... | collective-permute-start | bytes 2015240 | tf_op jit(solution)/shard_map/ppermute | solution.py:263
  21.2 8.7 %collective-permute-start.7 = (bf16[512,512]{1,0:T(8,128)(2,1)S(1)}, bf16[512,512]{1,0:T(8,128)(2,1)S(1)}, u32[]{:S(2)}, u32[]{:S(2)}) collective-permute-start(bf16[512,512]{1,0:T(8,128)(2,1)S(1)} %collective-permute-done.4.refs_2_.refs_6_), channel_id=1, source_target_pairs={{0,1},{1,0},{2,3},{3,2},{4,5},{5,4},{6,7},{7,6},{8,9},{9,8},{10,11... | collective-permute-start | bytes 1572872 | tf_op jit(solution)/shard_map/ppermute | solution.py:259
  21.2 10.3 %collective-permute-start.2 = (bf16[512,512]{1,0:T(8,128)(2,1)S(1)}, bf16[512,512]{1,0:T(8,128)(2,1)S(1)}, u32[]{:S(2)}, u32[]{:S(2)}) collective-permute-start(bf16[512,512]{1,0:T(8,128)(2,1)S(1)} %first.1.first_ref.refs_0_.refs_2_), channel_id=1, source_target_pairs={{0,1},{1,0},{2,3},{3,2},{4,5},{5,4},{6,7},{7,6},{8,9},{9,8},{10,11... | collective-permute-start | bytes 1572872 | tf_op jit(solution)/shard_map/ppermute | solution.py:259
  25.0 1.6 %collective-permute-start.8 = (bf16[272,512]{1,0:T(8,128)(2,1)S(1)}, bf16[272,512]{1,0:T(8,128)(2,1)S(1)}, u32[]{:S(2)}, u32[]{:S(2)}) collective-permute-start(bf16[272,512]{1,0:T(8,128)(2,1)S(1)} %collective-permute-done.5.refs_3_.refs_7_), channel_id=1, source_target_pairs={{0,1},{1,0},{2,3},{3,2},{4,5},{5,4},{6,7},{7,6},{8,9},{9,8},{10,11... | collective-permute-start | bytes 835592 | tf_op jit(solution)/shard_map/ppermute | solution.py:259
  25.0 6.4 %collective-permute-start.3 = (bf16[272,512]{1,0:T(8,128)(2,1)S(1)}, bf16[272,512]{1,0:T(8,128)(2,1)S(1)}, u32[]{:S(2)}, u32[]{:S(2)}) collective-permute-start(bf16[272,512]{1,0:T(8,128)(2,1)S(1)} %get-tuple-element.42.refs_1_.refs_3_), channel_id=1, source_target_pairs={{0,1},{1,0},{2,3},{3,2},{4,5},{5,4},{6,7},{7,6},{8,9},{9,8},{10,11... | collective-permute-start | bytes 835592 | tf_op jit(solution)/shard_map/ppermute | solution.py:259
  26.6 12.5 %collective-permute-start.10 = (bf16[128,512]{1,0:T(8,128)(2,1)S(1)}, bf16[128,512]{1,0:T(8,128)(2,1)S(1)}, u32[]{:S(2)}, u32[]{:S(2)}) collective-permute-start(bf16[128,512]{1,0:T(8,128)(2,1)S(1)} %get-tuple-element.52), channel_id=1, source_target_pairs={{0,12},{1,13},{2,14},{3,15},{8,4},{9,5},{10,6},{11,7},{16,28},{17,... | collective-permute-start | bytes 393224 | tf_op jit(solution)/shard_map/ppermute | solution.py:263
  29.9 11.8 %collective-permute-start.1 = (bf16[128,512]{1,0:T(8,128)(2,1)S(1)}, bf16[128,512]{1,0:T(8,128)(2,1)S(1)}, u32[]{:S(2)}, u32[]{:S(2)}) collective-permute-start(bf16[128,512]{1,0:T(8,128)(2,1)S(1)} %get-tuple-element.41), channel_id=1, source_target_pairs={{0,8},{1,9},{2,10},{3,11},{4,0},{5,1},{6,2},{7,3},{8,12},{9,13},{1... | collective-permute-start | bytes 393224 | tf_op jit(solution)/shard_map/ppermute | solution.py:263
  40.3 7.3 %collective-permute-start.11 = (f32[8,128]{1,0:T(8,128)S(1)}, f32[8,128]{1,0:T(8,128)S(1)}, u32[]{:S(2)}, u32[]{:S(2)}) collective-permute-start(f32[8,128]{1,0:T(8,128)S(1)} %get-tuple-element.67), channel_id=1, source_target_pairs={{12,0},{13,1},{14,2},{15,3},{4,8},{5,9},{6,10},{7,11},{28,16},{29,... | collective-permute-start | bytes 12296 | tf_op jit(solution)/shard_map/ppermute | solution.py:263
  42.9 6.6 %collective-permute-start.12 = (f32[8,128]{1,0:T(8,128)S(1)}, f32[8,128]{1,0:T(8,128)S(1)}, u32[]{:S(2)}, u32[]{:S(2)}) collective-permute-start(f32[8,128]{1,0:T(8,128)S(1)} %get-tuple-element.68), channel_id=1, source_target_pairs={{8,0},{9,1},{10,2},{11,3},{0,4},{1,5},{2,6},{3,7},{12,8},{13,9},{1... | collective-permute-start | bytes 12296 | tf_op jit(solution)/shard_map/ppermute | solution.py:263
  47.6 3.0 %collective-permute-start.13 = (f32[8,128]{1,0:T(8,128)S(1)}, f32[8,128]{1,0:T(8,128)S(1)}, u32[]{:S(2)}, u32[]{:S(2)}) collective-permute-start(f32[8,128]{1,0:T(8,128)S(1)} %get-tuple-element.70), channel_id=1, source_target_pairs={{0,3},{1,2},{2,1},{3,0},{4,7},{5,6},{6,5},{7,4},{8,11},{9,10},{10,... | collective-permute-start | bytes 12296 | tf_op jit(solution)/shard_map/ppermute | solution.py:259
  47.6 3.6 %collective-permute-start.14 = (f32[8,128]{1,0:T(8,128)S(1)}, f32[8,128]{1,0:T(8,128)S(1)}, u32[]{:S(2)}, u32[]{:S(2)}) collective-permute-start(f32[8,128]{1,0:T(8,128)S(1)} %get-tuple-element.72), channel_id=1, source_target_pairs={{0,2},{1,3},{2,0},{3,1},{4,6},{5,7},{6,4},{7,5},{8,10},{9,11},{10,... | collective-permute-start | bytes 12296 | tf_op jit(solution)/shard_map/ppermute | solution.py:259
  49.1 2.1 %collective-permute-start.15 = (f32[8,128]{1,0:T(8,128)S(1)}, f32[8,128]{1,0:T(8,128)S(1)}, u32[]{:S(2)}, u32[]{:S(2)}) collective-permute-start(f32[8,128]{1,0:T(8,128)S(1)} %get-tuple-element.74), channel_id=1, source_target_pairs={{0,1},{1,0},{2,3},{3,2},{4,5},{5,4},{6,7},{7,6},{8,9},{9,8},{10,11... | collective-permute-start | bytes 12296 | tf_op jit(solution)/shard_map/ppermute | solution.py:259

commit v19 on v15

--- a/solution.py
+++ b/solution.py
@@ -269,7 +269,7 @@
     )
     plane = (*own, *near, *beside, *across)
     plane_best = [best] + [jnp.full(lanes.shape, -1.0, jnp.float32)] * (PLANE - 1)
-    backs, masks = [], {}
+    backs = []
     for n, (pairs, received) in enumerate(away):
         away_best = jnp.full(lanes.shape, -1.0, jnp.float32)
         if n:
@@ -284,17 +284,19 @@
                 (lanes,) * (PLANE + 1),
                 "cross",
             )
-        backs.append(lax.ppermute(away_best, "dp", [(t, s) for s, t in pairs]))
+        answer = after(away_best, *(back for back, _ in backs[:1]))
+        back = lax.ppermute(answer, "dp", [(t, s) for s, t in pairs]).reshape(-1)[:rows]
+        sent = None
         if len(pairs) < peers:
             sources = sum(1 << z for z in {s // PLANE for s, _ in pairs})
             sent = (jnp.int32(sources) >> (lax.axis_index("dp") // PLANE)) & 1
-            masks[n] = jnp.broadcast_to(sent == 1, (rows,))
+        backs.append((back, sent))
     best = plane_best[0].reshape(-1)[:rows]
     for distance in (3, 2, 1):
-        backs.append(mate(after(plane_best[distance], *backs[:1]), distance))
-    for n, back in enumerate(backs):
-        back = back.reshape(-1)[:rows]
-        best = jnp.maximum(best, jnp.where(masks[n], back, -1.0) if n in masks else back)
+        back = mate(after(plane_best[distance], backs[0][0]), distance)
+        backs.insert(-1, (back.reshape(-1)[:rows], None))
+    for back, sent in backs:
+        best = jnp.maximum(back if sent is None else jnp.where(sent == 1, back, -1.0), best)
     return best
 
 

time: 50 us -> 50.3 us (level)
  starting transfers between devices: 17.5 us -> 19.2 us
  waiting for transfers between devices: 21 us -> 19.5 us
    ppermute x9, waiting for transfers between devices: 17.4 us -> 14.7 us  [mate(): return lax.ppermute(value, 'dp', [(i, i ^ distance) for i in range(peers)])]
    ppermute x2, starting transfers between devices: 4.26 us -> 5.96 us  [local(): lax.ppermute(answer, 'dp', [(t, s) for s, t in pairs]).reshape(-1)[:rows]]
    ppermute x2, waiting for transfers between devices: 0.01 us -> 1.27 us  [local(): lax.ppermute(answer, 'dp', [(t, s) for s, t in pairs]).reshape(-1)[:rows]]
  transfers between devices with their start and end apart: 15 -> 15, of which waited for: 6 -> 5; matrix products, arithmetic and copies ran while one was open for 0% -> 0% of each run, Pallas kernels for 18% -> 18%
where the time goes in v19:
time: 50.3 us; the launch traced here: 50.1 us
  waiting for transfers between devices  19.5 us (39%)
  starting transfers between devices  19.2 us (38%)
  Pallas kernels  9.08 us (18%)
  local copies, waits for them, and re-layouts  1.51 us (3%)
  other arithmetic  0.6 us (1%)
    ppermute x9, waiting for transfers between devices, mate(): return lax.ppermute(value, 'dp', [(i, i ^ distance) for i in range(peers)])  14.7 us
    pallas_call x7, Pallas kernels, kernel(): pl.pallas_call(body, out_shape=tuple(outputs), in_specs=whole(len(inputs)...  9.08 us
    ppermute x4, starting transfers between devices, local(): away.append((pairs, [lax.ppermute(part, 'dp', pairs) for part in parts]))  8.23 us
    ppermute x2, starting transfers between devices, local(): lax.ppermute(answer, 'dp', [(t, s) for s, t in pairs]).reshape(-1)[:rows]  5.96 us
    ppermute x9, starting transfers between devices, mate(): return lax.ppermute(value, 'dp', [(i, i ^ distance) for i in range(peers)])  5.03 us
    ppermute x4, waiting for transfers between devices, local(): away.append((pairs, [lax.ppermute(part, 'dp', pairs) for part in parts]))  3.54 us
    unnamed x10, local copies, waits for them, and re-layouts  1.42 us
    ppermute x2, waiting for transfers between devices, local(): lax.ppermute(answer, 'dp', [(t, s) for s, t in pairs]).reshape(-1)[:rows]  1.27 us
  transfers between devices with their start and end apart: 15, of which 5 were waited for; matrix products, arithmetic and copies ran while one was open for 0% of the time, Pallas kernels for 18%

profile of v19, /device:TPU:0, one launch (start us, length us, event | category | flops | bytes accessed | tf_op | source)
XLA Modules:
  0.0 50.1 jit_solution(10897994811034905915)
XLA Ops:
  0.0 1.4 %copy-done = f32[768,512]{1,0:T(8,128)S(1)} copy-done((f32[768,512]{1,0:T(8,128)S(1)}, f32[768,512]{1,0:T(8,128)}, u32[]{:S(2)}) %copy-start) | copy-done | bytes 1572888
  1.6 4.1 %collective-permute-start.6 = (bf16[512,512]{1,0:T(8,128)(2,1)S(1)}, bf16[512,512]{1,0:T(8,128)(2,1)S(1)}, u32[]{:S(2)}, u32[]{:S(2)}) collective-permute-start(bf16[512,512]{1,0:T(8,128)(2,1)S(1)} %first.1.first_ref.refs_0_.refs_2_.refs_3_), channel_id=1, source_target_pairs={{0,8},{1,9},{2,10},{3,11},{4,0},{5,1},{6,2},{7,3},{8,12},{9,13},{1... | collective-permute-start | bytes 1572872 | tf_op jit(solution)/shard_map/ppermute | solution.py:253
  5.7 1.5 %collective-permute-start.4 = (bf16[512,512]{1,0:T(8,128)(2,1)S(1)}, bf16[512,512]{1,0:T(8,128)(2,1)S(1)}, u32[]{:S(2)}, u32[]{:S(2)}) collective-permute-start(bf16[512,512]{1,0:T(8,128)(2,1)S(1)} %first.1.first_ref.refs_0_.refs_2_.refs_3_), channel_id=1, source_target_pairs={{0,2},{1,3},{2,0},{3,1},{4,6},{5,7},{6,4},{7,5},{8,10},{9,11},{10,... | collective-permute-start | bytes 1572872 | tf_op jit(solution)/shard_map/ppermute | solution.py:245
  7.4 0.6 %collective-permute-start.5 = (bf16[272,512]{1,0:T(8,128)(2,1)S(1)}, bf16[272,512]{1,0:T(8,128)(2,1)S(1)}, u32[]{:S(2)}, u32[]{:S(2)}) collective-permute-start(bf16[272,512]{1,0:T(8,128)(2,1)S(1)} %get-tuple-element.31.refs_1_.refs_3_.refs_4_), channel_id=1, source_target_pairs={{0,2},{1,3},{2,0},{3,1},{4,6},{5,7},{6,4},{7,5},{8,10},{9,11},{10,... | collective-permute-start | bytes 835592 | tf_op jit(solution)/shard_map/ppermute | solution.py:245
  8.0 1.6 %collective-permute-start.7 = (bf16[272,512]{1,0:T(8,128)(2,1)S(1)}, bf16[272,512]{1,0:T(8,128)(2,1)S(1)}, u32[]{:S(2)}, u32[]{:S(2)}) collective-permute-start(bf16[272,512]{1,0:T(8,128)(2,1)S(1)} %get-tuple-element.31.refs_1_.refs_3_.refs_4_), channel_id=1, source_target_pairs={{0,8},{1,9},{2,10},{3,11},{4,0},{5,1},{6,2},{7,3},{8,12},{9,13},{1... | collective-permute-start | bytes 835592 | tf_op jit(solution)/shard_map/ppermute | solution.py:253
  9.6 1.3 %collective-permute-start = (bf16[528,512]{1,0:T(8,128)(2,1)S(1)}, bf16[528,512]{1,0:T(8,128)(2,1)S(1)}, u32[]{:S(2)}, u32[]{:S(2)}) collective-permute-start(bf16[528,512]{1,0:T(8,128)(2,1)S(1)} %get-tuple-element.29), channel_id=1, source_target_pairs={{12,0},{13,1},{14,2},{15,3},{4,8},{5,9},{6,10},{7,11},{28,16},{29,... | collective-permute-start | bytes 1622024 | tf_op jit(solution)/shard_map/ppermute | solution.py:253
  10.9 14.1 %collective-permute-done.5.refs_3_.refs_8_.refs_7_ = bf16[272,512]{1,0:T(8,128)(2,1)S(1)} collective-permute-done((bf16[272,512]{1,0:T(8,128)(2,1)S(1)}, bf16[272,512]{1,0:T(8,128)(2,1)S(1)}, u32[]{:S(2)}, u32[]{:S(2)}) %collective-permute-start.5) | collective-permute-done | bytes 278560 | tf_op jit(solution)/shard_map/ppermute | solution.py:245
  25.1 0.5 collective-permute-start.8
  25.6 0.4 collective-permute-start.3
  26.1 0.5 %collective-permute-done.9.refs_5_.refs_10_.refs_9_ = bf16[272,512]{1,0:T(8,128)(2,1)S(1)} collective-permute-done((bf16[272,512]{1,0:T(8,128)(2,1)S(1)}, bf16[272,512]{1,0:T(8,128)(2,1)S(1)}, u32[]{:S(2)}, u32[]{:S(2)}) %collective-permute-start.9) | collective-permute-done | bytes 278560 | tf_op jit(solution)/shard_map/ppermute | solution.py:245
  26.6 1.3 %collective-permute-start.1 = (bf16[256,512]{1,0:T(8,128)(2,1)S(1)}, bf16[256,512]{1,0:T(8,128)(2,1)S(1)}, u32[]{:S(2)}, u32[]{:S(2)}) collective-permute-start(bf16[256,512]{1,0:T(8,128)(2,1)S(1)} %get-tuple-element.30), channel_id=1, source_target_pairs={{12,0},{13,1},{14,2},{15,3},{4,8},{5,9},{6,10},{7,11},{28,16},{29,... | collective-permute-start | bytes 786440 | tf_op jit(solution)/shard_map/ppermute | solution.py:253
  27.9 1.4 %plane_far.1.refs_6_ = f32[8,128]{1,0:T(8,128)S(1)} custom-call(bf16[512,512]{1,0:T(8,128)(2,1)S(1)} %first.1.first_ref.refs_0_.refs_2_.refs_3_, bf16[272,512]{1,0:T(8,128)(2,1)S(1)} %get-tuple-element.31.refs_1_.refs_3_.refs_4_, bf16[512,512]{1,0:T(8,128)(2,1)S(1)} %collective-permute-done.4.refs_2_.refs_7_.refs_6_, ...), custom_call_target="tpu_custom_call" | custom-call | flops 1 | bytes 1 | tf_op jit(solution)/shard_map/plane_far/pallas_call | solution.py:222
  29.4 1.4 %plane_near.1.refs_12_ = f32[8,128]{1,0:T(8,128)S(1)} custom-call(bf16[512,512]{1,0:T(8,128)(2,1)S(1)} %first.1.first_ref.refs_0_.refs_2_.refs_3_, bf16[272,512]{1,0:T(8,128)(2,1)S(1)} %get-tuple-element.31.refs_1_.refs_3_.refs_4_, bf16[512,512]{1,0:T(8,128)(2,1)S(1)} %first.1.first_ref.refs_0_.refs_2_.refs_3_, ...), custom_call_target="tpu_custom_call" | custom-call | flops 1 | bytes 1 | tf_op jit(solution)/shard_map/plane_near/pallas_call | solution.py:222
  30.8 2.8 %cross.3 = (f32[8,128]{1,0:T(8,128)S(1)}, f32[8,128]{1,0:T(8,128)S(1)}, f32[8,128]{1,0:T(8,128)S(1)}, f32[8,128]{1,0:T(8,128)S(1)}, f32[8,128]{1,0:T(8,128)S(1)}) custom-call(bf16[272,512]{1,0:T(8,128)(2,1)S(1)} %collective-permute-done.7.refs_0_.refs_2_, bf16[512,512]{1,0:T(8,128)(2,1)S(1)} %collective-permute-done.6.refs_1_, ...), custom_call_target="tpu_custom_call" | custom-call | flops 1 | bytes 1 | tf_op jit(solution)/shard_map/cross/pallas_call | solution.py:222
  33.6 2.8 %collective-permute-start.10 = (f32[8,128]{1,0:T(8,128)S(1)}, f32[8,128]{1,0:T(8,128)S(1)}, u32[]{:S(2)}, u32[]{:S(2)}) collective-permute-start(f32[8,128]{1,0:T(8,128)S(1)} %get-tuple-element.44), channel_id=1, source_target_pairs={{8,0},{9,1},{10,2},{11,3},{0,4},{1,5},{2,6},{3,7},{12,8},{13,9},{1... | collective-permute-start | bytes 12296 | tf_op jit(solution)/shard_map/ppermute | solution.py:288
  36.5 0.9 %collective-permute-done.refs_0_.refs_1_ = bf16[528,512]{1,0:T(8,128)(2,1)S(1)} collective-permute-done((bf16[528,512]{1,0:T(8,128)(2,1)S(1)}, bf16[528,512]{1,0:T(8,128)(2,1)S(1)}, u32[]{:S(2)}, u32[]{:S(2)}) %collective-permute-start) | collective-permute-done | bytes 540704 | tf_op jit(solution)/shard_map/ppermute | solution.py:253
  37.4 1.9 %cross.4 = (f32[8,128]{1,0:T(8,128)S(1)}, f32[8,128]{1,0:T(8,128)S(1)}, f32[8,128]{1,0:T(8,128)S(1)}, f32[8,128]{1,0:T(8,128)S(1)}, f32[8,128]{1,0:T(8,128)S(1)}) custom-call(bf16[528,512]{1,0:T(8,128)(2,1)S(1)} %collective-permute-done.refs_0_.refs_1_, bf16[528,512]{1,0:T(8,128)(2,1)S(1)} %collective-permute-done.refs_0_.refs_1_, ...), custom_call_target="tpu_custom_call" | custom-call | flops 1 | bytes 1 | tf_op jit(solution)/shard_map/cross/pallas_call | solution.py:222
  39.3 2.6 %collective-permute-done.1.refs_1_ = bf16[256,512]{1,0:T(8,128)(2,1)S(1)} collective-permute-done((bf16[256,512]{1,0:T(8,128)(2,1)S(1)}, bf16[256,512]{1,0:T(8,128)(2,1)S(1)}, u32[]{:S(2)}, u32[]{:S(2)}) %collective-permute-start.1) | collective-permute-done | bytes 262176 | tf_op jit(solution)/shard_map/ppermute | solution.py:253
  41.9 1.2 %cross.5 = (f32[8,128]{1,0:T(8,128)S(1)}, f32[8,128]{1,0:T(8,128)S(1)}, f32[8,128]{1,0:T(8,128)S(1)}, f32[8,128]{1,0:T(8,128)S(1)}, f32[8,128]{1,0:T(8,128)S(1)}) custom-call(bf16[528,512]{1,0:T(8,128)(2,1)S(1)} %collective-permute-done.refs_0_.refs_1_, bf16[256,512]{1,0:T(8,128)(2,1)S(1)} %collective-permute-done.1.refs_1_, ...), custom_call_target="tpu_custom_call" | custom-call | flops 1 | bytes 1 | tf_op jit(solution)/shard_map/cross/pallas_call | solution.py:222
  43.2 1.6 %collective-permute-start.13 = (f32[8,128]{1,0:T(8,128)S(1)}, f32[8,128]{1,0:T(8,128)S(1)}, u32[]{:S(2)}, u32[]{:S(2)}) collective-permute-start(f32[8,128]{1,0:T(8,128)S(1)} %get-tuple-element.49), channel_id=1, source_target_pairs={{0,2},{1,3},{2,0},{3,1},{4,6},{5,7},{6,4},{7,5},{8,10},{9,11},{10,... | collective-permute-start | bytes 12296 | tf_op jit(solution)/shard_map/ppermute | solution.py:245
  44.7 0.3 collective-permute-start.12
  45.0 3.1 %collective-permute-start.11 = (f32[8,128]{1,0:T(8,128)S(1)}, f32[8,128]{1,0:T(8,128)S(1)}, u32[]{:S(2)}, u32[]{:S(2)}) collective-permute-start(f32[8,128]{1,0:T(8,128)S(1)} %get-tuple-element.45), channel_id=1, source_target_pairs={{0,12},{1,13},{2,14},{3,15},{8,4},{9,5},{10,6},{11,7},{16,28},{17,... | collective-permute-start | bytes 12296 | tf_op jit(solution)/shard_map/ppermute | solution.py:288
  48.2 1.3 %collective-permute-done.11 = f32[8,128]{1,0:T(8,128)S(1)} collective-permute-done((f32[8,128]{1,0:T(8,128)S(1)}, f32[8,128]{1,0:T(8,128)S(1)}, u32[]{:S(2)}, u32[]{:S(2)}) %collective-permute-start.11) | collective-permute-done | bytes 4128 | tf_op jit(solution)/shard_map/ppermute | solution.py:288
  49.5 0.6 %fusion.3 = f32[768]{0:T(1024)} fusion(f32[8,128]{1,0:T(8,128)S(1)} %get-tuple-element.52, f32[8,128]{1,0:T(8,128)S(1)} %collective-permute-done.14, f32[8,128]{1,0:T(8,128)S(1)} %collective-permute-done.13, f32[8,128]{1,0:T(8,128)S(1)} %collective-permute-done.12, f32[8,128]{1,0:T(8,128)S(1)} %collective-permute-done.11, pred[]{:T(512)S(6)} %eq.3, ...), kind=kLoop, calls=%fused_computation.4 | loop fusion | flops 4608 | bytes 21505 | tf_op jit(solution)/shard_map/max | solution.py:299
  (27 shorter events, 0.6 us)
Async XLA Ops:
  0.0 1.4 %copy-start = (f32[768,512]{1,0:T(8,128)S(1)}, f32[768,512]{1,0:T(8,128)}, u32[]{:S(2)}) copy-start(f32[768,512]{1,0:T(8,128)} %embeddings_ref.3) | copy-start | bytes 4718596
  1.4 5.8 %copy-start.2 = (s32[768]{0:T(1024)S(1)}, s32[768]{0:T(1024)}, u32[]{:S(2)}) copy-start(s32[768]{0:T(1024)} %param.5) | copy-start | bytes 9220
  1.4 5.8 %copy-start.3 = (s32[768]{0:T(1024)S(1)}, s32[768]{0:T(1024)}, u32[]{:S(2)}) copy-start(s32[768]{0:T(1024)} %param.6) | copy-start | bytes 9220
  1.4 5.8 %copy-start.4 = (s32[16]{0:T(128)S(1)}, s32[16]{0:T(128)}, u32[]{:S(2)}) copy-start(s32[16]{0:T(128)} %param.7) | copy-start | bytes 196
  1.4 5.9 %copy-start.1 = (f32[768,512]{1,0:T(8,128)S(1)}, f32[768,512]{1,0:T(8,128)}, u32[]{:S(2)}) copy-start(f32[768,512]{1,0:T(8,128)} %embeddings_ref.3) | copy-start | bytes 4718596
  1.6 23.4 %collective-permute-start.6 = (bf16[512,512]{1,0:T(8,128)(2,1)S(1)}, bf16[512,512]{1,0:T(8,128)(2,1)S(1)}, u32[]{:S(2)}, u32[]{:S(2)}) collective-permute-start(bf16[512,512]{1,0:T(8,128)(2,1)S(1)} %first.1.first_ref.refs_0_.refs_2_.refs_3_), channel_id=1, source_target_pairs={{0,8},{1,9},{2,10},{3,11},{4,0},{5,1},{6,2},{7,3},{8,12},{9,13},{1... | collective-permute-start | bytes 1572872 | tf_op jit(solution)/shard_map/ppermute | solution.py:253
  5.7 19.4 %collective-permute-start.4 = (bf16[512,512]{1,0:T(8,128)(2,1)S(1)}, bf16[512,512]{1,0:T(8,128)(2,1)S(1)}, u32[]{:S(2)}, u32[]{:S(2)}) collective-permute-start(bf16[512,512]{1,0:T(8,128)(2,1)S(1)} %first.1.first_ref.refs_0_.refs_2_.refs_3_), channel_id=1, source_target_pairs={{0,2},{1,3},{2,0},{3,1},{4,6},{5,7},{6,4},{7,5},{8,10},{9,11},{10,... | collective-permute-start | bytes 1572872 | tf_op jit(solution)/shard_map/ppermute | solution.py:245
  7.4 17.6 %collective-permute-start.5 = (bf16[272,512]{1,0:T(8,128)(2,1)S(1)}, bf16[272,512]{1,0:T(8,128)(2,1)S(1)}, u32[]{:S(2)}, u32[]{:S(2)}) collective-permute-start(bf16[272,512]{1,0:T(8,128)(2,1)S(1)} %get-tuple-element.31.refs_1_.refs_3_.refs_4_), channel_id=1, source_target_pairs={{0,2},{1,3},{2,0},{3,1},{4,6},{5,7},{6,4},{7,5},{8,10},{9,11},{10,... | collective-permute-start | bytes 835592 | tf_op jit(solution)/shard_map/ppermute | solution.py:245
  8.0 17.0 %collective-permute-start.7 = (bf16[272,512]{1,0:T(8,128)(2,1)S(1)}, bf16[272,512]{1,0:T(8,128)(2,1)S(1)}, u32[]{:S(2)}, u32[]{:S(2)}) collective-permute-start(bf16[272,512]{1,0:T(8,128)(2,1)S(1)} %get-tuple-element.31.refs_1_.refs_3_.refs_4_), channel_id=1, source_target_pairs={{0,8},{1,9},{2,10},{3,11},{4,0},{5,1},{6,2},{7,3},{8,12},{9,13},{1... | collective-permute-start | bytes 835592 | tf_op jit(solution)/shard_map/ppermute | solution.py:253
  9.6 27.8 %collective-permute-start = (bf16[528,512]{1,0:T(8,128)(2,1)S(1)}, bf16[528,512]{1,0:T(8,128)(2,1)S(1)}, u32[]{:S(2)}, u32[]{:S(2)}) collective-permute-start(bf16[528,512]{1,0:T(8,128)(2,1)S(1)} %get-tuple-element.29), channel_id=1, source_target_pairs={{12,0},{13,1},{14,2},{15,3},{4,8},{5,9},{6,10},{7,11},{28,16},{29,... | collective-permute-start | bytes 1622024 | tf_op jit(solution)/shard_map/ppermute | solution.py:253
  25.0 1.6 %collective-permute-start.9 = (bf16[272,512]{1,0:T(8,128)(2,1)S(1)}, bf16[272,512]{1,0:T(8,128)(2,1)S(1)}, u32[]{:S(2)}, u32[]{:S(2)}) collective-permute-start(bf16[272,512]{1,0:T(8,128)(2,1)S(1)} %collective-permute-done.5.refs_3_.refs_8_.refs_7_), channel_id=1, source_target_pairs={{0,1},{1,0},{2,3},{3,2},{4,5},{5,4},{6,7},{7,6},{8,9},{9,8},{10,11... | collective-permute-start | bytes 835592 | tf_op jit(solution)/shard_map/ppermute | solution.py:245
  25.1 2.8 %collective-permute-start.8 = (bf16[512,512]{1,0:T(8,128)(2,1)S(1)}, bf16[512,512]{1,0:T(8,128)(2,1)S(1)}, u32[]{:S(2)}, u32[]{:S(2)}) collective-permute-start(bf16[512,512]{1,0:T(8,128)(2,1)S(1)} %collective-permute-done.4.refs_2_.refs_7_.refs_6_), channel_id=1, source_target_pairs={{0,1},{1,0},{2,3},{3,2},{4,5},{5,4},{6,7},{7,6},{8,9},{9,8},{10,11... | collective-permute-start | bytes 1572872 | tf_op jit(solution)/shard_map/ppermute | solution.py:245
  25.6 3.8 %collective-permute-start.2 = (bf16[512,512]{1,0:T(8,128)(2,1)S(1)}, bf16[512,512]{1,0:T(8,128)(2,1)S(1)}, u32[]{:S(2)}, u32[]{:S(2)}) collective-permute-start(bf16[512,512]{1,0:T(8,128)(2,1)S(1)} %first.1.first_ref.refs_0_.refs_2_.refs_3_), channel_id=1, source_target_pairs={{0,1},{1,0},{2,3},{3,2},{4,5},{5,4},{6,7},{7,6},{8,9},{9,8},{10,11... | collective-permute-start | bytes 1572872 | tf_op jit(solution)/shard_map/ppermute | solution.py:245
  25.6 3.7 %collective-permute-start.3 = (bf16[272,512]{1,0:T(8,128)(2,1)S(1)}, bf16[272,512]{1,0:T(8,128)(2,1)S(1)}, u32[]{:S(2)}, u32[]{:S(2)}) collective-permute-start(bf16[272,512]{1,0:T(8,128)(2,1)S(1)} %get-tuple-element.31.refs_1_.refs_3_.refs_4_), channel_id=1, source_target_pairs={{0,1},{1,0},{2,3},{3,2},{4,5},{5,4},{6,7},{7,6},{8,9},{9,8},{10,11... | collective-permute-start | bytes 835592 | tf_op jit(solution)/shard_map/ppermute | solution.py:245
  26.6 15.3 %collective-permute-start.1 = (bf16[256,512]{1,0:T(8,128)(2,1)S(1)}, bf16[256,512]{1,0:T(8,128)(2,1)S(1)}, u32[]{:S(2)}, u32[]{:S(2)}) collective-permute-start(bf16[256,512]{1,0:T(8,128)(2,1)S(1)} %get-tuple-element.30), channel_id=1, source_target_pairs={{12,0},{13,1},{14,2},{15,3},{4,8},{5,9},{6,10},{7,11},{28,16},{29,... | collective-permute-start | bytes 786440 | tf_op jit(solution)/shard_map/ppermute | solution.py:253
  33.6 9.4 %collective-permute-start.10 = (f32[8,128]{1,0:T(8,128)S(1)}, f32[8,128]{1,0:T(8,128)S(1)}, u32[]{:S(2)}, u32[]{:S(2)}) collective-permute-start(f32[8,128]{1,0:T(8,128)S(1)} %get-tuple-element.44), channel_id=1, source_target_pairs={{8,0},{9,1},{10,2},{11,3},{0,4},{1,5},{2,6},{3,7},{12,8},{13,9},{1... | collective-permute-start | bytes 12296 | tf_op jit(solution)/shard_map/ppermute | solution.py:288
  43.1 5.1 %collective-permute-start.14 = (f32[8,128]{1,0:T(8,128)S(1)}, f32[8,128]{1,0:T(8,128)S(1)}, u32[]{:S(2)}, u32[]{:S(2)}) collective-permute-start(f32[8,128]{1,0:T(8,128)S(1)} %get-tuple-element.51), channel_id=1, source_target_pairs={{0,3},{1,2},{2,1},{3,0},{4,7},{5,6},{6,5},{7,4},{8,11},{9,10},{10,... | collective-permute-start | bytes 12296 | tf_op jit(solution)/shard_map/ppermute | solution.py:245
  43.2 5.0 %collective-permute-start.13 = (f32[8,128]{1,0:T(8,128)S(1)}, f32[8,128]{1,0:T(8,128)S(1)}, u32[]{:S(2)}, u32[]{:S(2)}) collective-permute-start(f32[8,128]{1,0:T(8,128)S(1)} %get-tuple-element.49), channel_id=1, source_target_pairs={{0,2},{1,3},{2,0},{3,1},{4,6},{5,7},{6,4},{7,5},{8,10},{9,11},{10,... | collective-permute-start | bytes 12296 | tf_op jit(solution)/shard_map/ppermute | solution.py:245
  44.7 3.5 %collective-permute-start.12 = (f32[8,128]{1,0:T(8,128)S(1)}, f32[8,128]{1,0:T(8,128)S(1)}, u32[]{:S(2)}, u32[]{:S(2)}) collective-permute-start(f32[8,128]{1,0:T(8,128)S(1)} %get-tuple-element.47), channel_id=1, source_target_pairs={{0,1},{1,0},{2,3},{3,2},{4,5},{5,4},{6,7},{7,6},{8,9},{9,8},{10,11... | collective-permute-start | bytes 12296 | tf_op jit(solution)/shard_map/ppermute | solution.py:245
  45.0 4.5 %collective-permute-start.11 = (f32[8,128]{1,0:T(8,128)S(1)}, f32[8,128]{1,0:T(8,128)S(1)}, u32[]{:S(2)}, u32[]{:S(2)}) collective-permute-start(f32[8,128]{1,0:T(8,128)S(1)} %get-tuple-element.45), channel_id=1, source_target_pairs={{0,12},{1,13},{2,14},{3,15},{8,4},{9,5},{10,6},{11,7},{16,28},{17,... | collective-permute-start | bytes 12296 | tf_op jit(solution)/shard_map/ppermute | solution.py:288

commit v20 on v19

--- a/solution.py
+++ b/solution.py
@@ -294,7 +294,7 @@
     best = plane_best[0].reshape(-1)[:rows]
     for distance in (3, 2, 1):
         back = mate(after(plane_best[distance], backs[0][0]), distance)
-        backs.insert(-1, (back.reshape(-1)[:rows], None))
+        backs.append((back.reshape(-1)[:rows], None))
     for back, sent in backs:
         best = jnp.maximum(back if sent is None else jnp.where(sent == 1, back, -1.0), best)
     return best

time: 50.3 us -> 51.3 us (1.020)
  waiting for transfers between devices: 19.5 us -> 20.5 us
    ppermute x9, waiting for transfers between devices: 14.7 us -> 17 us  [mate(): return lax.ppermute(value, 'dp', [(i, i ^ distance) for i in range(peers)])]
    ppermute x2, waiting for transfers between devices: 1.27 us -> 0.01 us  [local(): lax.ppermute(answer, 'dp', [(t, s) for s, t in pairs]).reshape(-1)[:rows]]
  transfers between devices with their start and end apart: 15 -> 15, of which waited for: 5 -> 6; matrix products, arithmetic and copies ran while one was open for 0% -> 0% of each run, Pallas kernels for 18% -> 17%
where the time goes in v20:
time: 51.3 us; the launch traced here: 51.1 us
  waiting for transfers between devices  20.5 us (40%)
  starting transfers between devices  19.3 us (38%)
  Pallas kernels  9.08 us (18%)
  local copies, waits for them, and re-layouts  1.51 us (3%)
  other arithmetic  0.6 us (1%)
    ppermute x9, waiting for transfers between devices, mate(): return lax.ppermute(value, 'dp', [(i, i ^ distance) for i in range(peers)])  17 us
    pallas_call x7, Pallas kernels, kernel(): pl.pallas_call(body, out_shape=tuple(outputs), in_specs=whole(len(inputs)...  9.08 us
    ppermute x4, starting transfers between devices, local(): away.append((pairs, [lax.ppermute(part, 'dp', pairs) for part in parts]))  8.23 us
    ppermute x2, starting transfers between devices, local(): lax.ppermute(answer, 'dp', [(t, s) for s, t in pairs]).reshape(-1)[:rows]  6.03 us
    ppermute x9, starting transfers between devices, mate(): return lax.ppermute(value, 'dp', [(i, i ^ distance) for i in range(peers)])  5.03 us
    ppermute x4, waiting for transfers between devices, local(): away.append((pairs, [lax.ppermute(part, 'dp', pairs) for part in parts]))  3.54 us
    unnamed x10, local copies, waits for them, and re-layouts  1.42 us
  transfers between devices with their start and end apart: 15, of which 6 were waited for; matrix products, arithmetic and copies ran while one was open for 0% of the time, Pallas kernels for 17%

profile of v20, /device:TPU:0, one launch (start us, length us, event | category | flops | bytes accessed | tf_op | source)
XLA Modules:
  0.0 51.1 jit_solution(14184602542623693210)
XLA Ops:
  0.0 1.4 %copy-done = f32[768,512]{1,0:T(8,128)S(1)} copy-done((f32[768,512]{1,0:T(8,128)S(1)}, f32[768,512]{1,0:T(8,128)}, u32[]{:S(2)}) %copy-start) | copy-done | bytes 1572888
  1.6 4.1 %collective-permute-start.6 = (bf16[512,512]{1,0:T(8,128)(2,1)S(1)}, bf16[512,512]{1,0:T(8,128)(2,1)S(1)}, u32[]{:S(2)}, u32[]{:S(2)}) collective-permute-start(bf16[512,512]{1,0:T(8,128)(2,1)S(1)} %first.1.first_ref.refs_0_.refs_2_.refs_3_), channel_id=1, source_target_pairs={{0,8},{1,9},{2,10},{3,11},{4,0},{5,1},{6,2},{7,3},{8,12},{9,13},{1... | collective-permute-start | bytes 1572872 | tf_op jit(solution)/shard_map/ppermute | solution.py:253
  5.7 1.5 %collective-permute-start.4 = (bf16[512,512]{1,0:T(8,128)(2,1)S(1)}, bf16[512,512]{1,0:T(8,128)(2,1)S(1)}, u32[]{:S(2)}, u32[]{:S(2)}) collective-permute-start(bf16[512,512]{1,0:T(8,128)(2,1)S(1)} %first.1.first_ref.refs_0_.refs_2_.refs_3_), channel_id=1, source_target_pairs={{0,2},{1,3},{2,0},{3,1},{4,6},{5,7},{6,4},{7,5},{8,10},{9,11},{10,... | collective-permute-start | bytes 1572872 | tf_op jit(solution)/shard_map/ppermute | solution.py:245
  7.4 0.6 %collective-permute-start.5 = (bf16[272,512]{1,0:T(8,128)(2,1)S(1)}, bf16[272,512]{1,0:T(8,128)(2,1)S(1)}, u32[]{:S(2)}, u32[]{:S(2)}) collective-permute-start(bf16[272,512]{1,0:T(8,128)(2,1)S(1)} %get-tuple-element.31.refs_1_.refs_3_.refs_4_), channel_id=1, source_target_pairs={{0,2},{1,3},{2,0},{3,1},{4,6},{5,7},{6,4},{7,5},{8,10},{9,11},{10,... | collective-permute-start | bytes 835592 | tf_op jit(solution)/shard_map/ppermute | solution.py:245
  8.0 1.6 %collective-permute-start.7 = (bf16[272,512]{1,0:T(8,128)(2,1)S(1)}, bf16[272,512]{1,0:T(8,128)(2,1)S(1)}, u32[]{:S(2)}, u32[]{:S(2)}) collective-permute-start(bf16[272,512]{1,0:T(8,128)(2,1)S(1)} %get-tuple-element.31.refs_1_.refs_3_.refs_4_), channel_id=1, source_target_pairs={{0,8},{1,9},{2,10},{3,11},{4,0},{5,1},{6,2},{7,3},{8,12},{9,13},{1... | collective-permute-start | bytes 835592 | tf_op jit(solution)/shard_map/ppermute | solution.py:253
  9.6 1.3 %collective-permute-start = (bf16[528,512]{1,0:T(8,128)(2,1)S(1)}, bf16[528,512]{1,0:T(8,128)(2,1)S(1)}, u32[]{:S(2)}, u32[]{:S(2)}) collective-permute-start(bf16[528,512]{1,0:T(8,128)(2,1)S(1)} %get-tuple-element.29), channel_id=1, source_target_pairs={{12,0},{13,1},{14,2},{15,3},{4,8},{5,9},{6,10},{7,11},{28,16},{29,... | collective-permute-start | bytes 1622024 | tf_op jit(solution)/shard_map/ppermute | solution.py:253
  10.9 14.1 %collective-permute-done.5.refs_3_.refs_8_.refs_7_ = bf16[272,512]{1,0:T(8,128)(2,1)S(1)} collective-permute-done((bf16[272,512]{1,0:T(8,128)(2,1)S(1)}, bf16[272,512]{1,0:T(8,128)(2,1)S(1)}, u32[]{:S(2)}, u32[]{:S(2)}) %collective-permute-start.5) | collective-permute-done | bytes 278560 | tf_op jit(solution)/shard_map/ppermute | solution.py:245
  25.1 0.5 collective-permute-start.8
  26.1 0.5 %collective-permute-done.9.refs_5_.refs_10_.refs_9_ = bf16[272,512]{1,0:T(8,128)(2,1)S(1)} collective-permute-done((bf16[272,512]{1,0:T(8,128)(2,1)S(1)}, bf16[272,512]{1,0:T(8,128)(2,1)S(1)}, u32[]{:S(2)}, u32[]{:S(2)}) %collective-permute-start.9) | collective-permute-done | bytes 278560 | tf_op jit(solution)/shard_map/ppermute | solution.py:245
  26.6 1.3 %collective-permute-start.1 = (bf16[256,512]{1,0:T(8,128)(2,1)S(1)}, bf16[256,512]{1,0:T(8,128)(2,1)S(1)}, u32[]{:S(2)}, u32[]{:S(2)}) collective-permute-start(bf16[256,512]{1,0:T(8,128)(2,1)S(1)} %get-tuple-element.30), channel_id=1, source_target_pairs={{12,0},{13,1},{14,2},{15,3},{4,8},{5,9},{6,10},{7,11},{28,16},{29,... | collective-permute-start | bytes 786440 | tf_op jit(solution)/shard_map/ppermute | solution.py:253
  27.9 1.4 %plane_far.1.refs_6_ = f32[8,128]{1,0:T(8,128)S(1)} custom-call(bf16[512,512]{1,0:T(8,128)(2,1)S(1)} %first.1.first_ref.refs_0_.refs_2_.refs_3_, bf16[272,512]{1,0:T(8,128)(2,1)S(1)} %get-tuple-element.31.refs_1_.refs_3_.refs_4_, bf16[512,512]{1,0:T(8,128)(2,1)S(1)} %collective-permute-done.4.refs_2_.refs_7_.refs_6_, ...), custom_call_target="tpu_custom_call" | custom-call | flops 1 | bytes 1 | tf_op jit(solution)/shard_map/plane_far/pallas_call | solution.py:222
  29.4 1.4 %plane_near.1.refs_12_ = f32[8,128]{1,0:T(8,128)S(1)} custom-call(bf16[512,512]{1,0:T(8,128)(2,1)S(1)} %first.1.first_ref.refs_0_.refs_2_.refs_3_, bf16[272,512]{1,0:T(8,128)(2,1)S(1)} %get-tuple-element.31.refs_1_.refs_3_.refs_4_, bf16[512,512]{1,0:T(8,128)(2,1)S(1)} %first.1.first_ref.refs_0_.refs_2_.refs_3_, ...), custom_call_target="tpu_custom_call" | custom-call | flops 1 | bytes 1 | tf_op jit(solution)/shard_map/plane_near/pallas_call | solution.py:222
  30.8 2.8 %cross.3 = (f32[8,128]{1,0:T(8,128)S(1)}, f32[8,128]{1,0:T(8,128)S(1)}, f32[8,128]{1,0:T(8,128)S(1)}, f32[8,128]{1,0:T(8,128)S(1)}, f32[8,128]{1,0:T(8,128)S(1)}) custom-call(bf16[272,512]{1,0:T(8,128)(2,1)S(1)} %collective-permute-done.7.refs_0_.refs_2_, bf16[512,512]{1,0:T(8,128)(2,1)S(1)} %collective-permute-done.6.refs_1_, ...), custom_call_target="tpu_custom_call" | custom-call | flops 1 | bytes 1 | tf_op jit(solution)/shard_map/cross/pallas_call | solution.py:222
  33.6 2.8 %collective-permute-start.10 = (f32[8,128]{1,0:T(8,128)S(1)}, f32[8,128]{1,0:T(8,128)S(1)}, u32[]{:S(2)}, u32[]{:S(2)}) collective-permute-start(f32[8,128]{1,0:T(8,128)S(1)} %get-tuple-element.44), channel_id=1, source_target_pairs={{8,0},{9,1},{10,2},{11,3},{0,4},{1,5},{2,6},{3,7},{12,8},{13,9},{1... | collective-permute-start | bytes 12296 | tf_op jit(solution)/shard_map/ppermute | solution.py:288
  36.5 0.9 %collective-permute-done.refs_0_.refs_1_ = bf16[528,512]{1,0:T(8,128)(2,1)S(1)} collective-permute-done((bf16[528,512]{1,0:T(8,128)(2,1)S(1)}, bf16[528,512]{1,0:T(8,128)(2,1)S(1)}, u32[]{:S(2)}, u32[]{:S(2)}) %collective-permute-start) | collective-permute-done | bytes 540704 | tf_op jit(solution)/shard_map/ppermute | solution.py:253
  37.4 1.9 %cross.4 = (f32[8,128]{1,0:T(8,128)S(1)}, f32[8,128]{1,0:T(8,128)S(1)}, f32[8,128]{1,0:T(8,128)S(1)}, f32[8,128]{1,0:T(8,128)S(1)}, f32[8,128]{1,0:T(8,128)S(1)}) custom-call(bf16[528,512]{1,0:T(8,128)(2,1)S(1)} %collective-permute-done.refs_0_.refs_1_, bf16[528,512]{1,0:T(8,128)(2,1)S(1)} %collective-permute-done.refs_0_.refs_1_, ...), custom_call_target="tpu_custom_call" | custom-call | flops 1 | bytes 1 | tf_op jit(solution)/shard_map/cross/pallas_call | solution.py:222
  39.3 2.6 %collective-permute-done.1.refs_1_ = bf16[256,512]{1,0:T(8,128)(2,1)S(1)} collective-permute-done((bf16[256,512]{1,0:T(8,128)(2,1)S(1)}, bf16[256,512]{1,0:T(8,128)(2,1)S(1)}, u32[]{:S(2)}, u32[]{:S(2)}) %collective-permute-start.1) | collective-permute-done | bytes 262176 | tf_op jit(solution)/shard_map/ppermute | solution.py:253
  41.9 1.2 %cross.5 = (f32[8,128]{1,0:T(8,128)S(1)}, f32[8,128]{1,0:T(8,128)S(1)}, f32[8,128]{1,0:T(8,128)S(1)}, f32[8,128]{1,0:T(8,128)S(1)}, f32[8,128]{1,0:T(8,128)S(1)}) custom-call(bf16[528,512]{1,0:T(8,128)(2,1)S(1)} %collective-permute-done.refs_0_.refs_1_, bf16[256,512]{1,0:T(8,128)(2,1)S(1)} %collective-permute-done.1.refs_1_, ...), custom_call_target="tpu_custom_call" | custom-call | flops 1 | bytes 1 | tf_op jit(solution)/shard_map/cross/pallas_call | solution.py:222
  43.1 3.2 %collective-permute-start.14 = (f32[8,128]{1,0:T(8,128)S(1)}, f32[8,128]{1,0:T(8,128)S(1)}, u32[]{:S(2)}, u32[]{:S(2)}) collective-permute-start(f32[8,128]{1,0:T(8,128)S(1)} %get-tuple-element.51), channel_id=1, source_target_pairs={{0,12},{1,13},{2,14},{3,15},{8,4},{9,5},{10,6},{11,7},{16,28},{17,... | collective-permute-start | bytes 12296 | tf_op jit(solution)/shard_map/ppermute | solution.py:288
  46.3 0.6 %collective-permute-start.13 = (f32[8,128]{1,0:T(8,128)S(1)}, f32[8,128]{1,0:T(8,128)S(1)}, u32[]{:S(2)}, u32[]{:S(2)}) collective-permute-start(f32[8,128]{1,0:T(8,128)S(1)} %get-tuple-element.49), channel_id=1, source_target_pairs={{0,3},{1,2},{2,1},{3,0},{4,7},{5,6},{6,5},{7,4},{8,11},{9,10},{10,... | collective-permute-start | bytes 12296 | tf_op jit(solution)/shard_map/ppermute | solution.py:245
  46.9 1.0 %collective-permute-start.12 = (f32[8,128]{1,0:T(8,128)S(1)}, f32[8,128]{1,0:T(8,128)S(1)}, u32[]{:S(2)}, u32[]{:S(2)}) collective-permute-start(f32[8,128]{1,0:T(8,128)S(1)} %get-tuple-element.47), channel_id=1, source_target_pairs={{0,2},{1,3},{2,0},{3,1},{4,6},{5,7},{6,4},{7,5},{8,10},{9,11},{10,... | collective-permute-start | bytes 12296 | tf_op jit(solution)/shard_map/ppermute | solution.py:245
  48.2 1.2 %collective-permute-done.13 = f32[8,128]{1,0:T(8,128)S(1)} collective-permute-done((f32[8,128]{1,0:T(8,128)S(1)}, f32[8,128]{1,0:T(8,128)S(1)}, u32[]{:S(2)}, u32[]{:S(2)}) %collective-permute-start.13) | collective-permute-done | bytes 4128 | tf_op jit(solution)/shard_map/ppermute | solution.py:245
  49.4 1.1 %collective-permute-done.12 = f32[8,128]{1,0:T(8,128)S(1)} collective-permute-done((f32[8,128]{1,0:T(8,128)S(1)}, f32[8,128]{1,0:T(8,128)S(1)}, u32[]{:S(2)}, u32[]{:S(2)}) %collective-permute-start.12) | collective-permute-done | bytes 4128 | tf_op jit(solution)/shard_map/ppermute | solution.py:245
  50.5 0.6 %fusion.3 = f32[768]{0:T(1024)} fusion(f32[8,128]{1,0:T(8,128)S(1)} %get-tuple-element.52, f32[8,128]{1,0:T(8,128)S(1)} %collective-permute-done.14, f32[8,128]{1,0:T(8,128)S(1)} %collective-permute-done.13, f32[8,128]{1,0:T(8,128)S(1)} %collective-permute-done.12, f32[8,128]{1,0:T(8,128)S(1)} %collective-permute-done.11, pred[]{:T(512)S(6)} %eq.3, ...), kind=kLoop, calls=%fused_computation.4 | loop fusion | flops 4608 | bytes 21505 | tf_op jit(solution)/shard_map/max | solution.py:299
  (27 shorter events, 1.2 us)
Async XLA Ops:
  0.0 1.4 %copy-start = (f32[768,512]{1,0:T(8,128)S(1)}, f32[768,512]{1,0:T(8,128)}, u32[]{:S(2)}) copy-start(f32[768,512]{1,0:T(8,128)} %embeddings_ref.3) | copy-start | bytes 4718596
  1.4 5.8 %copy-start.2 = (s32[768]{0:T(1024)S(1)}, s32[768]{0:T(1024)}, u32[]{:S(2)}) copy-start(s32[768]{0:T(1024)} %param.5) | copy-start | bytes 9220
  1.4 5.8 %copy-start.3 = (s32[768]{0:T(1024)S(1)}, s32[768]{0:T(1024)}, u32[]{:S(2)}) copy-start(s32[768]{0:T(1024)} %param.6) | copy-start | bytes 9220
  1.4 5.8 %copy-start.4 = (s32[16]{0:T(128)S(1)}, s32[16]{0:T(128)}, u32[]{:S(2)}) copy-start(s32[16]{0:T(128)} %param.7) | copy-start | bytes 196
  1.4 5.9 %copy-start.1 = (f32[768,512]{1,0:T(8,128)S(1)}, f32[768,512]{1,0:T(8,128)}, u32[]{:S(2)}) copy-start(f32[768,512]{1,0:T(8,128)} %embeddings_ref.3) | copy-start | bytes 4718596
  1.6 23.4 %collective-permute-start.6 = (bf16[512,512]{1,0:T(8,128)(2,1)S(1)}, bf16[512,512]{1,0:T(8,128)(2,1)S(1)}, u32[]{:S(2)}, u32[]{:S(2)}) collective-permute-start(bf16[512,512]{1,0:T(8,128)(2,1)S(1)} %first.1.first_ref.refs_0_.refs_2_.refs_3_), channel_id=1, source_target_pairs={{0,8},{1,9},{2,10},{3,11},{4,0},{5,1},{6,2},{7,3},{8,12},{9,13},{1... | collective-permute-start | bytes 1572872 | tf_op jit(solution)/shard_map/ppermute | solution.py:253
  5.7 19.4 %collective-permute-start.4 = (bf16[512,512]{1,0:T(8,128)(2,1)S(1)}, bf16[512,512]{1,0:T(8,128)(2,1)S(1)}, u32[]{:S(2)}, u32[]{:S(2)}) collective-permute-start(bf16[512,512]{1,0:T(8,128)(2,1)S(1)} %first.1.first_ref.refs_0_.refs_2_.refs_3_), channel_id=1, source_target_pairs={{0,2},{1,3},{2,0},{3,1},{4,6},{5,7},{6,4},{7,5},{8,10},{9,11},{10,... | collective-permute-start | bytes 1572872 | tf_op jit(solution)/shard_map/ppermute | solution.py:245
  7.4 17.6 %collective-permute-start.5 = (bf16[272,512]{1,0:T(8,128)(2,1)S(1)}, bf16[272,512]{1,0:T(8,128)(2,1)S(1)}, u32[]{:S(2)}, u32[]{:S(2)}) collective-permute-start(bf16[272,512]{1,0:T(8,128)(2,1)S(1)} %get-tuple-element.31.refs_1_.refs_3_.refs_4_), channel_id=1, source_target_pairs={{0,2},{1,3},{2,0},{3,1},{4,6},{5,7},{6,4},{7,5},{8,10},{9,11},{10,... | collective-permute-start | bytes 835592 | tf_op jit(solution)/shard_map/ppermute | solution.py:245
  8.0 17.0 %collective-permute-start.7 = (bf16[272,512]{1,0:T(8,128)(2,1)S(1)}, bf16[272,512]{1,0:T(8,128)(2,1)S(1)}, u32[]{:S(2)}, u32[]{:S(2)}) collective-permute-start(bf16[272,512]{1,0:T(8,128)(2,1)S(1)} %get-tuple-element.31.refs_1_.refs_3_.refs_4_), channel_id=1, source_target_pairs={{0,8},{1,9},{2,10},{3,11},{4,0},{5,1},{6,2},{7,3},{8,12},{9,13},{1... | collective-permute-start | bytes 835592 | tf_op jit(solution)/shard_map/ppermute | solution.py:253
  9.6 27.8 %collective-permute-start = (bf16[528,512]{1,0:T(8,128)(2,1)S(1)}, bf16[528,512]{1,0:T(8,128)(2,1)S(1)}, u32[]{:S(2)}, u32[]{:S(2)}) collective-permute-start(bf16[528,512]{1,0:T(8,128)(2,1)S(1)} %get-tuple-element.29), channel_id=1, source_target_pairs={{12,0},{13,1},{14,2},{15,3},{4,8},{5,9},{6,10},{7,11},{28,16},{29,... | collective-permute-start | bytes 1622024 | tf_op jit(solution)/shard_map/ppermute | solution.py:253
  25.0 1.6 %collective-permute-start.9 = (bf16[272,512]{1,0:T(8,128)(2,1)S(1)}, bf16[272,512]{1,0:T(8,128)(2,1)S(1)}, u32[]{:S(2)}, u32[]{:S(2)}) collective-permute-start(bf16[272,512]{1,0:T(8,128)(2,1)S(1)} %collective-permute-done.5.refs_3_.refs_8_.refs_7_), channel_id=1, source_target_pairs={{0,1},{1,0},{2,3},{3,2},{4,5},{5,4},{6,7},{7,6},{8,9},{9,8},{10,11... | collective-permute-start | bytes 835592 | tf_op jit(solution)/shard_map/ppermute | solution.py:245
  25.1 2.8 %collective-permute-start.8 = (bf16[512,512]{1,0:T(8,128)(2,1)S(1)}, bf16[512,512]{1,0:T(8,128)(2,1)S(1)}, u32[]{:S(2)}, u32[]{:S(2)}) collective-permute-start(bf16[512,512]{1,0:T(8,128)(2,1)S(1)} %collective-permute-done.4.refs_2_.refs_7_.refs_6_), channel_id=1, source_target_pairs={{0,1},{1,0},{2,3},{3,2},{4,5},{5,4},{6,7},{7,6},{8,9},{9,8},{10,11... | collective-permute-start | bytes 1572872 | tf_op jit(solution)/shard_map/ppermute | solution.py:245
  25.6 3.8 %collective-permute-start.2 = (bf16[512,512]{1,0:T(8,128)(2,1)S(1)}, bf16[512,512]{1,0:T(8,128)(2,1)S(1)}, u32[]{:S(2)}, u32[]{:S(2)}) collective-permute-start(bf16[512,512]{1,0:T(8,128)(2,1)S(1)} %first.1.first_ref.refs_0_.refs_2_.refs_3_), channel_id=1, source_target_pairs={{0,1},{1,0},{2,3},{3,2},{4,5},{5,4},{6,7},{7,6},{8,9},{9,8},{10,11... | collective-permute-start | bytes 1572872 | tf_op jit(solution)/shard_map/ppermute | solution.py:245
  25.6 3.7 %collective-permute-start.3 = (bf16[272,512]{1,0:T(8,128)(2,1)S(1)}, bf16[272,512]{1,0:T(8,128)(2,1)S(1)}, u32[]{:S(2)}, u32[]{:S(2)}) collective-permute-start(bf16[272,512]{1,0:T(8,128)(2,1)S(1)} %get-tuple-element.31.refs_1_.refs_3_.refs_4_), channel_id=1, source_target_pairs={{0,1},{1,0},{2,3},{3,2},{4,5},{5,4},{6,7},{7,6},{8,9},{9,8},{10,11... | collective-permute-start | bytes 835592 | tf_op jit(solution)/shard_map/ppermute | solution.py:245
  26.6 15.3 %collective-permute-start.1 = (bf16[256,512]{1,0:T(8,128)(2,1)S(1)}, bf16[256,512]{1,0:T(8,128)(2,1)S(1)}, u32[]{:S(2)}, u32[]{:S(2)}) collective-permute-start(bf16[256,512]{1,0:T(8,128)(2,1)S(1)} %get-tuple-element.30), channel_id=1, source_target_pairs={{12,0},{13,1},{14,2},{15,3},{4,8},{5,9},{6,10},{7,11},{28,16},{29,... | collective-permute-start | bytes 786440 | tf_op jit(solution)/shard_map/ppermute | solution.py:253
  33.6 9.4 %collective-permute-start.10 = (f32[8,128]{1,0:T(8,128)S(1)}, f32[8,128]{1,0:T(8,128)S(1)}, u32[]{:S(2)}, u32[]{:S(2)}) collective-permute-start(f32[8,128]{1,0:T(8,128)S(1)} %get-tuple-element.44), channel_id=1, source_target_pairs={{8,0},{9,1},{10,2},{11,3},{0,4},{1,5},{2,6},{3,7},{12,8},{13,9},{1... | collective-permute-start | bytes 12296 | tf_op jit(solution)/shard_map/ppermute | solution.py:288
  43.1 5.1 %collective-permute-start.14 = (f32[8,128]{1,0:T(8,128)S(1)}, f32[8,128]{1,0:T(8,128)S(1)}, u32[]{:S(2)}, u32[]{:S(2)}) collective-permute-start(f32[8,128]{1,0:T(8,128)S(1)} %get-tuple-element.51), channel_id=1, source_target_pairs={{0,12},{1,13},{2,14},{3,15},{8,4},{9,5},{10,6},{11,7},{16,28},{17,... | collective-permute-start | bytes 12296 | tf_op jit(solution)/shard_map/ppermute | solution.py:288
  46.3 3.1 %collective-permute-start.13 = (f32[8,128]{1,0:T(8,128)S(1)}, f32[8,128]{1,0:T(8,128)S(1)}, u32[]{:S(2)}, u32[]{:S(2)}) collective-permute-start(f32[8,128]{1,0:T(8,128)S(1)} %get-tuple-element.49), channel_id=1, source_target_pairs={{0,3},{1,2},{2,1},{3,0},{4,7},{5,6},{6,5},{7,4},{8,11},{9,10},{10,... | collective-permute-start | bytes 12296 | tf_op jit(solution)/shard_map/ppermute | solution.py:245
  46.9 3.6 %collective-permute-start.12 = (f32[8,128]{1,0:T(8,128)S(1)}, f32[8,128]{1,0:T(8,128)S(1)}, u32[]{:S(2)}, u32[]{:S(2)}) collective-permute-start(f32[8,128]{1,0:T(8,128)S(1)} %get-tuple-element.47), channel_id=1, source_target_pairs={{0,2},{1,3},{2,0},{3,1},{4,6},{5,7},{6,4},{7,5},{8,10},{9,11},{10,... | collective-permute-start | bytes 12296 | tf_op jit(solution)/shard_map/ppermute | solution.py:245
  48.0 2.6 %collective-permute-start.11 = (f32[8,128]{1,0:T(8,128)S(1)}, f32[8,128]{1,0:T(8,128)S(1)}, u32[]{:S(2)}, u32[]{:S(2)}) collective-permute-start(f32[8,128]{1,0:T(8,128)S(1)} %get-tuple-element.45), channel_id=1, source_target_pairs={{0,1},{1,0},{2,3},{3,2},{4,5},{5,4},{6,7},{7,6},{8,9},{9,8},{10,11... | collective-permute-start | bytes 12296 | tf_op jit(solution)/shard_map/ppermute | solution.py:245

commit v21 on v14

--- a/solution.py
+++ b/solution.py
@@ -12,6 +12,7 @@
 PAD = 16
 BASE = 64.0
 TILE = 256
+WIDE = 512
 FIRST = 512
 HEAD = 512
 VMEM_LIMIT = 24 * 2**20
@@ -116,12 +117,12 @@
     )
 
 
-def row_slices(block):
+def row_slices(block, most=TILE):
     slices = []
     for first, part in unit_parts(block):
         count = part.shape[0]
-        for row in range(0, count, TILE):
-            size = min(TILE, count - row)
+        for row in range(0, count, most):
+            size = min(most, count - row)
             slices.append((first + row, part.at[row : row + size]))
     return slices
 
@@ -170,7 +171,7 @@
             column = tag_columns(tags[0], start + tile, TILE)
             row_best = jnp.full((TILE, 128), -1.0, jnp.float32)
             for which in range(PLANE):
-                for first, part in row_slices(blocks[which]):
+                for first, part in row_slices(blocks[which], WIDE):
                     found = dot_rows(values, part[...])
                     for lane in range(0, part.shape[0], 128):
                         row = (first + lane) // 128

time: 49.4 us -> 49.4 us (level)
  no operation moved by 1% of the time
where the time goes in v21:
time: 49.4 us; the launch traced here: 49.2 us
  waiting for transfers between devices  19.9 us (40%)
  starting transfers between devices  17.9 us (36%)
  Pallas kernels  9.08 us (18%)
  local copies, waits for them, and re-layouts  1.51 us (3%)
  other arithmetic  0.6 us (1%)
    ppermute x9, waiting for transfers between devices, mate(): return lax.ppermute(value, 'dp', [(i, i ^ distance) for i in range(peers)])  13.7 us
    ppermute x4, starting transfers between devices, local(): away.append((pairs, [lax.ppermute(part, 'dp', pairs) for part in parts]))  11.5 us
    pallas_call x7, Pallas kernels, kernel(): pl.pallas_call(body, out_shape=tuple(outputs), in_specs=whole(len(inputs)...  9.08 us
    ppermute x9, starting transfers between devices, mate(): return lax.ppermute(value, 'dp', [(i, i ^ distance) for i in range(peers)])  5.03 us
    ppermute x2, waiting for transfers between devices, local(): backs.append(lax.ppermute(away_best, 'dp', [(t, s) for s, t in pairs]))  4.05 us
    ppermute x4, waiting for transfers between devices, local(): away.append((pairs, [lax.ppermute(part, 'dp', pairs) for part in parts]))  2.19 us
    unnamed x10, local copies, waits for them, and re-layouts  1.42 us
    ppermute x2, starting transfers between devices, local(): backs.append(lax.ppermute(away_best, 'dp', [(t, s) for s, t in pairs]))  1.35 us
  transfers between devices with their start and end apart: 15, of which 4 were waited for; matrix products, arithmetic and copies ran while one was open for 0% of the time, Pallas kernels for 18%

profile of v21, /device:TPU:0, one launch (start us, length us, event | category | flops | bytes accessed | tf_op | source)
XLA Modules:
  0.0 49.2 jit_solution(15507450772854181917)
XLA Ops:
  0.0 1.4 %copy-done = f32[768,512]{1,0:T(8,128)S(1)} copy-done((f32[768,512]{1,0:T(8,128)S(1)}, f32[768,512]{1,0:T(8,128)}, u32[]{:S(2)}) %copy-start) | copy-done | bytes 1572888
  1.4 0.2 first.1.first_ref.refs_0_.refs_2_.refs_3_
  1.6 4.1 %collective-permute-start.6 = (bf16[512,512]{1,0:T(8,128)(2,1)S(1)}, bf16[512,512]{1,0:T(8,128)(2,1)S(1)}, u32[]{:S(2)}, u32[]{:S(2)}) collective-permute-start(bf16[512,512]{1,0:T(8,128)(2,1)S(1)} %first.1.first_ref.refs_0_.refs_2_.refs_3_), channel_id=1, source_target_pairs={{0,8},{1,9},{2,10},{3,11},{4,0},{5,1},{6,2},{7,3},{8,12},{9,13},{1... | collective-permute-start | bytes 1572872 | tf_op jit(solution)/shard_map/ppermute | solution.py:254
  5.7 1.5 %collective-permute-start.4 = (bf16[512,512]{1,0:T(8,128)(2,1)S(1)}, bf16[512,512]{1,0:T(8,128)(2,1)S(1)}, u32[]{:S(2)}, u32[]{:S(2)}) collective-permute-start(bf16[512,512]{1,0:T(8,128)(2,1)S(1)} %first.1.first_ref.refs_0_.refs_2_.refs_3_), channel_id=1, source_target_pairs={{0,2},{1,3},{2,0},{3,1},{4,6},{5,7},{6,4},{7,5},{8,10},{9,11},{10,... | collective-permute-start | bytes 1572872 | tf_op jit(solution)/shard_map/ppermute | solution.py:246
  7.3 0.2 rest.1
  7.4 0.6 %collective-permute-start.5 = (bf16[272,512]{1,0:T(8,128)(2,1)S(1)}, bf16[272,512]{1,0:T(8,128)(2,1)S(1)}, u32[]{:S(2)}, u32[]{:S(2)}) collective-permute-start(bf16[272,512]{1,0:T(8,128)(2,1)S(1)} %get-tuple-element.30.refs_1_.refs_3_.refs_4_), channel_id=1, source_target_pairs={{0,2},{1,3},{2,0},{3,1},{4,6},{5,7},{6,4},{7,5},{8,10},{9,11},{10,... | collective-permute-start | bytes 835592 | tf_op jit(solution)/shard_map/ppermute | solution.py:246
  8.0 1.6 %collective-permute-start.7 = (bf16[272,512]{1,0:T(8,128)(2,1)S(1)}, bf16[272,512]{1,0:T(8,128)(2,1)S(1)}, u32[]{:S(2)}, u32[]{:S(2)}) collective-permute-start(bf16[272,512]{1,0:T(8,128)(2,1)S(1)} %get-tuple-element.30.refs_1_.refs_3_.refs_4_), channel_id=1, source_target_pairs={{0,8},{1,9},{2,10},{3,11},{4,0},{5,1},{6,2},{7,3},{8,12},{9,13},{1... | collective-permute-start | bytes 835592 | tf_op jit(solution)/shard_map/ppermute | solution.py:254
  9.6 2.3 %collective-permute-start = (bf16[528,512]{1,0:T(8,128)(2,1)S(1)}, bf16[528,512]{1,0:T(8,128)(2,1)S(1)}, u32[]{:S(2)}, u32[]{:S(2)}) collective-permute-start(bf16[528,512]{1,0:T(8,128)(2,1)S(1)} %get-tuple-element.28), channel_id=1, source_target_pairs={{0,12},{1,13},{2,14},{3,15},{8,4},{9,5},{10,6},{11,7},{16,28},{17,... | collective-permute-start | bytes 1622024 | tf_op jit(solution)/shard_map/ppermute | solution.py:254
  11.9 13.1 %collective-permute-done.5.refs_3_.refs_8_.refs_7_ = bf16[272,512]{1,0:T(8,128)(2,1)S(1)} collective-permute-done((bf16[272,512]{1,0:T(8,128)(2,1)S(1)}, bf16[272,512]{1,0:T(8,128)(2,1)S(1)}, u32[]{:S(2)}, u32[]{:S(2)}) %collective-permute-start.5) | collective-permute-done | bytes 278560 | tf_op jit(solution)/shard_map/ppermute | solution.py:246
  25.1 0.5 %collective-permute-start.8 = (bf16[512,512]{1,0:T(8,128)(2,1)S(1)}, bf16[512,512]{1,0:T(8,128)(2,1)S(1)}, u32[]{:S(2)}, u32[]{:S(2)}) collective-permute-start(bf16[512,512]{1,0:T(8,128)(2,1)S(1)} %collective-permute-done.4.refs_2_.refs_7_.refs_6_), channel_id=1, source_target_pairs={{0,1},{1,0},{2,3},{3,2},{4,5},{5,4},{6,7},{7,6},{8,9},{9,8},{10,11... | collective-permute-start | bytes 1572872 | tf_op jit(solution)/shard_map/ppermute | solution.py:246
  25.6 0.4 collective-permute-start.3
  26.1 0.5 %collective-permute-done.9.refs_5_.refs_10_.refs_9_ = bf16[272,512]{1,0:T(8,128)(2,1)S(1)} collective-permute-done((bf16[272,512]{1,0:T(8,128)(2,1)S(1)}, bf16[272,512]{1,0:T(8,128)(2,1)S(1)}, u32[]{:S(2)}, u32[]{:S(2)}) %collective-permute-start.9) | collective-permute-done | bytes 278560 | tf_op jit(solution)/shard_map/ppermute | solution.py:246
  26.6 3.6 %collective-permute-start.1 = (bf16[256,512]{1,0:T(8,128)(2,1)S(1)}, bf16[256,512]{1,0:T(8,128)(2,1)S(1)}, u32[]{:S(2)}, u32[]{:S(2)}) collective-permute-start(bf16[256,512]{1,0:T(8,128)(2,1)S(1)} %get-tuple-element.29), channel_id=1, source_target_pairs={{0,12},{1,13},{2,14},{3,15},{8,4},{9,5},{10,6},{11,7},{16,28},{17,... | collective-permute-start | bytes 786440 | tf_op jit(solution)/shard_map/ppermute | solution.py:254
  30.2 1.4 %plane_far.1.refs_6_ = f32[8,128]{1,0:T(8,128)S(1)} custom-call(bf16[512,512]{1,0:T(8,128)(2,1)S(1)} %first.1.first_ref.refs_0_.refs_2_.refs_3_, bf16[272,512]{1,0:T(8,128)(2,1)S(1)} %get-tuple-element.30.refs_1_.refs_3_.refs_4_, bf16[512,512]{1,0:T(8,128)(2,1)S(1)} %collective-permute-done.4.refs_2_.refs_7_.refs_6_, ...), custom_call_target="tpu_custom_call" | custom-call | flops 1 | bytes 1 | tf_op jit(solution)/shard_map/plane_far/pallas_call | solution.py:223
  31.6 1.4 %plane_near.1.refs_12_ = f32[8,128]{1,0:T(8,128)S(1)} custom-call(bf16[512,512]{1,0:T(8,128)(2,1)S(1)} %first.1.first_ref.refs_0_.refs_2_.refs_3_, bf16[272,512]{1,0:T(8,128)(2,1)S(1)} %get-tuple-element.30.refs_1_.refs_3_.refs_4_, bf16[512,512]{1,0:T(8,128)(2,1)S(1)} %first.1.first_ref.refs_0_.refs_2_.refs_3_, ...), custom_call_target="tpu_custom_call" | custom-call | flops 1 | bytes 1 | tf_op jit(solution)/shard_map/plane_near/pallas_call | solution.py:223
  33.1 2.8 %cross.3 = (f32[8,128]{1,0:T(8,128)S(1)}, f32[8,128]{1,0:T(8,128)S(1)}, f32[8,128]{1,0:T(8,128)S(1)}, f32[8,128]{1,0:T(8,128)S(1)}, f32[8,128]{1,0:T(8,128)S(1)}) custom-call(bf16[272,512]{1,0:T(8,128)(2,1)S(1)} %collective-permute-done.7.refs_0_.refs_2_, bf16[512,512]{1,0:T(8,128)(2,1)S(1)} %collective-permute-done.6.refs_1_, ...), custom_call_target="tpu_custom_call" | custom-call | flops 1 | bytes 1 | tf_op jit(solution)/shard_map/cross/pallas_call | solution.py:223
  36.0 1.9 %cross.4 = (f32[8,128]{1,0:T(8,128)S(1)}, f32[8,128]{1,0:T(8,128)S(1)}, f32[8,128]{1,0:T(8,128)S(1)}, f32[8,128]{1,0:T(8,128)S(1)}, f32[8,128]{1,0:T(8,128)S(1)}) custom-call(bf16[528,512]{1,0:T(8,128)(2,1)S(1)} %collective-permute-done.refs_0_.refs_1_, bf16[528,512]{1,0:T(8,128)(2,1)S(1)} %collective-permute-done.refs_0_.refs_1_, ...), custom_call_target="tpu_custom_call" | custom-call | flops 1 | bytes 1 | tf_op jit(solution)/shard_map/cross/pallas_call | solution.py:223
  37.9 2.2 %collective-permute-done.1.refs_1_ = bf16[256,512]{1,0:T(8,128)(2,1)S(1)} collective-permute-done((bf16[256,512]{1,0:T(8,128)(2,1)S(1)}, bf16[256,512]{1,0:T(8,128)(2,1)S(1)}, u32[]{:S(2)}, u32[]{:S(2)}) %collective-permute-start.1) | collective-permute-done | bytes 262176 | tf_op jit(solution)/shard_map/ppermute | solution.py:254
  40.1 1.2 %cross.5 = (f32[8,128]{1,0:T(8,128)S(1)}, f32[8,128]{1,0:T(8,128)S(1)}, f32[8,128]{1,0:T(8,128)S(1)}, f32[8,128]{1,0:T(8,128)S(1)}, f32[8,128]{1,0:T(8,128)S(1)}) custom-call(bf16[528,512]{1,0:T(8,128)(2,1)S(1)} %collective-permute-done.refs_0_.refs_1_, bf16[256,512]{1,0:T(8,128)(2,1)S(1)} %collective-permute-done.1.refs_1_, ...), custom_call_target="tpu_custom_call" | custom-call | flops 1 | bytes 1 | tf_op jit(solution)/shard_map/cross/pallas_call | solution.py:223
  41.3 1.3 %collective-permute-start.11 = (f32[8,128]{1,0:T(8,128)S(1)}, f32[8,128]{1,0:T(8,128)S(1)}, u32[]{:S(2)}, u32[]{:S(2)}) collective-permute-start(f32[8,128]{1,0:T(8,128)S(1)} %get-tuple-element.44), channel_id=1, source_target_pairs={{12,0},{13,1},{14,2},{15,3},{4,8},{5,9},{6,10},{7,11},{28,16},{29,... | collective-permute-start | bytes 12296 | tf_op jit(solution)/shard_map/ppermute | solution.py:288
  42.7 1.6 %collective-permute-start.13 = (f32[8,128]{1,0:T(8,128)S(1)}, f32[8,128]{1,0:T(8,128)S(1)}, u32[]{:S(2)}, u32[]{:S(2)}) collective-permute-start(f32[8,128]{1,0:T(8,128)S(1)} %get-tuple-element.48), channel_id=1, source_target_pairs={{0,2},{1,3},{2,0},{3,1},{4,6},{5,7},{6,4},{7,5},{8,10},{9,11},{10,... | collective-permute-start | bytes 12296 | tf_op jit(solution)/shard_map/ppermute | solution.py:246
  44.2 0.3 collective-permute-start.12
  44.5 4.0 %collective-permute-done.11 = f32[8,128]{1,0:T(8,128)S(1)} collective-permute-done((f32[8,128]{1,0:T(8,128)S(1)}, f32[8,128]{1,0:T(8,128)S(1)}, u32[]{:S(2)}, u32[]{:S(2)}) %collective-permute-start.11) | collective-permute-done | bytes 4128 | tf_op jit(solution)/shard_map/ppermute | solution.py:288
  48.6 0.6 %maximum_bitcast_fusion = f32[768]{0:T(1024)} fusion(f32[8,128]{1,0:T(8,128)S(1)} %collective-permute-done.14, f32[8,128]{1,0:T(8,128)S(1)} %collective-permute-done.13, f32[8,128]{1,0:T(8,128)S(1)} %collective-permute-done.12, f32[8,128]{1,0:T(8,128)S(1)} %collective-permute-done.11, f32[8,128]{1,0:T(8,128)S(1)} %collective-permute-done.10, ...), kind=kLoop, calls=%fused_computation | loop fusion | flops 4608 | bytes 21505 | tf_op jit(solution)/shard_map/max | solution.py:298
  (27 shorter events, 0.3 us)
Async XLA Ops:
  0.0 1.4 %copy-start = (f32[768,512]{1,0:T(8,128)S(1)}, f32[768,512]{1,0:T(8,128)}, u32[]{:S(2)}) copy-start(f32[768,512]{1,0:T(8,128)} %embeddings_ref.3) | copy-start | bytes 4718596
  1.4 5.8 %copy-start.2 = (s32[768]{0:T(1024)S(1)}, s32[768]{0:T(1024)}, u32[]{:S(2)}) copy-start(s32[768]{0:T(1024)} %param.5) | copy-start | bytes 9220
  1.4 5.8 %copy-start.3 = (s32[768]{0:T(1024)S(1)}, s32[768]{0:T(1024)}, u32[]{:S(2)}) copy-start(s32[768]{0:T(1024)} %param.6) | copy-start | bytes 9220
  1.4 5.8 %copy-start.4 = (s32[16]{0:T(128)S(1)}, s32[16]{0:T(128)}, u32[]{:S(2)}) copy-start(s32[16]{0:T(128)} %param.7) | copy-start | bytes 196
  1.4 5.9 %copy-start.1 = (f32[768,512]{1,0:T(8,128)S(1)}, f32[768,512]{1,0:T(8,128)}, u32[]{:S(2)}) copy-start(f32[768,512]{1,0:T(8,128)} %embeddings_ref.3) | copy-start | bytes 4718596
  1.6 23.4 %collective-permute-start.6 = (bf16[512,512]{1,0:T(8,128)(2,1)S(1)}, bf16[512,512]{1,0:T(8,128)(2,1)S(1)}, u32[]{:S(2)}, u32[]{:S(2)}) collective-permute-start(bf16[512,512]{1,0:T(8,128)(2,1)S(1)} %first.1.first_ref.refs_0_.refs_2_.refs_3_), channel_id=1, source_target_pairs={{0,8},{1,9},{2,10},{3,11},{4,0},{5,1},{6,2},{7,3},{8,12},{9,13},{1... | collective-permute-start | bytes 1572872 | tf_op jit(solution)/shard_map/ppermute | solution.py:254
  5.7 19.4 %collective-permute-start.4 = (bf16[512,512]{1,0:T(8,128)(2,1)S(1)}, bf16[512,512]{1,0:T(8,128)(2,1)S(1)}, u32[]{:S(2)}, u32[]{:S(2)}) collective-permute-start(bf16[512,512]{1,0:T(8,128)(2,1)S(1)} %first.1.first_ref.refs_0_.refs_2_.refs_3_), channel_id=1, source_target_pairs={{0,2},{1,3},{2,0},{3,1},{4,6},{5,7},{6,4},{7,5},{8,10},{9,11},{10,... | collective-permute-start | bytes 1572872 | tf_op jit(solution)/shard_map/ppermute | solution.py:246
  7.4 17.6 %collective-permute-start.5 = (bf16[272,512]{1,0:T(8,128)(2,1)S(1)}, bf16[272,512]{1,0:T(8,128)(2,1)S(1)}, u32[]{:S(2)}, u32[]{:S(2)}) collective-permute-start(bf16[272,512]{1,0:T(8,128)(2,1)S(1)} %get-tuple-element.30.refs_1_.refs_3_.refs_4_), channel_id=1, source_target_pairs={{0,2},{1,3},{2,0},{3,1},{4,6},{5,7},{6,4},{7,5},{8,10},{9,11},{10,... | collective-permute-start | bytes 835592 | tf_op jit(solution)/shard_map/ppermute | solution.py:246
  8.0 17.0 %collective-permute-start.7 = (bf16[272,512]{1,0:T(8,128)(2,1)S(1)}, bf16[272,512]{1,0:T(8,128)(2,1)S(1)}, u32[]{:S(2)}, u32[]{:S(2)}) collective-permute-start(bf16[272,512]{1,0:T(8,128)(2,1)S(1)} %get-tuple-element.30.refs_1_.refs_3_.refs_4_), channel_id=1, source_target_pairs={{0,8},{1,9},{2,10},{3,11},{4,0},{5,1},{6,2},{7,3},{8,12},{9,13},{1... | collective-permute-start | bytes 835592 | tf_op jit(solution)/shard_map/ppermute | solution.py:254
  9.6 26.4 %collective-permute-start = (bf16[528,512]{1,0:T(8,128)(2,1)S(1)}, bf16[528,512]{1,0:T(8,128)(2,1)S(1)}, u32[]{:S(2)}, u32[]{:S(2)}) collective-permute-start(bf16[528,512]{1,0:T(8,128)(2,1)S(1)} %get-tuple-element.28), channel_id=1, source_target_pairs={{0,12},{1,13},{2,14},{3,15},{8,4},{9,5},{10,6},{11,7},{16,28},{17,... | collective-permute-start | bytes 1622024 | tf_op jit(solution)/shard_map/ppermute | solution.py:254
  25.0 1.6 %collective-permute-start.9 = (bf16[272,512]{1,0:T(8,128)(2,1)S(1)}, bf16[272,512]{1,0:T(8,128)(2,1)S(1)}, u32[]{:S(2)}, u32[]{:S(2)}) collective-permute-start(bf16[272,512]{1,0:T(8,128)(2,1)S(1)} %collective-permute-done.5.refs_3_.refs_8_.refs_7_), channel_id=1, source_target_pairs={{0,1},{1,0},{2,3},{3,2},{4,5},{5,4},{6,7},{7,6},{8,9},{9,8},{10,11... | collective-permute-start | bytes 835592 | tf_op jit(solution)/shard_map/ppermute | solution.py:246
  25.1 5.1 %collective-permute-start.8 = (bf16[512,512]{1,0:T(8,128)(2,1)S(1)}, bf16[512,512]{1,0:T(8,128)(2,1)S(1)}, u32[]{:S(2)}, u32[]{:S(2)}) collective-permute-start(bf16[512,512]{1,0:T(8,128)(2,1)S(1)} %collective-permute-done.4.refs_2_.refs_7_.refs_6_), channel_id=1, source_target_pairs={{0,1},{1,0},{2,3},{3,2},{4,5},{5,4},{6,7},{7,6},{8,9},{9,8},{10,11... | collective-permute-start | bytes 1572872 | tf_op jit(solution)/shard_map/ppermute | solution.py:246
  25.6 6.1 %collective-permute-start.2 = (bf16[512,512]{1,0:T(8,128)(2,1)S(1)}, bf16[512,512]{1,0:T(8,128)(2,1)S(1)}, u32[]{:S(2)}, u32[]{:S(2)}) collective-permute-start(bf16[512,512]{1,0:T(8,128)(2,1)S(1)} %first.1.first_ref.refs_0_.refs_2_.refs_3_), channel_id=1, source_target_pairs={{0,1},{1,0},{2,3},{3,2},{4,5},{5,4},{6,7},{7,6},{8,9},{9,8},{10,11... | collective-permute-start | bytes 1572872 | tf_op jit(solution)/shard_map/ppermute | solution.py:246
  25.6 6.0 %collective-permute-start.3 = (bf16[272,512]{1,0:T(8,128)(2,1)S(1)}, bf16[272,512]{1,0:T(8,128)(2,1)S(1)}, u32[]{:S(2)}, u32[]{:S(2)}) collective-permute-start(bf16[272,512]{1,0:T(8,128)(2,1)S(1)} %get-tuple-element.30.refs_1_.refs_3_.refs_4_), channel_id=1, source_target_pairs={{0,1},{1,0},{2,3},{3,2},{4,5},{5,4},{6,7},{7,6},{8,9},{9,8},{10,11... | collective-permute-start | bytes 835592 | tf_op jit(solution)/shard_map/ppermute | solution.py:246
  26.6 13.5 %collective-permute-start.1 = (bf16[256,512]{1,0:T(8,128)(2,1)S(1)}, bf16[256,512]{1,0:T(8,128)(2,1)S(1)}, u32[]{:S(2)}, u32[]{:S(2)}) collective-permute-start(bf16[256,512]{1,0:T(8,128)(2,1)S(1)} %get-tuple-element.29), channel_id=1, source_target_pairs={{0,12},{1,13},{2,14},{3,15},{8,4},{9,5},{10,6},{11,7},{16,28},{17,... | collective-permute-start | bytes 786440 | tf_op jit(solution)/shard_map/ppermute | solution.py:254
  35.9 6.7 %collective-permute-start.10 = (f32[8,128]{1,0:T(8,128)S(1)}, f32[8,128]{1,0:T(8,128)S(1)}, u32[]{:S(2)}, u32[]{:S(2)}) collective-permute-start(f32[8,128]{1,0:T(8,128)S(1)} %get-tuple-element.43), channel_id=1, source_target_pairs={{8,0},{9,1},{10,2},{11,3},{0,4},{1,5},{2,6},{3,7},{12,8},{13,9},{1... | collective-permute-start | bytes 12296 | tf_op jit(solution)/shard_map/ppermute | solution.py:288
  41.3 7.3 %collective-permute-start.11 = (f32[8,128]{1,0:T(8,128)S(1)}, f32[8,128]{1,0:T(8,128)S(1)}, u32[]{:S(2)}, u32[]{:S(2)}) collective-permute-start(f32[8,128]{1,0:T(8,128)S(1)} %get-tuple-element.44), channel_id=1, source_target_pairs={{12,0},{13,1},{14,2},{15,3},{4,8},{5,9},{6,10},{7,11},{28,16},{29,... | collective-permute-start | bytes 12296 | tf_op jit(solution)/shard_map/ppermute | solution.py:288
  42.6 6.0 %collective-permute-start.14 = (f32[8,128]{1,0:T(8,128)S(1)}, f32[8,128]{1,0:T(8,128)S(1)}, u32[]{:S(2)}, u32[]{:S(2)}) collective-permute-start(f32[8,128]{1,0:T(8,128)S(1)} %get-tuple-element.50), channel_id=1, source_target_pairs={{0,1},{1,0},{2,3},{3,2},{4,5},{5,4},{6,7},{7,6},{8,9},{9,8},{10,11... | collective-permute-start | bytes 12296 | tf_op jit(solution)/shard_map/ppermute | solution.py:246
  42.7 5.9 %collective-permute-start.13 = (f32[8,128]{1,0:T(8,128)S(1)}, f32[8,128]{1,0:T(8,128)S(1)}, u32[]{:S(2)}, u32[]{:S(2)}) collective-permute-start(f32[8,128]{1,0:T(8,128)S(1)} %get-tuple-element.48), channel_id=1, source_target_pairs={{0,2},{1,3},{2,0},{3,1},{4,6},{5,7},{6,4},{7,5},{8,10},{9,11},{10,... | collective-permute-start | bytes 12296 | tf_op jit(solution)/shard_map/ppermute | solution.py:246
  44.2 4.3 %collective-permute-start.12 = (f32[8,128]{1,0:T(8,128)S(1)}, f32[8,128]{1,0:T(8,128)S(1)}, u32[]{:S(2)}, u32[]{:S(2)}) collective-permute-start(f32[8,128]{1,0:T(8,128)S(1)} %get-tuple-element.46), channel_id=1, source_target_pairs={{0,3},{1,2},{2,1},{3,0},{4,7},{5,6},{6,5},{7,4},{8,11},{9,10},{10,... | collective-permute-start | bytes 12296 | tf_op jit(solution)/shard_map/ppermute | solution.py:246

commit v22 on v14

--- a/solution.py
+++ b/solution.py
@@ -294,7 +294,7 @@
         backs.append(mate(after(plane_best[distance], *backs[:1]), distance))
     for n, back in enumerate(backs):
         back = back.reshape(-1)[:rows]
-        best = jnp.maximum(best, jnp.where(masks[n], back, -1.0) if n in masks else back)
+        best = jnp.maximum(jnp.where(masks[n], back, -1.0) if n in masks else back, best)
     return best
 
 

time: 49.4 us -> 49.4 us (level)
  no operation moved by 1% of the time
where the time goes in v22:
time: 49.4 us; the launch traced here: 49.2 us
  waiting for transfers between devices  19.9 us (40%)
  starting transfers between devices  17.9 us (36%)
  Pallas kernels  9.08 us (18%)
  local copies, waits for them, and re-layouts  1.51 us (3%)
  other arithmetic  0.6 us (1%)
    ppermute x9, waiting for transfers between devices, mate(): return lax.ppermute(value, 'dp', [(i, i ^ distance) for i in range(peers)])  13.7 us
    ppermute x4, starting transfers between devices, local(): away.append((pairs, [lax.ppermute(part, 'dp', pairs) for part in parts]))  11.5 us
    pallas_call x7, Pallas kernels, kernel(): pl.pallas_call(body, out_shape=tuple(outputs), in_specs=whole(len(inputs)...  9.08 us
    ppermute x9, starting transfers between devices, mate(): return lax.ppermute(value, 'dp', [(i, i ^ distance) for i in range(peers)])  5.03 us
    ppermute x2, waiting for transfers between devices, local(): backs.append(lax.ppermute(away_best, 'dp', [(t, s) for s, t in pairs]))  4.06 us
    ppermute x4, waiting for transfers between devices, local(): away.append((pairs, [lax.ppermute(part, 'dp', pairs) for part in parts]))  2.19 us
    unnamed x10, local copies, waits for them, and re-layouts  1.42 us
    ppermute x2, starting transfers between devices, local(): backs.append(lax.ppermute(away_best, 'dp', [(t, s) for s, t in pairs]))  1.35 us
  transfers between devices with their start and end apart: 15, of which 4 were waited for; matrix products, arithmetic and copies ran while one was open for 0% of the time, Pallas kernels for 18%

profile of v22, /device:TPU:0, one launch (start us, length us, event | category | flops | bytes accessed | tf_op | source)
XLA Modules:
  0.0 49.2 jit_solution(12401859252565502233)
XLA Ops:
  0.0 1.4 %copy-done = f32[768,512]{1,0:T(8,128)S(1)} copy-done((f32[768,512]{1,0:T(8,128)S(1)}, f32[768,512]{1,0:T(8,128)}, u32[]{:S(2)}) %copy-start) | copy-done | bytes 1572888
  1.4 0.2 first.1.first_ref.refs_0_.refs_2_.refs_3_
  1.6 4.1 %collective-permute-start.6 = (bf16[512,512]{1,0:T(8,128)(2,1)S(1)}, bf16[512,512]{1,0:T(8,128)(2,1)S(1)}, u32[]{:S(2)}, u32[]{:S(2)}) collective-permute-start(bf16[512,512]{1,0:T(8,128)(2,1)S(1)} %first.1.first_ref.refs_0_.refs_2_.refs_3_), channel_id=1, source_target_pairs={{0,8},{1,9},{2,10},{3,11},{4,0},{5,1},{6,2},{7,3},{8,12},{9,13},{1... | collective-permute-start | bytes 1572872 | tf_op jit(solution)/shard_map/ppermute | solution.py:253
  5.7 1.5 %collective-permute-start.4 = (bf16[512,512]{1,0:T(8,128)(2,1)S(1)}, bf16[512,512]{1,0:T(8,128)(2,1)S(1)}, u32[]{:S(2)}, u32[]{:S(2)}) collective-permute-start(bf16[512,512]{1,0:T(8,128)(2,1)S(1)} %first.1.first_ref.refs_0_.refs_2_.refs_3_), channel_id=1, source_target_pairs={{0,2},{1,3},{2,0},{3,1},{4,6},{5,7},{6,4},{7,5},{8,10},{9,11},{10,... | collective-permute-start | bytes 1572872 | tf_op jit(solution)/shard_map/ppermute | solution.py:245
  7.4 0.6 %collective-permute-start.5 = (bf16[272,512]{1,0:T(8,128)(2,1)S(1)}, bf16[272,512]{1,0:T(8,128)(2,1)S(1)}, u32[]{:S(2)}, u32[]{:S(2)}) collective-permute-start(bf16[272,512]{1,0:T(8,128)(2,1)S(1)} %get-tuple-element.30.refs_1_.refs_3_.refs_4_), channel_id=1, source_target_pairs={{0,2},{1,3},{2,0},{3,1},{4,6},{5,7},{6,4},{7,5},{8,10},{9,11},{10,... | collective-permute-start | bytes 835592 | tf_op jit(solution)/shard_map/ppermute | solution.py:245
  8.0 1.6 %collective-permute-start.7 = (bf16[272,512]{1,0:T(8,128)(2,1)S(1)}, bf16[272,512]{1,0:T(8,128)(2,1)S(1)}, u32[]{:S(2)}, u32[]{:S(2)}) collective-permute-start(bf16[272,512]{1,0:T(8,128)(2,1)S(1)} %get-tuple-element.30.refs_1_.refs_3_.refs_4_), channel_id=1, source_target_pairs={{0,8},{1,9},{2,10},{3,11},{4,0},{5,1},{6,2},{7,3},{8,12},{9,13},{1... | collective-permute-start | bytes 835592 | tf_op jit(solution)/shard_map/ppermute | solution.py:253
  9.6 2.3 %collective-permute-start = (bf16[528,512]{1,0:T(8,128)(2,1)S(1)}, bf16[528,512]{1,0:T(8,128)(2,1)S(1)}, u32[]{:S(2)}, u32[]{:S(2)}) collective-permute-start(bf16[528,512]{1,0:T(8,128)(2,1)S(1)} %get-tuple-element.28), channel_id=1, source_target_pairs={{0,12},{1,13},{2,14},{3,15},{8,4},{9,5},{10,6},{11,7},{16,28},{17,... | collective-permute-start | bytes 1622024 | tf_op jit(solution)/shard_map/ppermute | solution.py:253
  11.9 13.1 %collective-permute-done.5.refs_3_.refs_8_.refs_7_ = bf16[272,512]{1,0:T(8,128)(2,1)S(1)} collective-permute-done((bf16[272,512]{1,0:T(8,128)(2,1)S(1)}, bf16[272,512]{1,0:T(8,128)(2,1)S(1)}, u32[]{:S(2)}, u32[]{:S(2)}) %collective-permute-start.5) | collective-permute-done | bytes 278560 | tf_op jit(solution)/shard_map/ppermute | solution.py:245
  25.1 0.5 %collective-permute-start.8 = (bf16[512,512]{1,0:T(8,128)(2,1)S(1)}, bf16[512,512]{1,0:T(8,128)(2,1)S(1)}, u32[]{:S(2)}, u32[]{:S(2)}) collective-permute-start(bf16[512,512]{1,0:T(8,128)(2,1)S(1)} %collective-permute-done.4.refs_2_.refs_7_.refs_6_), channel_id=1, source_target_pairs={{0,1},{1,0},{2,3},{3,2},{4,5},{5,4},{6,7},{7,6},{8,9},{9,8},{10,11... | collective-permute-start | bytes 1572872 | tf_op jit(solution)/shard_map/ppermute | solution.py:245
  25.6 0.4 collective-permute-start.3
  26.1 0.5 %collective-permute-done.9.refs_5_.refs_10_.refs_9_ = bf16[272,512]{1,0:T(8,128)(2,1)S(1)} collective-permute-done((bf16[272,512]{1,0:T(8,128)(2,1)S(1)}, bf16[272,512]{1,0:T(8,128)(2,1)S(1)}, u32[]{:S(2)}, u32[]{:S(2)}) %collective-permute-start.9) | collective-permute-done | bytes 278560 | tf_op jit(solution)/shard_map/ppermute | solution.py:245
  26.6 3.6 %collective-permute-start.1 = (bf16[256,512]{1,0:T(8,128)(2,1)S(1)}, bf16[256,512]{1,0:T(8,128)(2,1)S(1)}, u32[]{:S(2)}, u32[]{:S(2)}) collective-permute-start(bf16[256,512]{1,0:T(8,128)(2,1)S(1)} %get-tuple-element.29), channel_id=1, source_target_pairs={{0,12},{1,13},{2,14},{3,15},{8,4},{9,5},{10,6},{11,7},{16,28},{17,... | collective-permute-start | bytes 786440 | tf_op jit(solution)/shard_map/ppermute | solution.py:253
  30.2 1.4 %plane_far.1.refs_6_ = f32[8,128]{1,0:T(8,128)S(1)} custom-call(bf16[512,512]{1,0:T(8,128)(2,1)S(1)} %first.1.first_ref.refs_0_.refs_2_.refs_3_, bf16[272,512]{1,0:T(8,128)(2,1)S(1)} %get-tuple-element.30.refs_1_.refs_3_.refs_4_, bf16[512,512]{1,0:T(8,128)(2,1)S(1)} %collective-permute-done.4.refs_2_.refs_7_.refs_6_, ...), custom_call_target="tpu_custom_call" | custom-call | flops 1 | bytes 1 | tf_op jit(solution)/shard_map/plane_far/pallas_call | solution.py:222
  31.6 1.4 %plane_near.1.refs_12_ = f32[8,128]{1,0:T(8,128)S(1)} custom-call(bf16[512,512]{1,0:T(8,128)(2,1)S(1)} %first.1.first_ref.refs_0_.refs_2_.refs_3_, bf16[272,512]{1,0:T(8,128)(2,1)S(1)} %get-tuple-element.30.refs_1_.refs_3_.refs_4_, bf16[512,512]{1,0:T(8,128)(2,1)S(1)} %first.1.first_ref.refs_0_.refs_2_.refs_3_, ...), custom_call_target="tpu_custom_call" | custom-call | flops 1 | bytes 1 | tf_op jit(solution)/shard_map/plane_near/pallas_call | solution.py:222
  33.1 2.8 %cross.3 = (f32[8,128]{1,0:T(8,128)S(1)}, f32[8,128]{1,0:T(8,128)S(1)}, f32[8,128]{1,0:T(8,128)S(1)}, f32[8,128]{1,0:T(8,128)S(1)}, f32[8,128]{1,0:T(8,128)S(1)}) custom-call(bf16[272,512]{1,0:T(8,128)(2,1)S(1)} %collective-permute-done.7.refs_0_.refs_2_, bf16[512,512]{1,0:T(8,128)(2,1)S(1)} %collective-permute-done.6.refs_1_, ...), custom_call_target="tpu_custom_call" | custom-call | flops 1 | bytes 1 | tf_op jit(solution)/shard_map/cross/pallas_call | solution.py:222
  36.0 1.9 %cross.4 = (f32[8,128]{1,0:T(8,128)S(1)}, f32[8,128]{1,0:T(8,128)S(1)}, f32[8,128]{1,0:T(8,128)S(1)}, f32[8,128]{1,0:T(8,128)S(1)}, f32[8,128]{1,0:T(8,128)S(1)}) custom-call(bf16[528,512]{1,0:T(8,128)(2,1)S(1)} %collective-permute-done.refs_0_.refs_1_, bf16[528,512]{1,0:T(8,128)(2,1)S(1)} %collective-permute-done.refs_0_.refs_1_, ...), custom_call_target="tpu_custom_call" | custom-call | flops 1 | bytes 1 | tf_op jit(solution)/shard_map/cross/pallas_call | solution.py:222
  37.9 2.2 %collective-permute-done.1.refs_1_ = bf16[256,512]{1,0:T(8,128)(2,1)S(1)} collective-permute-done((bf16[256,512]{1,0:T(8,128)(2,1)S(1)}, bf16[256,512]{1,0:T(8,128)(2,1)S(1)}, u32[]{:S(2)}, u32[]{:S(2)}) %collective-permute-start.1) | collective-permute-done | bytes 262176 | tf_op jit(solution)/shard_map/ppermute | solution.py:253
  40.1 1.2 %cross.5 = (f32[8,128]{1,0:T(8,128)S(1)}, f32[8,128]{1,0:T(8,128)S(1)}, f32[8,128]{1,0:T(8,128)S(1)}, f32[8,128]{1,0:T(8,128)S(1)}, f32[8,128]{1,0:T(8,128)S(1)}) custom-call(bf16[528,512]{1,0:T(8,128)(2,1)S(1)} %collective-permute-done.refs_0_.refs_1_, bf16[256,512]{1,0:T(8,128)(2,1)S(1)} %collective-permute-done.1.refs_1_, ...), custom_call_target="tpu_custom_call" | custom-call | flops 1 | bytes 1 | tf_op jit(solution)/shard_map/cross/pallas_call | solution.py:222
  41.3 1.3 %collective-permute-start.14 = (f32[8,128]{1,0:T(8,128)S(1)}, f32[8,128]{1,0:T(8,128)S(1)}, u32[]{:S(2)}, u32[]{:S(2)}) collective-permute-start(f32[8,128]{1,0:T(8,128)S(1)} %get-tuple-element.49), channel_id=1, source_target_pairs={{12,0},{13,1},{14,2},{15,3},{4,8},{5,9},{6,10},{7,11},{28,16},{29,... | collective-permute-start | bytes 12296 | tf_op jit(solution)/shard_map/ppermute | solution.py:287
  42.6 0.2 collective-permute-start.13
  42.8 1.5 %collective-permute-start.12 = (f32[8,128]{1,0:T(8,128)S(1)}, f32[8,128]{1,0:T(8,128)S(1)}, u32[]{:S(2)}, u32[]{:S(2)}) collective-permute-start(f32[8,128]{1,0:T(8,128)S(1)} %get-tuple-element.46), channel_id=1, source_target_pairs={{0,2},{1,3},{2,0},{3,1},{4,6},{5,7},{6,4},{7,5},{8,10},{9,11},{10,... | collective-permute-start | bytes 12296 | tf_op jit(solution)/shard_map/ppermute | solution.py:245
  44.2 0.3 collective-permute-start.11
  44.5 4.1 %collective-permute-done.14 = f32[8,128]{1,0:T(8,128)S(1)} collective-permute-done((f32[8,128]{1,0:T(8,128)S(1)}, f32[8,128]{1,0:T(8,128)S(1)}, u32[]{:S(2)}, u32[]{:S(2)}) %collective-permute-start.14) | collective-permute-done | bytes 4128 | tf_op jit(solution)/shard_map/ppermute | solution.py:287
  48.6 0.6 %maximum_bitcast_fusion = f32[768]{0:T(1024)} fusion(f32[8,128]{1,0:T(8,128)S(1)} %get-tuple-element.50, f32[8,128]{1,0:T(8,128)S(1)} %collective-permute-done.10, f32[8,128]{1,0:T(8,128)S(1)} %collective-permute-done.14, f32[8,128]{1,0:T(8,128)S(1)} %collective-permute-done.13, f32[8,128]{1,0:T(8,128)S(1)} %collective-permute-done.12, ...), kind=kLoop, calls=%fused_computation | loop fusion | flops 4608 | bytes 21505 | tf_op jit(solution)/shard_map/max | solution.py:297
  (27 shorter events, 0.4 us)
Async XLA Ops:
  0.0 1.4 %copy-start = (f32[768,512]{1,0:T(8,128)S(1)}, f32[768,512]{1,0:T(8,128)}, u32[]{:S(2)}) copy-start(f32[768,512]{1,0:T(8,128)} %embeddings_ref.3) | copy-start | bytes 4718596
  1.4 5.8 %copy-start.2 = (s32[768]{0:T(1024)S(1)}, s32[768]{0:T(1024)}, u32[]{:S(2)}) copy-start(s32[768]{0:T(1024)} %param.5) | copy-start | bytes 9220
  1.4 5.8 %copy-start.3 = (s32[768]{0:T(1024)S(1)}, s32[768]{0:T(1024)}, u32[]{:S(2)}) copy-start(s32[768]{0:T(1024)} %param.6) | copy-start | bytes 9220
  1.4 5.8 %copy-start.4 = (s32[16]{0:T(128)S(1)}, s32[16]{0:T(128)}, u32[]{:S(2)}) copy-start(s32[16]{0:T(128)} %param.7) | copy-start | bytes 196
  1.4 5.9 %copy-start.1 = (f32[768,512]{1,0:T(8,128)S(1)}, f32[768,512]{1,0:T(8,128)}, u32[]{:S(2)}) copy-start(f32[768,512]{1,0:T(8,128)} %embeddings_ref.3) | copy-start | bytes 4718596
  1.6 23.4 %collective-permute-start.6 = (bf16[512,512]{1,0:T(8,128)(2,1)S(1)}, bf16[512,512]{1,0:T(8,128)(2,1)S(1)}, u32[]{:S(2)}, u32[]{:S(2)}) collective-permute-start(bf16[512,512]{1,0:T(8,128)(2,1)S(1)} %first.1.first_ref.refs_0_.refs_2_.refs_3_), channel_id=1, source_target_pairs={{0,8},{1,9},{2,10},{3,11},{4,0},{5,1},{6,2},{7,3},{8,12},{9,13},{1... | collective-permute-start | bytes 1572872 | tf_op jit(solution)/shard_map/ppermute | solution.py:253
  5.7 19.4 %collective-permute-start.4 = (bf16[512,512]{1,0:T(8,128)(2,1)S(1)}, bf16[512,512]{1,0:T(8,128)(2,1)S(1)}, u32[]{:S(2)}, u32[]{:S(2)}) collective-permute-start(bf16[512,512]{1,0:T(8,128)(2,1)S(1)} %first.1.first_ref.refs_0_.refs_2_.refs_3_), channel_id=1, source_target_pairs={{0,2},{1,3},{2,0},{3,1},{4,6},{5,7},{6,4},{7,5},{8,10},{9,11},{10,... | collective-permute-start | bytes 1572872 | tf_op jit(solution)/shard_map/ppermute | solution.py:245
  7.4 17.6 %collective-permute-start.5 = (bf16[272,512]{1,0:T(8,128)(2,1)S(1)}, bf16[272,512]{1,0:T(8,128)(2,1)S(1)}, u32[]{:S(2)}, u32[]{:S(2)}) collective-permute-start(bf16[272,512]{1,0:T(8,128)(2,1)S(1)} %get-tuple-element.30.refs_1_.refs_3_.refs_4_), channel_id=1, source_target_pairs={{0,2},{1,3},{2,0},{3,1},{4,6},{5,7},{6,4},{7,5},{8,10},{9,11},{10,... | collective-permute-start | bytes 835592 | tf_op jit(solution)/shard_map/ppermute | solution.py:245
  8.0 17.0 %collective-permute-start.7 = (bf16[272,512]{1,0:T(8,128)(2,1)S(1)}, bf16[272,512]{1,0:T(8,128)(2,1)S(1)}, u32[]{:S(2)}, u32[]{:S(2)}) collective-permute-start(bf16[272,512]{1,0:T(8,128)(2,1)S(1)} %get-tuple-element.30.refs_1_.refs_3_.refs_4_), channel_id=1, source_target_pairs={{0,8},{1,9},{2,10},{3,11},{4,0},{5,1},{6,2},{7,3},{8,12},{9,13},{1... | collective-permute-start | bytes 835592 | tf_op jit(solution)/shard_map/ppermute | solution.py:253
  9.6 26.4 %collective-permute-start = (bf16[528,512]{1,0:T(8,128)(2,1)S(1)}, bf16[528,512]{1,0:T(8,128)(2,1)S(1)}, u32[]{:S(2)}, u32[]{:S(2)}) collective-permute-start(bf16[528,512]{1,0:T(8,128)(2,1)S(1)} %get-tuple-element.28), channel_id=1, source_target_pairs={{0,12},{1,13},{2,14},{3,15},{8,4},{9,5},{10,6},{11,7},{16,28},{17,... | collective-permute-start | bytes 1622024 | tf_op jit(solution)/shard_map/ppermute | solution.py:253
  25.0 1.6 %collective-permute-start.9 = (bf16[272,512]{1,0:T(8,128)(2,1)S(1)}, bf16[272,512]{1,0:T(8,128)(2,1)S(1)}, u32[]{:S(2)}, u32[]{:S(2)}) collective-permute-start(bf16[272,512]{1,0:T(8,128)(2,1)S(1)} %collective-permute-done.5.refs_3_.refs_8_.refs_7_), channel_id=1, source_target_pairs={{0,1},{1,0},{2,3},{3,2},{4,5},{5,4},{6,7},{7,6},{8,9},{9,8},{10,11... | collective-permute-start | bytes 835592 | tf_op jit(solution)/shard_map/ppermute | solution.py:245
  25.1 5.1 %collective-permute-start.8 = (bf16[512,512]{1,0:T(8,128)(2,1)S(1)}, bf16[512,512]{1,0:T(8,128)(2,1)S(1)}, u32[]{:S(2)}, u32[]{:S(2)}) collective-permute-start(bf16[512,512]{1,0:T(8,128)(2,1)S(1)} %collective-permute-done.4.refs_2_.refs_7_.refs_6_), channel_id=1, source_target_pairs={{0,1},{1,0},{2,3},{3,2},{4,5},{5,4},{6,7},{7,6},{8,9},{9,8},{10,11... | collective-permute-start | bytes 1572872 | tf_op jit(solution)/shard_map/ppermute | solution.py:245
  25.6 6.1 %collective-permute-start.2 = (bf16[512,512]{1,0:T(8,128)(2,1)S(1)}, bf16[512,512]{1,0:T(8,128)(2,1)S(1)}, u32[]{:S(2)}, u32[]{:S(2)}) collective-permute-start(bf16[512,512]{1,0:T(8,128)(2,1)S(1)} %first.1.first_ref.refs_0_.refs_2_.refs_3_), channel_id=1, source_target_pairs={{0,1},{1,0},{2,3},{3,2},{4,5},{5,4},{6,7},{7,6},{8,9},{9,8},{10,11... | collective-permute-start | bytes 1572872 | tf_op jit(solution)/shard_map/ppermute | solution.py:245
  25.6 6.0 %collective-permute-start.3 = (bf16[272,512]{1,0:T(8,128)(2,1)S(1)}, bf16[272,512]{1,0:T(8,128)(2,1)S(1)}, u32[]{:S(2)}, u32[]{:S(2)}) collective-permute-start(bf16[272,512]{1,0:T(8,128)(2,1)S(1)} %get-tuple-element.30.refs_1_.refs_3_.refs_4_), channel_id=1, source_target_pairs={{0,1},{1,0},{2,3},{3,2},{4,5},{5,4},{6,7},{7,6},{8,9},{9,8},{10,11... | collective-permute-start | bytes 835592 | tf_op jit(solution)/shard_map/ppermute | solution.py:245
  26.6 13.5 %collective-permute-start.1 = (bf16[256,512]{1,0:T(8,128)(2,1)S(1)}, bf16[256,512]{1,0:T(8,128)(2,1)S(1)}, u32[]{:S(2)}, u32[]{:S(2)}) collective-permute-start(bf16[256,512]{1,0:T(8,128)(2,1)S(1)} %get-tuple-element.29), channel_id=1, source_target_pairs={{0,12},{1,13},{2,14},{3,15},{8,4},{9,5},{10,6},{11,7},{16,28},{17,... | collective-permute-start | bytes 786440 | tf_op jit(solution)/shard_map/ppermute | solution.py:253
  35.9 6.7 %collective-permute-start.10 = (f32[8,128]{1,0:T(8,128)S(1)}, f32[8,128]{1,0:T(8,128)S(1)}, u32[]{:S(2)}, u32[]{:S(2)}) collective-permute-start(f32[8,128]{1,0:T(8,128)S(1)} %get-tuple-element.43), channel_id=1, source_target_pairs={{8,0},{9,1},{10,2},{11,3},{0,4},{1,5},{2,6},{3,7},{12,8},{13,9},{1... | collective-permute-start | bytes 12296 | tf_op jit(solution)/shard_map/ppermute | solution.py:287
  41.3 7.3 %collective-permute-start.14 = (f32[8,128]{1,0:T(8,128)S(1)}, f32[8,128]{1,0:T(8,128)S(1)}, u32[]{:S(2)}, u32[]{:S(2)}) collective-permute-start(f32[8,128]{1,0:T(8,128)S(1)} %get-tuple-element.49), channel_id=1, source_target_pairs={{12,0},{13,1},{14,2},{15,3},{4,8},{5,9},{6,10},{7,11},{28,16},{29,... | collective-permute-start | bytes 12296 | tf_op jit(solution)/shard_map/ppermute | solution.py:287
  42.6 6.0 %collective-permute-start.13 = (f32[8,128]{1,0:T(8,128)S(1)}, f32[8,128]{1,0:T(8,128)S(1)}, u32[]{:S(2)}, u32[]{:S(2)}) collective-permute-start(f32[8,128]{1,0:T(8,128)S(1)} %get-tuple-element.48), channel_id=1, source_target_pairs={{0,3},{1,2},{2,1},{3,0},{4,7},{5,6},{6,5},{7,4},{8,11},{9,10},{10,... | collective-permute-start | bytes 12296 | tf_op jit(solution)/shard_map/ppermute | solution.py:245
  42.8 5.8 %collective-permute-start.12 = (f32[8,128]{1,0:T(8,128)S(1)}, f32[8,128]{1,0:T(8,128)S(1)}, u32[]{:S(2)}, u32[]{:S(2)}) collective-permute-start(f32[8,128]{1,0:T(8,128)S(1)} %get-tuple-element.46), channel_id=1, source_target_pairs={{0,2},{1,3},{2,0},{3,1},{4,6},{5,7},{6,4},{7,5},{8,10},{9,11},{10,... | collective-permute-start | bytes 12296 | tf_op jit(solution)/shard_map/ppermute | solution.py:245
  44.2 4.3 %collective-permute-start.11 = (f32[8,128]{1,0:T(8,128)S(1)}, f32[8,128]{1,0:T(8,128)S(1)}, u32[]{:S(2)}, u32[]{:S(2)}) collective-permute-start(f32[8,128]{1,0:T(8,128)S(1)} %get-tuple-element.44), channel_id=1, source_target_pairs={{0,1},{1,0},{2,3},{3,2},{4,5},{5,4},{6,7},{7,6},{8,9},{9,8},{10,11... | collective-permute-start | bytes 12296 | tf_op jit(solution)/shard_map/ppermute | solution.py:245
